TPU v7x, 32 devices: a whole 2x2x4 slice. The times are simulated.
32 devices in a mesh: seq: 8 (over z, x), tp: 4 (over y, core).
Axes of the slice: x: 2, y: 2, z: 4, core: 2. Of those that a mesh axis runs over, the one named last changes fastest.
Arguments:
- token_inputs: bfloat16 [4, 64, 5120], P(None, 'seq'), may hold values from -6 to 6
- attn_gain: float32 [5120], replicated, may hold values from 0.1 to 1.9
- w_query: bfloat16 [5120, 4096], P(None, 'tp'), may hold values from -0.078125 to 0.078125
- key_projection: bfloat16 [5120, 1024], P(None, 'tp'), may hold values from -0.078125 to 0.078125
- value_projection: bfloat16 [5120, 1024], P(None, 'tp'), may hold values from -0.078125 to 0.078125
- w_output: bfloat16 [4096, 5120], P('tp'), may hold values from -0.09375 to 0.09375
- mlp_gain: float32 [5120], replicated, may hold values from 0.1 to 1.9
- w_gate: bfloat16 [5120, 32768], P(None, ('seq', 'tp')), may hold values from -0.078125 to 0.078125
- w_up: bfloat16 [5120, 32768], P(None, ('seq', 'tp')), may hold values from -0.078125 to 0.078125
- w_down: bfloat16 [32768, 5120], P(('seq', 'tp')), may hold values from -0.03125 to 0.03125
- key_cache: bfloat16 [288, 8, 256, 128], P('seq', 'tp'), may hold values from -300 to 300
- paged_value_cache: bfloat16 [288, 8, 256, 128], P('seq', 'tp'), may hold values from -6 to 6
- cache_lengths: int32 [64], replicated, may hold values from 1 to 32768, as said below
- page_request: int32 [288], P('seq'), may hold values from -1 to 63, as said below
- page_number: int32 [288], P('seq'), may hold values from 0 to 127, as said below
- request_slot: int32 [64], replicated, may hold values from 0 to 63, each once
Outputs:
- attended: bfloat16 [4, 64, 5120], P(None, 'seq')
- layer_out: bfloat16 [4, 64, 5120], P(None, 'seq')
Inputs may be any that keep to these rules, and one draw needn't show every extreme that they name: `cache_lengths`: one request holds exactly 32768 positions. `page_request`: the pages of request r that hold its positions are numbered 0 to ceil(cache_lengths[r] / 256) - 1, and each of them is held by exactly one pool page; every other pool page is free (-1), and some page is free. `page_number`: 0 on free pages.
All inputs are finite; a program needn't handle non-finite values.
Results may differ from a plain program's by a relative error of at most 0.012.
Values may be sent and summed in bfloat16 or wider, within the bound.
No kernel may reach another device: no remote copies, remote signals or barrier semaphores. Data moves between devices by JAX's collectives and lax.ppermute only.
A program may use at most 128 MiB of HBM per device.

v0:
```python
import math

import jax
import jax.numpy as jnp
from jax import lax
from jax.sharding import PartitionSpec as P

STEPS = 4


rope_theta = 100000000.0
norm_eps = 1e-05
masked_low = -1e30


def rms_norm(values, gain):
    floats = values.astype(jnp.float32)
    square_mean = jnp.mean(floats * floats, axis=-1, keepdims=True)
    return floats * lax.rsqrt(square_mean + norm_eps) * gain


def apply_rotary(values, token_position):
    half_dim = values.shape[-1] // 2
    exponent = jnp.arange(half_dim, dtype=jnp.float32) * (2.0 / values.shape[-1])
    inverse_freq = rope_theta ** (-exponent)
    angles = token_position.astype(jnp.float32)[:, None] * inverse_freq[None, :]
    angles = angles[:, None, :]
    cosine = jnp.cos(angles)
    sine_part = jnp.sin(angles)
    first_half = values[..., :half_dim]
    second_half = values[..., half_dim:]
    return jnp.concatenate(
        [
            first_half * cosine - second_half * sine_part,
            second_half * cosine + first_half * sine_part,
        ],
        axis=-1,
    )


def local(
    token_inputs,
    attn_gain,
    w_query,
    key_projection,
    value_projection,
    w_output,
    mlp_gain,
    w_gate,
    w_up,
    w_down,
    key_cache,
    paged_value_cache,
    cache_lengths,
    page_request,
    page_number,
    request_slot,
):
    row_count = token_inputs.shape[1]
    total_rows = row_count * lax.axis_size("seq")
    page_count = key_cache.shape[0]
    kv_local = key_cache.shape[1]
    page_size = key_cache.shape[2]
    head_dim = key_cache.shape[3]
    heads_per_group = w_query.shape[1] // (kv_local * head_dim)
    scale_factor = head_dim ** (-0.5)
    first_row = lax.axis_index("seq") * row_count
    own_rows = first_row + jnp.arange(row_count, dtype=jnp.int32)
    row_ids = jnp.arange(total_rows, dtype=jnp.int32)
    inverse_slot = jnp.zeros((total_rows,), jnp.int32).at[request_slot].set(row_ids)
    row_lengths = cache_lengths[inverse_slot[own_rows]]
    page_live = page_request >= 0
    page_req = jnp.where(page_live, page_request, 0)
    page_row = request_slot[page_req]
    token_pos = page_number[:, None] * page_size + jnp.arange(page_size, dtype=jnp.int32)[None, :]
    token_mask = page_live[:, None] & (token_pos < cache_lengths[page_req][:, None])
    block_pages = math.gcd(page_count, max(1, 1024 // page_size))
    last_live = jnp.max(jnp.where(page_live, jnp.arange(page_count, dtype=jnp.int32) + 1, 0))
    block_total = (last_live + block_pages - 1) // block_pages
    recent_keys = []
    recent_values = []
    attended_list = []
    output_list = []
    for step_index in range(STEPS):
        hidden_in = token_inputs[step_index]
        token_position = row_lengths + step_index
        normalized_input = rms_norm(hidden_in, attn_gain).astype(jnp.bfloat16)
        query_head_rows = apply_rotary(
            jnp.dot(normalized_input, w_query, preferred_element_type=jnp.float32).reshape(
                row_count, kv_local * heads_per_group, head_dim
            ),
            token_position,
        )
        query_head_rows = query_head_rows.astype(jnp.bfloat16).reshape(
            row_count, kv_local, heads_per_group, head_dim
        )
        fresh_key = apply_rotary(
            jnp.dot(normalized_input, key_projection, preferred_element_type=jnp.float32).reshape(
                row_count, kv_local, head_dim
            ),
            token_position,
        ).astype(jnp.bfloat16)
        fresh_value = (
            jnp.dot(normalized_input, value_projection, preferred_element_type=jnp.float32)
            .astype(jnp.bfloat16)
            .reshape(row_count, kv_local, head_dim)
        )
        recent_keys.append(fresh_key)
        recent_values.append(fresh_value)
        all_queries = lax.all_gather(query_head_rows, "seq", axis=0, tiled=True)

        def block_step(block_index, running):
            run_max, run_sum, run_acc = running
            block_start = block_index * block_pages
            keys_block = lax.dynamic_slice_in_dim(key_cache, block_start, block_pages, 0)
            values_block = lax.dynamic_slice_in_dim(paged_value_cache, block_start, block_pages, 0)
            rows_block = lax.dynamic_slice_in_dim(page_row, block_start, block_pages, 0)
            mask_block = lax.dynamic_slice_in_dim(token_mask, block_start, block_pages, 0)
            live_block = lax.dynamic_slice_in_dim(page_live, block_start, block_pages, 0)
            page_query = all_queries[rows_block]
            scores = (
                jnp.einsum(
                    "pkgd,pktd->pkgt", page_query, keys_block, preferred_element_type=jnp.float32
                )
                * scale_factor
            )
            token_live = mask_block[:, None, None, :]
            scores = jnp.where(token_live, scores, masked_low)
            page_max = jnp.max(scores, axis=-1)
            weights = jnp.where(token_live, jnp.exp(scores - page_max[..., None]), 0.0)
            page_sum = jnp.sum(weights, axis=-1)
            page_acc = jnp.einsum(
                "pkgt,pktd->pkgd",
                weights.astype(jnp.bfloat16),
                values_block,
                preferred_element_type=jnp.float32,
            )
            page_owner = (rows_block[None, :] == row_ids[:, None]) & live_block[None, :]
            block_max = jnp.max(
                jnp.where(page_owner[:, :, None, None], page_max[None], masked_low), axis=1
            )
            new_max = jnp.maximum(run_max, block_max)
            factor = jnp.exp(page_max - new_max[rows_block])
            old_factor = jnp.exp(run_max - new_max)
            onehot = page_owner.astype(jnp.float32)
            run_sum = run_sum * old_factor + jnp.einsum(
                "rp,pkg->rkg", onehot, page_sum * factor, precision=lax.Precision.HIGHEST
            )
            run_acc = run_acc * old_factor[..., None] + jnp.einsum(
                "rp,pkgd->rkgd",
                onehot,
                page_acc * factor[..., None],
                precision=lax.Precision.HIGHEST,
            )
            return (new_max, run_sum, run_acc)

        start_stats = (
            jnp.full((total_rows, kv_local, heads_per_group), masked_low, jnp.float32),
            jnp.zeros((total_rows, kv_local, heads_per_group), jnp.float32),
            jnp.zeros((total_rows, kv_local, heads_per_group, head_dim), jnp.float32),
        )
        local_max, local_sum, local_acc = lax.fori_loop(0, block_total, block_step, start_stats)
        global_max = lax.pmax(local_max, "seq")
        factor = jnp.exp(local_max - global_max)
        own_sum, own_acc = (
            lax.psum_scatter(local_sum * factor, "seq", scatter_dimension=0, tiled=True),
            lax.psum_scatter(local_acc * factor[..., None], "seq", scatter_dimension=0, tiled=True),
        )
        own_max = lax.dynamic_slice_in_dim(global_max, first_row, row_count, 0)
        stacked_keys = jnp.stack(recent_keys)
        stacked_values = jnp.stack(recent_values)
        recent_scores = (
            jnp.einsum(
                "rkgd,jrkd->rkgj", query_head_rows, stacked_keys, preferred_element_type=jnp.float32
            )
            * scale_factor
        )
        recent_max = jnp.max(recent_scores, axis=-1)
        recent_weights = jnp.exp(recent_scores - recent_max[..., None])
        recent_sum = jnp.sum(recent_weights, axis=-1)
        recent_acc = jnp.einsum(
            "rkgj,jrkd->rkgd",
            recent_weights.astype(jnp.bfloat16),
            stacked_values,
            preferred_element_type=jnp.float32,
        )
        total_max = jnp.maximum(own_max, recent_max)
        cache_factor = jnp.exp(own_max - total_max)
        recent_factor = jnp.exp(recent_max - total_max)
        total_sum = own_sum * cache_factor + recent_sum * recent_factor
        total_acc = own_acc * cache_factor[..., None] + recent_acc * recent_factor[..., None]
        attention = (
            (total_acc / total_sum[..., None])
            .astype(jnp.bfloat16)
            .reshape(row_count, kv_local * heads_per_group * head_dim)
        )
        head_part = jnp.dot(attention, w_output, preferred_element_type=jnp.float32)
        attended = (hidden_in.astype(jnp.float32) + lax.psum(head_part, "tp")).astype(jnp.bfloat16)
        normed_mlp = rms_norm(attended, mlp_gain).astype(jnp.bfloat16)
        row_piece = lax.all_gather(normed_mlp, "seq", axis=0, tiled=True)
        gate_proj = jnp.dot(row_piece, w_gate, preferred_element_type=jnp.float32)
        up_proj = jnp.dot(row_piece, w_up, preferred_element_type=jnp.float32)
        activation = (jax.nn.silu(gate_proj) * up_proj).astype(jnp.bfloat16)
        partial_terms = jnp.dot(activation, w_down, preferred_element_type=jnp.float32)
        summed_units = lax.psum(partial_terms, "tp")
        mlp_result = lax.psum_scatter(summed_units, "seq", scatter_dimension=0, tiled=True)
        layer_out = (attended.astype(jnp.float32) + mlp_result).astype(jnp.bfloat16)
        attended_list.append(attended)
        output_list.append(layer_out)
    return (jnp.stack(attended_list), jnp.stack(output_list))


def solution(mesh):
    in_specs = (
        P(None, "seq", None),
        P(),
        P(None, "tp"),
        P(None, "tp"),
        P(None, "tp"),
        P("tp", None),
        P(),
        P(None, ("seq", "tp")),
        P(None, ("seq", "tp")),
        P(("seq", "tp"), None),
        P("seq", "tp", None, None),
        P("seq", "tp", None, None),
        P(),
        P("seq"),
        P("seq"),
        P(),
    )
    out_specs = (P(None, "seq", None), P(None, "seq", None))
    return jax.shard_map(local, mesh=mesh, in_specs=in_specs, out_specs=out_specs, check_vma=False)
```

profile of v0, /device:TPU:0, one launch (start us, length us, event | category | flops | bytes accessed | tf_op | source)
XLA Modules:
  0.0 1028.6 jit_solution(5581623119895966710)
XLA Ops:
  7.2 1.4 compare_select_fusion.7
  11.2 1.4 gather_fusion.8
  12.6 1.4 gather_fusion.9
  14.7 13.9 %copy.348 = bf16[1024,5120]{1,0:T(8,128)(2,1)} copy(bf16[1024,5120]{0,1:T(8,128)(2,1)} %bitcast.466) | data formatting | bytes 20971520 | tf_op jit(solution)/shard_map/dot_general | solution.py:89
  32.1 5.5 fusion.251
  38.1 32.3 %all_gather.27 = bf16[64,2,4,128]{3,2,1,0:T(4,128)(2,1)S(1)} all-gather(bf16[8,2,4,128]{3,2,1,0:T(4,128)(2,1)S(1)} %pad_maximum_fusion.5), channel_id=1, replica_groups=mesh['seq'=8,'tp'=4] {'seq'}, dimensions={0}, use_global_device_ids=true | all-gather | bytes 147456 | tf_op jit(solution)/shard_map/all_gather | solution.py:110
  71.2 51.7 %while.63 = (s32[]{:T(128)}, f32[64,2,4]{0,2,1:T(4,128)S(1)}, f32[64,2,4]{0,2,1:T(4,128)S(1)}, f32[64,2,4,128]{3,0,2,1:T(8,128)S(1)}, s32[]{:T(128)}, /*index=5*...) while((s32[]{:T(128)}, f32[64,2,4]{0,2,1:T(4,128)S(1)}, ...), condition=%wide.region_41.42_spmd.clone, body=%wide.region_37.41_spmd.clone.sunk | while | flops 7580690 | bytes 1773907 | solution.py:162
  122.9 5.5 fusion.247
  128.7 30.6 %all_gather.26 = bf16[64,2,4,128]{3,2,1,0:T(4,128)(2,1)S(1)} all-gather(bf16[8,2,4,128]{3,2,1,0:T(4,128)(2,1)S(1)} %pad_maximum_fusion.4), channel_id=1, replica_groups=mesh['seq'=8,'tp'=4] {'seq'}, dimensions={0}, use_global_device_ids=true | all-gather | bytes 147456 | tf_op jit(solution)/shard_map/all_gather | solution.py:110
  159.3 51.7 %while.62 = (s32[]{:T(128)}, f32[64,2,4]{0,2,1:T(4,128)S(1)}, f32[64,2,4]{0,2,1:T(4,128)S(1)}, f32[64,2,4,128]{3,0,2,1:T(8,128)S(1)}, s32[]{:T(128)}, /*index=5*...) while((s32[]{:T(128)}, f32[64,2,4]{0,2,1:T(4,128)S(1)}, ...), condition=%wide.region_29.30_spmd.clone, body=%wide.region_25.29_spmd.clone.sunk | while | flops 7580690 | bytes 1773907 | solution.py:162
  211.1 5.5 fusion.243
  216.9 32.5 %all_gather.25 = bf16[64,2,4,128]{3,2,1,0:T(4,128)(2,1)} all-gather(bf16[8,2,4,128]{3,2,1,0:T(4,128)(2,1)S(1)} %pad_maximum_fusion.3), channel_id=1, replica_groups=mesh['seq'=8,'tp'=4] {'seq'}, dimensions={0}, use_global_device_ids=true | all-gather | bytes 147456 | tf_op jit(solution)/shard_map/all_gather | solution.py:110
  249.5 73.0 %while.61 = (s32[]{:T(128)}, f32[64,2,4]{0,2,1:T(4,128)S(1)}, f32[64,2,4]{0,2,1:T(4,128)S(1)}, f32[64,2,4,128]{3,0,2,1:T(8,128)S(1)}, s32[]{:T(128)}, /*index=5*...) while((s32[]{:T(128)}, f32[64,2,4]{0,2,1:T(4,128)S(1)}, ...), condition=%wide.region_17.18_spmd.clone, body=%wide.region_13.17_spmd.clone.sunk | while | flops 7580690 | bytes 1773907 | solution.py:162
  250.3 1.5 gather_fusion.2
  258.4 1.5 gather_fusion.2
  266.5 1.5 gather_fusion.2
  274.7 1.5 gather_fusion.2
  282.8 1.5 gather_fusion.2
  290.9 1.5 gather_fusion.2
  299.0 1.5 gather_fusion.2
  307.1 1.5 gather_fusion.2
  315.2 1.5 gather_fusion.2
  322.4 5.6 fusion.239
  328.3 32.5 %all_gather.24 = bf16[64,2,4,128]{3,2,1,0:T(4,128)(2,1)} all-gather(bf16[8,2,4,128]{3,2,1,0:T(4,128)(2,1)S(1)} %pad_maximum_fusion.2), channel_id=1, replica_groups=mesh['seq'=8,'tp'=4] {'seq'}, dimensions={0}, use_global_device_ids=true | all-gather | bytes 147456 | tf_op jit(solution)/shard_map/all_gather | solution.py:110
  360.9 73.0 %while.60 = (s32[]{:T(128)}, f32[64,2,4]{0,2,1:T(4,128)S(1)}, f32[64,2,4]{0,2,1:T(4,128)S(1)}, f32[64,2,4,128]{3,0,2,1:T(8,128)S(1)}, s32[]{:T(128)}, /*index=5*...) while((s32[]{:T(128)}, f32[64,2,4]{0,2,1:T(4,128)S(1)}, ...), condition=%wide.region_7.8_spmd.clone, body=%wide.region_3.7_spmd.clone.sunk | while | flops 7580690 | bytes 1773907 | solution.py:162
  361.7 1.5 gather_fusion
  369.8 1.5 gather_fusion
  377.9 1.5 gather_fusion
  386.0 1.5 gather_fusion
  394.2 1.5 gather_fusion
  402.3 1.5 gather_fusion
  410.4 1.5 gather_fusion
  418.5 1.5 gather_fusion
  426.6 1.5 gather_fusion
  433.8 33.0 %all-reduce.9 = (f32[64,2,4]{0,2,1:T(4,128)S(1)}, f32[64,2,4]{0,2,1:T(4,128)S(1)}, f32[64,2,4]{0,2,1:T(4,128)S(1)}, f32[64,2,4]{0,2,1:T(4,128)S(1)}) all-reduce(f32[64,2,4]{0,2,1:T(4,128)S(1)} %get-tuple-element.272, f32[64,2,4]{0,2,1:T(4,128)S(1)} %get-tuple-element.269, ...), channel_id=1, replica_groups=mesh['seq'=8,'tp'=4] {'seq'}, use_global_device_ids=true, to_apply=%region_42.43 | all-reduce | flops 2048 | bytes 16384 | tf_op jit(solution)/shard_map/pmax | solution.py:163
  470.9 1.9 copy_multiply_fusion.2
  472.8 4.5 copy.349
  477.4 2.6 fusion.249
  480.1 2.6 fusion.245
  482.6 2.6 fusion.241
  485.2 2.5 fusion.237
  492.7 33.0 %all-reduce.7 = (f32[64,2,4]{0,2,1:T(4,128)S(1)}, f32[64,2,4]{0,2,1:T(4,128)S(1)}, f32[64,2,4]{0,2,1:T(4,128)S(1)}, f32[64,2,4]{0,2,1:T(4,128)S(1)}) all-reduce(f32[64,2,4]{0,2,1:T(4,128)S(1)} %bitcast.549, f32[64,2,4]{0,2,1:T(4,128)S(1)} %bitcast.550, f32[64,2,4]{0,2,1:T(4,128)S(1)} %bitcast.551, ...), channel_id=9, replica_groups=mesh['seq'=8,'tp'=4] {'seq'}, use_global_device_ids=true, to_apply=%region_45.46.clone | all-reduce | flops 2048 | bytes 16384
  528.9 6.1 fusion.298
  535.0 70.6 %all-reduce.16.cloned.1.call-done = (f32[64,2,4,128]{3,2,1,0:T(4,128)}, f32[64,2,4,128]{3,2,1,0:T(4,128)}, f32[64,2,4,128]{3,2,1,0:T(4,128)}) async-done(((f32[64,2,4,128]{3,2,1,0:T(4,128)}, f32[64,2,4,128]{3,2,1,0:T(4,128)}, f32[64,2,4,128]{3,2,1,0:T(4,128)}), (f32[64,2,4,128]{3,2,1,0:T(4,128)}, f32[64,2,4,128]{3,2,1,0:T(4,128)}, f32[64,2,4,128]{3,2,1,0:T(4,128)})) %all-reduce.16.cloned.1.call-update) | async-done | bytes 786448
  606.6 6.1 fusion.301
  613.7 6.1 fusion.300
  620.9 6.1 fusion.299
  627.3 33.0 %all-reduce.20.cloned.1.call-done = (f32[8,5120]{1,0:T(8,128)}, f32[8,5120]{1,0:T(8,128)}, f32[8,5120]{1,0:T(8,128)}, f32[8,5120]{1,0:T(8,128)}) async-done(((f32[8,5120]{1,0:T(8,128)}, f32[8,5120]{1,0:T(8,128)}, f32[8,5120]{1,0:T(8,128)}, f32[8,5120]{1,0:T(8,128)}), (f32[8,5120]{1,0:T(8,128)}, f32[8,5120]{1,0:T(8,128)}, f32[8,5120]{1,0:T(8,128)}, f32[8,5120]{1,0:T(8,128)})) %all-reduce.20.cloned.1.call-update) | async-done | bytes 655376 | tf_op jit(solution)/shard_map/psum | solution.py:198
  661.8 31.8 %all_gather.31 = bf16[64,5120]{1,0:T(8,128)(2,1)S(1)} all-gather(bf16[8,5120]{1,0:T(8,128)(2,1)S(1)} %get-tuple-element.562), channel_id=1, replica_groups=mesh['seq'=8,'tp'=4] {'seq'}, dimensions={0}, use_global_device_ids=true | all-gather | bytes 737280 | tf_op jit(solution)/shard_map/all_gather | solution.py:200
  693.7 5.9 fusion.305
  699.6 11.8 %fusion.84 = f32[64,5120]{1,0:T(8,128)} fusion(bf16[1024,5120]{1,0:T(8,128)(2,1)} %param.33, bf16[64,5120]{1,0:T(8,128)(2,1)S(1)} %all_gather.31, bf16[5120,1024]{1,0:T(8,128)(2,1)} %param.32, f32[64,1024]{1,0:T(8,128)S(1)} %fusion.305), kind=kOutput, calls=%fused_computation.151 | convolution fusion | flops 1342570496 | bytes 23199744 | tf_op jit(solution)/shard_map/dot_general | solution.py:204
  711.5 32.4 %all_gather.30 = bf16[64,5120]{1,0:T(8,128)(2,1)S(1)} all-gather(bf16[8,5120]{1,0:T(8,128)(2,1)S(1)} %get-tuple-element.561), channel_id=1, replica_groups=mesh['seq'=8,'tp'=4] {'seq'}, dimensions={0}, use_global_device_ids=true | all-gather | bytes 737280 | tf_op jit(solution)/shard_map/all_gather | solution.py:200
  743.9 5.9 fusion.304
  749.8 11.9 %fusion.85 = f32[64,5120]{1,0:T(8,128)} fusion(bf16[1024,5120]{1,0:T(8,128)(2,1)} %param.33, bf16[64,5120]{1,0:T(8,128)(2,1)S(1)} %all_gather.30, bf16[5120,1024]{1,0:T(8,128)(2,1)} %param.32, f32[64,1024]{1,0:T(8,128)S(1)} %fusion.304), kind=kOutput, calls=%fused_computation.152 | convolution fusion | flops 1342570496 | bytes 23199744 | tf_op jit(solution)/shard_map/dot_general | solution.py:204
  761.8 32.4 %all_gather.29 = bf16[64,5120]{1,0:T(8,128)(2,1)S(1)} all-gather(bf16[8,5120]{1,0:T(8,128)(2,1)S(1)} %get-tuple-element.560), channel_id=1, replica_groups=mesh['seq'=8,'tp'=4] {'seq'}, dimensions={0}, use_global_device_ids=true | all-gather | bytes 737280 | tf_op jit(solution)/shard_map/all_gather | solution.py:200
  794.2 6.0 fusion.303
  800.1 12.0 %fusion.86 = f32[64,5120]{1,0:T(8,128)} fusion(bf16[1024,5120]{1,0:T(8,128)(2,1)} %param.33, bf16[64,5120]{1,0:T(8,128)(2,1)S(1)} %all_gather.29, bf16[5120,1024]{1,0:T(8,128)(2,1)} %param.32, f32[64,1024]{1,0:T(8,128)S(1)} %fusion.303), kind=kOutput, calls=%fused_computation.153 | convolution fusion | flops 1342570496 | bytes 23199744 | tf_op jit(solution)/shard_map/dot_general | solution.py:204
  812.2 32.0 %all_gather.28 = bf16[64,5120]{1,0:T(8,128)(2,1)S(1)} all-gather(bf16[8,5120]{1,0:T(8,128)(2,1)S(1)} %get-tuple-element.559), channel_id=1, replica_groups=mesh['seq'=8,'tp'=4] {'seq'}, dimensions={0}, use_global_device_ids=true | all-gather | bytes 737280 | tf_op jit(solution)/shard_map/all_gather | solution.py:200
  844.1 6.8 fusion.302
  850.9 12.0 %fusion.87 = f32[64,5120]{1,0:T(8,128)} fusion(bf16[1024,5120]{1,0:T(8,128)(2,1)} %param.33, bf16[64,5120]{1,0:T(8,128)(2,1)S(1)} %all_gather.28, bf16[5120,1024]{1,0:T(8,128)(2,1)} %param.32, f32[64,1024]{1,0:T(8,128)} %fusion.302), kind=kOutput, calls=%fused_computation.154 | convolution fusion | flops 1342570496 | bytes 23199744 | tf_op jit(solution)/shard_map/dot_general | solution.py:204
  863.1 50.6 %reduce-scatter.14.cloned.1.call-done = f32[8,5120]{1,0:T(8,128)} async-done(((f32[64,5120]{1,0:T(8,128)}), f32[8,5120]{1,0:T(8,128)}) %reduce-scatter.14.cloned.1.call-update) | async-done | bytes 163856 | tf_op jit(solution)/shard_map/reduce_scatter | solution.py:206
  913.7 67.1 %reduce-scatter.12.cloned.1.call-done = f32[8,5120]{1,0:T(8,128)} async-done(((f32[64,5120]{1,0:T(8,128)}), f32[8,5120]{1,0:T(8,128)}) %reduce-scatter.12.cloned.1.call-update) | async-done | bytes 163856 | tf_op jit(solution)/shard_map/reduce_scatter | solution.py:206
  980.9 1.7 pad_maximum_fusion
  982.5 34.3 %all-reduce.18.cloned.1.call-done = (f32[8,5120]{1,0:T(8,128)}, f32[8,5120]{1,0:T(8,128)}, f32[8,5120]{1,0:T(8,128)}, f32[8,5120]{1,0:T(8,128)}) async-done(((f32[8,5120]{1,0:T(8,128)}, f32[8,5120]{1,0:T(8,128)}, f32[8,5120]{1,0:T(8,128)}, f32[8,5120]{1,0:T(8,128)}), (f32[8,5120]{1,0:T(8,128)}, f32[8,5120]{1,0:T(8,128)}, f32[8,5120]{1,0:T(8,128)}, f32[8,5120]{1,0:T(8,128)})) %all-reduce.18.cloned.1.call-update) | async-done | bytes 655376 | tf_op jit(solution)/shard_map/psum | solution.py:205
  (894 shorter events, 249.1 us)
Async XLA Ops:
  7.2 480.6 %copy-start = (bf16[5120,256]{1,0:T(8,128)(2,1)S(1)}, bf16[5120,256]{1,0:T(8,128)(2,1)}, u32[]{:S(2)}) copy-start(bf16[5120,256]{1,0:T(8,128)(2,1)} %param.28) | copy-start | bytes 7864324
  7.2 520.9 %reduce-scatter.10.cloned.1.call-start = ((), (), s32[]{:S(2)}) async-start(), calls=%async_computation.5 | async-start | bytes 294912 | tf_op jit(solution)/shard_map/reduce_scatter | solution.py:167
  14.7 13.9 %copy-start.4 = (bf16[4,8,5120]{2,1,0:T(8,128)(2,1)S(1)}, bf16[4,8,5120]{2,1,0:T(8,128)(2,1)}, u32[]{:S(2)}) copy-start(bf16[4,8,5120]{2,1,0:T(8,128)(2,1)} %param.24) | copy-start | bytes 983044
  14.7 16.2 %copy-start.2 = (s32[64]{0:T(128)S(1)}, s32[64]{0:T(128)}, u32[]{:S(2)}) copy-start(s32[64]{0:T(128)} %param.36) | copy-start | bytes 772
  14.7 17.4 %copy-start.6 = (f32[5120]{0:T(1024)S(1)}, f32[5120]{0:T(1024)}, u32[]{:S(2)}) copy-start(f32[5120]{0:T(1024)} %param.25) | copy-start | bytes 61444
  32.1 38.2 %copy-start.37 = (f32[8]{0:T(128)}, f32[8]{0:T(128)S(1)}, u32[]{:S(2)}) copy-start(f32[8]{0:T(128)S(1)} %get-tuple-element.600) | copy-start | bytes 100
  37.8 33.3 %copy-start.24 = (f32[8,64]{1,0:T(8,128)}, f32[8,64]{1,0:T(8,128)S(1)}, u32[]{:S(2)}) copy-start(f32[8,64]{1,0:T(8,128)S(1)} %get-tuple-element.585) | copy-start | bytes 6148
  37.8 33.3 %copy-start.22 = (f32[8,64]{1,0:T(8,128)}, f32[8,64]{1,0:T(8,128)S(1)}, u32[]{:S(2)}) copy-start(f32[8,64]{1,0:T(8,128)S(1)} %get-tuple-element.584) | copy-start | bytes 6148
  37.8 90.6 %copy-start.18 = (f32[8,64]{1,0:T(8,128)}, f32[8,64]{1,0:T(8,128)S(1)}, u32[]{:S(2)}) copy-start(f32[8,64]{1,0:T(8,128)S(1)} %get-tuple-element.582) | copy-start | bytes 6148
  37.8 90.6 %copy-start.20 = (f32[8,64]{1,0:T(8,128)}, f32[8,64]{1,0:T(8,128)S(1)}, u32[]{:S(2)}) copy-start(f32[8,64]{1,0:T(8,128)S(1)} %get-tuple-element.583) | copy-start | bytes 6148
  37.8 178.8 %copy-start.16 = (f32[8,64]{1,0:T(8,128)}, f32[8,64]{1,0:T(8,128)S(1)}, u32[]{:S(2)}) copy-start(f32[8,64]{1,0:T(8,128)S(1)} %get-tuple-element.581) | copy-start | bytes 6148
  38.1 33.0 %copy-start.8 = (bf16[8,2,4,128]{3,2,1,0:T(4,128)(2,1)}, bf16[8,2,4,128]{3,2,1,0:T(4,128)(2,1)S(1)}, u32[]{:S(2)}) copy-start(bf16[8,2,4,128]{3,2,1,0:T(4,128)(2,1)S(1)} %pad_maximum_fusion.5) | copy-start | bytes 49156
  122.9 88.2 %copy-start.42 = (f32[8]{0:T(128)S(1)}, f32[8]{0:T(128)}, u32[]{:S(2)}) copy-start(f32[8]{0:T(128)} %get-tuple-element.374) | copy-start | bytes 100
  122.9 88.2 %copy-start.43 = (f32[8]{0:T(128)S(1)}, f32[8]{0:T(128)}, u32[]{:S(2)}) copy-start(f32[8]{0:T(128)} %get-tuple-element.375) | copy-start | bytes 100
  128.7 88.0 %copy-start.10 = (bf16[8,2,4,128]{3,2,1,0:T(4,128)(2,1)}, bf16[8,2,4,128]{3,2,1,0:T(4,128)(2,1)S(1)}, u32[]{:S(2)}) copy-start(bf16[8,2,4,128]{3,2,1,0:T(4,128)(2,1)S(1)} %pad_maximum_fusion.4) | copy-start | bytes 49156
  211.1 5.8 copy-start.40
  211.1 111.3 %copy-start.38 = (f32[8]{0:T(128)}, f32[8]{0:T(128)S(1)}, u32[]{:S(2)}) copy-start(f32[8]{0:T(128)S(1)} %get-tuple-element.603) | copy-start | bytes 100
  216.9 32.6 %copy-start.12 = (bf16[8,2,4,128]{3,2,1,0:T(4,128)(2,1)}, bf16[8,2,4,128]{3,2,1,0:T(4,128)(2,1)S(1)}, u32[]{:S(2)}) copy-start(bf16[8,2,4,128]{3,2,1,0:T(4,128)(2,1)S(1)} %pad_maximum_fusion.3) | copy-start | bytes 49156
  322.4 38.4 %copy-start.3 = (f32[64,2,4,128]{3,0,2,1:T(8,128)}, f32[64,2,4,128]{3,0,2,1:T(8,128)S(1)}, u32[]{:S(2)}) copy-start(f32[64,2,4,128]{3,0,2,1:T(8,128)S(1)} %get-tuple-element.265) | copy-start | bytes 786436
  328.3 32.6 %copy-start.14 = (bf16[8,2,4,128]{3,2,1,0:T(4,128)(2,1)}, bf16[8,2,4,128]{3,2,1,0:T(4,128)(2,1)S(1)}, u32[]{:S(2)}) copy-start(bf16[8,2,4,128]{3,2,1,0:T(4,128)(2,1)S(1)} %pad_maximum_fusion.2) | copy-start | bytes 49156
  433.8 46.2 %copy-start.36 = (f32[8]{0:T(128)S(1)}, f32[8]{0:T(128)}, u32[]{:S(2)}) copy-start(f32[8]{0:T(128)} %get-tuple-element.601) | copy-start | bytes 100
  466.8 2.8 copy-start.34
  466.8 2.8 copy-start.32
  466.8 10.5 %copy-start.28 = (f32[64,2,4]{0,2,1:T(4,128)}, f32[64,2,4]{0,2,1:T(4,128)S(1)}, u32[]{:S(2)}) copy-start(f32[64,2,4]{0,2,1:T(4,128)S(1)} %get-tuple-element.476) | copy-start | bytes 6148
  466.8 10.5 %copy-start.30 = (f32[64,2,4]{0,2,1:T(4,128)}, f32[64,2,4]{0,2,1:T(4,128)S(1)}, u32[]{:S(2)}) copy-start(f32[64,2,4]{0,2,1:T(4,128)S(1)} %get-tuple-element.475) | copy-start | bytes 6148
  467.8 137.9 %all-reduce.16.cloned.1.call-start = ((), (), s32[]{:S(2)}) async-start(), calls=%async_computation.10 | async-start | bytes 1572864
  469.6 13.0 %copy-start.5 = (bf16[4,8,5120]{2,1,0:T(8,128)(2,1)S(1)}, bf16[4,8,5120]{2,1,0:T(8,128)(2,1)}, u32[]{:S(2)}) copy-start(bf16[4,8,5120]{2,1,0:T(8,128)(2,1)} %param.24) | copy-start | bytes 983044
  472.8 187.4 %all-reduce.20.cloned.1.call-start = ((), (), s32[]{:S(2)}) async-start(), calls=%async_computation.12 | async-start | bytes 1310720 | tf_op jit(solution)/shard_map/psum | solution.py:198
  472.8 16.5 %copy-start.41 = (f32[8]{0:T(128)S(1)}, f32[8]{0:T(128)}, u32[]{:S(2)}) copy-start(f32[8]{0:T(128)} %copy-done.40) | copy-start | bytes 100
  477.3 12.5 %copy-start.39 = (f32[8]{0:T(128)S(1)}, f32[8]{0:T(128)}, u32[]{:S(2)}) copy-start(f32[8]{0:T(128)} %copy-done.38) | copy-start | bytes 100
  477.3 13.0 %copy-start.23 = (f32[8,64]{1,0:T(8,128)S(1)}, f32[8,64]{1,0:T(8,128)}, u32[]{:S(2)}) copy-start(f32[8,64]{1,0:T(8,128)} %copy-done.22) | copy-start | bytes 6148
  477.3 13.0 %copy-start.25 = (f32[8,64]{1,0:T(8,128)S(1)}, f32[8,64]{1,0:T(8,128)}, u32[]{:S(2)}) copy-start(f32[8,64]{1,0:T(8,128)} %copy-done.24) | copy-start | bytes 6148
  477.3 13.1 %copy-start.19 = (f32[8,64]{1,0:T(8,128)S(1)}, f32[8,64]{1,0:T(8,128)}, u32[]{:S(2)}) copy-start(f32[8,64]{1,0:T(8,128)} %copy-done.18) | copy-start | bytes 6148
  477.3 13.1 %copy-start.21 = (f32[8,64]{1,0:T(8,128)S(1)}, f32[8,64]{1,0:T(8,128)}, u32[]{:S(2)}) copy-start(f32[8,64]{1,0:T(8,128)} %copy-done.20) | copy-start | bytes 6148
  477.4 13.2 %copy-start.17 = (f32[8,64]{1,0:T(8,128)S(1)}, f32[8,64]{1,0:T(8,128)}, u32[]{:S(2)}) copy-start(f32[8,64]{1,0:T(8,128)} %copy-done.16) | copy-start | bytes 6148
  477.4 13.6 %copy-start.9 = (bf16[8,2,4,128]{3,2,1,0:T(4,128)(2,1)S(1)}, bf16[8,2,4,128]{3,2,1,0:T(4,128)(2,1)}, u32[]{:S(2)}) copy-start(bf16[8,2,4,128]{3,2,1,0:T(4,128)(2,1)} %copy-done.8) | copy-start | bytes 49156
  480.0 11.5 %copy-start.44 = (u32[32]{0:T(128)S(1)}, u32[32]{0:T(128)}, u32[]{:S(2)}) copy-start(u32[32]{0:T(128)} %constant.161) | copy-start | bytes 388
  480.0 12.8 %copy-start.27 = (f32[64,1,8]{0,2,1:T(8,128)S(1)}, f32[64,1,8]{0,2,1:T(8,128)}, u32[]{:S(2)}) copy-start(f32[64,1,8]{0,2,1:T(8,128)} %get-tuple-element.664) | copy-start | bytes 6148
  480.0 45.8 %copy-start.35 = (f32[64,2,4]{0,2,1:T(4,128)S(1)}, f32[64,2,4]{0,2,1:T(4,128)}, u32[]{:S(2)}) copy-start(f32[64,2,4]{0,2,1:T(4,128)} %copy-done.34) | copy-start | bytes 6148
  480.0 46.1 %copy-start.11 = (bf16[8,2,4,128]{3,2,1,0:T(4,128)(2,1)S(1)}, bf16[8,2,4,128]{3,2,1,0:T(4,128)(2,1)}, u32[]{:S(2)}) copy-start(bf16[8,2,4,128]{3,2,1,0:T(4,128)(2,1)} %copy-done.10) | copy-start | bytes 49156
  480.0 46.5 %copy-start.33 = (f32[64,2,4]{0,2,1:T(4,128)S(1)}, f32[64,2,4]{0,2,1:T(4,128)}, u32[]{:S(2)}) copy-start(f32[64,2,4]{0,2,1:T(4,128)} %copy-done.32) | copy-start | bytes 6148
  480.0 46.9 %copy-start.13 = (bf16[8,2,4,128]{3,2,1,0:T(4,128)(2,1)S(1)}, bf16[8,2,4,128]{3,2,1,0:T(4,128)(2,1)}, u32[]{:S(2)}) copy-start(bf16[8,2,4,128]{3,2,1,0:T(4,128)(2,1)} %copy-done.12) | copy-start | bytes 49156
  480.0 47.3 %copy-start.31 = (f32[64,2,4]{0,2,1:T(4,128)S(1)}, f32[64,2,4]{0,2,1:T(4,128)}, u32[]{:S(2)}) copy-start(f32[64,2,4]{0,2,1:T(4,128)} %copy-done.30) | copy-start | bytes 6148
  480.0 47.6 %copy-start.15 = (bf16[8,2,4,128]{3,2,1,0:T(4,128)(2,1)S(1)}, bf16[8,2,4,128]{3,2,1,0:T(4,128)(2,1)}, u32[]{:S(2)}) copy-start(bf16[8,2,4,128]{3,2,1,0:T(4,128)(2,1)} %copy-done.14) | copy-start | bytes 49156
  480.1 47.9 %copy-start.29 = (f32[64,2,4]{0,2,1:T(4,128)S(1)}, f32[64,2,4]{0,2,1:T(4,128)}, u32[]{:S(2)}) copy-start(f32[64,2,4]{0,2,1:T(4,128)} %copy-done.28) | copy-start | bytes 6148
  619.8 41.8 %copy-start.26 = (f32[5120]{0:T(1024)S(1)}, f32[5120]{0:T(1024)}, u32[]{:S(2)}) copy-start(f32[5120]{0:T(1024)} %param.30) | copy-start | bytes 61444
  627.0 236.1 %reduce-scatter.18.cloned.1.call-start = ((), (), s32[]{:S(2)}) async-start(), calls=%async_computation.9 | async-start | bytes 1474560 | tf_op jit(solution)/shard_map/reduce_scatter | solution.py:206
  661.6 49.8 %copy-start.7 = (bf16[8,5120]{1,0:T(8,128)(2,1)}, bf16[8,5120]{1,0:T(8,128)(2,1)S(1)}, u32[]{:S(2)}) copy-start(bf16[8,5120]{1,0:T(8,128)(2,1)S(1)} %get-tuple-element.550) | copy-start | bytes 245764
  711.4 151.7 %reduce-scatter.16.cloned.1.call-start = ((), (), s32[]{:S(2)}) async-start(), calls=%async_computation.8 | async-start | bytes 1474560 | tf_op jit(solution)/shard_map/reduce_scatter | solution.py:206
  761.7 152.0 %reduce-scatter.14.cloned.1.call-start = ((), (), s32[]{:S(2)}) async-start(), calls=%async_computation.7 | async-start | bytes 1474560 | tf_op jit(solution)/shard_map/reduce_scatter | solution.py:206
  812.1 168.7 %reduce-scatter.12.cloned.1.call-start = ((), (), s32[]{:S(2)}) async-start(), calls=%async_computation.6 | async-start | bytes 1474560 | tf_op jit(solution)/shard_map/reduce_scatter | solution.py:206
  844.1 177.2 %copy-start.1 = (bf16[5120,256]{1,0:T(8,128)(2,1)S(1)}, bf16[5120,256]{1,0:T(8,128)(2,1)}, u32[]{:S(2)}) copy-start(bf16[5120,256]{1,0:T(8,128)(2,1)} %param.28) | copy-start | bytes 7864324
  863.0 153.8 %all-reduce.18.cloned.1.call-start = ((), (), s32[]{:S(2)}) async-start(), calls=%async_computation.11 | async-start | bytes 1310720 | tf_op jit(solution)/shard_map/psum | solution.py:205
Sparse Core Ops, SparseCore 0:
  467.9 59.0 reduce-scatter.9
  531.3 74.2 all-reduce.15
  627.1 33.0 all-reduce.19
  711.6 65.8 reduce-scatter.17
  781.1 65.3 reduce-scatter.15
  850.1 63.6 reduce-scatter.13
  917.5 63.3 reduce-scatter.11
  983.6 33.1 all-reduce.17
where the time goes:
time: 1040 us; the launch traced here: 1030 us
  blocking collectives  323 us (31%)
  waiting for transfers between devices  256 us (25%)
  matrix products  248 us (24%)
  local copies, waits for them, and re-layouts  143 us (14%)
  other arithmetic  38.4 us (4%)
  between operations  16.8 us (2%)
    all_gather x4, blocking collectives, local(): row_piece = lax.all_gather(normed_mlp, 'seq', axis=0, tiled=True)  129 us
    all_gather x4, blocking collectives, local(): all_queries = lax.all_gather(query_head_rows, 'seq', axis=0, tiled=True)  128 us
    reduce_scatter x4, waiting for transfers between devices, local(): lax.psum_scatter(summed_units, 'seq', scatter_dimension=0, tiled=True)  118 us
    unnamed x9, waiting for transfers between devices  70.7 us
    dot_general x36, matrix products, block_step(): jnp.einsum('pkgd,pktd->pkgt', page_query, keys_block, preferred_element_t...  49.1 us
    dot_general x4, matrix products, local(): jnp.dot(activation, w_down, preferred_element_type=jnp.float32)  47.7 us
    dot_general x36, matrix products, block_step(): jnp.einsum('pkgt,pktd->pkgd', weights.astype(jnp.bfloat16), values_block,...  46 us
    gather x36, local copies, waits for them, and re-layouts, block_step(): page_query = all_queries[rows_block]  36.9 us
  transfers between devices with their start and end apart: 8, of which 5 were waited for; matrix products, arithmetic and copies ran while one was open for 9% of the time, Pallas kernels for 0%

commit v1 on v0

v1 whole, which is shorter than its diff:
```python
import functools

import jax
import jax.numpy as jnp
from jax import lax
from jax.experimental import pallas as pl
from jax.experimental.pallas import tpu as pltpu
from jax.sharding import PartitionSpec as P

STEPS = 4
CORES = 2

rope_theta = 100000000.0
norm_eps = 1e-05
masked_low = -1e30
f32 = jnp.float32
bf16 = jnp.bfloat16


def split_axis(size):
    fast = 1
    while fast * fast * 4 <= size:
        fast *= 2
    return size // fast, fast


def swap(value, axis, mask):
    size = lax.axis_size(axis)
    return lax.ppermute(value, axis, [(i, i ^ mask) for i in range(size)])


def rms_norm(values, gain):
    floats = values.astype(f32)
    square_mean = jnp.mean(floats * floats, axis=-1, keepdims=True)
    return floats * lax.rsqrt(square_mean + norm_eps) * gain


def rotary_tables(token_position, head_dim):
    half_dim = head_dim // 2
    exponent = jnp.arange(half_dim, dtype=f32) * (2.0 / head_dim)
    inverse_freq = rope_theta ** (-exponent)
    angles = token_position.astype(f32)[:, None] * inverse_freq[None, :]
    return jnp.cos(angles)[:, None, :], jnp.sin(angles)[:, None, :]


def apply_rotary(values, cosine, sine):
    half_dim = values.shape[-1] // 2
    first_half = values[..., :half_dim]
    second_half = values[..., half_dim:]
    return jnp.concatenate(
        [first_half * cosine - second_half * sine, second_half * cosine + first_half * sine],
        axis=-1,
    )


def dot_t(a, b):
    return lax.dot_general(a, b, (((1,), (1,)), ((), ())), preferred_element_type=f32)


def round_trip(value):
    return value.astype(bf16).astype(f32)


def encode_stats(top, total, pairs):
    pieces = []
    rest = top
    for _ in range(3):
        piece = round_trip(rest)
        pieces.append(piece)
        rest = rest - piece
    rest = total
    for _ in range(2):
        piece = round_trip(rest)
        pieces.append(piece)
        rest = rest - piece
    tile = pieces[0]
    for i in range(1, 5):
        tile = tile + pltpu.roll(pieces[i], i * pairs, 1)
    return tile.astype(bf16)


def decode_stats(tile, pairs):
    values = tile.astype(f32)
    lanes = values.shape[1]
    shifted = [values] + [pltpu.roll(values, lanes - i * pairs, 1) for i in range(1, 5)]
    top = shifted[0] + shifted[1] + shifted[2]
    total = shifted[3] + shifted[4]
    return top, total


def pages_kernel(
    block_pages, slot_ref, valid_ref, query_ref, fresh_key_ref, fresh_value_ref, key_hbm, value_hbm,
    out_ref, key_buf, value_buf, top_ref, total_ref, acc_ref, sems,
):
    page_count, kv_local, page_size, head_dim = key_buf.shape
    blocks = page_count // block_pages
    groups, tiles = out_ref.shape[:2]
    pairs = tiles - 1
    rows = query_ref.shape[1]
    per_step = rows // STEPS
    scale = head_dim ** (-0.5)

    def copies(block):
        at = pl.ds(block * block_pages, block_pages)
        return (
            pltpu.make_async_copy(key_hbm.at[at], key_buf.at[at], sems.at[0, block]),
            pltpu.make_async_copy(value_hbm.at[at], value_buf.at[at], sems.at[1, block]),
        )

    for block in range(blocks):
        for copy in copies(block):
            copy.start()

    top_ref[...] = jnp.full(top_ref.shape, masked_low, f32)
    total_ref[...] = jnp.zeros(total_ref.shape, f32)
    acc_ref[...] = jnp.zeros(acc_ref.shape, f32)

    fresh = fresh_key_ref.shape[1]
    row_step = lax.broadcasted_iota(jnp.int32, (rows, fresh), 0) // per_step
    column = lax.broadcasted_iota(jnp.int32, (rows, fresh), 1)
    earlier = column <= row_step
    for i in range(pairs):
        scores = dot_t(query_ref[i], fresh_key_ref[i]) * scale
        scores = jnp.where(earlier, scores, masked_low)
        top = jnp.max(scores, axis=1, keepdims=True)
        weights = jnp.where(earlier, jnp.exp(scores - top), 0.0)
        top_ref[i] = jnp.broadcast_to(top, (rows, head_dim))
        total_ref[i] = jnp.broadcast_to(jnp.sum(weights, axis=1, keepdims=True), (rows, head_dim))
        acc_ref[i] = jnp.dot(weights.astype(bf16), fresh_value_ref[i], preferred_element_type=f32)

    lane = lax.broadcasted_iota(jnp.int32, (rows, page_size), 1)

    @pl.loop(0, blocks)
    def _(block):
        for copy in copies(block):
            copy.wait()
        found = []
        for i in range(block_pages):
            page = block * block_pages + i
            slot = slot_ref[page]
            live = lane < valid_ref[page]
            for head in range(kv_local):
                at = slot * kv_local + head
                scores = dot_t(query_ref[at], key_buf[page, head]) * scale
                scores = jnp.where(live, scores, masked_low)
                top = jnp.max(scores, axis=1, keepdims=True)
                weights = jnp.where(live, jnp.exp(scores - top), 0.0)
                total = jnp.sum(weights, axis=1, keepdims=True)
                acc = jnp.dot(weights.astype(bf16), value_buf[page, head], preferred_element_type=f32)
                found.append((at, top, total, acc))
        for at, top, total, acc in found:
            old_top = top_ref[at]
            new_top = jnp.maximum(old_top, top)
            old_factor = jnp.exp(old_top - new_top)
            factor = jnp.exp(top - new_top)
            top_ref[at] = new_top
            total_ref[at] = total_ref[at] * old_factor + total * factor
            acc_ref[at] = acc_ref[at] * old_factor + acc * factor

    out_lane = lax.broadcasted_iota(jnp.int32, (rows, head_dim), 1)

    @pl.loop(0, groups)
    def _(group):
        tops = jnp.zeros((rows, head_dim), f32)
        totals = jnp.zeros((rows, head_dim), f32)
        for i in range(pairs):
            at = group * pairs + i
            out_ref[group, i] = acc_ref[at].astype(bf16)
            tops = jnp.where(out_lane == i, top_ref[at], tops)
            totals = jnp.where(out_lane == i, total_ref[at], totals)
        out_ref[group, pairs] = encode_stats(tops, totals, pairs)


def attend_pages(queries, fresh_keys, fresh_values, key_cache, value_cache, slots, valid, groups):
    pairs = fresh_keys.shape[0]
    rows, head_dim = queries.shape[1:]
    page_count, kv_local, page_size, _ = key_cache.shape
    block_pages = 4
    while page_count % block_pages:
        block_pages -= 1
    blocks = page_count // block_pages
    count = queries.shape[0]
    vmem = pl.BlockSpec(memory_space=pltpu.VMEM)
    smem = pl.BlockSpec(memory_space=pltpu.SMEM)
    hbm = pl.BlockSpec(memory_space=pl.ANY)
    return pl.pallas_call(
        functools.partial(pages_kernel, block_pages),
        out_shape=jax.ShapeDtypeStruct((groups, pairs + 1, rows, head_dim), bf16),
        in_specs=[smem, smem, vmem, vmem, vmem, hbm, hbm],
        out_specs=vmem,
        scratch_shapes=[
            pltpu.VMEM(key_cache.shape, bf16),
            pltpu.VMEM(value_cache.shape, bf16),
            pltpu.VMEM((count, rows, head_dim), f32),
            pltpu.VMEM((count, rows, head_dim), f32),
            pltpu.VMEM((count, rows, head_dim), f32),
            pltpu.SemaphoreType.DMA((2, blocks)),
        ],
        compiler_params=pltpu.CompilerParams(vmem_limit_bytes=32 << 20),
        cost_estimate=pl.CostEstimate(
            flops=4 * rows * page_count * kv_local * page_size * head_dim,
            bytes_accessed=4 * page_count * kv_local * page_size * head_dim,
            transcendentals=0,
        ),
        name="attend_pages",
    )(slots, valid, queries, fresh_keys, fresh_values, key_cache, value_cache)


def merge_kernel(final, count, *refs):
    parts, out_ref = refs[:count], refs[count]
    groups, tiles, rows, head_dim = parts[0].shape
    pairs = tiles - 1
    scratch = refs[count + 1] if final else None
    for group in range(groups):
        stats = [decode_stats(part[group, pairs], pairs) for part in parts]
        top = functools.reduce(jnp.maximum, [s[0] for s in stats])
        factors = [jnp.exp(s[0] - top) for s in stats]
        total = functools.reduce(jnp.add, [s[1] * f for s, f in zip(stats, factors)])
        if final:
            inverse = 1.0 / total
            factors = [f * inverse for f in factors]
        for i in range(pairs):
            acc = functools.reduce(
                jnp.add,
                [part[group, i].astype(f32) * f[:, i : i + 1] for part, f in zip(parts, factors)],
            )
            if not final:
                out_ref[group, i] = acc.astype(bf16)
                continue
            kv_local = scratch.shape[1] // (rows // STEPS * head_dim)
            request, head = i // kv_local, i % kv_local
            per_step = rows // STEPS
            local_rows = pairs // kv_local
            for row in range(rows):
                step, member = row // per_step, row % per_step
                column = (head * per_step + member) * head_dim
                scratch[step * local_rows + request, column : column + head_dim] = acc[row]
        if not final:
            lane = lax.broadcasted_iota(jnp.int32, (rows, head_dim), 1)
            used = lane < pairs
            out_ref[group, pairs] = encode_stats(
                jnp.where(used, top, 0.0), jnp.where(used, total, 0.0), pairs
            )
    if final:
        out_ref[...] = scratch[...].astype(bf16)


def merge_parts(parts, out_shape=None):
    final = out_shape is not None
    vmem = pl.BlockSpec(memory_space=pltpu.VMEM)
    return pl.pallas_call(
        functools.partial(merge_kernel, final, len(parts)),
        out_shape=jax.ShapeDtypeStruct(out_shape if final else parts[0].shape, bf16),
        in_specs=[vmem] * len(parts),
        out_specs=vmem,
        scratch_shapes=[pltpu.VMEM(out_shape, f32)] if final else [],
        name="merge_parts",
    )(*parts)


def local(
    token_inputs,
    attn_gain,
    w_query,
    key_projection,
    value_projection,
    w_output,
    mlp_gain,
    w_gate,
    w_up,
    w_down,
    key_cache,
    paged_value_cache,
    cache_lengths,
    page_request,
    page_number,
    request_slot,
):
    steps, row_count, width = token_inputs.shape
    seq, tp = lax.axis_size("seq"), lax.axis_size("tp")
    deep, across = split_axis(seq)
    ways, cores = tp // CORES, CORES
    page_count, kv_local, page_size, head_dim = key_cache.shape
    heads_per_group = w_query.shape[1] // (kv_local * head_dim)
    rows = steps * row_count
    pairs = row_count * kv_local
    me, part = lax.axis_index("seq"), lax.axis_index("tp")
    quarter = width // tp

    own_rows = me * row_count + jnp.arange(row_count, dtype=jnp.int32)
    row_lengths = jnp.sum(
        jnp.where(request_slot[None, :] == own_rows[:, None], cache_lengths[None, :], 0), axis=1
    )
    page_live = page_request >= 0
    request_ids = jnp.arange(request_slot.shape[0], dtype=jnp.int32)
    is_request = request_ids[None, :] == page_request[:, None]
    page_row = jnp.sum(jnp.where(is_request, request_slot[None, :], 0), axis=1)
    page_length = jnp.sum(jnp.where(is_request, cache_lengths[None, :], 0), axis=1)
    valid = jnp.where(page_live, jnp.clip(page_length - page_number * page_size, 0, page_size), 0)
    mask = (page_row // row_count) ^ me
    slots = ((mask % across) * deep + mask // across) * row_count + page_row % row_count

    positions = (row_lengths[None, :] + jnp.arange(steps, dtype=jnp.int32)[:, None]).reshape(rows)
    cosine, sine = rotary_tables(positions, head_dim)
    normalized = rms_norm(token_inputs, attn_gain).astype(bf16).reshape(rows, width)
    query = apply_rotary(
        jnp.dot(normalized, w_query, preferred_element_type=f32).reshape(rows, -1, head_dim), cosine, sine
    ).astype(bf16)
    query = query.reshape(steps, row_count, kv_local, heads_per_group, head_dim)
    query = query.transpose(1, 2, 0, 3, 4).reshape(pairs, steps * heads_per_group, head_dim)

    shared = [query] + [swap(query, "seq", across * k) for k in range(1, deep)]
    shared = jnp.concatenate(shared, axis=0)
    queries = [shared] + [swap(shared, "seq", k) for k in range(1, across)]
    queries = jnp.concatenate(queries, axis=0)

    fresh_key = apply_rotary(
        jnp.dot(normalized, key_projection, preferred_element_type=f32).reshape(rows, -1, head_dim),
        cosine,
        sine,
    ).astype(bf16)
    fresh_value = jnp.dot(normalized, value_projection, preferred_element_type=f32).astype(bf16)

    def fresh_tiles(value):
        value = value.reshape(steps, row_count, kv_local, head_dim).transpose(1, 2, 0, 3)
        value = value.reshape(pairs, steps, head_dim)
        return jnp.pad(value, ((0, 0), (0, 16 - steps), (0, 0)))

    packed = attend_pages(
        queries,
        fresh_tiles(fresh_key),
        fresh_tiles(fresh_value),
        key_cache,
        paged_value_cache,
        slots,
        valid,
        seq,
    )
    sides = [packed[:deep]] + [swap(packed[k * deep : (k + 1) * deep], "seq", k) for k in range(1, across)]
    merged = merge_parts(sides)
    layers = [merged[:1]] + [swap(merged[k : k + 1], "seq", across * k) for k in range(1, deep)]
    attention = merge_parts(layers, (rows, kv_local * heads_per_group * head_dim))

    head_part = jnp.dot(attention, w_output, preferred_element_type=f32)

    def columns(value, slot):
        return lax.dynamic_slice_in_dim(value, (part ^ slot) * quarter, quarter, value.ndim - 1)

    own_input = columns(token_inputs.reshape(rows, width), 0)
    terms = [columns(head_part, slot) for slot in range(tp)]
    received = [swap(terms[slot].astype(bf16), "tp", slot) for slot in range(1, tp)]
    total = own_input.astype(f32) + terms[0]
    for term in received:
        total = total + term.astype(f32)
    own_attended = total.astype(bf16)

    layered = [own_attended] + [swap(own_attended, "seq", across * k) for k in range(1, deep)]
    near = jnp.concatenate(layered[: deep // 2], axis=0)
    far = jnp.concatenate(layered[deep // 2 :], axis=0)
    near = jnp.concatenate([near] + [swap(near, "seq", k) for k in range(1, across)], axis=0)
    far = jnp.stack([far] + [swap(far, "tp", CORES * k) for k in range(1, ways)])
    near = jnp.stack([near] + [swap(near, "tp", CORES * k) for k in range(1, ways)])
    far = jnp.concatenate([far] + [swap(far, "seq", k) for k in range(1, across)], axis=1)
    both = jnp.concatenate([near, far], axis=1)
    other = swap(both, "tp", 1)
    all_rows = both.shape[1]

    def assemble(pieces, other_pieces, height):
        whole = jnp.zeros((height, width), bf16)
        for k in range(ways):
            for core, source in ((0, pieces), (1, other_pieces)):
                at = (part ^ (k * CORES + core)) * quarter
                whole = lax.dynamic_update_slice_in_dim(whole, source[k], at, 1)
        return whole

    gathered = assemble(both, other, all_rows)
    attended = gathered[:rows].reshape(steps, row_count, width)

    normed_mlp = rms_norm(gathered, mlp_gain).astype(bf16)
    gate_proj = jnp.dot(normed_mlp, w_gate, preferred_element_type=f32)
    up_proj = jnp.dot(normed_mlp, w_up, preferred_element_type=f32)
    activation = (jax.nn.silu(gate_proj) * up_proj).astype(bf16)
    partial_terms = jnp.dot(activation, w_down, preferred_element_type=f32).astype(bf16)

    pieces = jnp.stack([columns(partial_terms, slot) for slot in range(tp)]).reshape(
        ways, cores, all_rows, quarter
    )
    summed = pieces[:, 0].astype(f32) + swap(pieces[:, 1], "tp", 1).astype(f32)
    summed = summed.astype(bf16)
    half = all_rows // 2
    near, far = summed[:, :half], summed[:, half:]

    def add(first, others):
        value = first.astype(f32)
        for other in others:
            value = value + other.astype(f32)
        return value

    near = add(near[0], [swap(near[k], "tp", CORES * k) for k in range(1, ways)]).astype(bf16)
    far = far.reshape(ways, across, half // across, quarter)
    far = add(far[:, 0], [swap(far[:, k], "seq", k) for k in range(1, across)]).astype(bf16)
    near = near.reshape(across, half // across, quarter)
    near = add(near[0], [swap(near[k], "seq", k) for k in range(1, across)]).astype(bf16)
    far = add(far[0], [swap(far[k], "tp", CORES * k) for k in range(1, ways)]).astype(bf16)
    layered = jnp.concatenate([near, far], axis=0).reshape(deep, rows, quarter)
    mlp_result = add(layered[0], [swap(layered[k], "seq", across * k) for k in range(1, deep)])
    own_out = (own_attended.astype(f32) + mlp_result).astype(bf16)

    spread = jnp.stack([own_out] + [swap(own_out, "tp", CORES * k) for k in range(1, ways)])
    layer_out = assemble(spread, swap(spread, "tp", 1), rows).reshape(steps, row_count, width)
    return attended, layer_out


def solution(mesh):
    in_specs = (
        P(None, "seq", None),
        P(),
        P(None, "tp"),
        P(None, "tp"),
        P(None, "tp"),
        P("tp", None),
        P(),
        P(None, ("seq", "tp")),
        P(None, ("seq", "tp")),
        P(("seq", "tp"), None),
        P("seq", "tp", None, None),
        P("seq", "tp", None, None),
        P(),
        P("seq"),
        P("seq"),
        P(),
    )
    out_specs = (P(None, "seq", None), P(None, "seq", None))
    return jax.shard_map(local, mesh=mesh, in_specs=in_specs, out_specs=out_specs, check_vma=False)
```

time: 1040 us -> 197 us (0.19); the launches traced: 1030 us -> 196 us
  blocking collectives: 323 us -> 0 us
  matrix products: 248 us -> 37.8 us
  waiting for transfers between devices: 256 us -> 57.4 us
  local copies, waits for them, and re-layouts: 143 us -> 32.1 us
  starting transfers between devices: 0.71 us -> 37.7 us
  other arithmetic: 38.4 us -> 4.81 us
  Pallas kernels: 0 us -> 25.5 us
  between operations: 16.8 us -> 1.18 us
    all_gather x8 -> x0, blocking collectives: 257 us -> none  [the longest x4 129 us: local(): row_piece = lax.all_gather(normed_mlp, 'seq', axis=0, tiled=True)]
    dot_general x139 -> x6, matrix products: 244 us -> 37.8 us  [the longest x1 14.6 us: local(): jnp.dot(activation, w_down, preferred_element_type=f32).astype(bf16)]
    reduce_scatter x5 -> x0, waiting for transfers between devices: 118 us -> none  [the longest x4 118 us: local(): lax.psum_scatter(summed_units, 'seq', scatter_dimension=0, tiled=True)]
    gather x76 -> x0, local copies, waits for them, and re-layouts: 76.8 us -> none  [the longest x36 36.9 us: block_step(): page_query = all_queries[rows_block]]
    unnamed x9 -> x0, waiting for transfers between devices: 70.7 us -> none
    psum x2 -> x0, waiting for transfers between devices: 67.2 us -> none  [the longest x1 34.3 us: local(): summed_units = lax.psum(partial_terms, 'tp')]
    ppermute x0 -> x29, waiting for transfers between devices: none -> 57.4 us  [swap(): return lax.ppermute(value, axis, [(i, i ^ mask) for i in range(size)])]
    ppermute x0 -> x29, starting transfers between devices: none -> 37.7 us  [swap(): return lax.ppermute(value, axis, [(i, i ^ mask) for i in range(size)])]
  transfers between devices with their start and end apart: 8 -> 29, of which waited for: 5 -> 18; matrix products, arithmetic and copies ran while one was open for 9% -> 5% of each run, Pallas kernels for 0% -> 0%
where the time goes in v1:
time: 197 us; the launch traced here: 196 us
  waiting for transfers between devices  57.4 us (29%)
  matrix products  37.8 us (19%)
  starting transfers between devices  37.7 us (19%)
  local copies, waits for them, and re-layouts  32.1 us (16%)
  Pallas kernels  25.5 us (13%)
  other arithmetic  4.81 us (2%)
    ppermute x29, waiting for transfers between devices, swap(): return lax.ppermute(value, axis, [(i, i ^ mask) for i in range(size)])  57.4 us
    ppermute x29, starting transfers between devices, swap(): return lax.ppermute(value, axis, [(i, i ^ mask) for i in range(size)])  37.7 us
    pallas_call x1, Pallas kernels, attend_pages(): pl.pallas_call(functools.partial(pages_kernel, block_pages), out_shape=ja...  20.9 us
    dot_general x1, matrix products, local(): jnp.dot(activation, w_down, preferred_element_type=f32).astype(bf16)  14.6 us
    dot_general x1, local copies, waits for them, and re-layouts, local(): jnp.dot(normalized, w_query, preferred_element_type=f32)  13.8 us
    dot_general x1, matrix products, local(): gate_proj = jnp.dot(normed_mlp, w_gate, preferred_element_type=f32)  8.18 us
    unnamed x39, local copies, waits for them, and re-layouts  6.83 us
    dot_general x1, matrix products, local(): head_part = jnp.dot(attention, w_output, preferred_element_type=f32)  5.92 us
  transfers between devices with their start and end apart: 29, of which 18 were waited for; matrix products, arithmetic and copies ran while one was open for 5% of the time, Pallas kernels for 0%

profile of v1, /device:TPU:0, one launch (start us, length us, event | category | flops | bytes accessed | tf_op | source)
XLA Modules:
  0.0 196.5 jit_solution(2443979627246104171)
XLA Ops:
  0.7 1.0 select_reduce_fusion.2
  1.8 1.1 fusion.9
  2.9 13.8 %copy.49 = bf16[1024,5120]{1,0:T(8,128)(2,1)} copy(bf16[1024,5120]{0,1:T(8,128)(2,1)} %bitcast.120) | data formatting | bytes 20971520 | tf_op jit(solution)/shard_map/dot_general | solution.py:307
  16.9 5.8 %fusion.23 = f32[32,8,128]{2,0,1:T(8,128)S(1)} fusion(bf16[8,128,5120]{2,1,0:T(8,128)(2,1)} %bitcast.119, bf16[4,8,5120]{2,1,0:T(8,128)(2,1)S(1)} %copy-done.5, f32[5120]{0:T(1024)S(1)} %copy-done.8, f32[4,8]{1,0:T(4,128)S(1)} %add_rsqrt_fusion), kind=kOutput, calls=%fused_computation.49 | convolution fusion | flops 336199680 | bytes 10965120 | tf_op jit(solution)/shard_map/dot_general | solution.py:307
  23.0 3.1 %collective-permute-start = (bf16[16,16,128]{2,1,0:T(8,128)(2,1)S(1)}, bf16[16,16,128]{2,1,0:T(8,128)(2,1)S(1)}, u32[]{:S(2)}, u32[]{:S(2)}) collective-permute-start(bf16[16,16,128]{2,1,0:T(8,128)(2,1)S(1)} %bitcast.132), channel_id=1, source_target_pairs={{0,8},{4,12},{8,0},{12,4},{16,24},{20,28},{24,16},{28,20},{1,9},{5... | collective-permute-start | bytes 196616 | tf_op jit(solution)/shard_map/ppermute | solution.py:29
  26.1 2.6 %collective-permute-start.1 = (bf16[16,16,128]{2,1,0:T(8,128)(2,1)S(1)}, bf16[16,16,128]{2,1,0:T(8,128)(2,1)S(1)}, u32[]{:S(2)}, u32[]{:S(2)}) collective-permute-start(bf16[16,16,128]{2,1,0:T(8,128)(2,1)S(1)} %bitcast.133), channel_id=1, source_target_pairs={{0,16},{4,20},{8,24},{12,28},{16,0},{20,4},{24,8},{28,12},{1,17},{... | collective-permute-start | bytes 196616 | tf_op jit(solution)/shard_map/ppermute | solution.py:29
  28.7 4.4 %copy.50 = bf16[256,5120]{1,0:T(8,128)(2,1)} copy(bf16[256,5120]{0,1:T(8,128)(2,1)} %bitcast.125) | data formatting | bytes 5242880 | tf_op jit(solution)/shard_map/dot_general | solution.py:318
  33.2 2.7 %fusion.21 = f32[32,2,128]{2,0,1:T(8,128)S(1)} fusion(bf16[2,128,5120]{2,1,0:T(8,128)(2,1)} %bitcast.123, bf16[4,8,5120]{2,1,0:T(8,128)(2,1)S(1)} %copy-done.5, f32[5120]{0:T(1024)S(1)} %copy-done.8, f32[4,8]{1,0:T(4,128)S(1)} %add_rsqrt_fusion), kind=kOutput, calls=%fused_computation.47 | convolution fusion | flops 84541440 | bytes 3002496 | tf_op jit(solution)/shard_map/dot_general | solution.py:318
  36.2 0.6 fusion.5
  37.0 1.8 collective-permute-start.3
  38.9 5.7 %collective-permute-done.3 = bf16[64,16,128]{2,1,0:T(8,128)(2,1)S(1)} collective-permute-done((bf16[64,16,128]{2,1,0:T(8,128)(2,1)S(1)}, bf16[64,16,128]{2,1,0:T(8,128)(2,1)S(1)}, u32[]{:S(2)}, u32[]{:S(2)}) %collective-permute-start.3) | collective-permute-done | bytes 262176 | tf_op jit(solution)/shard_map/ppermute | solution.py:29
  44.6 2.3 %copy-done.2 = bf16[36,2,256,128]{3,2,1,0:T(8,128)(2,1)S(1)} copy-done((bf16[36,2,256,128]{3,2,1,0:T(8,128)(2,1)S(1)}, bf16[36,2,256,128]{3,2,1,0:T(8,128)(2,1)}, u32[]{:S(2)}) %copy-start.2) | copy-done | bytes 4718616
  47.0 2.3 %copy-done.3 = bf16[36,2,256,128]{3,2,1,0:T(8,128)(2,1)S(1)} copy-done((bf16[36,2,256,128]{3,2,1,0:T(8,128)(2,1)S(1)}, bf16[36,2,256,128]{3,2,1,0:T(8,128)(2,1)}, u32[]{:S(2)}) %copy-start.3) | copy-done | bytes 4718616
  49.3 20.9 %attend_pages.1 = bf16[8,17,16,128]{3,2,1,0:T(8,128)(2,1)S(1)} custom-call(s32[36]{0:T(128)S(1)} %get-tuple-element.30.slot_ref, s32[36]{0:T(128)S(1)} %get-tuple-element.29.valid_ref, bf16[128,16,128]{2,1,0:T(8,128)(2,1)S(1)} %constant_dynamic-update-slice_fusion.query_ref, bf16[16,16,128]{2,1,0:T(8,128)(2,1)S(1)} %pad.7.fresh_key_ref, ...), custom_call_target="tpu_custom_call" | custom-call | flops 150994944 | bytes 9437184 | tf_op jit(solution)/shard_map/attend_pages/pallas_call | solution.py:186
  70.2 0.7 fusion.38
  70.9 1.5 collective-permute-start.4
  72.4 5.4 %collective-permute-done.4.refs_1_ = bf16[4,17,16,128]{3,2,1,0:T(8,128)(2,1)S(1)} collective-permute-done((bf16[4,17,16,128]{3,2,1,0:T(8,128)(2,1)S(1)}, bf16[4,17,16,128]{3,2,1,0:T(8,128)(2,1)S(1)}, u32[]{:S(2)}, u32[]{:S(2)}) %collective-permute-start.4) | collective-permute-done | bytes 278560 | tf_op jit(solution)/shard_map/ppermute | solution.py:29
  77.9 0.7 copy-done.7
  78.6 2.6 %merge_parts.2 = bf16[4,17,16,128]{3,2,1,0:T(8,128)(2,1)} custom-call(bf16[4,17,16,128]{3,2,1,0:T(8,128)(2,1)} %get-tuple-element.14.refs_0_, bf16[4,17,16,128]{3,2,1,0:T(8,128)(2,1)} %copy-done.7), custom_call_target="tpu_custom_call" | custom-call | tf_op jit(solution)/shard_map/merge_parts/pallas_call | solution.py:251
  81.2 1.6 fusion.39
  82.8 0.3 collective-permute-start.5
  83.2 3.5 %collective-permute-start.6 = (bf16[1,17,16,128]{3,2,1,0:T(8,128)(2,1)S(1)}, bf16[1,17,16,128]{3,2,1,0:T(8,128)(2,1)S(1)}, u32[]{:S(2)}, u32[]{:S(2)}) collective-permute-start(bf16[1,17,16,128]{3,2,1,0:T(8,128)(2,1)S(1)} %get-tuple-element.18), channel_id=1, source_target_pairs={{0,16},{4,20},{8,24},{12,28},{16,0},{20,4},{24,8},{28,12},{1,17},{... | collective-permute-start | bytes 208904 | tf_op jit(solution)/shard_map/ppermute | solution.py:29
  86.7 0.6 collective-permute-start.7
  87.2 2.9 %collective-permute-done.6.refs_2_ = bf16[1,17,16,128]{3,2,1,0:T(8,128)(2,1)S(1)} collective-permute-done((bf16[1,17,16,128]{3,2,1,0:T(8,128)(2,1)S(1)}, bf16[1,17,16,128]{3,2,1,0:T(8,128)(2,1)S(1)}, u32[]{:S(2)}, u32[]{:S(2)}) %collective-permute-start.6) | collective-permute-done | bytes 69664 | tf_op jit(solution)/shard_map/ppermute | solution.py:29
  90.2 2.6 %collective-permute-done.7.refs_3_ = bf16[1,17,16,128]{3,2,1,0:T(8,128)(2,1)S(1)} collective-permute-done((bf16[1,17,16,128]{3,2,1,0:T(8,128)(2,1)S(1)}, bf16[1,17,16,128]{3,2,1,0:T(8,128)(2,1)S(1)}, u32[]{:S(2)}, u32[]{:S(2)}) %collective-permute-start.7) | collective-permute-done | bytes 69664 | tf_op jit(solution)/shard_map/ppermute | solution.py:29
  92.8 0.6 copy-done.11
  93.4 2.0 merge_parts.3
  95.4 5.9 %fusion.41 = f32[32,5120]{1,0:T(8,128)S(1)} fusion(bf16[32,1024]{1,0:T(8,128)(2,1)} %merge_parts.3, bf16[1024,5120]{1,0:T(8,128)(2,1)} %param.21), kind=kOutput, calls=%fused_computation.114 | convolution fusion | flops 335544320 | bytes 11206656 | tf_op jit(solution)/shard_map/dot_general | solution.py:344
  101.4 1.6 collective-permute-start.8
  103.0 0.5 collective-permute-start.9
  103.5 2.5 %collective-permute-done.10 = bf16[32,1280]{1,0:T(8,128)(2,1)S(1)} collective-permute-done((bf16[32,1280]{1,0:T(8,128)(2,1)S(1)}, bf16[32,1280]{1,0:T(8,128)(2,1)S(1)}, u32[]{:S(2)}, u32[]{:S(2)}) %collective-permute-start.10) | collective-permute-done | bytes 81952 | tf_op jit(solution)/shard_map/ppermute | solution.py:29
  106.1 1.8 collective-permute-done.9
  108.0 1.3 collective-permute-start.14
  109.4 3.0 %collective-permute-start.15 = (bf16[32,1280]{1,0:T(8,128)(2,1)S(1)}, bf16[32,1280]{1,0:T(8,128)(2,1)S(1)}, u32[]{:S(2)}, u32[]{:S(2)}) collective-permute-start(bf16[32,1280]{1,0:T(8,128)(2,1)S(1)} %add_convert_fusion.2), channel_id=1, source_target_pairs={{0,24},{4,28},{8,16},{12,20},{16,8},{20,12},{24,0},{28,4},{1,25},{... | collective-permute-start | bytes 245768 | tf_op jit(solution)/shard_map/ppermute | solution.py:29
  112.4 0.5 collective-permute-done.11
  113.0 1.6 collective-permute-start.12
  114.5 2.8 %collective-permute-done.14 = bf16[32,1280]{1,0:T(8,128)(2,1)S(1)} collective-permute-done((bf16[32,1280]{1,0:T(8,128)(2,1)S(1)}, bf16[32,1280]{1,0:T(8,128)(2,1)S(1)}, u32[]{:S(2)}, u32[]{:S(2)}) %collective-permute-start.14) | collective-permute-done | bytes 81952 | tf_op jit(solution)/shard_map/ppermute | solution.py:29
  117.4 0.9 collective-permute-start.16
  118.4 1.2 collective-permute-start.13
  119.6 4.1 %collective-permute-done.16 = bf16[64,1280]{1,0:T(8,128)(2,1)S(1)} collective-permute-done((bf16[64,1280]{1,0:T(8,128)(2,1)S(1)}, bf16[64,1280]{1,0:T(8,128)(2,1)S(1)}, u32[]{:S(2)}, u32[]{:S(2)}) %collective-permute-start.16) | collective-permute-done | bytes 163872 | tf_op jit(solution)/shard_map/ppermute | solution.py:29
  123.7 1.6 collective-permute-start.17
  125.3 1.9 collective-permute-done.13
  127.2 3.7 %collective-permute-done.17 = bf16[2,64,1280]{2,1,0:T(8,128)(2,1)S(1)} collective-permute-done((bf16[2,64,1280]{2,1,0:T(8,128)(2,1)S(1)}, bf16[2,64,1280]{2,1,0:T(8,128)(2,1)S(1)}, u32[]{:S(2)}, u32[]{:S(2)}) %collective-permute-start.17) | collective-permute-done | bytes 327712 | tf_op jit(solution)/shard_map/ppermute | solution.py:29
  131.4 2.6 %collective-permute-done.18 = bf16[2,256,1280]{2,1,0:T(8,128)(2,1)S(1)} collective-permute-done((bf16[2,256,1280]{2,1,0:T(8,128)(2,1)S(1)}, bf16[2,256,1280]{2,1,0:T(8,128)(2,1)S(1)}, u32[]{:S(2)}, u32[]{:S(2)}) %collective-permute-start.18) | collective-permute-done | bytes 1310752 | tf_op jit(solution)/shard_map/ppermute | solution.py:29
  134.3 0.6 fusion
  134.9 8.2 %fusion.7 = f32[256,1024]{1,0:T(8,128)} fusion(bf16[5120,1024]{1,0:T(8,128)(2,1)} %param.23, bf16[256,5120]{1,0:T(8,128)(2,1)S(1)} %fusion.12, f32[5120]{0:T(1024)S(1)} %copy-done.16, f32[256]{0:T(256)S(1)} %add_rsqrt_fusion.1), kind=kOutput, calls=%fused_computation.18 | convolution fusion | flops 2689597440 | bytes 14177280 | tf_op jit(solution)/shard_map/dot_general | solution.py:380
  143.1 14.6 %convolution_convert_fusion = bf16[256,5120]{1,0:T(8,128)(2,1)} fusion(bf16[1024,5120]{1,0:T(8,128)(2,1)} %param.25, bf16[5120,1024]{1,0:T(8,128)(2,1)} %param.24, f32[256,1024]{1,0:T(8,128)} %fusion.7, bf16[256,5120]{1,0:T(8,128)(2,1)S(1)} %fusion.12, f32[5120]{0:T(1024)S(1)} %copy-done.16, f32[256]{0:T(256)S(1)} %add_rsqrt_fusion.1), kind=kOutput, calls=%fused_computation.2 | convolution fusion | flops 5376835584 | bytes 27284480 | tf_op jit(solution)/shard_map/dot_general | solution.py:383
  157.7 1.9 dynamic-slice_bitcast_fusion.3
  160.2 2.9 %collective-permute-done.19 = bf16[2,256,1280]{2,1,0:T(8,128)(2,1)S(1)} collective-permute-done((bf16[2,256,1280]{2,1,0:T(8,128)(2,1)S(1)}, bf16[2,256,1280]{2,1,0:T(8,128)(2,1)S(1)}, u32[]{:S(2)}, u32[]{:S(2)}) %collective-permute-start.19) | collective-permute-done | bytes 1310752 | tf_op jit(solution)/shard_map/ppermute | solution.py:29
  163.1 0.3 fusion.3
  163.5 1.0 collective-permute-start.20
  164.6 1.6 collective-permute-start.23
  166.1 7.2 %collective-permute-done.20 = bf16[128,1280]{1,0:T(8,128)(2,1)S(1)} collective-permute-done((bf16[128,1280]{1,0:T(8,128)(2,1)S(1)}, bf16[128,1280]{1,0:T(8,128)(2,1)S(1)}, u32[]{:S(2)}, u32[]{:S(2)}) %collective-permute-start.20) | collective-permute-done | bytes 327712 | tf_op jit(solution)/shard_map/ppermute | solution.py:29
  173.5 1.6 collective-permute-start.21
  175.1 1.0 collective-permute-start.24
  176.1 2.8 %collective-permute-done.21 = bf16[64,1280]{1,0:T(8,128)(2,1)S(1)} collective-permute-done((bf16[64,1280]{1,0:T(8,128)(2,1)S(1)}, bf16[64,1280]{1,0:T(8,128)(2,1)S(1)}, u32[]{:S(2)}, u32[]{:S(2)}) %collective-permute-start.21) | collective-permute-done | bytes 163872 | tf_op jit(solution)/shard_map/ppermute | solution.py:29
  179.0 2.3 %collective-permute-start.22 = (bf16[32,1280]{1,0:T(8,128)(2,1)S(1)}, bf16[32,1280]{1,0:T(8,128)(2,1)S(1)}, u32[]{:S(2)}, u32[]{:S(2)}) collective-permute-start(bf16[32,1280]{1,0:T(8,128)(2,1)S(1)} %slice.163), channel_id=1, source_target_pairs={{0,8},{4,12},{8,0},{12,4},{16,24},{20,28},{24,16},{28,20},{1,9},{5... | collective-permute-start | bytes 245768 | tf_op jit(solution)/shard_map/ppermute | solution.py:29
  181.4 1.4 collective-permute-start.25
  182.8 2.4 %collective-permute-start.26 = (bf16[32,1280]{1,0:T(8,128)(2,1)S(1)}, bf16[32,1280]{1,0:T(8,128)(2,1)S(1)}, u32[]{:S(2)}, u32[]{:S(2)}) collective-permute-start(bf16[32,1280]{1,0:T(8,128)(2,1)S(1)} %get-tuple-element.22), channel_id=1, source_target_pairs={{0,24},{4,28},{8,16},{12,20},{16,8},{20,12},{24,0},{28,4},{1,25},{... | collective-permute-start | bytes 245768 | tf_op jit(solution)/shard_map/ppermute | solution.py:29
  185.2 4.0 %collective-permute-done.25 = bf16[32,1280]{1,0:T(8,128)(2,1)S(1)} collective-permute-done((bf16[32,1280]{1,0:T(8,128)(2,1)S(1)}, bf16[32,1280]{1,0:T(8,128)(2,1)S(1)}, u32[]{:S(2)}, u32[]{:S(2)}) %collective-permute-start.25) | collective-permute-done | bytes 81952 | tf_op jit(solution)/shard_map/ppermute | solution.py:29
  189.3 0.8 collective-permute-start.27
  190.2 3.7 %collective-permute-done.27 = bf16[32,1280]{1,0:T(8,128)(2,1)S(1)} collective-permute-done((bf16[32,1280]{1,0:T(8,128)(2,1)S(1)}, bf16[32,1280]{1,0:T(8,128)(2,1)S(1)}, u32[]{:S(2)}, u32[]{:S(2)}) %collective-permute-start.27) | collective-permute-done | bytes 81952 | tf_op jit(solution)/shard_map/ppermute | solution.py:29
  193.9 1.7 slice_bitcast_fusion.10
  195.7 0.7 copy-done.6
  (105 shorter events, 3.6 us)
Async XLA Ops:
  0.6 35.5 %copy-start = (bf16[5120,256]{1,0:T(8,128)(2,1)S(1)}, bf16[5120,256]{1,0:T(8,128)(2,1)}, u32[]{:S(2)}) copy-start(bf16[5120,256]{1,0:T(8,128)(2,1)} %param.20) | copy-start | bytes 7864324
  2.9 13.9 %copy-start.5 = (bf16[4,8,5120]{2,1,0:T(8,128)(2,1)S(1)}, bf16[4,8,5120]{2,1,0:T(8,128)(2,1)}, u32[]{:S(2)}) copy-start(bf16[4,8,5120]{2,1,0:T(8,128)(2,1)} %param.16) | copy-start | bytes 983044
  2.9 13.9 %copy-start.8 = (f32[5120]{0:T(1024)S(1)}, f32[5120]{0:T(1024)}, u32[]{:S(2)}) copy-start(f32[5120]{0:T(1024)} %param.17) | copy-start | bytes 61444
  23.0 13.9 %collective-permute-start = (bf16[16,16,128]{2,1,0:T(8,128)(2,1)S(1)}, bf16[16,16,128]{2,1,0:T(8,128)(2,1)S(1)}, u32[]{:S(2)}, u32[]{:S(2)}) collective-permute-start(bf16[16,16,128]{2,1,0:T(8,128)(2,1)S(1)} %bitcast.132), channel_id=1, source_target_pairs={{0,8},{4,12},{8,0},{12,4},{16,24},{20,28},{24,16},{28,20},{1,9},{5... | collective-permute-start | bytes 196616 | tf_op jit(solution)/shard_map/ppermute | solution.py:29
  26.1 10.9 %collective-permute-start.1 = (bf16[16,16,128]{2,1,0:T(8,128)(2,1)S(1)}, bf16[16,16,128]{2,1,0:T(8,128)(2,1)S(1)}, u32[]{:S(2)}, u32[]{:S(2)}) collective-permute-start(bf16[16,16,128]{2,1,0:T(8,128)(2,1)S(1)} %bitcast.133), channel_id=1, source_target_pairs={{0,16},{4,20},{8,24},{12,28},{16,0},{20,4},{24,8},{28,12},{1,17},{... | collective-permute-start | bytes 196616 | tf_op jit(solution)/shard_map/ppermute | solution.py:29
  28.7 8.3 %collective-permute-start.2 = (bf16[16,16,128]{2,1,0:T(8,128)(2,1)S(1)}, bf16[16,16,128]{2,1,0:T(8,128)(2,1)S(1)}, u32[]{:S(2)}, u32[]{:S(2)}) collective-permute-start(bf16[16,16,128]{2,1,0:T(8,128)(2,1)S(1)} %bitcast.134), channel_id=1, source_target_pairs={{0,24},{4,28},{8,16},{12,20},{16,8},{20,12},{24,0},{28,4},{1,25},{... | collective-permute-start | bytes 196616 | tf_op jit(solution)/shard_map/ppermute | solution.py:29
  33.1 2.8 %copy-start.12 = (s32[36]{0:T(128)S(1)}, s32[36]{0:T(128)}, u32[]{:S(2)}) copy-start(s32[36]{0:T(128)} %param.29) | copy-start | bytes 436
  33.1 2.8 %copy-start.13 = (s32[64]{0:T(128)S(1)}, s32[64]{0:T(128)}, u32[]{:S(2)}) copy-start(s32[64]{0:T(128)} %param.28) | copy-start | bytes 772
  33.1 2.8 %copy-start.14 = (s32[64]{0:T(128)S(1)}, s32[64]{0:T(128)}, u32[]{:S(2)}) copy-start(s32[64]{0:T(128)} %param.31) | copy-start | bytes 772
  33.1 3.8 %copy-start.15 = (s32[36]{0:T(128)S(1)}, s32[36]{0:T(128)}, u32[]{:S(2)}) copy-start(s32[36]{0:T(128)} %param.30) | copy-start | bytes 436
  37.0 7.5 %collective-permute-start.3 = (bf16[64,16,128]{2,1,0:T(8,128)(2,1)S(1)}, bf16[64,16,128]{2,1,0:T(8,128)(2,1)S(1)}, u32[]{:S(2)}, u32[]{:S(2)}) collective-permute-start(bf16[64,16,128]{2,1,0:T(8,128)(2,1)S(1)} %pad_maximum_fusion.4), channel_id=1, source_target_pairs={{0,4},{4,0},{8,12},{12,8},{16,20},{20,16},{24,28},{28,24},{1,5},{5... | collective-permute-start | bytes 786440 | tf_op jit(solution)/shard_map/ppermute | solution.py:29
  44.6 2.3 %copy-start.2 = (bf16[36,2,256,128]{3,2,1,0:T(8,128)(2,1)S(1)}, bf16[36,2,256,128]{3,2,1,0:T(8,128)(2,1)}, u32[]{:S(2)}) copy-start(bf16[36,2,256,128]{3,2,1,0:T(8,128)(2,1)} %key_hbm.1) | copy-start | bytes 14155780
  47.0 2.3 %copy-start.3 = (bf16[36,2,256,128]{3,2,1,0:T(8,128)(2,1)S(1)}, bf16[36,2,256,128]{3,2,1,0:T(8,128)(2,1)}, u32[]{:S(2)}) copy-start(bf16[36,2,256,128]{3,2,1,0:T(8,128)(2,1)} %value_hbm.1) | copy-start | bytes 14155780
  70.9 6.9 %collective-permute-start.4 = (bf16[4,17,16,128]{3,2,1,0:T(8,128)(2,1)S(1)}, bf16[4,17,16,128]{3,2,1,0:T(8,128)(2,1)S(1)}, u32[]{:S(2)}, u32[]{:S(2)}) collective-permute-start(bf16[4,17,16,128]{3,2,1,0:T(8,128)(2,1)S(1)} %get-tuple-element.13), channel_id=1, source_target_pairs={{0,4},{4,0},{8,12},{12,8},{16,20},{20,16},{24,28},{28,24},{1,5},{5... | collective-permute-start | bytes 835592 | tf_op jit(solution)/shard_map/ppermute | solution.py:29
  77.9 0.7 copy-start.7
  82.8 4.4 %collective-permute-start.5 = (bf16[1,17,16,128]{3,2,1,0:T(8,128)(2,1)S(1)}, bf16[1,17,16,128]{3,2,1,0:T(8,128)(2,1)S(1)}, u32[]{:S(2)}, u32[]{:S(2)}) collective-permute-start(bf16[1,17,16,128]{3,2,1,0:T(8,128)(2,1)S(1)} %get-tuple-element.19), channel_id=1, source_target_pairs={{0,8},{4,12},{8,0},{12,4},{16,24},{20,28},{24,16},{28,20},{1,9},{5... | collective-permute-start | bytes 208904 | tf_op jit(solution)/shard_map/ppermute | solution.py:29
  83.2 7.0 %collective-permute-start.6 = (bf16[1,17,16,128]{3,2,1,0:T(8,128)(2,1)S(1)}, bf16[1,17,16,128]{3,2,1,0:T(8,128)(2,1)S(1)}, u32[]{:S(2)}, u32[]{:S(2)}) collective-permute-start(bf16[1,17,16,128]{3,2,1,0:T(8,128)(2,1)S(1)} %get-tuple-element.18), channel_id=1, source_target_pairs={{0,16},{4,20},{8,24},{12,28},{16,0},{20,4},{24,8},{28,12},{1,17},{... | collective-permute-start | bytes 208904 | tf_op jit(solution)/shard_map/ppermute | solution.py:29
  86.7 6.1 %collective-permute-start.7 = (bf16[1,17,16,128]{3,2,1,0:T(8,128)(2,1)S(1)}, bf16[1,17,16,128]{3,2,1,0:T(8,128)(2,1)S(1)}, u32[]{:S(2)}, u32[]{:S(2)}) collective-permute-start(bf16[1,17,16,128]{3,2,1,0:T(8,128)(2,1)S(1)} %get-tuple-element.17), channel_id=1, source_target_pairs={{0,24},{4,28},{8,16},{12,20},{16,8},{20,12},{24,0},{28,4},{1,25},{... | collective-permute-start | bytes 208904 | tf_op jit(solution)/shard_map/ppermute | solution.py:29
  87.2 5.6 %copy-start.9 = (bf16[1,17,16,128]{3,2,1,0:T(8,128)(2,1)}, bf16[1,17,16,128]{3,2,1,0:T(8,128)(2,1)S(1)}, u32[]{:S(2)}) copy-start(bf16[1,17,16,128]{3,2,1,0:T(8,128)(2,1)S(1)} %collective-permute-done.5.refs_1_) | copy-start | bytes 208900
  90.2 2.6 %copy-start.10 = (bf16[1,17,16,128]{3,2,1,0:T(8,128)(2,1)}, bf16[1,17,16,128]{3,2,1,0:T(8,128)(2,1)S(1)}, u32[]{:S(2)}) copy-start(bf16[1,17,16,128]{3,2,1,0:T(8,128)(2,1)S(1)} %collective-permute-done.6.refs_2_) | copy-start | bytes 208900
  92.8 0.6 copy-start.11
  101.3 4.7 %collective-permute-start.10 = (bf16[32,1280]{1,0:T(8,128)(2,1)S(1)}, bf16[32,1280]{1,0:T(8,128)(2,1)S(1)}, u32[]{:S(2)}, u32[]{:S(2)}) collective-permute-start(bf16[32,1280]{1,0:T(8,128)(2,1)S(1)} %get-tuple-element.11), channel_id=1, source_target_pairs={{0,3},{1,2},{2,1},{3,0},{4,7},{5,6},{6,5},{7,4},{8,11},{9,10},{10,... | collective-permute-start | bytes 245768 | tf_op jit(solution)/shard_map/ppermute | solution.py:29
  101.4 4.7 %collective-permute-start.8 = (bf16[32,1280]{1,0:T(8,128)(2,1)S(1)}, bf16[32,1280]{1,0:T(8,128)(2,1)S(1)}, u32[]{:S(2)}, u32[]{:S(2)}) collective-permute-start(bf16[32,1280]{1,0:T(8,128)(2,1)S(1)} %get-tuple-element.10), channel_id=1, source_target_pairs={{0,1},{1,0},{2,3},{3,2},{4,5},{5,4},{6,7},{7,6},{8,9},{9,8},{10,11... | collective-permute-start | bytes 245768 | tf_op jit(solution)/shard_map/ppermute | solution.py:29
  103.0 4.9 %collective-permute-start.9 = (bf16[32,1280]{1,0:T(8,128)(2,1)S(1)}, bf16[32,1280]{1,0:T(8,128)(2,1)S(1)}, u32[]{:S(2)}, u32[]{:S(2)}) collective-permute-start(bf16[32,1280]{1,0:T(8,128)(2,1)S(1)} %get-tuple-element.12), channel_id=1, source_target_pairs={{0,2},{1,3},{2,0},{3,1},{4,6},{5,7},{6,4},{7,5},{8,10},{9,11},{10,... | collective-permute-start | bytes 245768 | tf_op jit(solution)/shard_map/ppermute | solution.py:29
  108.0 5.0 %collective-permute-start.11 = (bf16[32,1280]{1,0:T(8,128)(2,1)S(1)}, bf16[32,1280]{1,0:T(8,128)(2,1)S(1)}, u32[]{:S(2)}, u32[]{:S(2)}) collective-permute-start(bf16[32,1280]{1,0:T(8,128)(2,1)S(1)} %add_convert_fusion.2), channel_id=1, source_target_pairs={{0,8},{4,12},{8,0},{12,4},{16,24},{20,28},{24,16},{28,20},{1,9},{5... | collective-permute-start | bytes 245768 | tf_op jit(solution)/shard_map/ppermute | solution.py:29
  108.0 9.3 %collective-permute-start.14 = (bf16[32,1280]{1,0:T(8,128)(2,1)S(1)}, bf16[32,1280]{1,0:T(8,128)(2,1)S(1)}, u32[]{:S(2)}, u32[]{:S(2)}) collective-permute-start(bf16[32,1280]{1,0:T(8,128)(2,1)S(1)} %add_convert_fusion.2), channel_id=1, source_target_pairs={{0,16},{4,20},{8,24},{12,28},{16,0},{20,4},{24,8},{28,12},{1,17},{... | collective-permute-start | bytes 245768 | tf_op jit(solution)/shard_map/ppermute | solution.py:29
  109.4 8.0 %collective-permute-start.15 = (bf16[32,1280]{1,0:T(8,128)(2,1)S(1)}, bf16[32,1280]{1,0:T(8,128)(2,1)S(1)}, u32[]{:S(2)}, u32[]{:S(2)}) collective-permute-start(bf16[32,1280]{1,0:T(8,128)(2,1)S(1)} %add_convert_fusion.2), channel_id=1, source_target_pairs={{0,24},{4,28},{8,16},{12,20},{16,8},{20,12},{24,0},{28,4},{1,25},{... | collective-permute-start | bytes 245768 | tf_op jit(solution)/shard_map/ppermute | solution.py:29
  113.0 5.4 %collective-permute-start.12 = (bf16[64,1280]{1,0:T(8,128)(2,1)S(1)}, bf16[64,1280]{1,0:T(8,128)(2,1)S(1)}, u32[]{:S(2)}, u32[]{:S(2)}) collective-permute-start(bf16[64,1280]{1,0:T(8,128)(2,1)S(1)} %pad_maximum_fusion.5), channel_id=1, source_target_pairs={{0,4},{4,0},{8,12},{12,8},{16,20},{20,16},{24,28},{28,24},{1,5},{5... | collective-permute-start | bytes 491528 | tf_op jit(solution)/shard_map/ppermute | solution.py:29
  117.4 6.3 %collective-permute-start.16 = (bf16[64,1280]{1,0:T(8,128)(2,1)S(1)}, bf16[64,1280]{1,0:T(8,128)(2,1)S(1)}, u32[]{:S(2)}, u32[]{:S(2)}) collective-permute-start(bf16[64,1280]{1,0:T(8,128)(2,1)S(1)} %constant_dynamic-update-slice_fusion.5), channel_id=1, source_target_pairs={{0,2},{1,3},{2,0},{3,1},{4,6},{5,7},{6,4},{7,5},{8,10},{9,11},{10,... | collective-permute-start | bytes 491528 | tf_op jit(solution)/shard_map/ppermute | solution.py:29
  118.4 8.8 %collective-permute-start.13 = (bf16[128,1280]{1,0:T(8,128)(2,1)S(1)}, bf16[128,1280]{1,0:T(8,128)(2,1)S(1)}, u32[]{:S(2)}, u32[]{:S(2)}) collective-permute-start(bf16[128,1280]{1,0:T(8,128)(2,1)S(1)} %get-tuple-element.16), channel_id=1, source_target_pairs={{0,2},{1,3},{2,0},{3,1},{4,6},{5,7},{6,4},{7,5},{8,10},{9,11},{10,... | collective-permute-start | bytes 983048 | tf_op jit(solution)/shard_map/ppermute | solution.py:29
  123.7 7.1 %collective-permute-start.17 = (bf16[2,64,1280]{2,1,0:T(8,128)(2,1)S(1)}, bf16[2,64,1280]{2,1,0:T(8,128)(2,1)S(1)}, u32[]{:S(2)}, u32[]{:S(2)}) collective-permute-start(bf16[2,64,1280]{2,1,0:T(8,128)(2,1)S(1)} %pad_maximum_fusion.3), channel_id=1, source_target_pairs={{0,4},{4,0},{8,12},{12,8},{16,20},{20,16},{24,28},{28,24},{1,5},{5... | collective-permute-start | bytes 983048 | tf_op jit(solution)/shard_map/ppermute | solution.py:29
  130.9 3.1 %collective-permute-start.18 = (bf16[2,256,1280]{2,1,0:T(8,128)(2,1)S(1)}, bf16[2,256,1280]{2,1,0:T(8,128)(2,1)S(1)}, u32[]{:S(2)}, u32[]{:S(2)}) collective-permute-start(bf16[2,256,1280]{2,1,0:T(8,128)(2,1)S(1)} %pad_maximum_fusion.1), channel_id=1, source_target_pairs={{0,1},{1,0},{2,3},{3,2},{4,5},{5,4},{6,7},{7,6},{8,9},{9,8},{10,11... | collective-permute-start | bytes 3932168 | tf_op jit(solution)/shard_map/ppermute | solution.py:29
  134.1 0.8 copy-start.16
  134.3 8.8 %copy-start.4 = (bf16[256,5120]{1,0:T(8,128)(2,1)}, bf16[256,5120]{1,0:T(8,128)(2,1)S(1)}, u32[]{:S(2)}) copy-start(bf16[256,5120]{1,0:T(8,128)(2,1)S(1)} %fusion.12) | copy-start | bytes 7864324
  160.0 3.1 %collective-permute-start.19 = (bf16[2,256,1280]{2,1,0:T(8,128)(2,1)S(1)}, bf16[2,256,1280]{2,1,0:T(8,128)(2,1)S(1)}, u32[]{:S(2)}, u32[]{:S(2)}) collective-permute-start(bf16[2,256,1280]{2,1,0:T(8,128)(2,1)S(1)} %slice_bitcast_fusion), channel_id=1, source_target_pairs={{0,1},{1,0},{2,3},{3,2},{4,5},{5,4},{6,7},{7,6},{8,9},{9,8},{10,11... | collective-permute-start | bytes 3932168 | tf_op jit(solution)/shard_map/ppermute | solution.py:29
  163.5 9.8 %collective-permute-start.20 = (bf16[128,1280]{1,0:T(8,128)(2,1)S(1)}, bf16[128,1280]{1,0:T(8,128)(2,1)S(1)}, u32[]{:S(2)}, u32[]{:S(2)}) collective-permute-start(bf16[128,1280]{1,0:T(8,128)(2,1)S(1)} %slice_bitcast_fusion.8), channel_id=1, source_target_pairs={{0,2},{1,3},{2,0},{3,1},{4,6},{5,7},{6,4},{7,5},{8,10},{9,11},{10,... | collective-permute-start | bytes 983048 | tf_op jit(solution)/shard_map/ppermute | solution.py:29
  164.6 10.4 %collective-permute-start.23 = (bf16[2,64,1280]{2,1,0:T(8,128)(2,1)S(1)}, bf16[2,64,1280]{2,1,0:T(8,128)(2,1)S(1)}, u32[]{:S(2)}, u32[]{:S(2)}) collective-permute-start(bf16[2,64,1280]{2,1,0:T(8,128)(2,1)S(1)} %slice_bitcast_fusion.6), channel_id=1, source_target_pairs={{0,4},{4,0},{8,12},{12,8},{16,20},{20,16},{24,28},{28,24},{1,5},{5... | collective-permute-start | bytes 983048 | tf_op jit(solution)/shard_map/ppermute | solution.py:29
  173.4 23.0 %copy-start.1 = (bf16[5120,256]{1,0:T(8,128)(2,1)S(1)}, bf16[5120,256]{1,0:T(8,128)(2,1)}, u32[]{:S(2)}) copy-start(bf16[5120,256]{1,0:T(8,128)(2,1)} %param.20) | copy-start | bytes 7864324
  173.5 5.5 %collective-permute-start.21 = (bf16[64,1280]{1,0:T(8,128)(2,1)S(1)}, bf16[64,1280]{1,0:T(8,128)(2,1)S(1)}, u32[]{:S(2)}, u32[]{:S(2)}) collective-permute-start(bf16[64,1280]{1,0:T(8,128)(2,1)S(1)} %slice.161), channel_id=1, source_target_pairs={{0,4},{4,0},{8,12},{12,8},{16,20},{20,16},{24,28},{28,24},{1,5},{5... | collective-permute-start | bytes 491528 | tf_op jit(solution)/shard_map/ppermute | solution.py:29
  175.1 6.2 %collective-permute-start.24 = (bf16[64,1280]{1,0:T(8,128)(2,1)S(1)}, bf16[64,1280]{1,0:T(8,128)(2,1)S(1)}, u32[]{:S(2)}, u32[]{:S(2)}) collective-permute-start(bf16[64,1280]{1,0:T(8,128)(2,1)S(1)} %slice_bitcast_fusion.11), channel_id=1, source_target_pairs={{0,2},{1,3},{2,0},{3,1},{4,6},{5,7},{6,4},{7,5},{8,10},{9,11},{10,... | collective-permute-start | bytes 491528 | tf_op jit(solution)/shard_map/ppermute | solution.py:29
  179.0 6.2 %collective-permute-start.22 = (bf16[32,1280]{1,0:T(8,128)(2,1)S(1)}, bf16[32,1280]{1,0:T(8,128)(2,1)S(1)}, u32[]{:S(2)}, u32[]{:S(2)}) collective-permute-start(bf16[32,1280]{1,0:T(8,128)(2,1)S(1)} %slice.163), channel_id=1, source_target_pairs={{0,8},{4,12},{8,0},{12,4},{16,24},{20,28},{24,16},{28,20},{1,9},{5... | collective-permute-start | bytes 245768 | tf_op jit(solution)/shard_map/ppermute | solution.py:29
  181.4 7.9 %collective-permute-start.25 = (bf16[32,1280]{1,0:T(8,128)(2,1)S(1)}, bf16[32,1280]{1,0:T(8,128)(2,1)S(1)}, u32[]{:S(2)}, u32[]{:S(2)}) collective-permute-start(bf16[32,1280]{1,0:T(8,128)(2,1)S(1)} %get-tuple-element.21), channel_id=1, source_target_pairs={{0,16},{4,20},{8,24},{12,28},{16,0},{20,4},{24,8},{28,12},{1,17},{... | collective-permute-start | bytes 245768 | tf_op jit(solution)/shard_map/ppermute | solution.py:29
  182.8 6.5 %collective-permute-start.26 = (bf16[32,1280]{1,0:T(8,128)(2,1)S(1)}, bf16[32,1280]{1,0:T(8,128)(2,1)S(1)}, u32[]{:S(2)}, u32[]{:S(2)}) collective-permute-start(bf16[32,1280]{1,0:T(8,128)(2,1)S(1)} %get-tuple-element.22), channel_id=1, source_target_pairs={{0,24},{4,28},{8,16},{12,20},{16,8},{20,12},{24,0},{28,4},{1,25},{... | collective-permute-start | bytes 245768 | tf_op jit(solution)/shard_map/ppermute | solution.py:29
  189.3 4.5 %collective-permute-start.27 = (bf16[32,1280]{1,0:T(8,128)(2,1)S(1)}, bf16[32,1280]{1,0:T(8,128)(2,1)S(1)}, u32[]{:S(2)}, u32[]{:S(2)}) collective-permute-start(bf16[32,1280]{1,0:T(8,128)(2,1)S(1)} %get-tuple-element.5), channel_id=1, source_target_pairs={{0,2},{1,3},{2,0},{3,1},{4,6},{5,7},{6,4},{7,5},{8,10},{9,11},{10,... | collective-permute-start | bytes 245768 | tf_op jit(solution)/shard_map/ppermute | solution.py:29
  193.9 1.8 collective-permute-start.28
  195.7 0.7 copy-start.6

commit v2 on v1

v2 whole, which is shorter than its diff:
```python
import functools

import jax
import jax.numpy as jnp
from jax import lax
from jax.experimental import pallas as pl
from jax.experimental.pallas import tpu as pltpu
from jax.sharding import PartitionSpec as P

STEPS = 4
CORES = 2

rope_theta = 100000000.0
norm_eps = 1e-05
masked_low = -1e30
f32 = jnp.float32
bf16 = jnp.bfloat16


def split_axis(size):
    fast = 1
    while fast * fast * 4 <= size:
        fast *= 2
    return size // fast, fast


def swap(value, axis, mask):
    size = lax.axis_size(axis)
    return lax.ppermute(value, axis, [(i, i ^ mask) for i in range(size)])


def dot_t(a, b):
    return lax.dot_general(a, b, (((1,), (1,)), ((), ())), preferred_element_type=f32)


def round_trip(value):
    return value.astype(bf16).astype(f32)


def encode_stats(top, total, pairs):
    pieces = []
    rest = top
    for _ in range(3):
        piece = round_trip(rest)
        pieces.append(piece)
        rest = rest - piece
    rest = total
    for _ in range(2):
        piece = round_trip(rest)
        pieces.append(piece)
        rest = rest - piece
    tile = pieces[0]
    for i in range(1, 5):
        tile = tile + pltpu.roll(pieces[i], i * pairs, 1)
    return tile.astype(bf16)


def decode_stats(tile, pairs):
    values = tile.astype(f32)
    lanes = values.shape[1]
    shifted = [values] + [pltpu.roll(values, lanes - i * pairs, 1) for i in range(1, 5)]
    top = shifted[0] + shifted[1] + shifted[2]
    total = shifted[3] + shifted[4]
    return top, total


def pages_kernel(
    block_pages, slot_ref, valid_ref, query_ref, fresh_key_ref, fresh_value_ref, key_hbm, value_hbm,
    out_ref, key_buf, value_buf, top_ref, total_ref, acc_ref, sems,
):
    page_count, kv_local, page_size, head_dim = key_buf.shape
    blocks = page_count // block_pages
    groups, tiles = out_ref.shape[:2]
    pairs = tiles - 1
    rows = query_ref.shape[1]
    per_step = rows // STEPS
    scale = head_dim ** (-0.5)

    def copies(block):
        at = pl.ds(block * block_pages, block_pages)
        return (
            pltpu.make_async_copy(key_hbm.at[at], key_buf.at[at], sems.at[0, block]),
            pltpu.make_async_copy(value_hbm.at[at], value_buf.at[at], sems.at[1, block]),
        )

    for block in range(blocks):
        for copy in copies(block):
            copy.start()

    top_ref[...] = jnp.full(top_ref.shape, masked_low, f32)
    total_ref[...] = jnp.zeros(total_ref.shape, f32)
    acc_ref[...] = jnp.zeros(acc_ref.shape, f32)

    def weigh(scores, live):
        scores = [jnp.where(keep, score * scale, masked_low) for score, keep in zip(scores, live)]
        tops = [jnp.max(score, axis=1, keepdims=True) for score in scores]
        weights = [
            jnp.where(keep, jnp.exp(score - top), 0.0) for score, top, keep in zip(scores, tops, live)
        ]
        totals = [jnp.sum(weight, axis=1, keepdims=True) for weight in weights]
        return tops, totals, [weight.astype(bf16) for weight in weights]

    fresh = fresh_key_ref.shape[1]
    row_step = lax.broadcasted_iota(jnp.int32, (rows, fresh), 0) // per_step
    column = lax.broadcasted_iota(jnp.int32, (rows, fresh), 1)
    scores = [dot_t(query_ref[i], fresh_key_ref[i]) for i in range(pairs)]
    tops, totals, weights = weigh(scores, [column <= row_step] * pairs)
    accs = [jnp.dot(weights[i], fresh_value_ref[i], preferred_element_type=f32) for i in range(pairs)]
    for i in range(pairs):
        top_ref[i] = jnp.broadcast_to(tops[i], (rows, head_dim))
        total_ref[i] = jnp.broadcast_to(totals[i], (rows, head_dim))
        acc_ref[i] = accs[i]

    lane = lax.broadcasted_iota(jnp.int32, (rows, page_size), 1)

    @pl.loop(0, blocks)
    def _(block):
        for copy in copies(block):
            copy.wait()
        pages = [block * block_pages + i for i in range(block_pages)]
        places = [(page, head) for page in pages for head in range(kv_local)]
        at = [slot_ref[page] * kv_local + head for page, head in places]
        live = [lane < valid_ref[page] for page, _ in places]
        scores = [dot_t(query_ref[i], key_buf[page, head]) for i, (page, head) in zip(at, places)]
        tops, totals, weights = weigh(scores, live)
        accs = [
            jnp.dot(weight, value_buf[page, head], preferred_element_type=f32)
            for weight, (page, head) in zip(weights, places)
        ]
        for i, top, total, acc in zip(at, tops, totals, accs):
            old_top = top_ref[i]
            new_top = jnp.maximum(old_top, top)
            old_factor = jnp.exp(old_top - new_top)
            factor = jnp.exp(top - new_top)
            top_ref[i] = new_top
            total_ref[i] = total_ref[i] * old_factor + total * factor
            acc_ref[i] = acc_ref[i] * old_factor + acc * factor

    out_lane = lax.broadcasted_iota(jnp.int32, (rows, head_dim), 1)

    @pl.loop(0, groups)
    def _(group):
        tops = jnp.zeros((rows, head_dim), f32)
        totals = jnp.zeros((rows, head_dim), f32)
        for i in range(pairs):
            at = group * pairs + i
            out_ref[group, i] = acc_ref[at].astype(bf16)
            tops = jnp.where(out_lane == i, top_ref[at], tops)
            totals = jnp.where(out_lane == i, total_ref[at], totals)
        out_ref[group, pairs] = encode_stats(tops, totals, pairs)


def attend_pages(queries, fresh_keys, fresh_values, key_cache, value_cache, slots, valid, groups):
    pairs = fresh_keys.shape[0]
    rows, head_dim = queries.shape[1:]
    page_count, kv_local, page_size, _ = key_cache.shape
    block_pages = 6
    while page_count % block_pages:
        block_pages -= 1
    blocks = page_count // block_pages
    count = queries.shape[0]
    vmem = pl.BlockSpec(memory_space=pltpu.VMEM)
    smem = pl.BlockSpec(memory_space=pltpu.SMEM)
    hbm = pl.BlockSpec(memory_space=pl.ANY)
    return pl.pallas_call(
        functools.partial(pages_kernel, block_pages),
        out_shape=jax.ShapeDtypeStruct((groups, pairs + 1, rows, head_dim), bf16),
        in_specs=[smem, smem, vmem, vmem, vmem, hbm, hbm],
        out_specs=vmem,
        scratch_shapes=[
            pltpu.VMEM(key_cache.shape, bf16),
            pltpu.VMEM(value_cache.shape, bf16),
            pltpu.VMEM((count, rows, head_dim), f32),
            pltpu.VMEM((count, rows, head_dim), f32),
            pltpu.VMEM((count, rows, head_dim), f32),
            pltpu.SemaphoreType.DMA((2, blocks)),
        ],
        compiler_params=pltpu.CompilerParams(vmem_limit_bytes=60 << 20),
        cost_estimate=pl.CostEstimate(
            flops=4 * rows * page_count * kv_local * page_size * head_dim,
            bytes_accessed=4 * page_count * kv_local * page_size * head_dim,
            transcendentals=0,
        ),
        name="attend_pages",
    )(slots, valid, queries, fresh_keys, fresh_values, key_cache, value_cache)


def merge_tile(parts, group, pairs):
    stats = [decode_stats(part[group, pairs], pairs) for part in parts]
    top = functools.reduce(jnp.maximum, [s[0] for s in stats])
    factors = [jnp.exp(s[0] - top) for s in stats]
    total = functools.reduce(jnp.add, [s[1] * f for s, f in zip(stats, factors)])
    return top, total, factors


def merge_pair(parts, factors, group, i):
    return functools.reduce(
        jnp.add, [part[group, i].astype(f32) * f[:, i : i + 1] for part, f in zip(parts, factors)]
    )


def merge_kernel(count, *refs):
    parts, out_ref = refs[:count], refs[count]
    groups, tiles, rows, head_dim = parts[0].shape
    pairs = tiles - 1
    used = lax.broadcasted_iota(jnp.int32, (rows, head_dim), 1) < pairs
    for group in range(groups):
        top, total, factors = merge_tile(parts, group, pairs)
        for i in range(pairs):
            out_ref[group, i] = merge_pair(parts, factors, group, i).astype(bf16)
        out_ref[group, pairs] = encode_stats(
            jnp.where(used, top, 0.0), jnp.where(used, total, 0.0), pairs
        )


vmem = pl.BlockSpec(memory_space=pltpu.VMEM)
smem = pl.BlockSpec(memory_space=pltpu.SMEM)
hbm = pl.BlockSpec(memory_space=pl.ANY)


def merge_parts(parts):
    return pl.pallas_call(
        functools.partial(merge_kernel, len(parts)),
        out_shape=jax.ShapeDtypeStruct(parts[0].shape, bf16),
        in_specs=[vmem] * len(parts),
        out_specs=vmem,
        compiler_params=pltpu.CompilerParams(vmem_limit_bytes=8 << 20),
        name="merge_parts",
    )(*parts)


def start_all(copies):
    for copy in copies:
        copy.start()


def query_kernel(
    kv_local, me_ref, slots_ref, lengths_ref, input_ref, gain_ref, weight_hbm,
    query_ref, normalized_ref, cosine_ref, sine_ref, weight_buf, total_ref, tile_ref, sems,
):
    steps, row_count, width = input_ref.shape
    head_dim = cosine_ref.shape[1]
    heads = weight_buf.shape[1] // head_dim
    group = heads // kv_local
    chunks = sems.shape[0]
    depth = width // chunks
    copies = []
    for chunk in range(chunks):
        at = pl.ds(chunk * depth, depth)
        copies.append(pltpu.make_async_copy(weight_hbm.at[at], weight_buf.at[at], sems.at[chunk]))
    start_all(copies)

    gain = gain_ref[...]
    for step in range(0, steps, 2):
        pair = []
        for at in (step, step + 1):
            floats = input_ref[at].astype(f32)
            mean = jnp.mean(floats * floats, axis=1, keepdims=True)
            pair.append(floats * lax.rsqrt(mean + norm_eps) * gain)
        normalized_ref[step * row_count : (step + 2) * row_count] = jnp.concatenate(pair, axis=0).astype(bf16)

    requests = slots_ref.shape[1]
    own = me_ref[0] * row_count + lax.broadcasted_iota(jnp.int32, (row_count, requests), 0)
    length = jnp.sum(jnp.where(slots_ref[...] == own, lengths_ref[...], 0), axis=1, keepdims=True)
    half = head_dim // 2
    lane = lax.broadcasted_iota(jnp.int32, (row_count, head_dim), 1)
    exponent = jnp.where(lane < half, lane, lane - half).astype(f32) * (2.0 / head_dim)
    inverse_freq = rope_theta ** (-exponent)
    for step in range(steps):
        angles = (length + step).astype(f32) * inverse_freq
        sine = jnp.sin(angles)
        cosine_ref[step * row_count : (step + 1) * row_count] = jnp.cos(angles)
        sine_ref[step * row_count : (step + 1) * row_count] = jnp.where(lane < half, -sine, sine)

    for chunk, copy in enumerate(copies):
        copy.wait()
        at = slice(chunk * depth, (chunk + 1) * depth)
        product = jnp.dot(normalized_ref[:, at], weight_buf[at], preferred_element_type=f32)
        total_ref[...] = product if chunk == 0 else total_ref[...] + product

    cosine, sine = cosine_ref[...], sine_ref[...]
    tile_rows = steps * group
    for head in range(heads):
        value = total_ref[:, head * head_dim : (head + 1) * head_dim]
        value = value * cosine + pltpu.roll(value, half, 1) * sine
        for step in range(steps):
            first = head // group * tile_rows + step * group + head % group
            tile_ref[pl.ds(first, row_count, stride=kv_local * tile_rows), :] = value[
                step * row_count : (step + 1) * row_count
            ]
    query_ref[...] = tile_ref[...].reshape(query_ref.shape).astype(bf16)


def project_queries(me, request_slot, cache_lengths, token_inputs, gain, weight, kv_local, head_dim):
    steps, row_count, width = token_inputs.shape
    rows = steps * row_count
    columns = weight.shape[1]
    tile_rows = columns // (kv_local * head_dim) * steps
    pairs = row_count * kv_local
    chunks = 4
    return pl.pallas_call(
        functools.partial(query_kernel, kv_local),
        out_shape=(
            jax.ShapeDtypeStruct((pairs, tile_rows, head_dim), bf16),
            jax.ShapeDtypeStruct((rows, width), bf16),
            jax.ShapeDtypeStruct((rows, head_dim), f32),
            jax.ShapeDtypeStruct((rows, head_dim), f32),
        ),
        in_specs=[smem, vmem, vmem, vmem, vmem, hbm],
        out_specs=(vmem, vmem, vmem, vmem),
        scratch_shapes=[
            pltpu.VMEM((width, columns), bf16),
            pltpu.VMEM((rows, columns), f32),
            pltpu.VMEM((pairs * tile_rows, head_dim), f32),
            pltpu.SemaphoreType.DMA((chunks,)),
        ],
        compiler_params=pltpu.CompilerParams(vmem_limit_bytes=58 << 20),
        cost_estimate=pl.CostEstimate(
            flops=2 * rows * width * columns, bytes_accessed=2 * width * columns, transcendentals=0
        ),
        name="project_queries",
    )(
        me.reshape(1),
        request_slot.reshape(1, -1),
        cache_lengths.reshape(1, -1),
        token_inputs,
        gain.reshape(1, width),
        weight,
    )


def fresh_kernel(
    kv_local, normalized_ref, cosine_ref, sine_ref, key_hbm, value_hbm,
    key_ref, value_ref, key_buf, value_buf, key_tile, value_tile, sems,
):
    rows, width = normalized_ref.shape
    head_dim = cosine_ref.shape[1]
    row_count = rows // STEPS
    pads = key_ref.shape[1]
    copies = [
        pltpu.make_async_copy(key_hbm, key_buf, sems.at[0]),
        pltpu.make_async_copy(value_hbm, value_buf, sems.at[1]),
    ]
    start_all(copies)
    key_tile[...] = jnp.zeros(key_tile.shape, f32)
    value_tile[...] = jnp.zeros(value_tile.shape, f32)
    cosine, sine = cosine_ref[...], sine_ref[...]
    for copy, buf, tile in ((copies[0], key_buf, key_tile), (copies[1], value_buf, value_tile)):
        copy.wait()
        product = jnp.dot(normalized_ref[...], buf[...], preferred_element_type=f32)
        for head in range(kv_local):
            value = product[:, head * head_dim : (head + 1) * head_dim]
            if buf is key_buf:
                value = value * cosine + pltpu.roll(value, head_dim // 2, 1) * sine
            for step in range(STEPS):
                tile[pl.ds(head * pads + step, row_count, stride=kv_local * pads), :] = value[
                    step * row_count : (step + 1) * row_count
                ]
    key_ref[...] = key_tile[...].reshape(key_ref.shape).astype(bf16)
    value_ref[...] = value_tile[...].reshape(value_ref.shape).astype(bf16)


def project_fresh(normalized, cosine, sine, key_projection, value_projection, kv_local, head_dim):
    rows, width = normalized.shape
    pairs = rows // STEPS * kv_local
    pads = 16
    columns = key_projection.shape[1]
    return pl.pallas_call(
        functools.partial(fresh_kernel, kv_local),
        out_shape=(jax.ShapeDtypeStruct((pairs, pads, head_dim), bf16),) * 2,
        in_specs=[vmem, vmem, vmem, hbm, hbm],
        out_specs=(vmem, vmem),
        scratch_shapes=[
            pltpu.VMEM((width, columns), bf16),
            pltpu.VMEM((width, columns), bf16),
            pltpu.VMEM((pairs * pads, head_dim), f32),
            pltpu.VMEM((pairs * pads, head_dim), f32),
            pltpu.SemaphoreType.DMA((2,)),
        ],
        compiler_params=pltpu.CompilerParams(vmem_limit_bytes=58 << 20),
        cost_estimate=pl.CostEstimate(
            flops=4 * rows * width * columns, bytes_accessed=4 * width * columns, transcendentals=0
        ),
        name="project_fresh",
    )(normalized, cosine, sine, key_projection, value_projection)


def out_kernel(
    count, kv_local, part_ref, input_ref, weight_hbm, *refs
):
    parts = refs[:count]
    own_ref, term_ref, weight_buf, tile_ref, attention_ref, sems = refs[count:]
    tp = sems.shape[0]
    quarter = own_ref.shape[1]
    part = part_ref[0]
    copies = []
    for slot in range(tp):
        at = pl.multiple_of((part ^ slot) * quarter, quarter)
        copies.append(
            pltpu.make_async_copy(
                weight_hbm.at[:, pl.ds(at, quarter)], weight_buf.at[slot], sems.at[slot]
            )
        )
    order = list(range(1, tp)) + [0]
    start_all([copies[slot] for slot in order])

    _, tiles, tile_rows, head_dim = parts[0].shape
    pairs = tiles - 1
    row_count = pairs // kv_local
    group = tile_rows // STEPS
    _, total, factors = merge_tile(parts, 0, pairs)
    inverse = 1.0 / total
    factors = [f * inverse for f in factors]
    for i in range(pairs):
        acc = merge_pair(parts, factors, 0, i)
        request, head = i // kv_local, i % kv_local
        for row in range(tile_rows):
            step, member = row // group, row % group
            column = (head * group + member) * head_dim
            at = step * row_count + request
            tile_ref[at : at + 1, column : column + head_dim] = acc[row : row + 1]
    attention_ref[...] = tile_ref[...].astype(bf16)
    for slot in order:
        copies[slot].wait()
        product = jnp.dot(attention_ref[...], weight_buf[slot], preferred_element_type=f32)
        if slot == 0:
            own_ref[...] = input_ref[...].astype(f32) + product
        else:
            term_ref[slot - 1] = product.astype(bf16)


def project_out(part, parts, own_input, weight, tp, kv_local):
    rows, quarter = own_input.shape
    depth = weight.shape[0]
    return pl.pallas_call(
        functools.partial(out_kernel, len(parts), kv_local),
        out_shape=(
            jax.ShapeDtypeStruct((rows, quarter), f32),
            jax.ShapeDtypeStruct((tp - 1, rows, quarter), bf16),
        ),
        in_specs=[smem, vmem, hbm] + [vmem] * len(parts),
        out_specs=(vmem, vmem),
        scratch_shapes=[
            pltpu.VMEM((tp, depth, quarter), bf16),
            pltpu.VMEM((rows, depth), f32),
            pltpu.VMEM((rows, depth), bf16),
            pltpu.SemaphoreType.DMA((tp,)),
        ],
        compiler_params=pltpu.CompilerParams(vmem_limit_bytes=58 << 20),
        cost_estimate=pl.CostEstimate(
            flops=2 * rows * weight.size, bytes_accessed=2 * weight.size, transcendentals=0
        ),
        name="project_out",
    )(part.reshape(1), own_input, weight, *parts)


def gate_up_copies(part, core, ways, quarter, gate_hbm, up_hbm, gate_buf, up_buf, sems):
    copies = []
    for way in range(ways):
        at = pl.multiple_of((part ^ (way * CORES + core)) * quarter, quarter)
        copies.append(
            pltpu.make_async_copy(gate_hbm.at[pl.ds(at, quarter)], gate_buf.at[way], sems.at[0, way])
        )
        copies.append(pltpu.make_async_copy(up_hbm.at[pl.ds(at, quarter)], up_buf.at[way], sems.at[1, way]))
    return copies


def scaled_rows(part, core, way, rows_ref, gain_ref):
    floats = rows_ref[way].astype(f32)
    squares = jnp.sum(floats * floats, axis=1, keepdims=True)
    return (floats * gain_ref[part ^ (way * CORES + core)]).astype(bf16), squares


def gate_up_kernel(
    core, part_ref, rows_ref, gain_ref, gate_hbm, up_hbm, gate_ref, up_ref, square_ref,
    gate_buf, up_buf, scaled_ref, sems,
):
    ways, _, quarter = rows_ref.shape
    part = part_ref[0]
    copies = gate_up_copies(part, core, ways, quarter, gate_hbm, up_hbm, gate_buf, up_buf, sems)
    start_all(copies)
    square = 0.0
    for way in range(ways):
        scaled, squares = scaled_rows(part, core, way, rows_ref, gain_ref)
        scaled_ref[way] = scaled
        square = square + squares
    square_ref[...] = jnp.broadcast_to(square, square_ref.shape)
    for way in range(ways):
        for copy, buf, out in (
            (copies[2 * way], gate_buf, gate_ref),
            (copies[2 * way + 1], up_buf, up_ref),
        ):
            copy.wait()
            product = jnp.dot(scaled_ref[way], buf[way], preferred_element_type=f32)
            out[...] = product if way == 0 else out[...] + product


def gate_up_half(part, core, rows, gains, w_gate, w_up):
    ways, all_rows, quarter = rows.shape
    hidden = w_gate.shape[1]
    return pl.pallas_call(
        functools.partial(gate_up_kernel, core),
        out_shape=(
            jax.ShapeDtypeStruct((all_rows, hidden), f32),
            jax.ShapeDtypeStruct((all_rows, hidden), f32),
            jax.ShapeDtypeStruct((all_rows, 128), f32),
        ),
        in_specs=[smem, vmem, vmem, hbm, hbm],
        out_specs=(vmem, vmem, vmem),
        scratch_shapes=[
            pltpu.VMEM((ways, quarter, hidden), bf16),
            pltpu.VMEM((ways, quarter, hidden), bf16),
            pltpu.VMEM(rows.shape, bf16),
            pltpu.SemaphoreType.DMA((2, ways)),
        ],
        compiler_params=pltpu.CompilerParams(vmem_limit_bytes=48 << 20),
        cost_estimate=pl.CostEstimate(
            flops=4 * rows.size * hidden,
            bytes_accessed=4 * ways * quarter * hidden + 8 * all_rows * hidden,
            transcendentals=0,
        ),
        name="gate_up_half",
    )(part.reshape(1), rows, gains, w_gate, w_up)


def down_copies(part, core, ways, quarter, down_hbm, down_buf, sems):
    copies = []
    for way in range(ways):
        at = pl.multiple_of((part ^ (way * CORES + core)) * quarter, quarter)
        copies.append(
            pltpu.make_async_copy(down_hbm.at[:, pl.ds(at, quarter)], down_buf.at[way], sems.at[way])
        )
    return copies


def rest_kernel(
    width, part_ref, rows_ref, gain_ref, old_gate_ref, old_up_ref, square_ref, gate_hbm, up_hbm, down_hbm,
    activation_ref, term_ref, gate_buf, up_buf, down_buf, scaled_ref, gate_ref, up_ref, sems, down_sems,
):
    ways, _, quarter = rows_ref.shape
    part = part_ref[0]
    copies = gate_up_copies(part, 1, ways, quarter, gate_hbm, up_hbm, gate_buf, up_buf, sems)
    later = down_copies(part, 1, ways, quarter, down_hbm, down_buf, down_sems)
    start_all(copies + later)
    square = square_ref[:, :1]
    for way in range(ways):
        scaled, squares = scaled_rows(part, 1, way, rows_ref, gain_ref)
        scaled_ref[way] = scaled
        square = square + squares
    factor = lax.rsqrt(square * (1.0 / width) + norm_eps)
    for way in range(ways):
        for copy, buf, old, out in (
            (copies[2 * way], gate_buf, old_gate_ref, gate_ref),
            (copies[2 * way + 1], up_buf, old_up_ref, up_ref),
        ):
            copy.wait()
            product = jnp.dot(scaled_ref[way], buf[way], preferred_element_type=f32)
            out[...] = (old if way == 0 else out)[...] + product
    gate = gate_ref[...] * factor
    up = up_ref[...] * factor
    activation_ref[...] = (gate / (1.0 + jnp.exp(-gate)) * up).astype(bf16)
    for way in range(ways):
        later[way].wait()
        product = jnp.dot(activation_ref[...], down_buf[way], preferred_element_type=f32)
        term_ref[way] = product.astype(bf16)


def gate_up_rest(part, rows, gains, w_gate, w_up, w_down, sums, width):
    ways, all_rows, quarter = rows.shape
    hidden = w_gate.shape[1]
    return pl.pallas_call(
        functools.partial(rest_kernel, width),
        out_shape=(
            jax.ShapeDtypeStruct((all_rows, hidden), bf16),
            jax.ShapeDtypeStruct((ways, all_rows, quarter), bf16),
        ),
        in_specs=[smem, vmem, vmem, vmem, vmem, vmem, hbm, hbm, hbm],
        out_specs=(vmem, vmem),
        scratch_shapes=[
            pltpu.VMEM((ways, quarter, hidden), bf16),
            pltpu.VMEM((ways, quarter, hidden), bf16),
            pltpu.VMEM((ways, hidden, quarter), bf16),
            pltpu.VMEM(rows.shape, bf16),
            pltpu.VMEM((all_rows, hidden), f32),
            pltpu.VMEM((all_rows, hidden), f32),
            pltpu.SemaphoreType.DMA((2, ways)),
            pltpu.SemaphoreType.DMA((ways,)),
        ],
        compiler_params=pltpu.CompilerParams(vmem_limit_bytes=48 << 20),
        cost_estimate=pl.CostEstimate(
            flops=6 * rows.size * hidden, bytes_accessed=6 * ways * quarter * hidden, transcendentals=0
        ),
        name="gate_up_rest",
    )(part.reshape(1), rows, gains, *sums, w_gate, w_up, w_down)


def down_kernel(part_ref, activation_ref, down_hbm, term_ref, down_buf, sems):
    ways, _, quarter = term_ref.shape
    copies = down_copies(part_ref[0], 0, ways, quarter, down_hbm, down_buf, sems)
    start_all(copies)
    for way in range(ways):
        copies[way].wait()
        product = jnp.dot(activation_ref[...], down_buf[way], preferred_element_type=f32)
        term_ref[way] = product.astype(bf16)


def down_half(part, activation, w_down, ways):
    all_rows, hidden = activation.shape
    quarter = w_down.shape[1] // (ways * CORES)
    return pl.pallas_call(
        down_kernel,
        out_shape=jax.ShapeDtypeStruct((ways, all_rows, quarter), bf16),
        in_specs=[smem, vmem, hbm],
        out_specs=vmem,
        scratch_shapes=[
            pltpu.VMEM((ways, hidden, quarter), bf16),
            pltpu.SemaphoreType.DMA((ways,)),
        ],
        compiler_params=pltpu.CompilerParams(vmem_limit_bytes=48 << 20),
        cost_estimate=pl.CostEstimate(
            flops=w_down.size * all_rows, bytes_accessed=w_down.size, transcendentals=0
        ),
        name="down_half",
    )(part.reshape(1), activation, w_down)


def local(
    token_inputs,
    attn_gain,
    w_query,
    key_projection,
    value_projection,
    w_output,
    mlp_gain,
    w_gate,
    w_up,
    w_down,
    key_cache,
    paged_value_cache,
    cache_lengths,
    page_request,
    page_number,
    request_slot,
):
    steps, row_count, width = token_inputs.shape
    seq, tp = lax.axis_size("seq"), lax.axis_size("tp")
    deep, across = split_axis(seq)
    ways, cores = tp // CORES, CORES
    page_count, kv_local, page_size, head_dim = key_cache.shape
    heads_per_group = w_query.shape[1] // (kv_local * head_dim)
    rows = steps * row_count
    pairs = row_count * kv_local
    me, part = lax.axis_index("seq"), lax.axis_index("tp")
    quarter = width // tp

    page_live = page_request >= 0
    request_ids = jnp.arange(request_slot.shape[0], dtype=jnp.int32)
    is_request = request_ids[None, :] == page_request[:, None]
    page_row = jnp.sum(jnp.where(is_request, request_slot[None, :], 0), axis=1)
    page_length = jnp.sum(jnp.where(is_request, cache_lengths[None, :], 0), axis=1)
    valid = jnp.where(page_live, jnp.clip(page_length - page_number * page_size, 0, page_size), 0)
    mask = (page_row // row_count) ^ me
    slots = ((mask % across) * deep + mask // across) * row_count + page_row % row_count

    query, normalized, cosine, sine = project_queries(
        me, request_slot, cache_lengths, token_inputs, attn_gain, w_query, kv_local, head_dim
    )
    shared = [query] + [swap(query, "seq", across * k) for k in range(1, deep)]
    shared = jnp.concatenate(shared, axis=0)
    queries = [shared] + [swap(shared, "seq", k) for k in range(1, across)]
    queries = jnp.concatenate(queries, axis=0)

    fresh_keys, fresh_values = project_fresh(
        normalized, cosine, sine, key_projection, value_projection, kv_local, head_dim
    )

    packed = attend_pages(
        queries,
        fresh_keys,
        fresh_values,
        key_cache,
        paged_value_cache,
        slots,
        valid,
        seq,
    )
    sides = [packed[:deep]] + [swap(packed[k * deep : (k + 1) * deep], "seq", k) for k in range(1, across)]
    merged = merge_parts(sides)
    layers = [merged[:1]] + [swap(merged[k : k + 1], "seq", across * k) for k in range(1, deep)]
    own_input = lax.dynamic_slice_in_dim(token_inputs.reshape(rows, width), part * quarter, quarter, 1)
    own_term, terms = project_out(part, layers, own_input, w_output, tp, kv_local)
    total = own_term
    for slot in range(1, tp):
        total = total + swap(terms[slot - 1], "tp", slot).astype(f32)
    own_attended = total.astype(bf16)

    layered = [own_attended] + [swap(own_attended, "seq", across * k) for k in range(1, deep)]
    near = jnp.concatenate(layered[: deep // 2], axis=0)
    far = jnp.concatenate(layered[deep // 2 :], axis=0)
    near = jnp.concatenate([near] + [swap(near, "seq", k) for k in range(1, across)], axis=0)
    far = jnp.stack([far] + [swap(far, "tp", CORES * k) for k in range(1, ways)])
    near = jnp.stack([near] + [swap(near, "tp", CORES * k) for k in range(1, ways)])
    far = jnp.concatenate([far] + [swap(far, "seq", k) for k in range(1, across)], axis=1)
    both = jnp.concatenate([near, far], axis=1)
    other = swap(both, "tp", 1)
    all_rows = both.shape[1]

    def assemble(pieces, other_pieces, height):
        whole = jnp.zeros((height, width), bf16)
        for k in range(ways):
            for core, source in ((0, pieces), (1, other_pieces)):
                at = (part ^ (k * CORES + core)) * quarter
                whole = lax.dynamic_update_slice_in_dim(whole, source[k], at, 1)
        return whole

    gains = mlp_gain.reshape(tp, 1, quarter)
    sums = gate_up_half(part, 0, both, gains, w_gate, w_up)
    activation, other_terms = gate_up_rest(part, other, gains, w_gate, w_up, w_down, sums, width)
    received = swap(other_terms, "tp", 1)
    own_terms = down_half(part, activation, w_down, ways)
    summed = (own_terms.astype(f32) + received.astype(f32)).astype(bf16)
    attended = assemble(both[:, :rows], other[:, :rows], rows).reshape(steps, row_count, width)
    half = all_rows // 2
    near, far = summed[:, :half], summed[:, half:]

    def add(first, others):
        value = first.astype(f32)
        for other in others:
            value = value + other.astype(f32)
        return value

    near = add(near[0], [swap(near[k], "tp", CORES * k) for k in range(1, ways)]).astype(bf16)
    far = far.reshape(ways, across, half // across, quarter)
    far = add(far[:, 0], [swap(far[:, k], "seq", k) for k in range(1, across)]).astype(bf16)
    near = near.reshape(across, half // across, quarter)
    near = add(near[0], [swap(near[k], "seq", k) for k in range(1, across)]).astype(bf16)
    far = add(far[0], [swap(far[k], "tp", CORES * k) for k in range(1, ways)]).astype(bf16)
    layered = jnp.concatenate([near, far], axis=0).reshape(deep, rows, quarter)
    mlp_result = add(layered[0], [swap(layered[k], "seq", across * k) for k in range(1, deep)])
    own_out = (own_attended.astype(f32) + mlp_result).astype(bf16)

    spread = jnp.stack([own_out] + [swap(own_out, "tp", CORES * k) for k in range(1, ways)])
    layer_out = assemble(spread, swap(spread, "tp", 1), rows).reshape(steps, row_count, width)
    return attended, layer_out


def solution(mesh):
    in_specs = (
        P(None, "seq", None),
        P(),
        P(None, "tp"),
        P(None, "tp"),
        P(None, "tp"),
        P("tp", None),
        P(),
        P(None, ("seq", "tp")),
        P(None, ("seq", "tp")),
        P(("seq", "tp"), None),
        P("seq", "tp", None, None),
        P("seq", "tp", None, None),
        P(),
        P("seq"),
        P("seq"),
        P(),
    )
    out_specs = (P(None, "seq", None), P(None, "seq", None))
    return jax.shard_map(local, mesh=mesh, in_specs=in_specs, out_specs=out_specs, check_vma=False)
```

time: 197 us -> 145 us (0.74)
  matrix products: 37.8 us -> 0 us
  local copies, waits for them, and re-layouts: 32.1 us -> 8.17 us
  Pallas kernels: 25.5 us -> 42.2 us
  starting transfers between devices: 37.7 us -> 34.6 us
  waiting for transfers between devices: 57.4 us -> 54.4 us
    dot_general x6 -> x0, matrix products: 37.8 us -> none  [the longest x1 14.6 us: local(): jnp.dot(activation, w_down, preferred_element_type=f32).astype(bf16)]
    pallas_call x2 -> x7, Pallas kernels: 4.6 us -> 34.8 us  [the longest x1 7.2 us: gate_up_rest(): pl.pallas_call(functools.partial(rest_kernel, width), out_shape=(jax.Shap...]
    dot_general x2 -> x0, local copies, waits for them, and re-layouts: 18.2 us -> none  [the longest x1 13.8 us: local(): jnp.dot(normalized, w_query, preferred_element_type=f32)]
    pallas_call x1, Pallas kernels: 20.9 us -> 7.42 us  [attend_pages(): pl.pallas_call(functools.partial(pages_kernel, block_pages), out_shape=ja...]
    unnamed x39 -> x31, local copies, waits for them, and re-layouts: 6.83 us -> 2.74 us
    ppermute x29, starting transfers between devices: 37.7 us -> 34.6 us  [swap(): return lax.ppermute(value, axis, [(i, i ^ mask) for i in range(size)])]
    ppermute x29, waiting for transfers between devices: 57.4 us -> 54.4 us  [swap(): return lax.ppermute(value, axis, [(i, i ^ mask) for i in range(size)])]
    reduce_sum x3 -> x0, other arithmetic: 2.74 us -> none  [the longest x2 1.74 us: rms_norm(): square_mean = jnp.mean(floats * floats, axis=-1, keepdims=True)]
  transfers between devices with their start and end apart: 29 -> 29, of which waited for: 18 -> 19; matrix products, arithmetic and copies ran while one was open for 5% -> 3% of each run, Pallas kernels for 0% -> 10%
where the time goes in v2:
time: 145 us; the launch traced here: 144 us
  waiting for transfers between devices  54.4 us (38%)
  Pallas kernels  42.2 us (29%)
  starting transfers between devices  34.6 us (24%)
  local copies, waits for them, and re-layouts  8.17 us (6%)
  other arithmetic  3.92 us (3%)
    ppermute x29, waiting for transfers between devices, swap(): return lax.ppermute(value, axis, [(i, i ^ mask) for i in range(size)])  54.4 us
    ppermute x29, starting transfers between devices, swap(): return lax.ppermute(value, axis, [(i, i ^ mask) for i in range(size)])  34.6 us
    pallas_call x1, Pallas kernels, attend_pages(): pl.pallas_call(functools.partial(pages_kernel, block_pages), out_shape=ja...  7.42 us
    pallas_call x1, Pallas kernels, gate_up_rest(): pl.pallas_call(functools.partial(rest_kernel, width), out_shape=(jax.Shap...  7.2 us
    pallas_call x1, Pallas kernels, project_queries(): pl.pallas_call(functools.partial(query_kernel, kv_local), out_shape=(jax....  6.43 us
    pallas_call x1, Pallas kernels, project_out(): pl.pallas_call(functools.partial(out_kernel, len(parts), kv_local), out_s...  6.42 us
    pallas_call x1, Pallas kernels, project_fresh(): pl.pallas_call(functools.partial(fresh_kernel, kv_local), out_shape=(jax....  5.09 us
    pallas_call x1, Pallas kernels, gate_up_half(): pl.pallas_call(functools.partial(gate_up_kernel, core), out_shape=(jax.Sh...  5.04 us
  transfers between devices with their start and end apart: 29, of which 19 were waited for; matrix products, arithmetic and copies ran while one was open for 3% of the time, Pallas kernels for 10%

profile of v2, /device:TPU:0, one launch (start us, length us, event | category | flops | bytes accessed | tf_op | source)
XLA Modules:
  0.0 144.4 jit_solution(14141061232096453909)
XLA Ops:
  0.7 6.4 %project_queries.1 = (bf16[16,16,128]{2,1,0:T(8,128)(2,1)}, bf16[32,5120]{1,0:T(8,128)(2,1)}, f32[32,128]{1,0:T(8,128)}, f32[32,128]{1,0:T(8,128)}) custom-call(s32[1]{0:T(128)} %bitcast.2.me_ref, s32[1,64]{1,0:T(1,128)} %bitcast.89, s32[1,64]{1,0:T(1,128)} %bitcast.88, bf16[4,8,5120]{2,1,0:T(8,128)(2,1)} %input_ref.1, f32[1,5120]{1,0:T(1,128)} %bitcast.87, ...), custom_call_target="tpu_custom_call" | custom-call | flops 335544320 | bytes 10485760 | tf_op jit(solution)/shard_map/project_queries/pallas_call | solution.py:301
  7.1 3.1 %collective-permute-start = (bf16[16,16,128]{2,1,0:T(8,128)(2,1)}, bf16[16,16,128]{2,1,0:T(8,128)(2,1)S(1)}, u32[]{:S(2)}, u32[]{:S(2)}) collective-permute-start(bf16[16,16,128]{2,1,0:T(8,128)(2,1)} %get-tuple-element.15), channel_id=1, source_target_pairs={{0,8},{4,12},{8,0},{12,4},{16,24},{20,28},{24,16},{28,20},{1,9},{5... | collective-permute-start | bytes 196616 | tf_op jit(solution)/shard_map/ppermute | solution.py:29
  10.2 2.6 %collective-permute-start.1 = (bf16[16,16,128]{2,1,0:T(8,128)(2,1)}, bf16[16,16,128]{2,1,0:T(8,128)(2,1)S(1)}, u32[]{:S(2)}, u32[]{:S(2)}) collective-permute-start(bf16[16,16,128]{2,1,0:T(8,128)(2,1)} %get-tuple-element.15), channel_id=1, source_target_pairs={{0,16},{4,20},{8,24},{12,28},{16,0},{20,4},{24,8},{28,12},{1,17},{... | collective-permute-start | bytes 196616 | tf_op jit(solution)/shard_map/ppermute | solution.py:29
  12.8 0.2 select_reduce_fusion
  13.0 0.6 compare_select_fusion
  13.6 5.1 %project_fresh.1 = (bf16[16,16,128]{2,1,0:T(8,128)(2,1)}, bf16[16,16,128]{2,1,0:T(8,128)(2,1)}) custom-call(bf16[32,5120]{1,0:T(8,128)(2,1)} %get-tuple-element.16.normalized_ref, f32[32,128]{1,0:T(8,128)} %get-tuple-element.17.cosine_ref, f32[32,128]{1,0:T(8,128)} %get-tuple-element.18.sine_ref, bf16[5120,256]{1,0:T(8,128)(2,1)} %key_hbm.2, ...), custom_call_target="tpu_custom_call" | custom-call | flops 167772160 | bytes 5242880 | tf_op jit(solution)/shard_map/project_fresh/pallas_call | solution.py:368
  18.7 0.4 collective-permute-done.2
  19.1 1.6 %collective-permute-start.3 = (bf16[64,16,128]{2,1,0:T(8,128)(2,1)S(1)}, bf16[64,16,128]{2,1,0:T(8,128)(2,1)S(1)}, u32[]{:S(2)}, u32[]{:S(2)}) collective-permute-start(bf16[64,16,128]{2,1,0:T(8,128)(2,1)S(1)} %pad_maximum_fusion.3), channel_id=1, source_target_pairs={{0,4},{4,0},{8,12},{12,8},{16,20},{20,16},{24,28},{28,24},{1,5},{5... | collective-permute-start | bytes 786440 | tf_op jit(solution)/shard_map/ppermute | solution.py:29
  20.7 5.6 %collective-permute-done.3 = bf16[64,16,128]{2,1,0:T(8,128)(2,1)S(1)} collective-permute-done((bf16[64,16,128]{2,1,0:T(8,128)(2,1)S(1)}, bf16[64,16,128]{2,1,0:T(8,128)(2,1)S(1)}, u32[]{:S(2)}, u32[]{:S(2)}) %collective-permute-start.3) | collective-permute-done | bytes 262176 | tf_op jit(solution)/shard_map/ppermute | solution.py:29
  26.4 0.8 copy-done.1
  27.2 7.4 %attend_pages.1 = bf16[8,17,16,128]{3,2,1,0:T(8,128)(2,1)} custom-call(s32[36]{0:T(128)} %get-tuple-element.46.slot_ref, s32[36]{0:T(128)} %get-tuple-element.45.valid_ref, bf16[128,16,128]{2,1,0:T(8,128)(2,1)} %copy-done.1, bf16[16,16,128]{2,1,0:T(8,128)(2,1)} %get-tuple-element.19.fresh_key_ref, bf16[16,16,128]{2,1,0:T(8,128)(2,1)} %get-tuple-element.20.fresh_value_ref, ...), custom_call_target="tpu_custom_call" | custom-call | flops 150994944 | bytes 9437184 | tf_op jit(solution)/shard_map/attend_pages/pallas_call | solution.py:165
  34.6 1.1 fusion.13
  35.7 1.6 %collective-permute-start.4 = (bf16[4,17,16,128]{3,2,1,0:T(8,128)(2,1)S(1)}, bf16[4,17,16,128]{3,2,1,0:T(8,128)(2,1)S(1)}, u32[]{:S(2)}, u32[]{:S(2)}) collective-permute-start(bf16[4,17,16,128]{3,2,1,0:T(8,128)(2,1)S(1)} %get-tuple-element.32), channel_id=1, source_target_pairs={{0,4},{4,0},{8,12},{12,8},{16,20},{20,16},{24,28},{28,24},{1,5},{5... | collective-permute-start | bytes 835592 | tf_op jit(solution)/shard_map/ppermute | solution.py:29
  37.3 5.1 %collective-permute-done.4.refs_1_ = bf16[4,17,16,128]{3,2,1,0:T(8,128)(2,1)S(1)} collective-permute-done((bf16[4,17,16,128]{3,2,1,0:T(8,128)(2,1)S(1)}, bf16[4,17,16,128]{3,2,1,0:T(8,128)(2,1)S(1)}, u32[]{:S(2)}, u32[]{:S(2)}) %collective-permute-start.4) | collective-permute-done | bytes 278560 | tf_op jit(solution)/shard_map/ppermute | solution.py:29
  42.3 0.9 merge_parts.1
  43.2 0.6 fusion.14
  43.9 0.7 collective-permute-start.5
  44.6 3.5 %collective-permute-start.6 = (bf16[1,17,16,128]{3,2,1,0:T(8,128)(2,1)S(1)}, bf16[1,17,16,128]{3,2,1,0:T(8,128)(2,1)S(1)}, u32[]{:S(2)}, u32[]{:S(2)}) collective-permute-start(bf16[1,17,16,128]{3,2,1,0:T(8,128)(2,1)S(1)} %get-tuple-element.37), channel_id=1, source_target_pairs={{0,16},{4,20},{8,24},{12,28},{16,0},{20,4},{24,8},{28,12},{1,17},{... | collective-permute-start | bytes 208904 | tf_op jit(solution)/shard_map/ppermute | solution.py:29
  48.0 0.2 collective-permute-start.7
  48.3 1.5 %constant_dynamic-slice_fusion.input_ref = bf16[32,1280]{1,0:T(8,128)(2,1)} fusion(bf16[32,5120]{1,0:T(8,128)(2,1)} %bitcast.80, s32[]{:T(128)S(6)} %select_n.47), kind=kLoop, calls=%fused_computation.49 | loop fusion | bytes 163844 | tf_op jit(solution)/shard_map/dynamic_slice | solution.py:690
  49.8 1.8 %collective-permute-done.6.refs_2_ = bf16[1,17,16,128]{3,2,1,0:T(8,128)(2,1)S(1)} collective-permute-done((bf16[1,17,16,128]{3,2,1,0:T(8,128)(2,1)S(1)}, bf16[1,17,16,128]{3,2,1,0:T(8,128)(2,1)S(1)}, u32[]{:S(2)}, u32[]{:S(2)}) %collective-permute-start.6) | collective-permute-done | bytes 69664 | tf_op jit(solution)/shard_map/ppermute | solution.py:29
  51.5 2.6 %collective-permute-done.7.refs_3_ = bf16[1,17,16,128]{3,2,1,0:T(8,128)(2,1)S(1)} collective-permute-done((bf16[1,17,16,128]{3,2,1,0:T(8,128)(2,1)S(1)}, bf16[1,17,16,128]{3,2,1,0:T(8,128)(2,1)S(1)}, u32[]{:S(2)}, u32[]{:S(2)}) %collective-permute-start.7) | collective-permute-done | bytes 69664 | tf_op jit(solution)/shard_map/ppermute | solution.py:29
  54.2 0.6 copy-done.8
  54.8 6.4 %project_out.1 = (f32[32,1280]{1,0:T(8,128)}, bf16[3,32,1280]{2,1,0:T(8,128)(2,1)}) custom-call(s32[1]{0:T(128)} %bitcast.part_ref, bf16[32,1280]{1,0:T(8,128)(2,1)} %constant_dynamic-slice_fusion.input_ref, bf16[1024,5120]{1,0:T(8,128)(2,1)} %weight_hbm.3, bf16[1,17,16,128]{3,2,1,0:T(8,128)(2,1)} %get-tuple-element.39.refs_0_, ...), custom_call_target="tpu_custom_call" | custom-call | flops 335544320 | bytes 10485760 | tf_op jit(solution)/shard_map/project_out/pallas_call | solution.py:435
  61.2 1.0 slice_bitcast_fusion.14
  62.3 1.6 %collective-permute-start.8 = (bf16[32,1280]{1,0:T(8,128)(2,1)S(1)}, bf16[32,1280]{1,0:T(8,128)(2,1)S(1)}, u32[]{:S(2)}, u32[]{:S(2)}) collective-permute-start(bf16[32,1280]{1,0:T(8,128)(2,1)S(1)} %get-tuple-element.40), channel_id=1, source_target_pairs={{0,1},{1,0},{2,3},{3,2},{4,5},{5,4},{6,7},{7,6},{8,9},{9,8},{10,11... | collective-permute-start | bytes 245768 | tf_op jit(solution)/shard_map/ppermute | solution.py:29
  63.9 0.5 collective-permute-start.9
  64.4 2.5 %collective-permute-done.10 = bf16[32,1280]{1,0:T(8,128)(2,1)S(1)} collective-permute-done((bf16[32,1280]{1,0:T(8,128)(2,1)S(1)}, bf16[32,1280]{1,0:T(8,128)(2,1)S(1)}, u32[]{:S(2)}, u32[]{:S(2)}) %collective-permute-start.10) | collective-permute-done | bytes 81952 | tf_op jit(solution)/shard_map/ppermute | solution.py:29
  66.9 1.8 %collective-permute-done.9 = bf16[32,1280]{1,0:T(8,128)(2,1)S(1)} collective-permute-done((bf16[32,1280]{1,0:T(8,128)(2,1)S(1)}, bf16[32,1280]{1,0:T(8,128)(2,1)S(1)}, u32[]{:S(2)}, u32[]{:S(2)}) %collective-permute-start.9) | collective-permute-done | bytes 81952 | tf_op jit(solution)/shard_map/ppermute | solution.py:29
  68.8 1.0 add_convert_fusion.3
  69.8 1.1 collective-permute-start.15
  70.9 2.4 %collective-permute-start.11 = (bf16[32,1280]{1,0:T(8,128)(2,1)S(1)}, bf16[32,1280]{1,0:T(8,128)(2,1)S(1)}, u32[]{:S(2)}, u32[]{:S(2)}) collective-permute-start(bf16[32,1280]{1,0:T(8,128)(2,1)S(1)} %add_convert_fusion.3), channel_id=1, source_target_pairs={{0,8},{4,12},{8,0},{12,4},{16,24},{20,28},{24,16},{28,20},{1,9},{5... | collective-permute-start | bytes 245768 | tf_op jit(solution)/shard_map/ppermute | solution.py:29
  73.3 4.3 %collective-permute-done.14 = bf16[32,1280]{1,0:T(8,128)(2,1)S(1)} collective-permute-done((bf16[32,1280]{1,0:T(8,128)(2,1)S(1)}, bf16[32,1280]{1,0:T(8,128)(2,1)S(1)}, u32[]{:S(2)}, u32[]{:S(2)}) %collective-permute-start.14) | collective-permute-done | bytes 81952 | tf_op jit(solution)/shard_map/ppermute | solution.py:29
  77.6 0.8 collective-permute-start.16
  78.4 1.6 %collective-permute-start.12 = (bf16[64,1280]{1,0:T(8,128)(2,1)S(1)}, bf16[64,1280]{1,0:T(8,128)(2,1)S(1)}, u32[]{:S(2)}, u32[]{:S(2)}) collective-permute-start(bf16[64,1280]{1,0:T(8,128)(2,1)S(1)} %pad_maximum_fusion.4), channel_id=1, source_target_pairs={{0,4},{4,0},{8,12},{12,8},{16,20},{20,16},{24,28},{28,24},{1,5},{5... | collective-permute-start | bytes 491528 | tf_op jit(solution)/shard_map/ppermute | solution.py:29
  80.0 3.0 %collective-permute-done.16 = bf16[64,1280]{1,0:T(8,128)(2,1)S(1)} collective-permute-done((bf16[64,1280]{1,0:T(8,128)(2,1)S(1)}, bf16[64,1280]{1,0:T(8,128)(2,1)S(1)}, u32[]{:S(2)}, u32[]{:S(2)}) %collective-permute-start.16) | collective-permute-done | bytes 163872 | tf_op jit(solution)/shard_map/ppermute | solution.py:29
  83.0 1.6 %collective-permute-start.17 = (bf16[2,64,1280]{2,1,0:T(8,128)(2,1)S(1)}, bf16[2,64,1280]{2,1,0:T(8,128)(2,1)S(1)}, u32[]{:S(2)}, u32[]{:S(2)}) collective-permute-start(bf16[2,64,1280]{2,1,0:T(8,128)(2,1)S(1)} %pad_maximum_fusion.2), channel_id=1, source_target_pairs={{0,4},{4,0},{8,12},{12,8},{16,20},{20,16},{24,28},{28,24},{1,5},{5... | collective-permute-start | bytes 983048 | tf_op jit(solution)/shard_map/ppermute | solution.py:29
  84.6 1.0 collective-permute-done.12
  85.6 1.4 collective-permute-start.13
  87.0 4.5 %collective-permute-done.17 = bf16[2,64,1280]{2,1,0:T(8,128)(2,1)S(1)} collective-permute-done((bf16[2,64,1280]{2,1,0:T(8,128)(2,1)S(1)}, bf16[2,64,1280]{2,1,0:T(8,128)(2,1)S(1)}, u32[]{:S(2)}, u32[]{:S(2)}) %collective-permute-start.17) | collective-permute-done | bytes 327712 | tf_op jit(solution)/shard_map/ppermute | solution.py:29
  91.5 1.7 %collective-permute-done.13 = bf16[128,1280]{1,0:T(8,128)(2,1)S(1)} collective-permute-done((bf16[128,1280]{1,0:T(8,128)(2,1)S(1)}, bf16[128,1280]{1,0:T(8,128)(2,1)S(1)}, u32[]{:S(2)}, u32[]{:S(2)}) %collective-permute-start.13) | collective-permute-done | bytes 327712 | tf_op jit(solution)/shard_map/ppermute | solution.py:29
  93.2 0.1 pad_maximum_fusion.rows_ref
  93.4 0.5 copy-done.2
  93.9 5.0 %gate_up_half.1 = (f32[256,1024]{1,0:T(8,128)S(1)}, f32[256,1024]{1,0:T(8,128)S(1)}, f32[256,128]{1,0:T(8,128)S(1)}) custom-call(s32[1]{0:T(128)} %bitcast.part_ref, bf16[2,256,1280]{2,1,0:T(8,128)(2,1)S(1)} %pad_maximum_fusion.rows_ref, f32[4,1,1280]{2,1,0:T(1,128)S(1)} %bitcast.72, bf16[5120,1024]{1,0:T(8,128)(2,1)} %gate_hbm.3, bf16[5120,1024]{1,0:T(8,128)(2,1)} %up_hbm.3), custom_call_target="tpu_custom_call" | custom-call | flops 2684354560 | bytes 12582912 | tf_op jit(solution)/shard_map/gate_up_half/pallas_call | solution.py:501
  99.0 7.2 %gate_up_rest.1 = (bf16[256,1024]{1,0:T(8,128)(2,1)S(1)}, bf16[2,256,1280]{2,1,0:T(8,128)(2,1)S(1)}) custom-call(s32[1]{0:T(128)} %bitcast.part_ref, bf16[2,256,1280]{2,1,0:T(8,128)(2,1)S(1)} %collective-permute-done.18.rows_ref, f32[4,1,1280]{2,1,0:T(1,128)S(1)} %bitcast.73, f32[256,1024]{1,0:T(8,128)S(1)} %get-tuple-element.23.old_gate_ref, ...), custom_call_target="tpu_custom_call" | custom-call | flops 4026531840 | bytes 15728640 | tf_op jit(solution)/shard_map/gate_up_rest/pallas_call | solution.py:571
  106.3 3.7 %down_half.1 = bf16[2,256,1280]{2,1,0:T(8,128)(2,1)S(1)} custom-call(s32[1]{0:T(128)} %bitcast.part_ref, bf16[256,1024]{1,0:T(8,128)(2,1)S(1)} %get-tuple-element.26.activation_ref, bf16[1024,5120]{1,0:T(8,128)(2,1)} %down_hbm.3), custom_call_target="tpu_custom_call" | custom-call | flops 1342177280 | bytes 5242880 | tf_op jit(solution)/shard_map/down_half/pallas_call | solution.py:610
  110.1 1.6 %add_convert_fusion = bf16[2,256,1280]{2,1,0:T(8,128)(2,1)S(1)} fusion(bf16[2,256,1280]{2,1,0:T(8,128)(2,1)} %collective-permute-done.19, bf16[2,256,1280]{2,1,0:T(8,128)(2,1)S(1)} %down_half.1), kind=kLoop, calls=%fused_computation | loop fusion | flops 2621440 | bytes 3932160 | tf_op jit(solution)/shard_map/convert_element_type | solution.py:721
  111.8 0.9 collective-permute-start.20
  112.8 1.6 %collective-permute-start.23 = (bf16[2,64,1280]{2,1,0:T(8,128)(2,1)S(1)}, bf16[2,64,1280]{2,1,0:T(8,128)(2,1)S(1)}, u32[]{:S(2)}, u32[]{:S(2)}) collective-permute-start(bf16[2,64,1280]{2,1,0:T(8,128)(2,1)S(1)} %slice_bitcast_fusion), channel_id=1, source_target_pairs={{0,4},{4,0},{8,12},{12,8},{16,20},{20,16},{24,28},{28,24},{1,5},{5... | collective-permute-start | bytes 983048 | tf_op jit(solution)/shard_map/ppermute | solution.py:29
  114.3 7.6 %collective-permute-done.20 = bf16[128,1280]{1,0:T(8,128)(2,1)S(1)} collective-permute-done((bf16[128,1280]{1,0:T(8,128)(2,1)S(1)}, bf16[128,1280]{1,0:T(8,128)(2,1)S(1)}, u32[]{:S(2)}, u32[]{:S(2)}) %collective-permute-start.20) | collective-permute-done | bytes 327712 | tf_op jit(solution)/shard_map/ppermute | solution.py:29
  122.0 1.6 %collective-permute-start.21 = (bf16[64,1280]{1,0:T(8,128)(2,1)S(1)}, bf16[64,1280]{1,0:T(8,128)(2,1)S(1)}, u32[]{:S(2)}, u32[]{:S(2)}) collective-permute-start(bf16[64,1280]{1,0:T(8,128)(2,1)S(1)} %slice.146), channel_id=1, source_target_pairs={{0,4},{4,0},{8,12},{12,8},{16,20},{20,16},{24,28},{28,24},{1,5},{5... | collective-permute-start | bytes 491528 | tf_op jit(solution)/shard_map/ppermute | solution.py:29
  123.7 0.9 collective-permute-start.24
  124.7 3.2 %collective-permute-done.21 = bf16[64,1280]{1,0:T(8,128)(2,1)S(1)} collective-permute-done((bf16[64,1280]{1,0:T(8,128)(2,1)S(1)}, bf16[64,1280]{1,0:T(8,128)(2,1)S(1)}, u32[]{:S(2)}, u32[]{:S(2)}) %collective-permute-start.21) | collective-permute-done | bytes 163872 | tf_op jit(solution)/shard_map/ppermute | solution.py:29
  128.0 1.0 collective-permute-start.22
  128.9 0.3 collective-permute-done.24
  129.4 1.1 collective-permute-start.25
  130.5 2.1 %collective-permute-start.26 = (bf16[32,1280]{1,0:T(8,128)(2,1)S(1)}, bf16[32,1280]{1,0:T(8,128)(2,1)S(1)}, u32[]{:S(2)}, u32[]{:S(2)}) collective-permute-start(bf16[32,1280]{1,0:T(8,128)(2,1)S(1)} %get-tuple-element.44), channel_id=1, source_target_pairs={{0,24},{4,28},{8,16},{12,20},{16,8},{20,12},{24,0},{28,4},{1,25},{... | collective-permute-start | bytes 245768 | tf_op jit(solution)/shard_map/ppermute | solution.py:29
  132.6 0.1 collective-permute-done.22
  132.7 4.9 %collective-permute-done.25 = bf16[32,1280]{1,0:T(8,128)(2,1)S(1)} collective-permute-done((bf16[32,1280]{1,0:T(8,128)(2,1)S(1)}, bf16[32,1280]{1,0:T(8,128)(2,1)S(1)}, u32[]{:S(2)}, u32[]{:S(2)}) %collective-permute-start.25) | collective-permute-done | bytes 81952 | tf_op jit(solution)/shard_map/ppermute | solution.py:29
  137.6 0.9 collective-permute-start.27
  138.6 0.9 fusion.6
  139.5 2.7 %collective-permute-done.27 = bf16[32,1280]{1,0:T(8,128)(2,1)S(1)} collective-permute-done((bf16[32,1280]{1,0:T(8,128)(2,1)S(1)}, bf16[32,1280]{1,0:T(8,128)(2,1)S(1)}, u32[]{:S(2)}, u32[]{:S(2)}) %collective-permute-start.27) | collective-permute-done | bytes 81952 | tf_op jit(solution)/shard_map/ppermute | solution.py:29
  142.3 1.3 collective-permute-done.28
  143.7 0.7 copy-done.3
  (70 shorter events, 1.2 us)
Async XLA Ops:
  0.6 12.2 %copy-start.9 = (s32[64]{0:T(128)S(1)}, s32[64]{0:T(128)}, u32[]{:S(2)}) copy-start(s32[64]{0:T(128)} %param.28) | copy-start | bytes 772
  0.6 12.2 %copy-start.10 = (s32[64]{0:T(128)S(1)}, s32[64]{0:T(128)}, u32[]{:S(2)}) copy-start(s32[64]{0:T(128)} %param.31) | copy-start | bytes 772
  0.7 12.1 %copy-start.11 = (s32[36]{0:T(128)S(1)}, s32[36]{0:T(128)}, u32[]{:S(2)}) copy-start(s32[36]{0:T(128)} %param.29) | copy-start | bytes 436
  0.7 12.3 %copy-start.12 = (s32[36]{0:T(128)S(1)}, s32[36]{0:T(128)}, u32[]{:S(2)}) copy-start(s32[36]{0:T(128)} %param.30) | copy-start | bytes 436
  7.1 11.6 %collective-permute-start = (bf16[16,16,128]{2,1,0:T(8,128)(2,1)}, bf16[16,16,128]{2,1,0:T(8,128)(2,1)S(1)}, u32[]{:S(2)}, u32[]{:S(2)}) collective-permute-start(bf16[16,16,128]{2,1,0:T(8,128)(2,1)} %get-tuple-element.15), channel_id=1, source_target_pairs={{0,8},{4,12},{8,0},{12,4},{16,24},{20,28},{24,16},{28,20},{1,9},{5... | collective-permute-start | bytes 196616 | tf_op jit(solution)/shard_map/ppermute | solution.py:29
  10.2 8.5 %collective-permute-start.1 = (bf16[16,16,128]{2,1,0:T(8,128)(2,1)}, bf16[16,16,128]{2,1,0:T(8,128)(2,1)S(1)}, u32[]{:S(2)}, u32[]{:S(2)}) collective-permute-start(bf16[16,16,128]{2,1,0:T(8,128)(2,1)} %get-tuple-element.15), channel_id=1, source_target_pairs={{0,16},{4,20},{8,24},{12,28},{16,0},{20,4},{24,8},{28,12},{1,17},{... | collective-permute-start | bytes 196616 | tf_op jit(solution)/shard_map/ppermute | solution.py:29
  12.8 6.3 %collective-permute-start.2 = (bf16[16,16,128]{2,1,0:T(8,128)(2,1)}, bf16[16,16,128]{2,1,0:T(8,128)(2,1)S(1)}, u32[]{:S(2)}, u32[]{:S(2)}) collective-permute-start(bf16[16,16,128]{2,1,0:T(8,128)(2,1)} %get-tuple-element.15), channel_id=1, source_target_pairs={{0,24},{4,28},{8,16},{12,20},{16,8},{20,12},{24,0},{28,4},{1,25},{... | collective-permute-start | bytes 196616 | tf_op jit(solution)/shard_map/ppermute | solution.py:29
  13.6 5.1 %copy-start.5 = (bf16[16,16,128]{2,1,0:T(8,128)(2,1)S(1)}, bf16[16,16,128]{2,1,0:T(8,128)(2,1)}, u32[]{:S(2)}) copy-start(bf16[16,16,128]{2,1,0:T(8,128)(2,1)} %get-tuple-element.15) | copy-start | bytes 196612
  19.1 7.2 %collective-permute-start.3 = (bf16[64,16,128]{2,1,0:T(8,128)(2,1)S(1)}, bf16[64,16,128]{2,1,0:T(8,128)(2,1)S(1)}, u32[]{:S(2)}, u32[]{:S(2)}) collective-permute-start(bf16[64,16,128]{2,1,0:T(8,128)(2,1)S(1)} %pad_maximum_fusion.3), channel_id=1, source_target_pairs={{0,4},{4,0},{8,12},{12,8},{16,20},{20,16},{24,28},{28,24},{1,5},{5... | collective-permute-start | bytes 786440 | tf_op jit(solution)/shard_map/ppermute | solution.py:29
  26.4 0.8 copy-start.1
  35.7 6.6 %collective-permute-start.4 = (bf16[4,17,16,128]{3,2,1,0:T(8,128)(2,1)S(1)}, bf16[4,17,16,128]{3,2,1,0:T(8,128)(2,1)S(1)}, u32[]{:S(2)}, u32[]{:S(2)}) collective-permute-start(bf16[4,17,16,128]{3,2,1,0:T(8,128)(2,1)S(1)} %get-tuple-element.32), channel_id=1, source_target_pairs={{0,4},{4,0},{8,12},{12,8},{16,20},{20,16},{24,28},{28,24},{1,5},{5... | collective-permute-start | bytes 835592 | tf_op jit(solution)/shard_map/ppermute | solution.py:29
  43.9 5.9 %collective-permute-start.5 = (bf16[1,17,16,128]{3,2,1,0:T(8,128)(2,1)S(1)}, bf16[1,17,16,128]{3,2,1,0:T(8,128)(2,1)S(1)}, u32[]{:S(2)}, u32[]{:S(2)}) collective-permute-start(bf16[1,17,16,128]{3,2,1,0:T(8,128)(2,1)S(1)} %get-tuple-element.38), channel_id=1, source_target_pairs={{0,8},{4,12},{8,0},{12,4},{16,24},{20,28},{24,16},{28,20},{1,9},{5... | collective-permute-start | bytes 208904 | tf_op jit(solution)/shard_map/ppermute | solution.py:29
  44.6 7.0 %collective-permute-start.6 = (bf16[1,17,16,128]{3,2,1,0:T(8,128)(2,1)S(1)}, bf16[1,17,16,128]{3,2,1,0:T(8,128)(2,1)S(1)}, u32[]{:S(2)}, u32[]{:S(2)}) collective-permute-start(bf16[1,17,16,128]{3,2,1,0:T(8,128)(2,1)S(1)} %get-tuple-element.37), channel_id=1, source_target_pairs={{0,16},{4,20},{8,24},{12,28},{16,0},{20,4},{24,8},{28,12},{1,17},{... | collective-permute-start | bytes 208904 | tf_op jit(solution)/shard_map/ppermute | solution.py:29
  48.0 6.1 %collective-permute-start.7 = (bf16[1,17,16,128]{3,2,1,0:T(8,128)(2,1)S(1)}, bf16[1,17,16,128]{3,2,1,0:T(8,128)(2,1)S(1)}, u32[]{:S(2)}, u32[]{:S(2)}) collective-permute-start(bf16[1,17,16,128]{3,2,1,0:T(8,128)(2,1)S(1)} %get-tuple-element.36), channel_id=1, source_target_pairs={{0,24},{4,28},{8,16},{12,20},{16,8},{20,12},{24,0},{28,4},{1,25},{... | collective-permute-start | bytes 208904 | tf_op jit(solution)/shard_map/ppermute | solution.py:29
  49.8 4.4 %copy-start.6 = (bf16[1,17,16,128]{3,2,1,0:T(8,128)(2,1)}, bf16[1,17,16,128]{3,2,1,0:T(8,128)(2,1)S(1)}, u32[]{:S(2)}) copy-start(bf16[1,17,16,128]{3,2,1,0:T(8,128)(2,1)S(1)} %collective-permute-done.5.refs_1_) | copy-start | bytes 208900
  51.5 2.6 %copy-start.7 = (bf16[1,17,16,128]{3,2,1,0:T(8,128)(2,1)}, bf16[1,17,16,128]{3,2,1,0:T(8,128)(2,1)S(1)}, u32[]{:S(2)}) copy-start(bf16[1,17,16,128]{3,2,1,0:T(8,128)(2,1)S(1)} %collective-permute-done.6.refs_2_) | copy-start | bytes 208900
  54.1 0.6 copy-start.8
  62.2 4.7 %collective-permute-start.10 = (bf16[32,1280]{1,0:T(8,128)(2,1)S(1)}, bf16[32,1280]{1,0:T(8,128)(2,1)S(1)}, u32[]{:S(2)}, u32[]{:S(2)}) collective-permute-start(bf16[32,1280]{1,0:T(8,128)(2,1)S(1)} %get-tuple-element.41), channel_id=1, source_target_pairs={{0,3},{1,2},{2,1},{3,0},{4,7},{5,6},{6,5},{7,4},{8,11},{9,10},{10,... | collective-permute-start | bytes 245768 | tf_op jit(solution)/shard_map/ppermute | solution.py:29
  62.3 4.7 %collective-permute-start.8 = (bf16[32,1280]{1,0:T(8,128)(2,1)S(1)}, bf16[32,1280]{1,0:T(8,128)(2,1)S(1)}, u32[]{:S(2)}, u32[]{:S(2)}) collective-permute-start(bf16[32,1280]{1,0:T(8,128)(2,1)S(1)} %get-tuple-element.40), channel_id=1, source_target_pairs={{0,1},{1,0},{2,3},{3,2},{4,5},{5,4},{6,7},{7,6},{8,9},{9,8},{10,11... | collective-permute-start | bytes 245768 | tf_op jit(solution)/shard_map/ppermute | solution.py:29
  63.9 4.9 %collective-permute-start.9 = (bf16[32,1280]{1,0:T(8,128)(2,1)S(1)}, bf16[32,1280]{1,0:T(8,128)(2,1)S(1)}, u32[]{:S(2)}, u32[]{:S(2)}) collective-permute-start(bf16[32,1280]{1,0:T(8,128)(2,1)S(1)} %get-tuple-element.42), channel_id=1, source_target_pairs={{0,2},{1,3},{2,0},{3,1},{4,6},{5,7},{6,4},{7,5},{8,10},{9,11},{10,... | collective-permute-start | bytes 245768 | tf_op jit(solution)/shard_map/ppermute | solution.py:29
  68.8 25.2 %copy-start = (f32[5120]{0:T(1024)S(1)}, f32[5120]{0:T(1024)}, u32[]{:S(2)}) copy-start(f32[5120]{0:T(1024)} %param.22) | copy-start | bytes 61444
  69.7 7.8 %collective-permute-start.14 = (bf16[32,1280]{1,0:T(8,128)(2,1)S(1)}, bf16[32,1280]{1,0:T(8,128)(2,1)S(1)}, u32[]{:S(2)}, u32[]{:S(2)}) collective-permute-start(bf16[32,1280]{1,0:T(8,128)(2,1)S(1)} %add_convert_fusion.3), channel_id=1, source_target_pairs={{0,16},{4,20},{8,24},{12,28},{16,0},{20,4},{24,8},{28,12},{1,17},{... | collective-permute-start | bytes 245768 | tf_op jit(solution)/shard_map/ppermute | solution.py:29
  69.8 7.8 %collective-permute-start.15 = (bf16[32,1280]{1,0:T(8,128)(2,1)S(1)}, bf16[32,1280]{1,0:T(8,128)(2,1)S(1)}, u32[]{:S(2)}, u32[]{:S(2)}) collective-permute-start(bf16[32,1280]{1,0:T(8,128)(2,1)S(1)} %add_convert_fusion.3), channel_id=1, source_target_pairs={{0,24},{4,28},{8,16},{12,20},{16,8},{20,12},{24,0},{28,4},{1,25},{... | collective-permute-start | bytes 245768 | tf_op jit(solution)/shard_map/ppermute | solution.py:29
  70.9 7.6 %collective-permute-start.11 = (bf16[32,1280]{1,0:T(8,128)(2,1)S(1)}, bf16[32,1280]{1,0:T(8,128)(2,1)S(1)}, u32[]{:S(2)}, u32[]{:S(2)}) collective-permute-start(bf16[32,1280]{1,0:T(8,128)(2,1)S(1)} %add_convert_fusion.3), channel_id=1, source_target_pairs={{0,8},{4,12},{8,0},{12,4},{16,24},{20,28},{24,16},{28,20},{1,9},{5... | collective-permute-start | bytes 245768 | tf_op jit(solution)/shard_map/ppermute | solution.py:29
  77.6 5.4 %collective-permute-start.16 = (bf16[64,1280]{1,0:T(8,128)(2,1)S(1)}, bf16[64,1280]{1,0:T(8,128)(2,1)S(1)}, u32[]{:S(2)}, u32[]{:S(2)}) collective-permute-start(bf16[64,1280]{1,0:T(8,128)(2,1)S(1)} %constant_dynamic-update-slice_fusion.5), channel_id=1, source_target_pairs={{0,2},{1,3},{2,0},{3,1},{4,6},{5,7},{6,4},{7,5},{8,10},{9,11},{10,... | collective-permute-start | bytes 491528 | tf_op jit(solution)/shard_map/ppermute | solution.py:29
  78.4 7.1 %collective-permute-start.12 = (bf16[64,1280]{1,0:T(8,128)(2,1)S(1)}, bf16[64,1280]{1,0:T(8,128)(2,1)S(1)}, u32[]{:S(2)}, u32[]{:S(2)}) collective-permute-start(bf16[64,1280]{1,0:T(8,128)(2,1)S(1)} %pad_maximum_fusion.4), channel_id=1, source_target_pairs={{0,4},{4,0},{8,12},{12,8},{16,20},{20,16},{24,28},{28,24},{1,5},{5... | collective-permute-start | bytes 491528 | tf_op jit(solution)/shard_map/ppermute | solution.py:29
  83.0 8.5 %collective-permute-start.17 = (bf16[2,64,1280]{2,1,0:T(8,128)(2,1)S(1)}, bf16[2,64,1280]{2,1,0:T(8,128)(2,1)S(1)}, u32[]{:S(2)}, u32[]{:S(2)}) collective-permute-start(bf16[2,64,1280]{2,1,0:T(8,128)(2,1)S(1)} %pad_maximum_fusion.2), channel_id=1, source_target_pairs={{0,4},{4,0},{8,12},{12,8},{16,20},{20,16},{24,28},{28,24},{1,5},{5... | collective-permute-start | bytes 983048 | tf_op jit(solution)/shard_map/ppermute | solution.py:29
  85.6 7.6 %collective-permute-start.13 = (bf16[128,1280]{1,0:T(8,128)(2,1)S(1)}, bf16[128,1280]{1,0:T(8,128)(2,1)S(1)}, u32[]{:S(2)}, u32[]{:S(2)}) collective-permute-start(bf16[128,1280]{1,0:T(8,128)(2,1)S(1)} %get-tuple-element.34), channel_id=1, source_target_pairs={{0,2},{1,3},{2,0},{3,1},{4,6},{5,7},{6,4},{7,5},{8,10},{9,11},{10,... | collective-permute-start | bytes 983048 | tf_op jit(solution)/shard_map/ppermute | solution.py:29
  93.2 0.7 copy-start.2
  93.3 5.7 %collective-permute-start.18 = (bf16[2,256,1280]{2,1,0:T(8,128)(2,1)S(1)}, bf16[2,256,1280]{2,1,0:T(8,128)(2,1)S(1)}, u32[]{:S(2)}, u32[]{:S(2)}) collective-permute-start(bf16[2,256,1280]{2,1,0:T(8,128)(2,1)S(1)} %pad_maximum_fusion.rows_ref), channel_id=1, source_target_pairs={{0,1},{1,0},{2,3},{3,2},{4,5},{5,4},{6,7},{7,6},{8,9},{9,8},{10,11... | collective-permute-start | bytes 3932168 | tf_op jit(solution)/shard_map/ppermute | solution.py:29
  106.2 3.9 %collective-permute-start.19 = (bf16[2,256,1280]{2,1,0:T(8,128)(2,1)S(1)}, bf16[2,256,1280]{2,1,0:T(8,128)(2,1)}, u32[]{:S(2)}, u32[]{:S(2)}) collective-permute-start(bf16[2,256,1280]{2,1,0:T(8,128)(2,1)S(1)} %get-tuple-element.27), channel_id=1, source_target_pairs={{0,1},{1,0},{2,3},{3,2},{4,5},{5,4},{6,7},{7,6},{8,9},{9,8},{10,11... | collective-permute-start | bytes 3932168 | tf_op jit(solution)/shard_map/ppermute | solution.py:29
  111.8 10.1 %collective-permute-start.20 = (bf16[128,1280]{1,0:T(8,128)(2,1)S(1)}, bf16[128,1280]{1,0:T(8,128)(2,1)S(1)}, u32[]{:S(2)}, u32[]{:S(2)}) collective-permute-start(bf16[128,1280]{1,0:T(8,128)(2,1)S(1)} %slice_bitcast_fusion.2), channel_id=1, source_target_pairs={{0,2},{1,3},{2,0},{3,1},{4,6},{5,7},{6,4},{7,5},{8,10},{9,11},{10,... | collective-permute-start | bytes 983048 | tf_op jit(solution)/shard_map/ppermute | solution.py:29
  112.8 10.8 %collective-permute-start.23 = (bf16[2,64,1280]{2,1,0:T(8,128)(2,1)S(1)}, bf16[2,64,1280]{2,1,0:T(8,128)(2,1)S(1)}, u32[]{:S(2)}, u32[]{:S(2)}) collective-permute-start(bf16[2,64,1280]{2,1,0:T(8,128)(2,1)S(1)} %slice_bitcast_fusion), channel_id=1, source_target_pairs={{0,4},{4,0},{8,12},{12,8},{16,20},{20,16},{24,28},{28,24},{1,5},{5... | collective-permute-start | bytes 983048 | tf_op jit(solution)/shard_map/ppermute | solution.py:29
  122.0 5.9 %collective-permute-start.21 = (bf16[64,1280]{1,0:T(8,128)(2,1)S(1)}, bf16[64,1280]{1,0:T(8,128)(2,1)S(1)}, u32[]{:S(2)}, u32[]{:S(2)}) collective-permute-start(bf16[64,1280]{1,0:T(8,128)(2,1)S(1)} %slice.146), channel_id=1, source_target_pairs={{0,4},{4,0},{8,12},{12,8},{16,20},{20,16},{24,28},{28,24},{1,5},{5... | collective-permute-start | bytes 491528 | tf_op jit(solution)/shard_map/ppermute | solution.py:29
  123.7 5.6 %collective-permute-start.24 = (bf16[64,1280]{1,0:T(8,128)(2,1)S(1)}, bf16[64,1280]{1,0:T(8,128)(2,1)S(1)}, u32[]{:S(2)}, u32[]{:S(2)}) collective-permute-start(bf16[64,1280]{1,0:T(8,128)(2,1)S(1)} %slice_bitcast_fusion.4), channel_id=1, source_target_pairs={{0,2},{1,3},{2,0},{3,1},{4,6},{5,7},{6,4},{7,5},{8,10},{9,11},{10,... | collective-permute-start | bytes 491528 | tf_op jit(solution)/shard_map/ppermute | solution.py:29
  128.0 4.7 %collective-permute-start.22 = (bf16[32,1280]{1,0:T(8,128)(2,1)S(1)}, bf16[32,1280]{1,0:T(8,128)(2,1)S(1)}, u32[]{:S(2)}, u32[]{:S(2)}) collective-permute-start(bf16[32,1280]{1,0:T(8,128)(2,1)S(1)} %slice.148), channel_id=1, source_target_pairs={{0,8},{4,12},{8,0},{12,4},{16,24},{20,28},{24,16},{28,20},{1,9},{5... | collective-permute-start | bytes 245768 | tf_op jit(solution)/shard_map/ppermute | solution.py:29
  129.4 8.2 %collective-permute-start.25 = (bf16[32,1280]{1,0:T(8,128)(2,1)S(1)}, bf16[32,1280]{1,0:T(8,128)(2,1)S(1)}, u32[]{:S(2)}, u32[]{:S(2)}) collective-permute-start(bf16[32,1280]{1,0:T(8,128)(2,1)S(1)} %get-tuple-element.43), channel_id=1, source_target_pairs={{0,16},{4,20},{8,24},{12,28},{16,0},{20,4},{24,8},{28,12},{1,17},{... | collective-permute-start | bytes 245768 | tf_op jit(solution)/shard_map/ppermute | solution.py:29
  130.5 7.1 %collective-permute-start.26 = (bf16[32,1280]{1,0:T(8,128)(2,1)S(1)}, bf16[32,1280]{1,0:T(8,128)(2,1)S(1)}, u32[]{:S(2)}, u32[]{:S(2)}) collective-permute-start(bf16[32,1280]{1,0:T(8,128)(2,1)S(1)} %get-tuple-element.44), channel_id=1, source_target_pairs={{0,24},{4,28},{8,16},{12,20},{16,8},{20,12},{24,0},{28,4},{1,25},{... | collective-permute-start | bytes 245768 | tf_op jit(solution)/shard_map/ppermute | solution.py:29
  137.6 4.5 %collective-permute-start.27 = (bf16[32,1280]{1,0:T(8,128)(2,1)S(1)}, bf16[32,1280]{1,0:T(8,128)(2,1)S(1)}, u32[]{:S(2)}, u32[]{:S(2)}) collective-permute-start(bf16[32,1280]{1,0:T(8,128)(2,1)S(1)} %get-tuple-element.31), channel_id=1, source_target_pairs={{0,2},{1,3},{2,0},{3,1},{4,6},{5,7},{6,4},{7,5},{8,10},{9,11},{10,... | collective-permute-start | bytes 245768 | tf_op jit(solution)/shard_map/ppermute | solution.py:29
  142.2 1.5 %collective-permute-start.28 = (bf16[2,32,1280]{2,1,0:T(8,128)(2,1)S(1)}, bf16[2,32,1280]{2,1,0:T(8,128)(2,1)S(1)}, u32[]{:S(2)}, u32[]{:S(2)}) collective-permute-start(bf16[2,32,1280]{2,1,0:T(8,128)(2,1)S(1)} %pad_maximum_fusion.5), channel_id=1, source_target_pairs={{0,1},{1,0},{2,3},{3,2},{4,5},{5,4},{6,7},{7,6},{8,9},{9,8},{10,11... | collective-permute-start | bytes 491528 | tf_op jit(solution)/shard_map/ppermute | solution.py:29
  142.3 1.4 copy-start.4
  143.7 0.7 copy-start.3

commit v3 on v2

--- a/solution.py
+++ b/solution.py
@@ -65,8 +65,8 @@
 
 
 def pages_kernel(
-    block_pages, slot_ref, valid_ref, query_ref, fresh_key_ref, fresh_value_ref, key_hbm, value_hbm,
-    out_ref, key_buf, value_buf, top_ref, total_ref, acc_ref, sems,
+    block_pages, slot_ref, valid_ref, query_ref, fresh_key_ref, fresh_value_ref, key_buf, value_buf,
+    out_ref, top_ref, total_ref, acc_ref,
 ):
     page_count, kv_local, page_size, head_dim = key_buf.shape
     blocks = page_count // block_pages
@@ -75,17 +75,6 @@
     rows = query_ref.shape[1]
     per_step = rows // STEPS
     scale = head_dim ** (-0.5)
-
-    def copies(block):
-        at = pl.ds(block * block_pages, block_pages)
-        return (
-            pltpu.make_async_copy(key_hbm.at[at], key_buf.at[at], sems.at[0, block]),
-            pltpu.make_async_copy(value_hbm.at[at], value_buf.at[at], sems.at[1, block]),
-        )
-
-    for block in range(blocks):
-        for copy in copies(block):
-            copy.start()
 
     top_ref[...] = jnp.full(top_ref.shape, masked_low, f32)
     total_ref[...] = jnp.zeros(total_ref.shape, f32)
@@ -115,8 +104,6 @@
 
     @pl.loop(0, blocks)
     def _(block):
-        for copy in copies(block):
-            copy.wait()
         pages = [block * block_pages + i for i in range(block_pages)]
         places = [(page, head) for page in pages for head in range(kv_local)]
         at = [slot_ref[page] * kv_local + head for page, head in places]
@@ -157,25 +144,18 @@
     block_pages = 6
     while page_count % block_pages:
         block_pages -= 1
-    blocks = page_count // block_pages
     count = queries.shape[0]
-    vmem = pl.BlockSpec(memory_space=pltpu.VMEM)
-    smem = pl.BlockSpec(memory_space=pltpu.SMEM)
-    hbm = pl.BlockSpec(memory_space=pl.ANY)
     return pl.pallas_call(
         functools.partial(pages_kernel, block_pages),
         out_shape=jax.ShapeDtypeStruct((groups, pairs + 1, rows, head_dim), bf16),
-        in_specs=[smem, smem, vmem, vmem, vmem, hbm, hbm],
+        in_specs=[smem, smem] + [vmem] * 5,
         out_specs=vmem,
         scratch_shapes=[
-            pltpu.VMEM(key_cache.shape, bf16),
-            pltpu.VMEM(value_cache.shape, bf16),
             pltpu.VMEM((count, rows, head_dim), f32),
             pltpu.VMEM((count, rows, head_dim), f32),
             pltpu.VMEM((count, rows, head_dim), f32),
-            pltpu.SemaphoreType.DMA((2, blocks)),
         ],
-        compiler_params=pltpu.CompilerParams(vmem_limit_bytes=60 << 20),
+        compiler_params=pltpu.CompilerParams(vmem_limit_bytes=14 << 20),
         cost_estimate=pl.CostEstimate(
             flops=4 * rows * page_count * kv_local * page_size * head_dim,
             bytes_accessed=4 * page_count * kv_local * page_size * head_dim,
@@ -227,6 +207,14 @@
         compiler_params=pltpu.CompilerParams(vmem_limit_bytes=8 << 20),
         name="merge_parts",
     )(*parts)
+
+
+def columns_of(ref, index, size):
+    return ref[:, pl.ds(pl.multiple_of(index * size, size), size)]
+
+
+def rows_of(ref, index, size):
+    return ref[pl.ds(pl.multiple_of(index * size, size), size), :]
 
 
 def start_all(copies):
@@ -377,7 +365,7 @@
             pltpu.VMEM((pairs * pads, head_dim), f32),
             pltpu.SemaphoreType.DMA((2,)),
         ],
-        compiler_params=pltpu.CompilerParams(vmem_limit_bytes=58 << 20),
+        compiler_params=pltpu.CompilerParams(vmem_limit_bytes=50 << 20),
         cost_estimate=pl.CostEstimate(
             flops=4 * rows * width * columns, bytes_accessed=4 * width * columns, transcendentals=0
         ),
@@ -446,12 +434,45 @@
             pltpu.VMEM((rows, depth), bf16),
             pltpu.SemaphoreType.DMA((tp,)),
         ],
-        compiler_params=pltpu.CompilerParams(vmem_limit_bytes=58 << 20),
+        compiler_params=pltpu.CompilerParams(vmem_limit_bytes=50 << 20),
         cost_estimate=pl.CostEstimate(
             flops=2 * rows * weight.size, bytes_accessed=2 * weight.size, transcendentals=0
         ),
         name="project_out",
     )(part.reshape(1), own_input, weight, *parts)
+
+
+def join_kernel(ways, near_count, *refs):
+    out_ref = refs[-1]
+    half = refs[0].shape[1]
+    row = 0
+    for group in range(2):
+        pieces = refs[group * near_count : (group + 1) * near_count]
+        height = pieces[0].shape[0]
+        for way in range(ways):
+            out_ref[way, row : row + height, :half] = pieces[way][...]
+        at = row
+        for piece in pieces[ways:]:
+            out_ref[:, at : at + piece.shape[1], half:] = piece[...]
+            at += piece.shape[1]
+        row += height
+
+
+def join_groups(near, far, ways):
+    pieces = near + far
+    columns = pieces[0].shape[1] + pieces[ways].shape[2]
+    all_rows = near[0].shape[0] + far[0].shape[0]
+    return pl.pallas_call(
+        functools.partial(join_kernel, ways, len(near)),
+        out_shape=jax.ShapeDtypeStruct((ways, all_rows, columns), bf16),
+        in_specs=[vmem] * len(pieces),
+        out_specs=vmem,
+        compiler_params=pltpu.CompilerParams(vmem_limit_bytes=8 << 20),
+        cost_estimate=pl.CostEstimate(
+            flops=0, bytes_accessed=4 * ways * all_rows * columns, transcendentals=0
+        ),
+        name="join_groups",
+    )(*pieces)
 
 
 def gate_up_copies(part, core, ways, quarter, gate_hbm, up_hbm, gate_buf, up_buf, sems):
@@ -513,7 +534,7 @@
             pltpu.VMEM(rows.shape, bf16),
             pltpu.SemaphoreType.DMA((2, ways)),
         ],
-        compiler_params=pltpu.CompilerParams(vmem_limit_bytes=48 << 20),
+        compiler_params=pltpu.CompilerParams(vmem_limit_bytes=40 << 20),
         cost_estimate=pl.CostEstimate(
             flops=4 * rows.size * hidden,
             bytes_accessed=4 * ways * quarter * hidden + 8 * all_rows * hidden,
@@ -586,7 +607,7 @@
             pltpu.SemaphoreType.DMA((2, ways)),
             pltpu.SemaphoreType.DMA((ways,)),
         ],
-        compiler_params=pltpu.CompilerParams(vmem_limit_bytes=48 << 20),
+        compiler_params=pltpu.CompilerParams(vmem_limit_bytes=40 << 20),
         cost_estimate=pl.CostEstimate(
             flops=6 * rows.size * hidden, bytes_accessed=6 * ways * quarter * hidden, transcendentals=0
         ),
@@ -622,6 +643,41 @@
         ),
         name="down_half",
     )(part.reshape(1), activation, w_down)
+
+
+def sum_kernel(ways, across, own_ref, other_ref, *out_refs):
+    all_rows, columns = own_ref.shape[1:]
+    half = out_refs[0].shape[1]
+    outs = iter(out_refs)
+    height = all_rows // 2
+    for row in (height, 0):
+        for way in range(ways):
+            at = (way, slice(row, row + height), slice(0, half))
+            next(outs)[...] = (own_ref[at].astype(f32) + other_ref[at].astype(f32)).astype(bf16)
+        step = height // across
+        for k in range(across):
+            out = next(outs)
+            for way in range(ways):
+                at = (way, slice(row + k * step, row + (k + 1) * step), slice(half, columns))
+                out[way] = (own_ref[at].astype(f32) + other_ref[at].astype(f32)).astype(bf16)
+
+
+def sum_terms(own, other, across, half):
+    ways, all_rows, columns = own.shape
+    height = all_rows // 2
+    group = [jax.ShapeDtypeStruct((height, half), bf16)] * ways
+    group = group + [jax.ShapeDtypeStruct((ways, height // across, columns - half), bf16)] * across
+    outs = pl.pallas_call(
+        functools.partial(sum_kernel, ways, across),
+        out_shape=group + group,
+        in_specs=[vmem, vmem],
+        out_specs=[vmem] * (2 * len(group)),
+        compiler_params=pltpu.CompilerParams(vmem_limit_bytes=8 << 20),
+        cost_estimate=pl.CostEstimate(flops=own.size, bytes_accessed=6 * own.size, transcendentals=0),
+        name="sum_terms",
+    )(own, other)
+    count = len(group)
+    return [(part[:ways], part[ways:]) for part in (outs[:count], outs[count:])]
 
 
 def local(
@@ -670,6 +726,7 @@
     queries = [shared] + [swap(shared, "seq", k) for k in range(1, across)]
     queries = jnp.concatenate(queries, axis=0)
 
+    normalized, shared = lax.optimization_barrier((normalized, shared))
     fresh_keys, fresh_values = project_fresh(
         normalized, cosine, sine, key_projection, value_projection, kv_local, head_dim
     )
@@ -694,23 +751,36 @@
         total = total + swap(terms[slot - 1], "tp", slot).astype(f32)
     own_attended = total.astype(bf16)
 
-    layered = [own_attended] + [swap(own_attended, "seq", across * k) for k in range(1, deep)]
-    near = jnp.concatenate(layered[: deep // 2], axis=0)
-    far = jnp.concatenate(layered[deep // 2 :], axis=0)
-    near = jnp.concatenate([near] + [swap(near, "seq", k) for k in range(1, across)], axis=0)
-    far = jnp.stack([far] + [swap(far, "tp", CORES * k) for k in range(1, ways)])
-    near = jnp.stack([near] + [swap(near, "tp", CORES * k) for k in range(1, ways)])
-    far = jnp.concatenate([far] + [swap(far, "seq", k) for k in range(1, across)], axis=1)
-    both = jnp.concatenate([near, far], axis=1)
+    half = (quarter + 255) // 256 * 128
+    count = deep // 2
+
+    def along_x(value):
+        return [value] + [swap(value, "seq", k) for k in range(1, across)]
+
+    def along_y(value):
+        return [value] + [swap(value, "tp", CORES * k) for k in range(1, ways)]
+
+    def spread_first(group):
+        first, second = group[:, :half], group[:, half:]
+        return along_x(first), along_y(second)
+
+    def spread_second(first, second):
+        return along_y(jnp.concatenate(first, axis=0)) + along_x(jnp.stack(second))
+
+    far = [swap(own_attended, "seq", across * k) for k in range(count, deep)]
+    near = [own_attended] + [swap(own_attended, "seq", across * k) for k in range(1, count)]
+    near = spread_first(jnp.concatenate(near, axis=0))
+    near, far = lax.optimization_barrier((near, far))
+    near = spread_second(*near)
+    far = spread_second(*spread_first(jnp.concatenate(far, axis=0)))
+    both = join_groups(near, far, ways)
     other = swap(both, "tp", 1)
     all_rows = both.shape[1]
 
-    def assemble(pieces, other_pieces, height):
+    def assemble(pieces, height):
         whole = jnp.zeros((height, width), bf16)
-        for k in range(ways):
-            for core, source in ((0, pieces), (1, other_pieces)):
-                at = (part ^ (k * CORES + core)) * quarter
-                whole = lax.dynamic_update_slice_in_dim(whole, source[k], at, 1)
+        for slot, piece in enumerate(pieces):
+            whole = lax.dynamic_update_slice_in_dim(whole, piece, (part ^ slot) * quarter, 1)
         return whole
 
     gains = mlp_gain.reshape(tp, 1, quarter)
@@ -718,29 +788,32 @@
     activation, other_terms = gate_up_rest(part, other, gains, w_gate, w_up, w_down, sums, width)
     received = swap(other_terms, "tp", 1)
     own_terms = down_half(part, activation, w_down, ways)
-    summed = (own_terms.astype(f32) + received.astype(f32)).astype(bf16)
-    attended = assemble(both[:, :rows], other[:, :rows], rows).reshape(steps, row_count, width)
-    half = all_rows // 2
-    near, far = summed[:, :half], summed[:, half:]
+    far, near = sum_terms(own_terms, received, across, half)
+    own_pieces = [piece[k, :rows] for k in range(ways) for piece in (both, other)]
+    attended = assemble(own_pieces, rows).reshape(steps, row_count, width)
 
     def add(first, others):
         value = first.astype(f32)
-        for other in others:
-            value = value + other.astype(f32)
+        for one in others:
+            value = value + one.astype(f32)
         return value
 
-    near = add(near[0], [swap(near[k], "tp", CORES * k) for k in range(1, ways)]).astype(bf16)
-    far = far.reshape(ways, across, half // across, quarter)
-    far = add(far[:, 0], [swap(far[:, k], "seq", k) for k in range(1, across)]).astype(bf16)
-    near = near.reshape(across, half // across, quarter)
-    near = add(near[0], [swap(near[k], "seq", k) for k in range(1, across)]).astype(bf16)
-    far = add(far[0], [swap(far[k], "tp", CORES * k) for k in range(1, ways)]).astype(bf16)
-    layered = jnp.concatenate([near, far], axis=0).reshape(deep, rows, quarter)
-    mlp_result = add(layered[0], [swap(layered[k], "seq", across * k) for k in range(1, deep)])
+    def collect_group(first, second):
+        first = add(first[0], [swap(first[k], "tp", CORES * k) for k in range(1, ways)]).astype(bf16)
+        second = add(second[0], [swap(second[k], "seq", k) for k in range(1, across)]).astype(bf16)
+        first = first.reshape(across, -1, half)
+        first = add(first[0], [swap(first[k], "seq", k) for k in range(1, across)]).astype(bf16)
+        second = add(second[0], [swap(second[k], "tp", CORES * k) for k in range(1, ways)]).astype(bf16)
+        return jnp.concatenate([first, second], axis=1).reshape(-1, rows, quarter)
+
+    far = collect_group(*far)
+    near = collect_group(*near)
+    far = [swap(far[k], "seq", across * (count + k)) for k in range(deep - count)]
+    near = [near[0]] + [swap(near[k], "seq", across * k) for k in range(1, count)]
+    mlp_result = add(near[0], near[1:] + far)
     own_out = (own_attended.astype(f32) + mlp_result).astype(bf16)
-
-    spread = jnp.stack([own_out] + [swap(own_out, "tp", CORES * k) for k in range(1, ways)])
-    layer_out = assemble(spread, swap(spread, "tp", 1), rows).reshape(steps, row_count, width)
+    pieces = [own_out] + [swap(own_out, "tp", slot) for slot in range(1, tp)]
+    layer_out = assemble(pieces, rows).reshape(steps, row_count, width)
     return attended, layer_out
 
 

time: 145 us -> 136 us (0.938)
  waiting for transfers between devices: 54.4 us -> 46.7 us
  Pallas kernels: 42.2 us -> 36.8 us
  starting transfers between devices: 34.6 us -> 39.2 us
  other arithmetic: 3.92 us -> 0.67 us
  local copies, waits for them, and re-layouts: 8.17 us -> 10.8 us
    ppermute x29 -> x38, waiting for transfers between devices: 54.4 us -> 46.7 us  [swap(): return lax.ppermute(value, axis, [(i, i ^ mask) for i in range(size)])]
    ppermute x29 -> x38, starting transfers between devices: 34.6 us -> 39.2 us  [swap(): return lax.ppermute(value, axis, [(i, i ^ mask) for i in range(size)])]
    unnamed x31 -> x41, local copies, waits for them, and re-layouts: 2.74 us -> 6.01 us
    dynamic_update_slice x7, local copies, waits for them, and re-layouts: 0.96 us -> 3.61 us  [assemble(): lax.dynamic_update_slice_in_dim(whole, piece, (part ^ slot) * quarter, 1)]
    pallas_call x1, Pallas kernels: 7.42 us -> 4.88 us  [attend_pages(): pl.pallas_call(functools.partial(pages_kernel, block_pages), out_shape=ja...]
    pallas_call x1, Pallas kernels: 5.09 us -> 2.9 us  [project_fresh(): pl.pallas_call(functools.partial(fresh_kernel, kv_local), out_shape=(jax....]
    convert_element_type x5 -> x8, other arithmetic: 1.86 us -> 0.26 us  [the longest x2 0.09 us: collect_group(): add(first[0], [swap(first[k], 'tp', CORES * k) for k in range(1, ways)])]
    pallas_call x1, Pallas kernels: 6.42 us -> 4.87 us  [project_out(): pl.pallas_call(functools.partial(out_kernel, len(parts), kv_local), out_s...]
  transfers between devices with their start and end apart: 29 -> 38, of which waited for: 19 -> 23; matrix products, arithmetic and copies ran while one was open for 3% -> 4% of each run, Pallas kernels for 10% -> 8%
where the time goes in v3:
time: 136 us; the launch traced here: 135 us
  waiting for transfers between devices  46.7 us (34%)
  starting transfers between devices  39.2 us (29%)
  Pallas kernels  36.8 us (27%)
  local copies, waits for them, and re-layouts  10.8 us (8%)
    ppermute x38, waiting for transfers between devices, swap(): return lax.ppermute(value, axis, [(i, i ^ mask) for i in range(size)])  46.7 us
    ppermute x38, starting transfers between devices, swap(): return lax.ppermute(value, axis, [(i, i ^ mask) for i in range(size)])  39.2 us
    pallas_call x1, Pallas kernels, gate_up_rest(): pl.pallas_call(functools.partial(rest_kernel, width), out_shape=(jax.Shap...  7.63 us
    pallas_call x1, Pallas kernels, project_queries(): pl.pallas_call(functools.partial(query_kernel, kv_local), out_shape=(jax....  6.96 us
    unnamed x41, local copies, waits for them, and re-layouts  6.01 us
    pallas_call x1, Pallas kernels, attend_pages(): pl.pallas_call(functools.partial(pages_kernel, block_pages), out_shape=ja...  4.88 us
    pallas_call x1, Pallas kernels, project_out(): pl.pallas_call(functools.partial(out_kernel, len(parts), kv_local), out_s...  4.87 us
    pallas_call x1, Pallas kernels, gate_up_half(): pl.pallas_call(functools.partial(gate_up_kernel, core), out_shape=(jax.Sh...  4.53 us
  transfers between devices with their start and end apart: 38, of which 23 were waited for; matrix products, arithmetic and copies ran while one was open for 4% of the time, Pallas kernels for 8%

profile of v3, /device:TPU:0, one launch (start us, length us, event | category | flops | bytes accessed | tf_op | source)
XLA Modules:
  0.0 135.3 jit_solution(13243359332419188420)
XLA Ops:
  0.7 7.0 %project_queries.1 = (bf16[16,16,128]{2,1,0:T(8,128)(2,1)}, bf16[32,5120]{1,0:T(8,128)(2,1)}, f32[32,128]{1,0:T(8,128)}, f32[32,128]{1,0:T(8,128)}) custom-call(s32[1]{0:T(128)} %bitcast.2.me_ref, s32[1,64]{1,0:T(1,128)} %bitcast.62, s32[1,64]{1,0:T(1,128)} %bitcast.61, bf16[4,8,5120]{2,1,0:T(8,128)(2,1)} %input_ref.1, f32[1,5120]{1,0:T(1,128)} %bitcast.60, ...), custom_call_target="tpu_custom_call" | custom-call | flops 335544320 | bytes 10485760 | tf_op jit(solution)/shard_map/project_queries/pallas_call | solution.py:289
  7.7 5.1 %collective-permute-start.2 = (bf16[16,16,128]{2,1,0:T(8,128)(2,1)}, bf16[16,16,128]{2,1,0:T(8,128)(2,1)S(1)}, u32[]{:S(2)}, u32[]{:S(2)}) collective-permute-start(bf16[16,16,128]{2,1,0:T(8,128)(2,1)} %get-tuple-element.30), channel_id=1, source_target_pairs={{0,24},{4,28},{8,16},{12,20},{16,8},{20,12},{24,0},{28,4},{1,25},{... | collective-permute-start | bytes 196616 | tf_op jit(solution)/shard_map/ppermute | solution.py:29
  12.8 0.6 collective-permute-start
  13.4 0.9 constant_dynamic-update-slice_fusion.3
  14.3 3.0 %collective-permute-done = bf16[16,16,128]{2,1,0:T(8,128)(2,1)S(1)} collective-permute-done((bf16[16,16,128]{2,1,0:T(8,128)(2,1)}, bf16[16,16,128]{2,1,0:T(8,128)(2,1)S(1)}, u32[]{:S(2)}, u32[]{:S(2)}) %collective-permute-start) | collective-permute-done | bytes 65568 | tf_op jit(solution)/shard_map/ppermute | solution.py:29
  17.3 1.3 collective-permute-done.1
  18.7 1.6 %collective-permute-start.3 = (bf16[64,16,128]{2,1,0:T(8,128)(2,1)S(1)}, bf16[64,16,128]{2,1,0:T(8,128)(2,1)S(1)}, u32[]{:S(2)}, u32[]{:S(2)}) collective-permute-start(bf16[64,16,128]{2,1,0:T(8,128)(2,1)S(1)} %get-tuple-element.78), channel_id=1, source_target_pairs={{0,4},{4,0},{8,12},{12,8},{16,20},{20,16},{24,28},{28,24},{1,5},{5... | collective-permute-start | bytes 786440 | tf_op jit(solution)/shard_map/ppermute | solution.py:29
  20.5 1.7 %copy-done.3 = bf16[5120,256]{1,0:T(8,128)(2,1)S(1)} copy-done((bf16[5120,256]{1,0:T(8,128)(2,1)S(1)}, bf16[5120,256]{1,0:T(8,128)(2,1)}, u32[]{:S(2)}) %copy-start.3) | copy-done | bytes 2621464
  22.2 1.0 copy-done.5
  23.2 0.7 copy-done.7
  23.9 0.7 copy-done.8
  24.6 2.9 %project_fresh.1 = (bf16[16,16,128]{2,1,0:T(8,128)(2,1)S(1)}, bf16[16,16,128]{2,1,0:T(8,128)(2,1)S(1)}) custom-call(bf16[32,5120]{1,0:T(8,128)(2,1)S(1)} %copy-done.5, f32[32,128]{1,0:T(8,128)S(1)} %copy-done.7, f32[32,128]{1,0:T(8,128)S(1)} %copy-done.8, bf16[5120,256]{1,0:T(8,128)(2,1)S(1)} %copy-done.3, bf16[5120,256]{1,0:T(8,128)(2,1)} %value_hbm.1), custom_call_target="tpu_custom_call" | custom-call | flops 167772160 | bytes 5242880 | tf_op jit(solution)/shard_map/project_fresh/pallas_call | solution.py:356
  27.7 4.9 %attend_pages.1 = bf16[8,17,16,128]{3,2,1,0:T(8,128)(2,1)S(1)} custom-call(s32[36]{0:T(128)S(1)} %get-tuple-element.87.slot_ref, s32[36]{0:T(128)S(1)} %get-tuple-element.86.valid_ref, bf16[128,16,128]{2,1,0:T(8,128)(2,1)S(1)} %constant_dynamic-update-slice_fusion.4.query_ref, bf16[16,16,128]{2,1,0:T(8,128)(2,1)S(1)} %get-tuple-element.35.fresh_key_ref, ...), custom_call_target="tpu_custom_call" | custom-call | flops 150994944 | bytes 9437184 | tf_op jit(solution)/shard_map/attend_pages/pallas_call | solution.py:148
  32.7 0.7 collective-permute-start.4
  33.3 7.5 %collective-permute-done.4.refs_1_ = bf16[4,17,16,128]{3,2,1,0:T(8,128)(2,1)S(1)} collective-permute-done((bf16[4,17,16,128]{3,2,1,0:T(8,128)(2,1)S(1)}, bf16[4,17,16,128]{3,2,1,0:T(8,128)(2,1)S(1)}, u32[]{:S(2)}, u32[]{:S(2)}) %collective-permute-start.4) | collective-permute-done | bytes 278560 | tf_op jit(solution)/shard_map/ppermute | solution.py:29
  40.9 0.9 merge_parts.1
  41.8 1.5 %collective-permute-start.7 = (bf16[1,17,16,128]{3,2,1,0:T(8,128)(2,1)S(1)}, bf16[1,17,16,128]{3,2,1,0:T(8,128)(2,1)S(1)}, u32[]{:S(2)}, u32[]{:S(2)}) collective-permute-start(bf16[1,17,16,128]{3,2,1,0:T(8,128)(2,1)S(1)} %get-tuple-element.64), channel_id=1, source_target_pairs={{0,24},{4,28},{8,16},{12,20},{16,8},{20,12},{24,0},{28,4},{1,25},{... | collective-permute-start | bytes 208904 | tf_op jit(solution)/shard_map/ppermute | solution.py:29
  43.3 2.9 %collective-permute-start.5 = (bf16[1,17,16,128]{3,2,1,0:T(8,128)(2,1)S(1)}, bf16[1,17,16,128]{3,2,1,0:T(8,128)(2,1)S(1)}, u32[]{:S(2)}, u32[]{:S(2)}) collective-permute-start(bf16[1,17,16,128]{3,2,1,0:T(8,128)(2,1)S(1)} %get-tuple-element.66), channel_id=1, source_target_pairs={{0,8},{4,12},{8,0},{12,4},{16,24},{20,28},{24,16},{28,20},{1,9},{5... | collective-permute-start | bytes 208904 | tf_op jit(solution)/shard_map/ppermute | solution.py:29
  46.2 0.9 constant_dynamic-slice_fusion.input_ref
  47.1 0.9 collective-permute-done.7.refs_3_
  48.0 1.5 %collective-permute-done.6.refs_2_ = bf16[1,17,16,128]{3,2,1,0:T(8,128)(2,1)S(1)} collective-permute-done((bf16[1,17,16,128]{3,2,1,0:T(8,128)(2,1)S(1)}, bf16[1,17,16,128]{3,2,1,0:T(8,128)(2,1)S(1)}, u32[]{:S(2)}, u32[]{:S(2)}) %collective-permute-start.6) | collective-permute-done | bytes 69664 | tf_op jit(solution)/shard_map/ppermute | solution.py:29
  49.4 4.9 %project_out.1 = (f32[32,1280]{1,0:T(8,128)S(1)}, bf16[3,32,1280]{2,1,0:T(8,128)(2,1)S(1)}) custom-call(s32[1]{0:T(128)} %bitcast.part_ref, bf16[32,1280]{1,0:T(8,128)(2,1)S(1)} %constant_dynamic-slice_fusion.input_ref, bf16[1024,5120]{1,0:T(8,128)(2,1)} %weight_hbm.3, bf16[1,17,16,128]{3,2,1,0:T(8,128)(2,1)S(1)} %get-tuple-element.67.refs_0_, ...), custom_call_target="tpu_custom_call" | custom-call | flops 335544320 | bytes 10485760 | tf_op jit(solution)/shard_map/project_out/pallas_call | solution.py:423
  54.4 1.6 %collective-permute-start.10 = (bf16[32,1280]{1,0:T(8,128)(2,1)S(1)}, bf16[32,1280]{1,0:T(8,128)(2,1)S(1)}, u32[]{:S(2)}, u32[]{:S(2)}) collective-permute-start(bf16[32,1280]{1,0:T(8,128)(2,1)S(1)} %get-tuple-element.69), channel_id=1, source_target_pairs={{0,3},{1,2},{2,1},{3,0},{4,7},{5,6},{6,5},{7,4},{8,11},{9,10},{10,... | collective-permute-start | bytes 245768 | tf_op jit(solution)/shard_map/ppermute | solution.py:29
  56.6 2.3 %collective-permute-done.10 = bf16[32,1280]{1,0:T(8,128)(2,1)S(1)} collective-permute-done((bf16[32,1280]{1,0:T(8,128)(2,1)S(1)}, bf16[32,1280]{1,0:T(8,128)(2,1)S(1)}, u32[]{:S(2)}, u32[]{:S(2)}) %collective-permute-start.10) | collective-permute-done | bytes 81952 | tf_op jit(solution)/shard_map/ppermute | solution.py:29
  58.8 2.2 %collective-permute-done.9 = bf16[32,1280]{1,0:T(8,128)(2,1)S(1)} collective-permute-done((bf16[32,1280]{1,0:T(8,128)(2,1)S(1)}, bf16[32,1280]{1,0:T(8,128)(2,1)S(1)}, u32[]{:S(2)}, u32[]{:S(2)}) %collective-permute-start.9) | collective-permute-done | bytes 81952 | tf_op jit(solution)/shard_map/ppermute | solution.py:29
  61.1 1.2 collective-permute-start.11
  62.2 1.4 %collective-permute-start.15 = (bf16[32,1280]{1,0:T(8,128)(2,1)S(1)}, bf16[32,1280]{1,0:T(8,128)(2,1)S(1)}, u32[]{:S(2)}, u32[]{:S(2)}) collective-permute-start(bf16[32,1280]{1,0:T(8,128)(2,1)S(1)} %add_convert_fusion.7), channel_id=1, source_target_pairs={{0,24},{4,28},{8,16},{12,20},{16,8},{20,12},{24,0},{28,4},{1,25},{... | collective-permute-start | bytes 245768 | tf_op jit(solution)/shard_map/ppermute | solution.py:29
  63.7 1.0 collective-permute-start.14
  64.6 1.0 collective-permute-done.11
  65.6 1.6 %collective-permute-start.13 = (bf16[64,640]{1,0:T(8,128)(2,1)S(1)}, bf16[64,640]{1,0:T(8,128)(2,1)S(1)}, u32[]{:S(2)}, u32[]{:S(2)}) collective-permute-start(bf16[64,640]{1,0:T(8,128)(2,1)S(1)} %get-tuple-element.41), channel_id=1, source_target_pairs={{0,2},{1,3},{2,0},{3,1},{4,6},{5,7},{6,4},{7,5},{8,10},{9,11},{10,... | collective-permute-start | bytes 245768 | tf_op jit(solution)/shard_map/ppermute | solution.py:29
  67.7 1.1 collective-permute-done.15
  68.8 3.3 %collective-permute-done.14 = bf16[32,1280]{1,0:T(8,128)(2,1)S(1)} collective-permute-done((bf16[32,1280]{1,0:T(8,128)(2,1)S(1)}, bf16[32,1280]{1,0:T(8,128)(2,1)S(1)}, u32[]{:S(2)}, u32[]{:S(2)}) %collective-permute-start.14) | collective-permute-done | bytes 81952 | tf_op jit(solution)/shard_map/ppermute | solution.py:29
  72.2 1.6 %collective-permute-start.20 = (bf16[64,640]{1,0:T(8,128)(2,1)S(1)}, bf16[64,640]{1,0:T(8,128)(2,1)S(1)}, u32[]{:S(2)}, u32[]{:S(2)}) collective-permute-start(bf16[64,640]{1,0:T(8,128)(2,1)S(1)} %get-tuple-element.74), channel_id=1, source_target_pairs={{0,2},{1,3},{2,0},{3,1},{4,6},{5,7},{6,4},{7,5},{8,10},{9,11},{10,... | collective-permute-start | bytes 245768 | tf_op jit(solution)/shard_map/ppermute | solution.py:29
  74.3 1.6 %collective-permute-start.17 = (bf16[2,64,640]{2,1,0:T(8,128)(2,1)S(1)}, bf16[2,64,640]{2,1,0:T(8,128)(2,1)S(1)}, u32[]{:S(2)}, u32[]{:S(2)}) collective-permute-start(bf16[2,64,640]{2,1,0:T(8,128)(2,1)S(1)} %pad_maximum_fusion.refs_2_), channel_id=1, source_target_pairs={{0,4},{4,0},{8,12},{12,8},{16,20},{20,16},{24,28},{28,24},{1,5},{5... | collective-permute-start | bytes 491528 | tf_op jit(solution)/shard_map/ppermute | solution.py:29
  75.9 0.6 collective-permute-start.16
  76.5 2.1 %collective-permute-done.18 = bf16[64,640]{1,0:T(8,128)(2,1)S(1)} collective-permute-done((bf16[64,640]{1,0:T(8,128)(2,1)S(1)}, bf16[64,640]{1,0:T(8,128)(2,1)S(1)}, u32[]{:S(2)}, u32[]{:S(2)}) %collective-permute-start.18) | collective-permute-done | bytes 81952 | tf_op jit(solution)/shard_map/ppermute | solution.py:29
  79.2 1.0 collective-permute-start.21
  80.1 1.6 %collective-permute-done.17.refs_3_ = bf16[2,64,640]{2,1,0:T(8,128)(2,1)S(1)} collective-permute-done((bf16[2,64,640]{2,1,0:T(8,128)(2,1)S(1)}, bf16[2,64,640]{2,1,0:T(8,128)(2,1)S(1)}, u32[]{:S(2)}, u32[]{:S(2)}) %collective-permute-start.17) | collective-permute-done | bytes 163872 | tf_op jit(solution)/shard_map/ppermute | solution.py:29
  82.2 1.8 %collective-permute-done.19.refs_5_ = bf16[128,640]{1,0:T(8,128)(2,1)S(1)} collective-permute-done((bf16[128,640]{1,0:T(8,128)(2,1)S(1)}, bf16[128,640]{1,0:T(8,128)(2,1)S(1)}, u32[]{:S(2)}, u32[]{:S(2)}) %collective-permute-start.19) | collective-permute-done | bytes 163872 | tf_op jit(solution)/shard_map/ppermute | solution.py:29
  84.8 4.5 %gate_up_half.1 = (f32[256,1024]{1,0:T(8,128)S(1)}, f32[256,1024]{1,0:T(8,128)S(1)}, f32[256,128]{1,0:T(8,128)S(1)}) custom-call(s32[1]{0:T(128)} %bitcast.part_ref, bf16[2,256,1280]{2,1,0:T(8,128)(2,1)S(1)} %join_groups.1.rows_ref, f32[4,1,1280]{2,1,0:T(1,128)S(1)} %bitcast.52, bf16[5120,1024]{1,0:T(8,128)(2,1)S(1)} %bitcast.51, bf16[5120,1024]{1,0:T(8,128)(2,1)} %up_hbm.3), custom_call_target="tpu_custom_call" | custom-call | flops 2684354560 | bytes 12582912 | tf_op jit(solution)/shard_map/gate_up_half/pallas_call | solution.py:522
  89.4 7.6 %gate_up_rest.1 = (bf16[256,1024]{1,0:T(8,128)(2,1)S(1)}, bf16[2,256,1280]{2,1,0:T(8,128)(2,1)S(1)}) custom-call(s32[1]{0:T(128)} %bitcast.part_ref, bf16[2,256,1280]{2,1,0:T(8,128)(2,1)S(1)} %collective-permute-done.22.rows_ref, f32[4,1,1280]{2,1,0:T(1,128)S(1)} %bitcast.53, f32[256,1024]{1,0:T(8,128)S(1)} %get-tuple-element.45.old_gate_ref, ...), custom_call_target="tpu_custom_call" | custom-call | flops 4026531840 | bytes 15728640 | tf_op jit(solution)/shard_map/gate_up_rest/pallas_call | solution.py:592
  97.4 0.9 fusion.8
  98.3 3.7 %down_half.1.own_ref = bf16[2,256,1280]{2,1,0:T(8,128)(2,1)S(1)} custom-call(s32[1]{0:T(128)} %bitcast.part_ref, bf16[256,1024]{1,0:T(8,128)(2,1)S(1)} %get-tuple-element.48.activation_ref, bf16[1024,5120]{1,0:T(8,128)(2,1)} %down_hbm.3), custom_call_target="tpu_custom_call" | custom-call | flops 1342177280 | bytes 5242880 | tf_op jit(solution)/shard_map/down_half/pallas_call | solution.py:631
  102.4 1.6 %collective-permute-start.24 = (bf16[128,640]{1,0:T(8,128)(2,1)S(1)}, bf16[128,640]{1,0:T(8,128)(2,1)S(1)}, u32[]{:S(2)}, u32[]{:S(2)}) collective-permute-start(bf16[128,640]{1,0:T(8,128)(2,1)S(1)} %get-tuple-element.51), channel_id=1, source_target_pairs={{0,2},{1,3},{2,0},{3,1},{4,6},{5,7},{6,4},{7,5},{8,10},{9,11},{10,... | collective-permute-start | bytes 491528 | tf_op jit(solution)/shard_map/ppermute | solution.py:29
  104.0 0.9 fusion.7
  104.9 1.0 collective-permute-start.26
  106.3 1.1 collective-permute-start.31
  107.4 2.0 %collective-permute-done.24 = bf16[128,640]{1,0:T(8,128)(2,1)S(1)} collective-permute-done((bf16[128,640]{1,0:T(8,128)(2,1)S(1)}, bf16[128,640]{1,0:T(8,128)(2,1)S(1)}, u32[]{:S(2)}, u32[]{:S(2)}) %collective-permute-start.24) | collective-permute-done | bytes 163872 | tf_op jit(solution)/shard_map/ppermute | solution.py:29
  109.4 0.8 collective-permute-start.25
  110.2 1.8 %collective-permute-done.26 = bf16[2,64,640]{2,1,0:T(8,128)(2,1)S(1)} collective-permute-done((bf16[2,64,640]{2,1,0:T(8,128)(2,1)S(1)}, bf16[2,64,640]{2,1,0:T(8,128)(2,1)S(1)}, u32[]{:S(2)}, u32[]{:S(2)}) %collective-permute-start.26) | collective-permute-done | bytes 163872 | tf_op jit(solution)/shard_map/ppermute | solution.py:29
  112.7 1.0 collective-permute-start.30
  113.6 1.9 %collective-permute-done.31 = bf16[2,64,640]{2,1,0:T(8,128)(2,1)S(1)} collective-permute-done((bf16[2,64,640]{2,1,0:T(8,128)(2,1)S(1)}, bf16[2,64,640]{2,1,0:T(8,128)(2,1)S(1)}, u32[]{:S(2)}, u32[]{:S(2)}) %collective-permute-start.31) | collective-permute-done | bytes 163872 | tf_op jit(solution)/shard_map/ppermute | solution.py:29
  115.9 1.1 collective-permute-done.25
  117.1 0.9 collective-permute-start.28
  118.1 2.0 %collective-permute-done.32 = bf16[64,640]{1,0:T(8,128)(2,1)S(1)} collective-permute-done((bf16[64,640]{1,0:T(8,128)(2,1)S(1)}, bf16[64,640]{1,0:T(8,128)(2,1)S(1)}, u32[]{:S(2)}, u32[]{:S(2)}) %collective-permute-start.32) | collective-permute-done | bytes 81952 | tf_op jit(solution)/shard_map/ppermute | solution.py:29
  120.2 2.9 %collective-permute-start.34 = (bf16[32,1280]{1,0:T(8,128)(2,1)S(1)}, bf16[32,1280]{1,0:T(8,128)(2,1)S(1)}, u32[]{:S(2)}, u32[]{:S(2)}) collective-permute-start(bf16[32,1280]{1,0:T(8,128)(2,1)S(1)} %get-tuple-element.72), channel_id=1, source_target_pairs={{0,24},{4,28},{8,16},{12,20},{16,8},{20,12},{24,0},{28,4},{1,25},{... | collective-permute-start | bytes 245768 | tf_op jit(solution)/shard_map/ppermute | solution.py:29
  123.1 0.9 fusion.6
  124.0 3.3 %collective-permute-done.33 = bf16[32,1280]{1,0:T(8,128)(2,1)S(1)} collective-permute-done((bf16[32,1280]{1,0:T(8,128)(2,1)S(1)}, bf16[32,1280]{1,0:T(8,128)(2,1)S(1)}, u32[]{:S(2)}, u32[]{:S(2)}) %collective-permute-start.33) | collective-permute-done | bytes 81952 | tf_op jit(solution)/shard_map/ppermute | solution.py:29
  127.4 0.9 fusion.5
  128.3 1.0 collective-permute-start.36
  129.3 0.9 collective-permute-start.37
  130.3 3.4 %collective-permute-done.36 = bf16[32,1280]{1,0:T(8,128)(2,1)S(1)} collective-permute-done((bf16[32,1280]{1,0:T(8,128)(2,1)S(1)}, bf16[32,1280]{1,0:T(8,128)(2,1)S(1)}, u32[]{:S(2)}, u32[]{:S(2)}) %collective-permute-start.36) | collective-permute-done | bytes 81952 | tf_op jit(solution)/shard_map/ppermute | solution.py:29
  133.7 0.9 collective-permute-done.37
  134.6 0.7 copy-done.9
  (104 shorter events, 7.0 us)
Async XLA Ops:
  0.6 19.6 %copy-start.11 = (s32[64]{0:T(128)S(1)}, s32[64]{0:T(128)}, u32[]{:S(2)}) copy-start(s32[64]{0:T(128)} %param.28) | copy-start | bytes 772
  0.6 19.6 %copy-start.12 = (s32[64]{0:T(128)S(1)}, s32[64]{0:T(128)}, u32[]{:S(2)}) copy-start(s32[64]{0:T(128)} %param.31) | copy-start | bytes 772
  0.7 19.6 %copy-start.13 = (s32[36]{0:T(128)S(1)}, s32[36]{0:T(128)}, u32[]{:S(2)}) copy-start(s32[36]{0:T(128)} %param.29) | copy-start | bytes 436
  0.7 19.7 %copy-start.14 = (s32[36]{0:T(128)S(1)}, s32[36]{0:T(128)}, u32[]{:S(2)}) copy-start(s32[36]{0:T(128)} %param.30) | copy-start | bytes 436
  0.7 26.9 %copy-start.2 = (bf16[36,2,256,128]{3,2,1,0:T(8,128)(2,1)S(1)}, bf16[36,2,256,128]{3,2,1,0:T(8,128)(2,1)}, u32[]{:S(2)}) copy-start(bf16[36,2,256,128]{3,2,1,0:T(8,128)(2,1)} %value_buf.1) | copy-start | bytes 14155780
  7.7 11.0 %collective-permute-start.2 = (bf16[16,16,128]{2,1,0:T(8,128)(2,1)}, bf16[16,16,128]{2,1,0:T(8,128)(2,1)S(1)}, u32[]{:S(2)}, u32[]{:S(2)}) collective-permute-start(bf16[16,16,128]{2,1,0:T(8,128)(2,1)} %get-tuple-element.30), channel_id=1, source_target_pairs={{0,24},{4,28},{8,16},{12,20},{16,8},{20,12},{24,0},{28,4},{1,25},{... | collective-permute-start | bytes 196616 | tf_op jit(solution)/shard_map/ppermute | solution.py:29
  12.8 5.8 %collective-permute-start.1 = (bf16[16,16,128]{2,1,0:T(8,128)(2,1)}, bf16[16,16,128]{2,1,0:T(8,128)(2,1)S(1)}, u32[]{:S(2)}, u32[]{:S(2)}) collective-permute-start(bf16[16,16,128]{2,1,0:T(8,128)(2,1)} %get-tuple-element.30), channel_id=1, source_target_pairs={{0,16},{4,20},{8,24},{12,28},{16,0},{20,4},{24,8},{28,12},{1,17},{... | collective-permute-start | bytes 196616 | tf_op jit(solution)/shard_map/ppermute | solution.py:29
  12.8 4.5 %collective-permute-start = (bf16[16,16,128]{2,1,0:T(8,128)(2,1)}, bf16[16,16,128]{2,1,0:T(8,128)(2,1)S(1)}, u32[]{:S(2)}, u32[]{:S(2)}) collective-permute-start(bf16[16,16,128]{2,1,0:T(8,128)(2,1)} %get-tuple-element.30), channel_id=1, source_target_pairs={{0,8},{4,12},{8,0},{12,4},{16,24},{20,28},{24,16},{28,20},{1,9},{5... | collective-permute-start | bytes 196616 | tf_op jit(solution)/shard_map/ppermute | solution.py:29
  18.7 8.8 %collective-permute-start.3 = (bf16[64,16,128]{2,1,0:T(8,128)(2,1)S(1)}, bf16[64,16,128]{2,1,0:T(8,128)(2,1)S(1)}, u32[]{:S(2)}, u32[]{:S(2)}) collective-permute-start(bf16[64,16,128]{2,1,0:T(8,128)(2,1)S(1)} %get-tuple-element.78), channel_id=1, source_target_pairs={{0,4},{4,0},{8,12},{12,8},{16,20},{20,16},{24,28},{28,24},{1,5},{5... | collective-permute-start | bytes 786440 | tf_op jit(solution)/shard_map/ppermute | solution.py:29
  20.4 1.7 %copy-start.3 = (bf16[5120,256]{1,0:T(8,128)(2,1)S(1)}, bf16[5120,256]{1,0:T(8,128)(2,1)}, u32[]{:S(2)}) copy-start(bf16[5120,256]{1,0:T(8,128)(2,1)} %key_hbm.1) | copy-start | bytes 7864324
  22.2 1.0 copy-start.5
  23.2 0.7 copy-start.7
  23.9 0.7 copy-start.8
  24.6 3.1 %copy-start.1 = (bf16[36,2,256,128]{3,2,1,0:T(8,128)(2,1)S(1)}, bf16[36,2,256,128]{3,2,1,0:T(8,128)(2,1)}, u32[]{:S(2)}) copy-start(bf16[36,2,256,128]{3,2,1,0:T(8,128)(2,1)} %key_buf.1) | copy-start | bytes 14155780
  32.6 52.1 %slice-start = ((s8[10485760]{0:T(1024)(128)(4,1)}), s8[2097152]{0:T(1024)(128)(4,1)S(1)}, s32[]{:S(2)}) async-start(s8[10485760]{0:T(1024)(128)(4,1)} %bitcast.50), calls=%async_computation | async-start | bytes 4194304
  32.7 8.2 %collective-permute-start.4 = (bf16[4,17,16,128]{3,2,1,0:T(8,128)(2,1)S(1)}, bf16[4,17,16,128]{3,2,1,0:T(8,128)(2,1)S(1)}, u32[]{:S(2)}, u32[]{:S(2)}) collective-permute-start(bf16[4,17,16,128]{3,2,1,0:T(8,128)(2,1)S(1)} %get-tuple-element.62), channel_id=1, source_target_pairs={{0,4},{4,0},{8,12},{12,8},{16,20},{20,16},{24,28},{28,24},{1,5},{5... | collective-permute-start | bytes 835592 | tf_op jit(solution)/shard_map/ppermute | solution.py:29
  41.8 6.2 %collective-permute-start.7 = (bf16[1,17,16,128]{3,2,1,0:T(8,128)(2,1)S(1)}, bf16[1,17,16,128]{3,2,1,0:T(8,128)(2,1)S(1)}, u32[]{:S(2)}, u32[]{:S(2)}) collective-permute-start(bf16[1,17,16,128]{3,2,1,0:T(8,128)(2,1)S(1)} %get-tuple-element.64), channel_id=1, source_target_pairs={{0,24},{4,28},{8,16},{12,20},{16,8},{20,12},{24,0},{28,4},{1,25},{... | collective-permute-start | bytes 208904 | tf_op jit(solution)/shard_map/ppermute | solution.py:29
  43.3 6.2 %collective-permute-start.6 = (bf16[1,17,16,128]{3,2,1,0:T(8,128)(2,1)S(1)}, bf16[1,17,16,128]{3,2,1,0:T(8,128)(2,1)S(1)}, u32[]{:S(2)}, u32[]{:S(2)}) collective-permute-start(bf16[1,17,16,128]{3,2,1,0:T(8,128)(2,1)S(1)} %get-tuple-element.65), channel_id=1, source_target_pairs={{0,16},{4,20},{8,24},{12,28},{16,0},{20,4},{24,8},{28,12},{1,17},{... | collective-permute-start | bytes 208904 | tf_op jit(solution)/shard_map/ppermute | solution.py:29
  43.3 6.1 %collective-permute-start.5 = (bf16[1,17,16,128]{3,2,1,0:T(8,128)(2,1)S(1)}, bf16[1,17,16,128]{3,2,1,0:T(8,128)(2,1)S(1)}, u32[]{:S(2)}, u32[]{:S(2)}) collective-permute-start(bf16[1,17,16,128]{3,2,1,0:T(8,128)(2,1)S(1)} %get-tuple-element.66), channel_id=1, source_target_pairs={{0,8},{4,12},{8,0},{12,4},{16,24},{20,28},{24,16},{28,20},{1,9},{5... | collective-permute-start | bytes 208904 | tf_op jit(solution)/shard_map/ppermute | solution.py:29
  49.4 35.3 %slice-start.1 = ((s8[10485760]{0:T(1024)(128)(4,1)}), s8[4194304]{0:T(1024)(128)(4,1)S(1)}, s32[]{:S(2)}) async-start(s8[10485760]{0:T(1024)(128)(4,1)} %bitcast.50), calls=%async_computation.1 | async-start | bytes 8388608
  49.4 35.3 %slice-start.2 = ((s8[10485760]{0:T(1024)(128)(4,1)}), s8[4194304]{0:T(1024)(128)(4,1)S(1)}, s32[]{:S(2)}) async-start(s8[10485760]{0:T(1024)(128)(4,1)} %bitcast.50), calls=%async_computation.2 | async-start | bytes 8388608
  54.4 2.2 %collective-permute-start.8 = (bf16[32,1280]{1,0:T(8,128)(2,1)S(1)}, bf16[32,1280]{1,0:T(8,128)(2,1)S(1)}, u32[]{:S(2)}, u32[]{:S(2)}) collective-permute-start(bf16[32,1280]{1,0:T(8,128)(2,1)S(1)} %get-tuple-element.68), channel_id=1, source_target_pairs={{0,1},{1,0},{2,3},{3,2},{4,5},{5,4},{6,7},{7,6},{8,9},{9,8},{10,11... | collective-permute-start | bytes 245768 | tf_op jit(solution)/shard_map/ppermute | solution.py:29
  54.4 4.4 %collective-permute-start.10 = (bf16[32,1280]{1,0:T(8,128)(2,1)S(1)}, bf16[32,1280]{1,0:T(8,128)(2,1)S(1)}, u32[]{:S(2)}, u32[]{:S(2)}) collective-permute-start(bf16[32,1280]{1,0:T(8,128)(2,1)S(1)} %get-tuple-element.69), channel_id=1, source_target_pairs={{0,3},{1,2},{2,1},{3,0},{4,7},{5,6},{6,5},{7,4},{8,11},{9,10},{10,... | collective-permute-start | bytes 245768 | tf_op jit(solution)/shard_map/ppermute | solution.py:29
  56.1 4.9 %collective-permute-start.9 = (bf16[32,1280]{1,0:T(8,128)(2,1)S(1)}, bf16[32,1280]{1,0:T(8,128)(2,1)S(1)}, u32[]{:S(2)}, u32[]{:S(2)}) collective-permute-start(bf16[32,1280]{1,0:T(8,128)(2,1)S(1)} %get-tuple-element.70), channel_id=1, source_target_pairs={{0,2},{1,3},{2,0},{3,1},{4,6},{5,7},{6,4},{7,5},{8,10},{9,11},{10,... | collective-permute-start | bytes 245768 | tf_op jit(solution)/shard_map/ppermute | solution.py:29
  61.0 23.7 %copy-start.6 = (f32[5120]{0:T(1024)S(1)}, f32[5120]{0:T(1024)}, u32[]{:S(2)}) copy-start(f32[5120]{0:T(1024)} %param.22) | copy-start | bytes 61444
  61.1 4.5 %collective-permute-start.11 = (bf16[32,1280]{1,0:T(8,128)(2,1)S(1)}, bf16[32,1280]{1,0:T(8,128)(2,1)S(1)}, u32[]{:S(2)}, u32[]{:S(2)}) collective-permute-start(bf16[32,1280]{1,0:T(8,128)(2,1)S(1)} %add_convert_fusion.7), channel_id=1, source_target_pairs={{0,8},{4,12},{8,0},{12,4},{16,24},{20,28},{24,16},{28,20},{1,9},{5... | collective-permute-start | bytes 245768 | tf_op jit(solution)/shard_map/ppermute | solution.py:29
  62.2 6.6 %collective-permute-start.15 = (bf16[32,1280]{1,0:T(8,128)(2,1)S(1)}, bf16[32,1280]{1,0:T(8,128)(2,1)S(1)}, u32[]{:S(2)}, u32[]{:S(2)}) collective-permute-start(bf16[32,1280]{1,0:T(8,128)(2,1)S(1)} %add_convert_fusion.7), channel_id=1, source_target_pairs={{0,24},{4,28},{8,16},{12,20},{16,8},{20,12},{24,0},{28,4},{1,25},{... | collective-permute-start | bytes 245768 | tf_op jit(solution)/shard_map/ppermute | solution.py:29
  63.7 8.5 %collective-permute-start.14 = (bf16[32,1280]{1,0:T(8,128)(2,1)S(1)}, bf16[32,1280]{1,0:T(8,128)(2,1)S(1)}, u32[]{:S(2)}, u32[]{:S(2)}) collective-permute-start(bf16[32,1280]{1,0:T(8,128)(2,1)S(1)} %add_convert_fusion.7), channel_id=1, source_target_pairs={{0,16},{4,20},{8,24},{12,28},{16,0},{20,4},{24,8},{28,12},{1,17},{... | collective-permute-start | bytes 245768 | tf_op jit(solution)/shard_map/ppermute | solution.py:29
  65.6 6.5 %collective-permute-start.13 = (bf16[64,640]{1,0:T(8,128)(2,1)S(1)}, bf16[64,640]{1,0:T(8,128)(2,1)S(1)}, u32[]{:S(2)}, u32[]{:S(2)}) collective-permute-start(bf16[64,640]{1,0:T(8,128)(2,1)S(1)} %get-tuple-element.41), channel_id=1, source_target_pairs={{0,2},{1,3},{2,0},{3,1},{4,6},{5,7},{6,4},{7,5},{8,10},{9,11},{10,... | collective-permute-start | bytes 245768 | tf_op jit(solution)/shard_map/ppermute | solution.py:29
  67.2 5.0 %collective-permute-start.12 = (bf16[64,640]{1,0:T(8,128)(2,1)S(1)}, bf16[64,640]{1,0:T(8,128)(2,1)S(1)}, u32[]{:S(2)}, u32[]{:S(2)}) collective-permute-start(bf16[64,640]{1,0:T(8,128)(2,1)S(1)} %get-tuple-element.39), channel_id=1, source_target_pairs={{0,4},{4,0},{8,12},{12,8},{16,20},{20,16},{24,28},{28,24},{1,5},{5... | collective-permute-start | bytes 245768 | tf_op jit(solution)/shard_map/ppermute | solution.py:29
  72.2 6.9 %collective-permute-start.20 = (bf16[64,640]{1,0:T(8,128)(2,1)S(1)}, bf16[64,640]{1,0:T(8,128)(2,1)S(1)}, u32[]{:S(2)}, u32[]{:S(2)}) collective-permute-start(bf16[64,640]{1,0:T(8,128)(2,1)S(1)} %get-tuple-element.74), channel_id=1, source_target_pairs={{0,2},{1,3},{2,0},{3,1},{4,6},{5,7},{6,4},{7,5},{8,10},{9,11},{10,... | collective-permute-start | bytes 245768 | tf_op jit(solution)/shard_map/ppermute | solution.py:29
  73.8 4.8 %collective-permute-start.18 = (bf16[64,640]{1,0:T(8,128)(2,1)S(1)}, bf16[64,640]{1,0:T(8,128)(2,1)S(1)}, u32[]{:S(2)}, u32[]{:S(2)}) collective-permute-start(bf16[64,640]{1,0:T(8,128)(2,1)S(1)} %get-tuple-element.75), channel_id=1, source_target_pairs={{0,4},{4,0},{8,12},{12,8},{16,20},{20,16},{24,28},{28,24},{1,5},{5... | collective-permute-start | bytes 245768 | tf_op jit(solution)/shard_map/ppermute | solution.py:29
  74.3 7.4 %collective-permute-start.17 = (bf16[2,64,640]{2,1,0:T(8,128)(2,1)S(1)}, bf16[2,64,640]{2,1,0:T(8,128)(2,1)S(1)}, u32[]{:S(2)}, u32[]{:S(2)}) collective-permute-start(bf16[2,64,640]{2,1,0:T(8,128)(2,1)S(1)} %pad_maximum_fusion.refs_2_), channel_id=1, source_target_pairs={{0,4},{4,0},{8,12},{12,8},{16,20},{20,16},{24,28},{28,24},{1,5},{5... | collective-permute-start | bytes 491528 | tf_op jit(solution)/shard_map/ppermute | solution.py:29
  75.9 6.3 %collective-permute-start.16 = (bf16[128,640]{1,0:T(8,128)(2,1)S(1)}, bf16[128,640]{1,0:T(8,128)(2,1)S(1)}, u32[]{:S(2)}, u32[]{:S(2)}) collective-permute-start(bf16[128,640]{1,0:T(8,128)(2,1)S(1)} %constant_dynamic-update-slice_fusion.9.refs_0_), channel_id=1, source_target_pairs={{0,2},{1,3},{2,0},{3,1},{4,6},{5,7},{6,4},{7,5},{8,10},{9,11},{10,... | collective-permute-start | bytes 491528 | tf_op jit(solution)/shard_map/ppermute | solution.py:29
  78.6 5.4 %collective-permute-start.19 = (bf16[128,640]{1,0:T(8,128)(2,1)S(1)}, bf16[128,640]{1,0:T(8,128)(2,1)S(1)}, u32[]{:S(2)}, u32[]{:S(2)}) collective-permute-start(bf16[128,640]{1,0:T(8,128)(2,1)S(1)} %pad_maximum_fusion.1.refs_4_), channel_id=1, source_target_pairs={{0,2},{1,3},{2,0},{3,1},{4,6},{5,7},{6,4},{7,5},{8,10},{9,11},{10,... | collective-permute-start | bytes 491528 | tf_op jit(solution)/shard_map/ppermute | solution.py:29
  79.2 5.4 %collective-permute-start.21 = (bf16[2,64,640]{2,1,0:T(8,128)(2,1)S(1)}, bf16[2,64,640]{2,1,0:T(8,128)(2,1)S(1)}, u32[]{:S(2)}, u32[]{:S(2)}) collective-permute-start(bf16[2,64,640]{2,1,0:T(8,128)(2,1)S(1)} %pad_maximum_fusion.2.refs_6_), channel_id=1, source_target_pairs={{0,4},{4,0},{8,12},{12,8},{16,20},{20,16},{24,28},{28,24},{1,5},{5... | collective-permute-start | bytes 491528 | tf_op jit(solution)/shard_map/ppermute | solution.py:29
  84.7 4.7 %copy-start = (bf16[2,256,1280]{2,1,0:T(8,128)(2,1)}, bf16[2,256,1280]{2,1,0:T(8,128)(2,1)S(1)}, u32[]{:S(2)}) copy-start(bf16[2,256,1280]{2,1,0:T(8,128)(2,1)S(1)} %join_groups.1.rows_ref) | copy-start | bytes 3932164
  84.7 4.7 %collective-permute-start.22 = (bf16[2,256,1280]{2,1,0:T(8,128)(2,1)S(1)}, bf16[2,256,1280]{2,1,0:T(8,128)(2,1)S(1)}, u32[]{:S(2)}, u32[]{:S(2)}) collective-permute-start(bf16[2,256,1280]{2,1,0:T(8,128)(2,1)S(1)} %join_groups.1.rows_ref), channel_id=1, source_target_pairs={{0,1},{1,0},{2,3},{3,2},{4,5},{5,4},{6,7},{7,6},{8,9},{9,8},{10,11... | collective-permute-start | bytes 3932168 | tf_op jit(solution)/shard_map/ppermute | solution.py:29
  89.3 7.6 %copy-start.4 = (bf16[2,256,1280]{2,1,0:T(8,128)(2,1)}, bf16[2,256,1280]{2,1,0:T(8,128)(2,1)S(1)}, u32[]{:S(2)}) copy-start(bf16[2,256,1280]{2,1,0:T(8,128)(2,1)S(1)} %collective-permute-done.22.rows_ref) | copy-start | bytes 3932164
  97.0 5.0 %collective-permute-start.23 = (bf16[2,256,1280]{2,1,0:T(8,128)(2,1)S(1)}, bf16[2,256,1280]{2,1,0:T(8,128)(2,1)S(1)}, u32[]{:S(2)}, u32[]{:S(2)}) collective-permute-start(bf16[2,256,1280]{2,1,0:T(8,128)(2,1)S(1)} %get-tuple-element.49), channel_id=1, source_target_pairs={{0,1},{1,0},{2,3},{3,2},{4,5},{5,4},{6,7},{7,6},{8,9},{9,8},{10,11... | collective-permute-start | bytes 3932168 | tf_op jit(solution)/shard_map/ppermute | solution.py:29
  102.4 7.0 %collective-permute-start.24 = (bf16[128,640]{1,0:T(8,128)(2,1)S(1)}, bf16[128,640]{1,0:T(8,128)(2,1)S(1)}, u32[]{:S(2)}, u32[]{:S(2)}) collective-permute-start(bf16[128,640]{1,0:T(8,128)(2,1)S(1)} %get-tuple-element.51), channel_id=1, source_target_pairs={{0,2},{1,3},{2,0},{3,1},{4,6},{5,7},{6,4},{7,5},{8,10},{9,11},{10,... | collective-permute-start | bytes 491528 | tf_op jit(solution)/shard_map/ppermute | solution.py:29
  104.9 7.1 %collective-permute-start.26 = (bf16[2,64,640]{2,1,0:T(8,128)(2,1)S(1)}, bf16[2,64,640]{2,1,0:T(8,128)(2,1)S(1)}, u32[]{:S(2)}, u32[]{:S(2)}) collective-permute-start(bf16[2,64,640]{2,1,0:T(8,128)(2,1)S(1)} %get-tuple-element.53), channel_id=1, source_target_pairs={{0,4},{4,0},{8,12},{12,8},{16,20},{20,16},{24,28},{28,24},{1,5},{5... | collective-permute-start | bytes 491528 | tf_op jit(solution)/shard_map/ppermute | solution.py:29
  105.8 6.7 %collective-permute-start.29 = (bf16[128,640]{1,0:T(8,128)(2,1)S(1)}, bf16[128,640]{1,0:T(8,128)(2,1)S(1)}, u32[]{:S(2)}, u32[]{:S(2)}) collective-permute-start(bf16[128,640]{1,0:T(8,128)(2,1)S(1)} %get-tuple-element.55), channel_id=1, source_target_pairs={{0,2},{1,3},{2,0},{3,1},{4,6},{5,7},{6,4},{7,5},{8,10},{9,11},{10,... | collective-permute-start | bytes 491528 | tf_op jit(solution)/shard_map/ppermute | solution.py:29
  106.3 9.2 %collective-permute-start.31 = (bf16[2,64,640]{2,1,0:T(8,128)(2,1)S(1)}, bf16[2,64,640]{2,1,0:T(8,128)(2,1)S(1)}, u32[]{:S(2)}, u32[]{:S(2)}) collective-permute-start(bf16[2,64,640]{2,1,0:T(8,128)(2,1)S(1)} %get-tuple-element.57), channel_id=1, source_target_pairs={{0,4},{4,0},{8,12},{12,8},{16,20},{20,16},{24,28},{28,24},{1,5},{5... | collective-permute-start | bytes 491528 | tf_op jit(solution)/shard_map/ppermute | solution.py:29
  109.4 7.6 %collective-permute-start.25 = (bf16[64,640]{1,0:T(8,128)(2,1)S(1)}, bf16[64,640]{1,0:T(8,128)(2,1)S(1)}, u32[]{:S(2)}, u32[]{:S(2)}) collective-permute-start(bf16[64,640]{1,0:T(8,128)(2,1)S(1)} %slice.139), channel_id=1, source_target_pairs={{0,4},{4,0},{8,12},{12,8},{16,20},{20,16},{24,28},{28,24},{1,5},{5... | collective-permute-start | bytes 245768 | tf_op jit(solution)/shard_map/ppermute | solution.py:29
  112.0 5.0 %collective-permute-start.27 = (bf16[64,640]{1,0:T(8,128)(2,1)S(1)}, bf16[64,640]{1,0:T(8,128)(2,1)S(1)}, u32[]{:S(2)}, u32[]{:S(2)}) collective-permute-start(bf16[64,640]{1,0:T(8,128)(2,1)S(1)} %slice_bitcast_fusion.2), channel_id=1, source_target_pairs={{0,2},{1,3},{2,0},{3,1},{4,6},{5,7},{6,4},{7,5},{8,10},{9,11},{10,... | collective-permute-start | bytes 245768 | tf_op jit(solution)/shard_map/ppermute | solution.py:29
  112.7 5.4 %collective-permute-start.30 = (bf16[64,640]{1,0:T(8,128)(2,1)S(1)}, bf16[64,640]{1,0:T(8,128)(2,1)S(1)}, u32[]{:S(2)}, u32[]{:S(2)}) collective-permute-start(bf16[64,640]{1,0:T(8,128)(2,1)S(1)} %slice.145), channel_id=1, source_target_pairs={{0,4},{4,0},{8,12},{12,8},{16,20},{20,16},{24,28},{28,24},{1,5},{5... | collective-permute-start | bytes 245768 | tf_op jit(solution)/shard_map/ppermute | solution.py:29
  115.5 4.5 %collective-permute-start.32 = (bf16[64,640]{1,0:T(8,128)(2,1)S(1)}, bf16[64,640]{1,0:T(8,128)(2,1)S(1)}, u32[]{:S(2)}, u32[]{:S(2)}) collective-permute-start(bf16[64,640]{1,0:T(8,128)(2,1)S(1)} %slice_bitcast_fusion), channel_id=1, source_target_pairs={{0,2},{1,3},{2,0},{3,1},{4,6},{5,7},{6,4},{7,5},{8,10},{9,11},{10,... | collective-permute-start | bytes 245768 | tf_op jit(solution)/shard_map/ppermute | solution.py:29
  117.1 6.9 %collective-permute-start.28 = (bf16[32,1280]{1,0:T(8,128)(2,1)S(1)}, bf16[32,1280]{1,0:T(8,128)(2,1)S(1)}, u32[]{:S(2)}, u32[]{:S(2)}) collective-permute-start(bf16[32,1280]{1,0:T(8,128)(2,1)S(1)} %pad_maximum_fusion.4), channel_id=1, source_target_pairs={{0,8},{4,12},{8,0},{12,4},{16,24},{20,28},{24,16},{28,20},{1,9},{5... | collective-permute-start | bytes 245768 | tf_op jit(solution)/shard_map/ppermute | solution.py:29
  120.1 7.2 %collective-permute-start.33 = (bf16[32,1280]{1,0:T(8,128)(2,1)S(1)}, bf16[32,1280]{1,0:T(8,128)(2,1)S(1)}, u32[]{:S(2)}, u32[]{:S(2)}) collective-permute-start(bf16[32,1280]{1,0:T(8,128)(2,1)S(1)} %get-tuple-element.71), channel_id=1, source_target_pairs={{0,16},{4,20},{8,24},{12,28},{16,0},{20,4},{24,8},{28,12},{1,17},{... | collective-permute-start | bytes 245768 | tf_op jit(solution)/shard_map/ppermute | solution.py:29
  120.2 7.1 %collective-permute-start.34 = (bf16[32,1280]{1,0:T(8,128)(2,1)S(1)}, bf16[32,1280]{1,0:T(8,128)(2,1)S(1)}, u32[]{:S(2)}, u32[]{:S(2)}) collective-permute-start(bf16[32,1280]{1,0:T(8,128)(2,1)S(1)} %get-tuple-element.72), channel_id=1, source_target_pairs={{0,24},{4,28},{8,16},{12,20},{16,8},{20,12},{24,0},{28,4},{1,25},{... | collective-permute-start | bytes 245768 | tf_op jit(solution)/shard_map/ppermute | solution.py:29
  127.4 2.9 %collective-permute-start.35 = (bf16[32,1280]{1,0:T(8,128)(2,1)S(1)}, bf16[32,1280]{1,0:T(8,128)(2,1)S(1)}, u32[]{:S(2)}, u32[]{:S(2)}) collective-permute-start(bf16[32,1280]{1,0:T(8,128)(2,1)S(1)} %get-tuple-element.61), channel_id=1, source_target_pairs={{0,1},{1,0},{2,3},{3,2},{4,5},{5,4},{6,7},{7,6},{8,9},{9,8},{10,11... | collective-permute-start | bytes 245768 | tf_op jit(solution)/shard_map/ppermute | solution.py:29
  128.3 6.3 %copy-start.10 = (bf16[32,5120]{1,0:T(8,128)(2,1)}, bf16[32,5120]{1,0:T(8,128)(2,1)S(1)}, u32[]{:S(2)}) copy-start(bf16[32,5120]{1,0:T(8,128)(2,1)S(1)} %fusion.5) | copy-start | bytes 983044
  128.3 5.3 %collective-permute-start.36 = (bf16[32,1280]{1,0:T(8,128)(2,1)S(1)}, bf16[32,1280]{1,0:T(8,128)(2,1)S(1)}, u32[]{:S(2)}, u32[]{:S(2)}) collective-permute-start(bf16[32,1280]{1,0:T(8,128)(2,1)S(1)} %get-tuple-element.61), channel_id=1, source_target_pairs={{0,2},{1,3},{2,0},{3,1},{4,6},{5,7},{6,4},{7,5},{8,10},{9,11},{10,... | collective-permute-start | bytes 245768 | tf_op jit(solution)/shard_map/ppermute | solution.py:29
  129.3 5.3 %collective-permute-start.37 = (bf16[32,1280]{1,0:T(8,128)(2,1)S(1)}, bf16[32,1280]{1,0:T(8,128)(2,1)S(1)}, u32[]{:S(2)}, u32[]{:S(2)}) collective-permute-start(bf16[32,1280]{1,0:T(8,128)(2,1)S(1)} %get-tuple-element.61), channel_id=1, source_target_pairs={{0,3},{1,2},{2,1},{3,0},{4,7},{5,6},{6,5},{7,4},{8,11},{9,10},{10,... | collective-permute-start | bytes 245768 | tf_op jit(solution)/shard_map/ppermute | solution.py:29
  134.6 0.7 copy-start.9

commit v4 on v3

--- a/solution.py
+++ b/solution.py
@@ -27,6 +27,17 @@
 def swap(value, axis, mask):
     size = lax.axis_size(axis)
     return lax.ppermute(value, axis, [(i, i ^ mask) for i in range(size)])
+
+
+def cross(value, x_first, k):
+    seq, tp = lax.axis_size("seq"), lax.axis_size("tp")
+    pairs = []
+    for s in range(seq):
+        for t in range(tp):
+            along_x = (t % CORES == 0) == x_first
+            partner = (s ^ k) * tp + t if along_x else s * tp + (t ^ (CORES * k))
+            pairs.append((s * tp + t, partner))
+    return lax.ppermute(value, ("seq", "tp"), pairs)
 
 
 def dot_t(a, b):
@@ -64,42 +75,31 @@
     return top, total
 
 
-def pages_kernel(
-    block_pages, slot_ref, valid_ref, query_ref, fresh_key_ref, fresh_value_ref, key_buf, value_buf,
-    out_ref, top_ref, total_ref, acc_ref,
-):
+def softmax_parts(scores, live, scale):
+    scores = [jnp.where(keep, score * scale, masked_low) for score, keep in zip(scores, live)]
+    tops = [jnp.max(score, axis=1, keepdims=True) for score in scores]
+    weights = [jnp.where(keep, jnp.exp(score - top), 0.0) for score, top, keep in zip(scores, tops, live)]
+    totals = [jnp.sum(weight, axis=1, keepdims=True) for weight in weights]
+    return tops, totals, [weight.astype(bf16) for weight in weights]
+
+
+def pages_kernel(block_pages, piece_count, near_count, slot_ref, valid_ref, *refs):
+    pieces = refs[:piece_count]
+    key_buf, value_buf, _ = refs[piece_count : piece_count + 3]
+    outs = refs[piece_count + 3 : -4]
+    query_ref, top_ref, total_ref, acc_ref = refs[-4:]
     page_count, kv_local, page_size, head_dim = key_buf.shape
     blocks = page_count // block_pages
-    groups, tiles = out_ref.shape[:2]
-    pairs = tiles - 1
+    pairs = outs[0].shape[1] - 1
+    deep = pieces[0].shape[0] // pairs
     rows = query_ref.shape[1]
-    per_step = rows // STEPS
     scale = head_dim ** (-0.5)
 
     top_ref[...] = jnp.full(top_ref.shape, masked_low, f32)
     total_ref[...] = jnp.zeros(total_ref.shape, f32)
     acc_ref[...] = jnp.zeros(acc_ref.shape, f32)
-
-    def weigh(scores, live):
-        scores = [jnp.where(keep, score * scale, masked_low) for score, keep in zip(scores, live)]
-        tops = [jnp.max(score, axis=1, keepdims=True) for score in scores]
-        weights = [
-            jnp.where(keep, jnp.exp(score - top), 0.0) for score, top, keep in zip(scores, tops, live)
-        ]
-        totals = [jnp.sum(weight, axis=1, keepdims=True) for weight in weights]
-        return tops, totals, [weight.astype(bf16) for weight in weights]
-
-    fresh = fresh_key_ref.shape[1]
-    row_step = lax.broadcasted_iota(jnp.int32, (rows, fresh), 0) // per_step
-    column = lax.broadcasted_iota(jnp.int32, (rows, fresh), 1)
-    scores = [dot_t(query_ref[i], fresh_key_ref[i]) for i in range(pairs)]
-    tops, totals, weights = weigh(scores, [column <= row_step] * pairs)
-    accs = [jnp.dot(weights[i], fresh_value_ref[i], preferred_element_type=f32) for i in range(pairs)]
-    for i in range(pairs):
-        top_ref[i] = jnp.broadcast_to(tops[i], (rows, head_dim))
-        total_ref[i] = jnp.broadcast_to(totals[i], (rows, head_dim))
-        acc_ref[i] = accs[i]
-
+    for i, piece in enumerate(pieces):
+        query_ref[i * deep * pairs : (i + 1) * deep * pairs] = piece[...]
     lane = lax.broadcasted_iota(jnp.int32, (rows, page_size), 1)
 
     @pl.loop(0, blocks)
@@ -109,7 +109,7 @@
         at = [slot_ref[page] * kv_local + head for page, head in places]
         live = [lane < valid_ref[page] for page, _ in places]
         scores = [dot_t(query_ref[i], key_buf[page, head]) for i, (page, head) in zip(at, places)]
-        tops, totals, weights = weigh(scores, live)
+        tops, totals, weights = softmax_parts(scores, live, scale)
         accs = [
             jnp.dot(weight, value_buf[page, head], preferred_element_type=f32)
             for weight, (page, head) in zip(weights, places)
@@ -124,33 +124,40 @@
             acc_ref[i] = acc_ref[i] * old_factor + acc * factor
 
     out_lane = lax.broadcasted_iota(jnp.int32, (rows, head_dim), 1)
-
-    @pl.loop(0, groups)
-    def _(group):
-        tops = jnp.zeros((rows, head_dim), f32)
-        totals = jnp.zeros((rows, head_dim), f32)
-        for i in range(pairs):
-            at = group * pairs + i
-            out_ref[group, i] = acc_ref[at].astype(bf16)
-            tops = jnp.where(out_lane == i, top_ref[at], tops)
-            totals = jnp.where(out_lane == i, total_ref[at], totals)
-        out_ref[group, pairs] = encode_stats(tops, totals, pairs)
-
-
-def attend_pages(queries, fresh_keys, fresh_values, key_cache, value_cache, slots, valid, groups):
-    pairs = fresh_keys.shape[0]
-    rows, head_dim = queries.shape[1:]
+    for number, out_ref in enumerate(outs):
+        start = number % piece_count * deep + (near_count if number >= piece_count else 0)
+
+        @pl.loop(0, out_ref.shape[0])
+        def _(group):
+            tops = jnp.zeros((rows, head_dim), f32)
+            totals = jnp.zeros((rows, head_dim), f32)
+            for i in range(pairs):
+                at = (start + group) * pairs + i
+                out_ref[group, i] = acc_ref[at].astype(bf16)
+                tops = jnp.where(out_lane == i, top_ref[at], tops)
+                totals = jnp.where(out_lane == i, total_ref[at], totals)
+            out_ref[group, pairs] = encode_stats(tops, totals, pairs)
+
+
+def attend_pages(pieces, key_cache, value_cache, slots, valid, near_count, pairs, after):
+    height, rows, head_dim = pieces[0].shape
+    deep = height // pairs
     page_count, kv_local, page_size, _ = key_cache.shape
     block_pages = 6
     while page_count % block_pages:
         block_pages -= 1
-    count = queries.shape[0]
-    return pl.pallas_call(
-        functools.partial(pages_kernel, block_pages),
-        out_shape=jax.ShapeDtypeStruct((groups, pairs + 1, rows, head_dim), bf16),
-        in_specs=[smem, smem] + [vmem] * 5,
-        out_specs=vmem,
+    count = height * len(pieces)
+    outs = pl.pallas_call(
+        functools.partial(pages_kernel, block_pages, len(pieces), near_count),
+        out_shape=[
+            jax.ShapeDtypeStruct((layers, pairs + 1, rows, head_dim), bf16)
+            for layers in (near_count, deep - near_count)
+            for _ in pieces
+        ],
+        in_specs=[smem, smem] + [vmem] * (len(pieces) + 2) + [hbm],
+        out_specs=[vmem] * (2 * len(pieces)),
         scratch_shapes=[
+            pltpu.VMEM((count, rows, head_dim), bf16),
             pltpu.VMEM((count, rows, head_dim), f32),
             pltpu.VMEM((count, rows, head_dim), f32),
             pltpu.VMEM((count, rows, head_dim), f32),
@@ -162,7 +169,8 @@
             transcendentals=0,
         ),
         name="attend_pages",
-    )(slots, valid, queries, fresh_keys, fresh_values, key_cache, value_cache)
+    )(slots, valid, *pieces, key_cache, value_cache, after)
+    return outs[: len(pieces)], outs[len(pieces) :]
 
 
 def merge_tile(parts, group, pairs):
@@ -180,17 +188,15 @@
 
 
 def merge_kernel(count, *refs):
-    parts, out_ref = refs[:count], refs[count]
-    groups, tiles, rows, head_dim = parts[0].shape
+    parts, outs = refs[:count], refs[count:]
+    _, tiles, rows, head_dim = parts[0].shape
     pairs = tiles - 1
     used = lax.broadcasted_iota(jnp.int32, (rows, head_dim), 1) < pairs
-    for group in range(groups):
+    for group, out_ref in enumerate(outs):
         top, total, factors = merge_tile(parts, group, pairs)
         for i in range(pairs):
-            out_ref[group, i] = merge_pair(parts, factors, group, i).astype(bf16)
-        out_ref[group, pairs] = encode_stats(
-            jnp.where(used, top, 0.0), jnp.where(used, total, 0.0), pairs
-        )
+            out_ref[0, i] = merge_pair(parts, factors, group, i).astype(bf16)
+        out_ref[0, pairs] = encode_stats(jnp.where(used, top, 0.0), jnp.where(used, total, 0.0), pairs)
 
 
 vmem = pl.BlockSpec(memory_space=pltpu.VMEM)
@@ -199,11 +205,12 @@
 
 
 def merge_parts(parts):
+    groups, *tile = parts[0].shape
     return pl.pallas_call(
         functools.partial(merge_kernel, len(parts)),
-        out_shape=jax.ShapeDtypeStruct(parts[0].shape, bf16),
+        out_shape=[jax.ShapeDtypeStruct((1, *tile), bf16)] * groups,
         in_specs=[vmem] * len(parts),
-        out_specs=vmem,
+        out_specs=[vmem] * groups,
         compiler_params=pltpu.CompilerParams(vmem_limit_bytes=8 << 20),
         name="merge_parts",
     )(*parts)
@@ -302,7 +309,7 @@
             pltpu.VMEM((pairs * tile_rows, head_dim), f32),
             pltpu.SemaphoreType.DMA((chunks,)),
         ],
-        compiler_params=pltpu.CompilerParams(vmem_limit_bytes=58 << 20),
+        compiler_params=pltpu.CompilerParams(vmem_limit_bytes=52 << 20),
         cost_estimate=pl.CostEstimate(
             flops=2 * rows * width * columns, bytes_accessed=2 * width * columns, transcendentals=0
         ),
@@ -317,14 +324,15 @@
     )
 
 
-def fresh_kernel(
-    kv_local, normalized_ref, cosine_ref, sine_ref, key_hbm, value_hbm,
-    key_ref, value_ref, key_buf, value_buf, key_tile, value_tile, sems,
+def recent_kernel(
+    kv_local, normalized_ref, cosine_ref, sine_ref, query_ref, key_hbm, value_hbm,
+    out_ref, key_buf, value_buf, key_tile, value_tile, sems,
 ):
     rows, width = normalized_ref.shape
     head_dim = cosine_ref.shape[1]
     row_count = rows // STEPS
-    pads = key_ref.shape[1]
+    pairs, tile_rows, _ = query_ref.shape
+    pads = key_tile.shape[0] // pairs
     copies = [
         pltpu.make_async_copy(key_hbm, key_buf, sems.at[0]),
         pltpu.make_async_copy(value_hbm, value_buf, sems.at[1]),
@@ -344,20 +352,33 @@
                 tile[pl.ds(head * pads + step, row_count, stride=kv_local * pads), :] = value[
                     step * row_count : (step + 1) * row_count
                 ]
-    key_ref[...] = key_tile[...].reshape(key_ref.shape).astype(bf16)
-    value_ref[...] = value_tile[...].reshape(value_ref.shape).astype(bf16)
-
-
-def project_fresh(normalized, cosine, sine, key_projection, value_projection, kv_local, head_dim):
+    keys = key_tile[...].reshape(pairs, pads, head_dim).astype(bf16)
+    values = value_tile[...].reshape(pairs, pads, head_dim).astype(bf16)
+    row_step = lax.broadcasted_iota(jnp.int32, (tile_rows, pads), 0) // (tile_rows // STEPS)
+    column = lax.broadcasted_iota(jnp.int32, (tile_rows, pads), 1)
+    scores = [dot_t(query_ref[i], keys[i]) for i in range(pairs)]
+    tops, totals, weights = softmax_parts(scores, [column <= row_step] * pairs, head_dim ** (-0.5))
+    accs = [jnp.dot(weights[i], values[i], preferred_element_type=f32) for i in range(pairs)]
+    lane = lax.broadcasted_iota(jnp.int32, (tile_rows, head_dim), 1)
+    all_tops = jnp.zeros((tile_rows, head_dim), f32)
+    all_totals = jnp.zeros((tile_rows, head_dim), f32)
+    for i in range(pairs):
+        out_ref[0, i] = accs[i].astype(bf16)
+        all_tops = jnp.where(lane == i, tops[i], all_tops)
+        all_totals = jnp.where(lane == i, totals[i], all_totals)
+    out_ref[0, pairs] = encode_stats(all_tops, all_totals, pairs)
+
+
+def recent_part(normalized, cosine, sine, query, key_projection, value_projection, kv_local, head_dim):
     rows, width = normalized.shape
-    pairs = rows // STEPS * kv_local
+    pairs, tile_rows, _ = query.shape
     pads = 16
     columns = key_projection.shape[1]
     return pl.pallas_call(
-        functools.partial(fresh_kernel, kv_local),
-        out_shape=(jax.ShapeDtypeStruct((pairs, pads, head_dim), bf16),) * 2,
-        in_specs=[vmem, vmem, vmem, hbm, hbm],
-        out_specs=(vmem, vmem),
+        functools.partial(recent_kernel, kv_local),
+        out_shape=jax.ShapeDtypeStruct((1, pairs + 1, tile_rows, head_dim), bf16),
+        in_specs=[vmem, vmem, vmem, vmem, hbm, hbm],
+        out_specs=vmem,
         scratch_shapes=[
             pltpu.VMEM((width, columns), bf16),
             pltpu.VMEM((width, columns), bf16),
@@ -369,8 +390,8 @@
         cost_estimate=pl.CostEstimate(
             flops=4 * rows * width * columns, bytes_accessed=4 * width * columns, transcendentals=0
         ),
-        name="project_fresh",
-    )(normalized, cosine, sine, key_projection, value_projection)
+        name="recent_part",
+    )(normalized, cosine, sine, query, key_projection, value_projection)
 
 
 def out_kernel(
@@ -442,6 +463,24 @@
     )(part.reshape(1), own_input, weight, *parts)
 
 
+def places(part, count):
+    core = part % CORES
+    for first in range(count):
+        for second in range(count):
+            way = jnp.where(core == 0, second, first)
+            column = jnp.where(core == 0, first, second)
+            yield first, second, way, column
+
+
+def places(part, count):
+    core = part % CORES
+    for first in range(count):
+        for second in range(count):
+            way = jnp.where(core == 0, second, first)
+            column = jnp.where(core == 0, first, second)
+            yield first, second, way, column
+
+
 def join_kernel(ways, near_count, *refs):
     out_ref = refs[-1]
     half = refs[0].shape[1]
@@ -534,7 +573,7 @@
             pltpu.VMEM(rows.shape, bf16),
             pltpu.SemaphoreType.DMA((2, ways)),
         ],
-        compiler_params=pltpu.CompilerParams(vmem_limit_bytes=40 << 20),
+        compiler_params=pltpu.CompilerParams(vmem_limit_bytes=46 << 20),
         cost_estimate=pl.CostEstimate(
             flops=4 * rows.size * hidden,
             bytes_accessed=4 * ways * quarter * hidden + 8 * all_rows * hidden,
@@ -645,39 +684,55 @@
     )(part.reshape(1), activation, w_down)
 
 
-def sum_kernel(ways, across, own_ref, other_ref, *out_refs):
-    all_rows, columns = own_ref.shape[1:]
-    half = out_refs[0].shape[1]
-    outs = iter(out_refs)
+def sum_kernel(part_ref, own_ref, other_ref, *out_refs):
+    count, all_rows, _ = own_ref.shape
     height = all_rows // 2
-    for row in (height, 0):
-        for way in range(ways):
-            at = (way, slice(row, row + height), slice(0, half))
-            next(outs)[...] = (own_ref[at].astype(f32) + other_ref[at].astype(f32)).astype(bf16)
-        step = height // across
-        for k in range(across):
-            out = next(outs)
-            for way in range(ways):
-                at = (way, slice(row + k * step, row + (k + 1) * step), slice(half, columns))
-                out[way] = (own_ref[at].astype(f32) + other_ref[at].astype(f32)).astype(bf16)
-
-
-def sum_terms(own, other, across, half):
-    ways, all_rows, columns = own.shape
-    height = all_rows // 2
-    group = [jax.ShapeDtypeStruct((height, half), bf16)] * ways
-    group = group + [jax.ShapeDtypeStruct((ways, height // across, columns - half), bf16)] * across
+    step = height // count
+    for group, row in enumerate((height, 0)):
+        outs = out_refs[group * count : (group + 1) * count]
+        for second, first, way, column in places(part_ref[0], count):
+            at = pl.ds(pl.multiple_of(row + column * step, 16), step)
+            total = own_ref[way, at, :].astype(f32) + other_ref[way, at, :].astype(f32)
+            outs[first][second * step : (second + 1) * step, :] = total.astype(bf16)
+
+
+def sum_terms(part, own, other):
+    count, all_rows, columns = own.shape
     outs = pl.pallas_call(
-        functools.partial(sum_kernel, ways, across),
-        out_shape=group + group,
-        in_specs=[vmem, vmem],
-        out_specs=[vmem] * (2 * len(group)),
+        sum_kernel,
+        out_shape=[jax.ShapeDtypeStruct((all_rows // 2, columns), bf16)] * (2 * count),
+        in_specs=[smem, vmem, vmem],
+        out_specs=[vmem] * (2 * count),
         compiler_params=pltpu.CompilerParams(vmem_limit_bytes=8 << 20),
         cost_estimate=pl.CostEstimate(flops=own.size, bytes_accessed=6 * own.size, transcendentals=0),
         name="sum_terms",
-    )(own, other)
-    count = len(group)
-    return [(part[:ways], part[ways:]) for part in (outs[:count], outs[count:])]
+    )(part.reshape(1), own, other)
+    return outs[:count], outs[count:]
+
+
+def assemble_kernel(part_ref, *refs):
+    out_ref = refs[-1]
+    height = out_ref.shape[0]
+    if len(refs[0].shape) == 3:
+        pieces = [ref.at[way] for way in range(refs[0].shape[0]) for ref in refs[:-1]]
+    else:
+        pieces = refs[:-1]
+    quarter = pieces[0].shape[1]
+    for slot, piece in enumerate(pieces):
+        at = pl.multiple_of((part_ref[0] ^ slot) * quarter, quarter)
+        out_ref[:, pl.ds(at, quarter)] = piece[:height, :]
+
+
+def assemble(part, height, pieces):
+    shares = sum(piece.shape[0] if piece.ndim == 3 else 1 for piece in pieces)
+    return pl.pallas_call(
+        assemble_kernel,
+        out_shape=jax.ShapeDtypeStruct((height, shares * pieces[0].shape[-1]), bf16),
+        in_specs=[smem] + [vmem] * len(pieces),
+        out_specs=vmem,
+        compiler_params=pltpu.CompilerParams(vmem_limit_bytes=8 << 20),
+        name="assemble",
+    )(part.reshape(1), *pieces)
 
 
 def local(
@@ -716,34 +771,31 @@
     page_length = jnp.sum(jnp.where(is_request, cache_lengths[None, :], 0), axis=1)
     valid = jnp.where(page_live, jnp.clip(page_length - page_number * page_size, 0, page_size), 0)
     mask = (page_row // row_count) ^ me
-    slots = ((mask % across) * deep + mask // across) * row_count + page_row % row_count
+    count = deep // 2
+    slots = mask % across * deep + mask // across
+    slots = slots * row_count + page_row % row_count
 
     query, normalized, cosine, sine = project_queries(
         me, request_slot, cache_lengths, token_inputs, attn_gain, w_query, kv_local, head_dim
     )
-    shared = [query] + [swap(query, "seq", across * k) for k in range(1, deep)]
-    shared = jnp.concatenate(shared, axis=0)
+    near = [query] + [swap(query, "seq", across * k) for k in range(1, count)]
+    far = [swap(query, "seq", across * k) for k in range(count, deep)]
+    shared = jnp.concatenate(near + far, axis=0)
     queries = [shared] + [swap(shared, "seq", k) for k in range(1, across)]
-    queries = jnp.concatenate(queries, axis=0)
-
     normalized, shared = lax.optimization_barrier((normalized, shared))
-    fresh_keys, fresh_values = project_fresh(
-        normalized, cosine, sine, key_projection, value_projection, kv_local, head_dim
+    recent = recent_part(
+        normalized, cosine, sine, query, key_projection, value_projection, kv_local, head_dim
     )
-
-    packed = attend_pages(
-        queries,
-        fresh_keys,
-        fresh_values,
-        key_cache,
-        paged_value_cache,
-        slots,
-        valid,
-        seq,
-    )
-    sides = [packed[:deep]] + [swap(packed[k * deep : (k + 1) * deep], "seq", k) for k in range(1, across)]
-    merged = merge_parts(sides)
-    layers = [merged[:1]] + [swap(merged[k : k + 1], "seq", across * k) for k in range(1, deep)]
+    near_parts, far_parts = attend_pages(queries, key_cache, paged_value_cache, slots, valid, count, pairs, recent)
+
+    def merge_x(parts):
+        return merge_parts([parts[0]] + [swap(parts[k], "seq", k) for k in range(1, across)])
+
+    far_parts = merge_x(far_parts)
+    layers = [swap(far_parts[k], "seq", across * (count + k)) for k in range(deep - count)]
+    near_parts = merge_x(near_parts)
+    layers = layers + [near_parts[0]] + [swap(near_parts[k], "seq", across * k) for k in range(1, count)]
+    layers.append(recent)
     own_input = lax.dynamic_slice_in_dim(token_inputs.reshape(rows, width), part * quarter, quarter, 1)
     own_term, terms = project_out(part, layers, own_input, w_output, tp, kv_local)
     total = own_term
@@ -752,8 +804,6 @@
     own_attended = total.astype(bf16)
 
     half = (quarter + 255) // 256 * 128
-    count = deep // 2
-
     def along_x(value):
         return [value] + [swap(value, "seq", k) for k in range(1, across)]
 
@@ -777,20 +827,13 @@
     other = swap(both, "tp", 1)
     all_rows = both.shape[1]
 
-    def assemble(pieces, height):
-        whole = jnp.zeros((height, width), bf16)
-        for slot, piece in enumerate(pieces):
-            whole = lax.dynamic_update_slice_in_dim(whole, piece, (part ^ slot) * quarter, 1)
-        return whole
-
     gains = mlp_gain.reshape(tp, 1, quarter)
     sums = gate_up_half(part, 0, both, gains, w_gate, w_up)
     activation, other_terms = gate_up_rest(part, other, gains, w_gate, w_up, w_down, sums, width)
     received = swap(other_terms, "tp", 1)
     own_terms = down_half(part, activation, w_down, ways)
-    far, near = sum_terms(own_terms, received, across, half)
-    own_pieces = [piece[k, :rows] for k in range(ways) for piece in (both, other)]
-    attended = assemble(own_pieces, rows).reshape(steps, row_count, width)
+    far, near = sum_terms(part, own_terms, received)
+    attended = assemble(part, rows, [both, other]).reshape(steps, row_count, width)
 
     def add(first, others):
         value = first.astype(f32)
@@ -798,22 +841,20 @@
             value = value + one.astype(f32)
         return value
 
-    def collect_group(first, second):
-        first = add(first[0], [swap(first[k], "tp", CORES * k) for k in range(1, ways)]).astype(bf16)
-        second = add(second[0], [swap(second[k], "seq", k) for k in range(1, across)]).astype(bf16)
-        first = first.reshape(across, -1, half)
-        first = add(first[0], [swap(first[k], "seq", k) for k in range(1, across)]).astype(bf16)
-        second = add(second[0], [swap(second[k], "tp", CORES * k) for k in range(1, ways)]).astype(bf16)
-        return jnp.concatenate([first, second], axis=1).reshape(-1, rows, quarter)
-
-    far = collect_group(*far)
-    near = collect_group(*near)
+    def collect_group(pieces):
+        total = add(pieces[0], [cross(pieces[k], False, k) for k in range(1, across)]).astype(bf16)
+        total = total.reshape(across, -1, quarter)
+        total = add(total[0], [cross(total[k], True, k) for k in range(1, across)]).astype(bf16)
+        return total.reshape(-1, rows, quarter)
+
+    far = collect_group(far)
+    near = collect_group(near)
     far = [swap(far[k], "seq", across * (count + k)) for k in range(deep - count)]
     near = [near[0]] + [swap(near[k], "seq", across * k) for k in range(1, count)]
     mlp_result = add(near[0], near[1:] + far)
     own_out = (own_attended.astype(f32) + mlp_result).astype(bf16)
     pieces = [own_out] + [swap(own_out, "tp", slot) for slot in range(1, tp)]
-    layer_out = assemble(pieces, rows).reshape(steps, row_count, width)
+    layer_out = assemble(part, rows, pieces).reshape(steps, row_count, width)
     return attended, layer_out
 
 

time: 136 us -> 131 us (0.963)
  local copies, waits for them, and re-layouts: 10.8 us -> 6.67 us
  starting transfers between devices: 39.2 us -> 42.3 us
  waiting for transfers between devices: 46.7 us -> 44 us
    ppermute x38 -> x31, waiting for transfers between devices: 46.7 us -> 33.8 us  [swap(): return lax.ppermute(value, axis, [(i, i ^ mask) for i in range(size)])]
    ppermute x0 -> x4, waiting for transfers between devices: none -> 10.2 us  [cross(): return lax.ppermute(value, ('seq', 'tp'), pairs)]
    ppermute x0 -> x4, starting transfers between devices: none -> 4.36 us  [cross(): return lax.ppermute(value, ('seq', 'tp'), pairs)]
    dynamic_update_slice x7 -> x0, local copies, waits for them, and re-layouts: 3.61 us -> none  [assemble(): lax.dynamic_update_slice_in_dim(whole, piece, (part ^ slot) * quarter, 1)]
    pallas_call x1, Pallas kernels: 6.96 us -> 4.91 us  [project_queries(): pl.pallas_call(functools.partial(query_kernel, kv_local), out_shape=(jax....]
    pallas_call x4 -> x7, Pallas kernels: 9.02 us -> 10.5 us  [the longest x1 4.81 us: attend_pages(): pl.pallas_call(functools.partial(pages_kernel, block_pages, len(pieces),...]
    ppermute x38 -> x31, starting transfers between devices: 39.2 us -> 37.9 us  [swap(): return lax.ppermute(value, axis, [(i, i ^ mask) for i in range(size)])]
    unnamed x41 -> x29, local copies, waits for them, and re-layouts: 6.01 us -> 5.66 us
  transfers between devices with their start and end apart: 38 -> 35, of which waited for: 23 -> 22; matrix products, arithmetic and copies ran while one was open for 4% -> 1% of each run, Pallas kernels for 8% -> 10%
where the time goes in v4:
time: 131 us
  waiting for transfers between devices  44 us (34%)
  starting transfers between devices  42.3 us (32%)
  Pallas kernels  36.3 us (28%)
  local copies, waits for them, and re-layouts  6.67 us (5%)
    ppermute x31, starting transfers between devices, swap(): return lax.ppermute(value, axis, [(i, i ^ mask) for i in range(size)])  37.9 us
    ppermute x31, waiting for transfers between devices, swap(): return lax.ppermute(value, axis, [(i, i ^ mask) for i in range(size)])  33.8 us
    ppermute x4, waiting for transfers between devices, cross(): return lax.ppermute(value, ('seq', 'tp'), pairs)  10.2 us
    pallas_call x1, Pallas kernels, gate_up_rest(): pl.pallas_call(functools.partial(rest_kernel, width), out_shape=(jax.Shap...  7.21 us
    unnamed x29, local copies, waits for them, and re-layouts  5.66 us
    pallas_call x1, Pallas kernels, gate_up_half(): pl.pallas_call(functools.partial(gate_up_kernel, core), out_shape=(jax.Sh...  5.05 us
    pallas_call x1, Pallas kernels, project_queries(): pl.pallas_call(functools.partial(query_kernel, kv_local), out_shape=(jax....  4.91 us
    pallas_call x1, Pallas kernels, attend_pages(): pl.pallas_call(functools.partial(pages_kernel, block_pages, len(pieces),...  4.81 us
  transfers between devices with their start and end apart: 35, of which 22 were waited for; matrix products, arithmetic and copies ran while one was open for 1% of the time, Pallas kernels for 10%

profile of v4, /device:TPU:0, one launch (start us, length us, event | category | flops | bytes accessed | tf_op | source)
XLA Modules:
  0.0 130.9 jit_solution(12500877055127470177)
XLA Ops:
  0.7 1.1 copy-done.1
  1.8 1.3 copy-done.3
  3.1 0.8 copy-done.4
  3.9 0.7 copy-done.5
  4.5 4.9 %project_queries.1 = (bf16[16,16,128]{2,1,0:T(8,128)(2,1)S(1)}, bf16[32,5120]{1,0:T(8,128)(2,1)S(1)}, f32[32,128]{1,0:T(8,128)S(1)}, f32[32,128]{1,0:T(8,128)S(1)}) custom-call(s32[1]{0:T(128)} %bitcast.2.me_ref, s32[1,64]{1,0:T(1,128)S(1)} %bitcast.29, s32[1,64]{1,0:T(1,128)S(1)} %bitcast.28, bf16[4,8,5120]{2,1,0:T(8,128)(2,1)S(1)} %copy-done.1, ...), custom_call_target="tpu_custom_call" | custom-call | flops 335544320 | bytes 10485760 | tf_op jit(solution)/shard_map/project_queries/pallas_call | solution.py:296
  9.5 5.1 %collective-permute-start.2 = (bf16[16,16,128]{2,1,0:T(8,128)(2,1)S(1)}, bf16[16,16,128]{2,1,0:T(8,128)(2,1)S(1)}, u32[]{:S(2)}, u32[]{:S(2)}) collective-permute-start(bf16[16,16,128]{2,1,0:T(8,128)(2,1)S(1)} %get-tuple-element.32.query_ref), channel_id=1, source_target_pairs={{0,24},{4,28},{8,16},{12,20},{16,8},{20,12},{24,0},{28,4},{1,25},{... | collective-permute-start | bytes 196616 | tf_op jit(solution)/shard_map/ppermute | solution.py:29
  14.6 0.6 collective-permute-start
  15.2 3.6 %collective-permute-done = bf16[16,16,128]{2,1,0:T(8,128)(2,1)S(1)} collective-permute-done((bf16[16,16,128]{2,1,0:T(8,128)(2,1)S(1)}, bf16[16,16,128]{2,1,0:T(8,128)(2,1)S(1)}, u32[]{:S(2)}, u32[]{:S(2)}) %collective-permute-start) | collective-permute-done | bytes 65568 | tf_op jit(solution)/shard_map/ppermute | solution.py:29
  18.9 1.3 %collective-permute-done.1 = bf16[16,16,128]{2,1,0:T(8,128)(2,1)S(1)} collective-permute-done((bf16[16,16,128]{2,1,0:T(8,128)(2,1)S(1)}, bf16[16,16,128]{2,1,0:T(8,128)(2,1)S(1)}, u32[]{:S(2)}, u32[]{:S(2)}) %collective-permute-start.1) | collective-permute-done | bytes 65568 | tf_op jit(solution)/shard_map/ppermute | solution.py:29
  20.2 1.6 %collective-permute-start.3 = (bf16[64,16,128]{2,1,0:T(8,128)(2,1)S(1)}, bf16[64,16,128]{2,1,0:T(8,128)(2,1)S(1)}, u32[]{:S(2)}, u32[]{:S(2)}) collective-permute-start(bf16[64,16,128]{2,1,0:T(8,128)(2,1)S(1)} %constant_dynamic-update-slice_fusion.refs_0_), channel_id=1, source_target_pairs={{0,4},{4,0},{8,12},{12,8},{16,20},{20,16},{24,28},{28,24},{1,5},{5... | collective-permute-start | bytes 786440 | tf_op jit(solution)/shard_map/ppermute | solution.py:29
  22.0 1.7 %copy-done = bf16[5120,256]{1,0:T(8,128)(2,1)S(1)} copy-done((bf16[5120,256]{1,0:T(8,128)(2,1)S(1)}, bf16[5120,256]{1,0:T(8,128)(2,1)}, u32[]{:S(2)}) %copy-start) | copy-done | bytes 2621464
  23.7 3.1 %recent_part.1.refs_4_ = bf16[1,17,16,128]{3,2,1,0:T(8,128)(2,1)S(1)} custom-call(bf16[32,5120]{1,0:T(8,128)(2,1)S(1)} %get-tuple-element.34.normalized_ref, f32[32,128]{1,0:T(8,128)S(1)} %get-tuple-element.35.cosine_ref, f32[32,128]{1,0:T(8,128)S(1)} %get-tuple-element.36.sine_ref, bf16[16,16,128]{2,1,0:T(8,128)(2,1)S(1)} %get-tuple-element.32.query_ref, ...), custom_call_target="tpu_custom_call" | custom-call | flops 167772160 | bytes 5242880 | tf_op jit(solution)/shard_map/recent_part/pallas_call | solution.py:377
  26.8 1.4 %collective-permute-done.3.refs_1_ = bf16[64,16,128]{2,1,0:T(8,128)(2,1)S(1)} collective-permute-done((bf16[64,16,128]{2,1,0:T(8,128)(2,1)S(1)}, bf16[64,16,128]{2,1,0:T(8,128)(2,1)S(1)}, u32[]{:S(2)}, u32[]{:S(2)}) %collective-permute-start.3) | collective-permute-done | bytes 262176 | tf_op jit(solution)/shard_map/ppermute | solution.py:29
  28.2 4.8 %attend_pages.1 = (bf16[2,17,16,128]{3,2,1,0:T(8,128)(2,1)S(1)}, bf16[2,17,16,128]{3,2,1,0:T(8,128)(2,1)S(1)}, bf16[2,17,16,128]{3,2,1,0:T(8,128)(2,1)S(1)}, bf16[2,17,16,128]{3,2,1,0:T(8,128)(2,1)S(1)}) custom-call(s32[36]{0:T(128)S(1)} %get-tuple-element.75.slot_ref, s32[36]{0:T(128)S(1)} %get-tuple-element.74.valid_ref, ...), custom_call_target="tpu_custom_call" | custom-call | flops 150994944 | bytes 9437184 | tf_op jit(solution)/shard_map/attend_pages/pallas_call | solution.py:150
  33.0 1.7 %collective-permute-start.4 = (bf16[2,17,16,128]{3,2,1,0:T(8,128)(2,1)S(1)}, bf16[2,17,16,128]{3,2,1,0:T(8,128)(2,1)S(1)}, u32[]{:S(2)}, u32[]{:S(2)}) collective-permute-start(bf16[2,17,16,128]{3,2,1,0:T(8,128)(2,1)S(1)} %get-tuple-element.38), channel_id=1, source_target_pairs={{0,4},{4,0},{8,12},{12,8},{16,20},{20,16},{24,28},{28,24},{1,5},{5... | collective-permute-start | bytes 417800 | tf_op jit(solution)/shard_map/ppermute | solution.py:29
  34.8 0.4 collective-permute-start.7
  35.1 3.9 %collective-permute-done.4.refs_1_ = bf16[2,17,16,128]{3,2,1,0:T(8,128)(2,1)S(1)} collective-permute-done((bf16[2,17,16,128]{3,2,1,0:T(8,128)(2,1)S(1)}, bf16[2,17,16,128]{3,2,1,0:T(8,128)(2,1)S(1)}, u32[]{:S(2)}, u32[]{:S(2)}) %collective-permute-start.4) | collective-permute-done | bytes 139296 | tf_op jit(solution)/shard_map/ppermute | solution.py:29
  39.1 0.4 merge_parts.2
  39.6 1.6 %collective-permute-start.6 = (bf16[1,17,16,128]{3,2,1,0:T(8,128)(2,1)S(1)}, bf16[1,17,16,128]{3,2,1,0:T(8,128)(2,1)S(1)}, u32[]{:S(2)}, u32[]{:S(2)}) collective-permute-start(bf16[1,17,16,128]{3,2,1,0:T(8,128)(2,1)S(1)} %get-tuple-element.40), channel_id=1, source_target_pairs={{0,24},{4,28},{8,16},{12,20},{16,8},{20,12},{24,0},{28,4},{1,25},{... | collective-permute-start | bytes 208904 | tf_op jit(solution)/shard_map/ppermute | solution.py:29
  41.2 0.4 merge_parts.3
  41.7 1.9 %collective-permute-start.8 = (bf16[1,17,16,128]{3,2,1,0:T(8,128)(2,1)S(1)}, bf16[1,17,16,128]{3,2,1,0:T(8,128)(2,1)S(1)}, u32[]{:S(2)}, u32[]{:S(2)}) collective-permute-start(bf16[1,17,16,128]{3,2,1,0:T(8,128)(2,1)S(1)} %get-tuple-element.44), channel_id=1, source_target_pairs={{0,8},{4,12},{8,0},{12,4},{16,24},{20,28},{24,16},{28,20},{1,9},{5... | collective-permute-start | bytes 208904 | tf_op jit(solution)/shard_map/ppermute | solution.py:29
  43.6 0.9 constant_dynamic-slice_fusion.input_ref
  44.8 1.1 collective-permute-done.6.refs_1_
  45.9 0.7 collective-permute-done.8.refs_3_
  46.6 4.7 %project_out.1 = (f32[32,1280]{1,0:T(8,128)S(1)}, bf16[3,32,1280]{2,1,0:T(8,128)(2,1)S(1)}) custom-call(s32[1]{0:T(128)} %bitcast.part_ref, bf16[32,1280]{1,0:T(8,128)(2,1)S(1)} %constant_dynamic-slice_fusion.input_ref, bf16[1024,5120]{1,0:T(8,128)(2,1)} %weight_hbm.3, bf16[1,17,16,128]{3,2,1,0:T(8,128)(2,1)S(1)} %collective-permute-done.5.refs_0_, ...), custom_call_target="tpu_custom_call" | custom-call | flops 335544320 | bytes 10485760 | tf_op jit(solution)/shard_map/project_out/pallas_call | solution.py:444
  51.5 1.9 %collective-permute-start.11 = (bf16[32,1280]{1,0:T(8,128)(2,1)S(1)}, bf16[32,1280]{1,0:T(8,128)(2,1)S(1)}, u32[]{:S(2)}, u32[]{:S(2)}) collective-permute-start(bf16[32,1280]{1,0:T(8,128)(2,1)S(1)} %get-tuple-element.65), channel_id=1, source_target_pairs={{0,3},{1,2},{2,1},{3,0},{4,7},{5,6},{6,5},{7,4},{8,11},{9,10},{10,... | collective-permute-start | bytes 245768 | tf_op jit(solution)/shard_map/ppermute | solution.py:29
  53.6 2.5 %collective-permute-done.11 = bf16[32,1280]{1,0:T(8,128)(2,1)S(1)} collective-permute-done((bf16[32,1280]{1,0:T(8,128)(2,1)S(1)}, bf16[32,1280]{1,0:T(8,128)(2,1)S(1)}, u32[]{:S(2)}, u32[]{:S(2)}) %collective-permute-start.11) | collective-permute-done | bytes 81952 | tf_op jit(solution)/shard_map/ppermute | solution.py:29
  56.1 2.0 %collective-permute-done.10 = bf16[32,1280]{1,0:T(8,128)(2,1)S(1)} collective-permute-done((bf16[32,1280]{1,0:T(8,128)(2,1)S(1)}, bf16[32,1280]{1,0:T(8,128)(2,1)S(1)}, u32[]{:S(2)}, u32[]{:S(2)}) %collective-permute-start.10) | collective-permute-done | bytes 81952 | tf_op jit(solution)/shard_map/ppermute | solution.py:29
  58.1 1.4 %collective-permute-start.12 = (bf16[32,1280]{1,0:T(8,128)(2,1)S(1)}, bf16[32,1280]{1,0:T(8,128)(2,1)S(1)}, u32[]{:S(2)}, u32[]{:S(2)}) collective-permute-start(bf16[32,1280]{1,0:T(8,128)(2,1)S(1)} %add_convert_fusion.5), channel_id=1, source_target_pairs={{0,8},{4,12},{8,0},{12,4},{16,24},{20,28},{24,16},{28,20},{1,9},{5... | collective-permute-start | bytes 245768 | tf_op jit(solution)/shard_map/ppermute | solution.py:29
  59.5 0.9 collective-permute-start.16
  60.4 1.3 collective-permute-start.15
  61.7 1.0 collective-permute-done.12
  62.7 1.8 %collective-permute-start.14 = (bf16[64,640]{1,0:T(8,128)(2,1)S(1)}, bf16[64,640]{1,0:T(8,128)(2,1)S(1)}, u32[]{:S(2)}, u32[]{:S(2)}) collective-permute-start(bf16[64,640]{1,0:T(8,128)(2,1)S(1)} %get-tuple-element.49), channel_id=1, source_target_pairs={{0,2},{1,3},{2,0},{3,1},{4,6},{5,7},{6,4},{7,5},{8,10},{9,11},{10,... | collective-permute-start | bytes 245768 | tf_op jit(solution)/shard_map/ppermute | solution.py:29
  64.4 1.5 %collective-permute-start.13 = (bf16[64,640]{1,0:T(8,128)(2,1)S(1)}, bf16[64,640]{1,0:T(8,128)(2,1)S(1)}, u32[]{:S(2)}, u32[]{:S(2)}) collective-permute-start(bf16[64,640]{1,0:T(8,128)(2,1)S(1)} %get-tuple-element.47), channel_id=1, source_target_pairs={{0,4},{4,0},{8,12},{12,8},{16,20},{20,16},{24,28},{28,24},{1,5},{5... | collective-permute-start | bytes 245768 | tf_op jit(solution)/shard_map/ppermute | solution.py:29
  65.9 3.1 %collective-permute-done.15 = bf16[32,1280]{1,0:T(8,128)(2,1)S(1)} collective-permute-done((bf16[32,1280]{1,0:T(8,128)(2,1)S(1)}, bf16[32,1280]{1,0:T(8,128)(2,1)S(1)}, u32[]{:S(2)}, u32[]{:S(2)}) %collective-permute-start.15) | collective-permute-done | bytes 81952 | tf_op jit(solution)/shard_map/ppermute | solution.py:29
  69.1 1.8 %collective-permute-start.21 = (bf16[64,640]{1,0:T(8,128)(2,1)S(1)}, bf16[64,640]{1,0:T(8,128)(2,1)S(1)}, u32[]{:S(2)}, u32[]{:S(2)}) collective-permute-start(bf16[64,640]{1,0:T(8,128)(2,1)S(1)} %get-tuple-element.70), channel_id=1, source_target_pairs={{0,2},{1,3},{2,0},{3,1},{4,6},{5,7},{6,4},{7,5},{8,10},{9,11},{10,... | collective-permute-start | bytes 245768 | tf_op jit(solution)/shard_map/ppermute | solution.py:29
  70.9 1.5 %collective-permute-start.19 = (bf16[64,640]{1,0:T(8,128)(2,1)S(1)}, bf16[64,640]{1,0:T(8,128)(2,1)S(1)}, u32[]{:S(2)}, u32[]{:S(2)}) collective-permute-start(bf16[64,640]{1,0:T(8,128)(2,1)S(1)} %get-tuple-element.71), channel_id=1, source_target_pairs={{0,4},{4,0},{8,12},{12,8},{16,20},{20,16},{24,28},{28,24},{1,5},{5... | collective-permute-start | bytes 245768 | tf_op jit(solution)/shard_map/ppermute | solution.py:29
  72.4 0.6 collective-permute-start.18
  73.4 2.5 %collective-permute-done.19 = bf16[64,640]{1,0:T(8,128)(2,1)S(1)} collective-permute-done((bf16[64,640]{1,0:T(8,128)(2,1)S(1)}, bf16[64,640]{1,0:T(8,128)(2,1)S(1)}, u32[]{:S(2)}, u32[]{:S(2)}) %collective-permute-start.19) | collective-permute-done | bytes 81952 | tf_op jit(solution)/shard_map/ppermute | solution.py:29
  75.9 0.4 collective-permute-start.20
  76.4 1.1 collective-permute-start.22
  77.5 1.8 %collective-permute-done.18.refs_3_ = bf16[2,64,640]{2,1,0:T(8,128)(2,1)S(1)} collective-permute-done((bf16[2,64,640]{2,1,0:T(8,128)(2,1)S(1)}, bf16[2,64,640]{2,1,0:T(8,128)(2,1)S(1)}, u32[]{:S(2)}, u32[]{:S(2)}) %collective-permute-start.18) | collective-permute-done | bytes 163872 | tf_op jit(solution)/shard_map/ppermute | solution.py:29
  79.3 2.0 %collective-permute-done.20.refs_5_ = bf16[128,640]{1,0:T(8,128)(2,1)S(1)} collective-permute-done((bf16[128,640]{1,0:T(8,128)(2,1)S(1)}, bf16[128,640]{1,0:T(8,128)(2,1)S(1)}, u32[]{:S(2)}, u32[]{:S(2)}) %collective-permute-start.20) | collective-permute-done | bytes 163872 | tf_op jit(solution)/shard_map/ppermute | solution.py:29
  81.3 0.4 collective-permute-done.22.refs_7_
  81.9 5.1 %gate_up_half.1 = (f32[256,1024]{1,0:T(8,128)S(1)}, f32[256,1024]{1,0:T(8,128)S(1)}, f32[256,128]{1,0:T(8,128)S(1)}) custom-call(s32[1]{0:T(128)} %bitcast.part_ref, bf16[2,256,1280]{2,1,0:T(8,128)(2,1)S(1)} %join_groups.1.refs_0_.rows_ref, f32[4,1,1280]{2,1,0:T(1,128)S(1)} %bitcast.25, bf16[5120,1024]{1,0:T(8,128)(2,1)} %gate_hbm.3, bf16[5120,1024]{1,0:T(8,128)(2,1)} %up_hbm.3), custom_call_target="tpu_custom_call" | custom-call | flops 2684354560 | bytes 12582912 | tf_op jit(solution)/shard_map/gate_up_half/pallas_call | solution.py:561
  87.0 7.2 %gate_up_rest.1 = (bf16[256,1024]{1,0:T(8,128)(2,1)S(1)}, bf16[2,256,1280]{2,1,0:T(8,128)(2,1)S(1)}) custom-call(s32[1]{0:T(128)} %bitcast.part_ref, bf16[2,256,1280]{2,1,0:T(8,128)(2,1)S(1)} %collective-permute-done.23.refs_1_.rows_ref, f32[4,1,1280]{2,1,0:T(1,128)S(1)} %bitcast.26, f32[256,1024]{1,0:T(8,128)S(1)} %get-tuple-element.53.old_gate_ref, ...), custom_call_target="tpu_custom_call" | custom-call | flops 4026531840 | bytes 15728640 | tf_op jit(solution)/shard_map/gate_up_rest/pallas_call | solution.py:631
  94.2 0.6 collective-permute-start.24
  94.8 3.7 %down_half.1.own_ref = bf16[2,256,1280]{2,1,0:T(8,128)(2,1)S(1)} custom-call(s32[1]{0:T(128)} %bitcast.part_ref, bf16[256,1024]{1,0:T(8,128)(2,1)S(1)} %get-tuple-element.56.activation_ref, bf16[1024,5120]{1,0:T(8,128)(2,1)} %down_hbm.3), custom_call_target="tpu_custom_call" | custom-call | flops 1342177280 | bytes 5242880 | tf_op jit(solution)/shard_map/down_half/pallas_call | solution.py:670
  98.8 1.8 %collective-permute-start.25 = (bf16[128,1280]{1,0:T(8,128)(2,1)S(1)}, bf16[128,1280]{1,0:T(8,128)(2,1)S(1)}, u32[]{:S(2)}, u32[]{:S(2)}) collective-permute-start(bf16[128,1280]{1,0:T(8,128)(2,1)S(1)} %get-tuple-element.59), channel_id=1, source_target_pairs={{0,2},{1,5},{2,0},{3,7},{4,6},{5,1},{6,4},{7,3},{8,10},{9,13},{10,... | collective-permute-start | bytes 983048 | tf_op jit(solution)/shard_map/ppermute | solution.py:40
  100.9 5.0 %collective-permute-done.25 = bf16[128,1280]{1,0:T(8,128)(2,1)S(1)} collective-permute-done((bf16[128,1280]{1,0:T(8,128)(2,1)S(1)}, bf16[128,1280]{1,0:T(8,128)(2,1)S(1)}, u32[]{:S(2)}, u32[]{:S(2)}) %collective-permute-start.25) | collective-permute-done | bytes 327712 | tf_op jit(solution)/shard_map/ppermute | solution.py:40
  106.1 1.1 collective-permute-start.26
  107.2 3.8 %collective-permute-done.28 = bf16[128,1280]{1,0:T(8,128)(2,1)S(1)} collective-permute-done((bf16[128,1280]{1,0:T(8,128)(2,1)S(1)}, bf16[128,1280]{1,0:T(8,128)(2,1)S(1)}, u32[]{:S(2)}, u32[]{:S(2)}) %collective-permute-start.28) | collective-permute-done | bytes 327712 | tf_op jit(solution)/shard_map/ppermute | solution.py:40
  111.1 1.1 collective-permute-start.29
  112.3 2.8 %collective-permute-start.27 = (bf16[32,1280]{1,0:T(8,128)(2,1)S(1)}, bf16[32,1280]{1,0:T(8,128)(2,1)S(1)}, u32[]{:S(2)}, u32[]{:S(2)}) collective-permute-start(bf16[32,1280]{1,0:T(8,128)(2,1)S(1)} %slice.75), channel_id=1, source_target_pairs={{0,8},{4,12},{8,0},{12,4},{16,24},{20,28},{24,16},{28,20},{1,9},{5... | collective-permute-start | bytes 245768 | tf_op jit(solution)/shard_map/ppermute | solution.py:29
  115.1 1.4 %collective-permute-done.29 = bf16[64,1280]{1,0:T(8,128)(2,1)S(1)} collective-permute-done((bf16[64,1280]{1,0:T(8,128)(2,1)S(1)}, bf16[64,1280]{1,0:T(8,128)(2,1)S(1)}, u32[]{:S(2)}, u32[]{:S(2)}) %collective-permute-start.29) | collective-permute-done | bytes 163872 | tf_op jit(solution)/shard_map/ppermute | solution.py:40
  116.6 4.7 %collective-permute-start.31 = (bf16[32,1280]{1,0:T(8,128)(2,1)S(1)}, bf16[32,1280]{1,0:T(8,128)(2,1)S(1)}, u32[]{:S(2)}, u32[]{:S(2)}) collective-permute-start(bf16[32,1280]{1,0:T(8,128)(2,1)S(1)} %get-tuple-element.68), channel_id=1, source_target_pairs={{0,24},{4,28},{8,16},{12,20},{16,8},{20,12},{24,0},{28,4},{1,25},{... | collective-permute-start | bytes 245768 | tf_op jit(solution)/shard_map/ppermute | solution.py:29
  121.3 0.7 collective-permute-done.30
  122.0 2.7 %collective-permute-done.31 = bf16[32,1280]{1,0:T(8,128)(2,1)S(1)} collective-permute-done((bf16[32,1280]{1,0:T(8,128)(2,1)S(1)}, bf16[32,1280]{1,0:T(8,128)(2,1)S(1)}, u32[]{:S(2)}, u32[]{:S(2)}) %collective-permute-start.31) | collective-permute-done | bytes 81952 | tf_op jit(solution)/shard_map/ppermute | solution.py:29
  124.8 0.8 collective-permute-start.33
  125.6 1.0 collective-permute-start.32
  126.6 0.7 assemble.2
  127.4 1.9 %collective-permute-done.34.refs_3_ = bf16[32,1280]{1,0:T(8,128)(2,1)S(1)} collective-permute-done((bf16[32,1280]{1,0:T(8,128)(2,1)S(1)}, bf16[32,1280]{1,0:T(8,128)(2,1)S(1)}, u32[]{:S(2)}, u32[]{:S(2)}) %collective-permute-start.34) | collective-permute-done | bytes 81952 | tf_op jit(solution)/shard_map/ppermute | solution.py:29
  129.3 0.8 collective-permute-done.33.refs_2_
  130.1 0.7 assemble.3
  (72 shorter events, 2.9 us)
Async XLA Ops:
  0.6 27.5 %slice-start = ((s8[4718592]{0:T(1024)(128)(4,1)}), s8[4194304]{0:T(1024)(128)(4,1)S(1)}, s32[]{:S(2)}) async-start(s8[4718592]{0:T(1024)(128)(4,1)} %bitcast.20), calls=%async_computation | async-start | bytes 8388608
  0.6 27.5 %slice-start.2 = ((s8[4718592]{0:T(1024)(128)(4,1)}), s8[4194304]{0:T(1024)(128)(4,1)S(1)}, s32[]{:S(2)}) async-start(s8[4718592]{0:T(1024)(128)(4,1)} %bitcast.22), calls=%async_computation.2 | async-start | bytes 8388608
  0.7 1.1 copy-start.1
  1.8 1.3 copy-start.3
  3.1 0.8 copy-start.4
  3.9 0.7 copy-start.5
  4.5 17.3 %copy-start.6 = (s32[36]{0:T(128)S(1)}, s32[36]{0:T(128)}, u32[]{:S(2)}) copy-start(s32[36]{0:T(128)} %param.29) | copy-start | bytes 436
  4.5 17.4 %copy-start.7 = (s32[36]{0:T(128)S(1)}, s32[36]{0:T(128)}, u32[]{:S(2)}) copy-start(s32[36]{0:T(128)} %param.30) | copy-start | bytes 436
  4.5 23.6 %slice-start.1 = ((s8[4718592]{0:T(1024)(128)(4,1)}), s8[524288]{0:T(1024)(128)(4,1)S(1)}, s32[]{:S(2)}) async-start(s8[4718592]{0:T(1024)(128)(4,1)} %bitcast.20), calls=%async_computation.1 | async-start | bytes 1048576
  4.5 23.6 %slice-start.3 = ((s8[4718592]{0:T(1024)(128)(4,1)}), s8[524288]{0:T(1024)(128)(4,1)S(1)}, s32[]{:S(2)}) async-start(s8[4718592]{0:T(1024)(128)(4,1)} %bitcast.22), calls=%async_computation.3 | async-start | bytes 1048576
  9.5 10.7 %collective-permute-start.2 = (bf16[16,16,128]{2,1,0:T(8,128)(2,1)S(1)}, bf16[16,16,128]{2,1,0:T(8,128)(2,1)S(1)}, u32[]{:S(2)}, u32[]{:S(2)}) collective-permute-start(bf16[16,16,128]{2,1,0:T(8,128)(2,1)S(1)} %get-tuple-element.32.query_ref), channel_id=1, source_target_pairs={{0,24},{4,28},{8,16},{12,20},{16,8},{20,12},{24,0},{28,4},{1,25},{... | collective-permute-start | bytes 196616 | tf_op jit(solution)/shard_map/ppermute | solution.py:29
  14.6 5.6 %collective-permute-start.1 = (bf16[16,16,128]{2,1,0:T(8,128)(2,1)S(1)}, bf16[16,16,128]{2,1,0:T(8,128)(2,1)S(1)}, u32[]{:S(2)}, u32[]{:S(2)}) collective-permute-start(bf16[16,16,128]{2,1,0:T(8,128)(2,1)S(1)} %get-tuple-element.32.query_ref), channel_id=1, source_target_pairs={{0,16},{4,20},{8,24},{12,28},{16,0},{20,4},{24,8},{28,12},{1,17},{... | collective-permute-start | bytes 196616 | tf_op jit(solution)/shard_map/ppermute | solution.py:29
  14.6 4.3 %collective-permute-start = (bf16[16,16,128]{2,1,0:T(8,128)(2,1)S(1)}, bf16[16,16,128]{2,1,0:T(8,128)(2,1)S(1)}, u32[]{:S(2)}, u32[]{:S(2)}) collective-permute-start(bf16[16,16,128]{2,1,0:T(8,128)(2,1)S(1)} %get-tuple-element.32.query_ref), channel_id=1, source_target_pairs={{0,8},{4,12},{8,0},{12,4},{16,24},{20,28},{24,16},{28,20},{1,9},{5... | collective-permute-start | bytes 196616 | tf_op jit(solution)/shard_map/ppermute | solution.py:29
  20.2 7.9 %collective-permute-start.3 = (bf16[64,16,128]{2,1,0:T(8,128)(2,1)S(1)}, bf16[64,16,128]{2,1,0:T(8,128)(2,1)S(1)}, u32[]{:S(2)}, u32[]{:S(2)}) collective-permute-start(bf16[64,16,128]{2,1,0:T(8,128)(2,1)S(1)} %constant_dynamic-update-slice_fusion.refs_0_), channel_id=1, source_target_pairs={{0,4},{4,0},{8,12},{12,8},{16,20},{20,16},{24,28},{28,24},{1,5},{5... | collective-permute-start | bytes 786440 | tf_op jit(solution)/shard_map/ppermute | solution.py:29
  22.0 1.7 %copy-start = (bf16[5120,256]{1,0:T(8,128)(2,1)S(1)}, bf16[5120,256]{1,0:T(8,128)(2,1)}, u32[]{:S(2)}) copy-start(bf16[5120,256]{1,0:T(8,128)(2,1)} %key_hbm.1) | copy-start | bytes 7864324
  33.0 6.0 %collective-permute-start.4 = (bf16[2,17,16,128]{3,2,1,0:T(8,128)(2,1)S(1)}, bf16[2,17,16,128]{3,2,1,0:T(8,128)(2,1)S(1)}, u32[]{:S(2)}, u32[]{:S(2)}) collective-permute-start(bf16[2,17,16,128]{3,2,1,0:T(8,128)(2,1)S(1)} %get-tuple-element.38), channel_id=1, source_target_pairs={{0,4},{4,0},{8,12},{12,8},{16,20},{20,16},{24,28},{28,24},{1,5},{5... | collective-permute-start | bytes 417800 | tf_op jit(solution)/shard_map/ppermute | solution.py:29
  34.8 6.5 %collective-permute-start.7 = (bf16[2,17,16,128]{3,2,1,0:T(8,128)(2,1)S(1)}, bf16[2,17,16,128]{3,2,1,0:T(8,128)(2,1)S(1)}, u32[]{:S(2)}, u32[]{:S(2)}) collective-permute-start(bf16[2,17,16,128]{3,2,1,0:T(8,128)(2,1)S(1)} %get-tuple-element.42), channel_id=1, source_target_pairs={{0,4},{4,0},{8,12},{12,8},{16,20},{20,16},{24,28},{28,24},{1,5},{5... | collective-permute-start | bytes 417800 | tf_op jit(solution)/shard_map/ppermute | solution.py:29
  39.5 5.3 %collective-permute-start.5 = (bf16[1,17,16,128]{3,2,1,0:T(8,128)(2,1)S(1)}, bf16[1,17,16,128]{3,2,1,0:T(8,128)(2,1)S(1)}, u32[]{:S(2)}, u32[]{:S(2)}) collective-permute-start(bf16[1,17,16,128]{3,2,1,0:T(8,128)(2,1)S(1)} %get-tuple-element.39), channel_id=1, source_target_pairs={{0,16},{4,20},{8,24},{12,28},{16,0},{20,4},{24,8},{28,12},{1,17},{... | collective-permute-start | bytes 208904 | tf_op jit(solution)/shard_map/ppermute | solution.py:29
  39.6 6.3 %collective-permute-start.6 = (bf16[1,17,16,128]{3,2,1,0:T(8,128)(2,1)S(1)}, bf16[1,17,16,128]{3,2,1,0:T(8,128)(2,1)S(1)}, u32[]{:S(2)}, u32[]{:S(2)}) collective-permute-start(bf16[1,17,16,128]{3,2,1,0:T(8,128)(2,1)S(1)} %get-tuple-element.40), channel_id=1, source_target_pairs={{0,24},{4,28},{8,16},{12,20},{16,8},{20,12},{24,0},{28,4},{1,25},{... | collective-permute-start | bytes 208904 | tf_op jit(solution)/shard_map/ppermute | solution.py:29
  41.7 4.9 %collective-permute-start.8 = (bf16[1,17,16,128]{3,2,1,0:T(8,128)(2,1)S(1)}, bf16[1,17,16,128]{3,2,1,0:T(8,128)(2,1)S(1)}, u32[]{:S(2)}, u32[]{:S(2)}) collective-permute-start(bf16[1,17,16,128]{3,2,1,0:T(8,128)(2,1)S(1)} %get-tuple-element.44), channel_id=1, source_target_pairs={{0,8},{4,12},{8,0},{12,4},{16,24},{20,28},{24,16},{28,20},{1,9},{5... | collective-permute-start | bytes 208904 | tf_op jit(solution)/shard_map/ppermute | solution.py:29
  51.4 30.6 %copy-start.2 = (f32[5120]{0:T(1024)S(1)}, f32[5120]{0:T(1024)}, u32[]{:S(2)}) copy-start(f32[5120]{0:T(1024)} %param.22) | copy-start | bytes 61444
  51.4 2.2 %collective-permute-start.9 = (bf16[32,1280]{1,0:T(8,128)(2,1)S(1)}, bf16[32,1280]{1,0:T(8,128)(2,1)S(1)}, u32[]{:S(2)}, u32[]{:S(2)}) collective-permute-start(bf16[32,1280]{1,0:T(8,128)(2,1)S(1)} %get-tuple-element.64), channel_id=1, source_target_pairs={{0,1},{1,0},{2,3},{3,2},{4,5},{5,4},{6,7},{7,6},{8,9},{9,8},{10,11... | collective-permute-start | bytes 245768 | tf_op jit(solution)/shard_map/ppermute | solution.py:29
  51.5 4.6 %collective-permute-start.11 = (bf16[32,1280]{1,0:T(8,128)(2,1)S(1)}, bf16[32,1280]{1,0:T(8,128)(2,1)S(1)}, u32[]{:S(2)}, u32[]{:S(2)}) collective-permute-start(bf16[32,1280]{1,0:T(8,128)(2,1)S(1)} %get-tuple-element.65), channel_id=1, source_target_pairs={{0,3},{1,2},{2,1},{3,0},{4,7},{5,6},{6,5},{7,4},{8,11},{9,10},{10,... | collective-permute-start | bytes 245768 | tf_op jit(solution)/shard_map/ppermute | solution.py:29
  53.3 4.7 %collective-permute-start.10 = (bf16[32,1280]{1,0:T(8,128)(2,1)S(1)}, bf16[32,1280]{1,0:T(8,128)(2,1)S(1)}, u32[]{:S(2)}, u32[]{:S(2)}) collective-permute-start(bf16[32,1280]{1,0:T(8,128)(2,1)S(1)} %get-tuple-element.66), channel_id=1, source_target_pairs={{0,2},{1,3},{2,0},{3,1},{4,6},{5,7},{6,4},{7,5},{8,10},{9,11},{10,... | collective-permute-start | bytes 245768 | tf_op jit(solution)/shard_map/ppermute | solution.py:29
  58.1 4.5 %collective-permute-start.12 = (bf16[32,1280]{1,0:T(8,128)(2,1)S(1)}, bf16[32,1280]{1,0:T(8,128)(2,1)S(1)}, u32[]{:S(2)}, u32[]{:S(2)}) collective-permute-start(bf16[32,1280]{1,0:T(8,128)(2,1)S(1)} %add_convert_fusion.5), channel_id=1, source_target_pairs={{0,8},{4,12},{8,0},{12,4},{16,24},{20,28},{24,16},{28,20},{1,9},{5... | collective-permute-start | bytes 245768 | tf_op jit(solution)/shard_map/ppermute | solution.py:29
  59.5 6.4 %collective-permute-start.16 = (bf16[32,1280]{1,0:T(8,128)(2,1)S(1)}, bf16[32,1280]{1,0:T(8,128)(2,1)S(1)}, u32[]{:S(2)}, u32[]{:S(2)}) collective-permute-start(bf16[32,1280]{1,0:T(8,128)(2,1)S(1)} %add_convert_fusion.5), channel_id=1, source_target_pairs={{0,24},{4,28},{8,16},{12,20},{16,8},{20,12},{24,0},{28,4},{1,25},{... | collective-permute-start | bytes 245768 | tf_op jit(solution)/shard_map/ppermute | solution.py:29
  60.4 8.6 %collective-permute-start.15 = (bf16[32,1280]{1,0:T(8,128)(2,1)S(1)}, bf16[32,1280]{1,0:T(8,128)(2,1)S(1)}, u32[]{:S(2)}, u32[]{:S(2)}) collective-permute-start(bf16[32,1280]{1,0:T(8,128)(2,1)S(1)} %add_convert_fusion.5), channel_id=1, source_target_pairs={{0,16},{4,20},{8,24},{12,28},{16,0},{20,4},{24,8},{28,12},{1,17},{... | collective-permute-start | bytes 245768 | tf_op jit(solution)/shard_map/ppermute | solution.py:29
  62.7 6.4 %collective-permute-start.14 = (bf16[64,640]{1,0:T(8,128)(2,1)S(1)}, bf16[64,640]{1,0:T(8,128)(2,1)S(1)}, u32[]{:S(2)}, u32[]{:S(2)}) collective-permute-start(bf16[64,640]{1,0:T(8,128)(2,1)S(1)} %get-tuple-element.49), channel_id=1, source_target_pairs={{0,2},{1,3},{2,0},{3,1},{4,6},{5,7},{6,4},{7,5},{8,10},{9,11},{10,... | collective-permute-start | bytes 245768 | tf_op jit(solution)/shard_map/ppermute | solution.py:29
  64.4 4.6 %collective-permute-start.13 = (bf16[64,640]{1,0:T(8,128)(2,1)S(1)}, bf16[64,640]{1,0:T(8,128)(2,1)S(1)}, u32[]{:S(2)}, u32[]{:S(2)}) collective-permute-start(bf16[64,640]{1,0:T(8,128)(2,1)S(1)} %get-tuple-element.47), channel_id=1, source_target_pairs={{0,4},{4,0},{8,12},{12,8},{16,20},{20,16},{24,28},{28,24},{1,5},{5... | collective-permute-start | bytes 245768 | tf_op jit(solution)/shard_map/ppermute | solution.py:29
  69.1 7.2 %collective-permute-start.21 = (bf16[64,640]{1,0:T(8,128)(2,1)S(1)}, bf16[64,640]{1,0:T(8,128)(2,1)S(1)}, u32[]{:S(2)}, u32[]{:S(2)}) collective-permute-start(bf16[64,640]{1,0:T(8,128)(2,1)S(1)} %get-tuple-element.70), channel_id=1, source_target_pairs={{0,2},{1,3},{2,0},{3,1},{4,6},{5,7},{6,4},{7,5},{8,10},{9,11},{10,... | collective-permute-start | bytes 245768 | tf_op jit(solution)/shard_map/ppermute | solution.py:29
  70.9 5.0 %collective-permute-start.19 = (bf16[64,640]{1,0:T(8,128)(2,1)S(1)}, bf16[64,640]{1,0:T(8,128)(2,1)S(1)}, u32[]{:S(2)}, u32[]{:S(2)}) collective-permute-start(bf16[64,640]{1,0:T(8,128)(2,1)S(1)} %get-tuple-element.71), channel_id=1, source_target_pairs={{0,4},{4,0},{8,12},{12,8},{16,20},{20,16},{24,28},{28,24},{1,5},{5... | collective-permute-start | bytes 245768 | tf_op jit(solution)/shard_map/ppermute | solution.py:29
  72.4 6.9 %collective-permute-start.18 = (bf16[2,64,640]{2,1,0:T(8,128)(2,1)S(1)}, bf16[2,64,640]{2,1,0:T(8,128)(2,1)S(1)}, u32[]{:S(2)}, u32[]{:S(2)}) collective-permute-start(bf16[2,64,640]{2,1,0:T(8,128)(2,1)S(1)} %pad_maximum_fusion.refs_2_), channel_id=1, source_target_pairs={{0,4},{4,0},{8,12},{12,8},{16,20},{20,16},{24,28},{28,24},{1,5},{5... | collective-permute-start | bytes 491528 | tf_op jit(solution)/shard_map/ppermute | solution.py:29
  73.0 6.3 %collective-permute-start.17 = (bf16[128,640]{1,0:T(8,128)(2,1)S(1)}, bf16[128,640]{1,0:T(8,128)(2,1)S(1)}, u32[]{:S(2)}, u32[]{:S(2)}) collective-permute-start(bf16[128,640]{1,0:T(8,128)(2,1)S(1)} %constant_dynamic-update-slice_fusion.4.refs_0_), channel_id=1, source_target_pairs={{0,2},{1,3},{2,0},{3,1},{4,6},{5,7},{6,4},{7,5},{8,10},{9,11},{10,... | collective-permute-start | bytes 491528 | tf_op jit(solution)/shard_map/ppermute | solution.py:29
  75.9 5.4 %collective-permute-start.20 = (bf16[128,640]{1,0:T(8,128)(2,1)S(1)}, bf16[128,640]{1,0:T(8,128)(2,1)S(1)}, u32[]{:S(2)}, u32[]{:S(2)}) collective-permute-start(bf16[128,640]{1,0:T(8,128)(2,1)S(1)} %pad_maximum_fusion.1.refs_4_), channel_id=1, source_target_pairs={{0,2},{1,3},{2,0},{3,1},{4,6},{5,7},{6,4},{7,5},{8,10},{9,11},{10,... | collective-permute-start | bytes 491528 | tf_op jit(solution)/shard_map/ppermute | solution.py:29
  76.4 5.4 %collective-permute-start.22 = (bf16[2,64,640]{2,1,0:T(8,128)(2,1)S(1)}, bf16[2,64,640]{2,1,0:T(8,128)(2,1)S(1)}, u32[]{:S(2)}, u32[]{:S(2)}) collective-permute-start(bf16[2,64,640]{2,1,0:T(8,128)(2,1)S(1)} %pad_maximum_fusion.2.refs_6_), channel_id=1, source_target_pairs={{0,4},{4,0},{8,12},{12,8},{16,20},{20,16},{24,28},{28,24},{1,5},{5... | collective-permute-start | bytes 491528 | tf_op jit(solution)/shard_map/ppermute | solution.py:29
  81.9 5.2 %collective-permute-start.23 = (bf16[2,256,1280]{2,1,0:T(8,128)(2,1)S(1)}, bf16[2,256,1280]{2,1,0:T(8,128)(2,1)S(1)}, u32[]{:S(2)}, u32[]{:S(2)}) collective-permute-start(bf16[2,256,1280]{2,1,0:T(8,128)(2,1)S(1)} %join_groups.1.refs_0_.rows_ref), channel_id=1, source_target_pairs={{0,1},{1,0},{2,3},{3,2},{4,5},{5,4},{6,7},{7,6},{8,9},{9,8},{10,11... | collective-permute-start | bytes 3932168 | tf_op jit(solution)/shard_map/ppermute | solution.py:29
  94.2 4.3 %collective-permute-start.24 = (bf16[2,256,1280]{2,1,0:T(8,128)(2,1)S(1)}, bf16[2,256,1280]{2,1,0:T(8,128)(2,1)S(1)}, u32[]{:S(2)}, u32[]{:S(2)}) collective-permute-start(bf16[2,256,1280]{2,1,0:T(8,128)(2,1)S(1)} %get-tuple-element.57), channel_id=1, source_target_pairs={{0,1},{1,0},{2,3},{3,2},{4,5},{5,4},{6,7},{7,6},{8,9},{9,8},{10,11... | collective-permute-start | bytes 3932168 | tf_op jit(solution)/shard_map/ppermute | solution.py:29
  98.8 7.1 %collective-permute-start.25 = (bf16[128,1280]{1,0:T(8,128)(2,1)S(1)}, bf16[128,1280]{1,0:T(8,128)(2,1)S(1)}, u32[]{:S(2)}, u32[]{:S(2)}) collective-permute-start(bf16[128,1280]{1,0:T(8,128)(2,1)S(1)} %get-tuple-element.59), channel_id=1, source_target_pairs={{0,2},{1,5},{2,0},{3,7},{4,6},{5,1},{6,4},{7,3},{8,10},{9,13},{10,... | collective-permute-start | bytes 983048 | tf_op jit(solution)/shard_map/ppermute | solution.py:40
  100.6 10.4 %collective-permute-start.28 = (bf16[128,1280]{1,0:T(8,128)(2,1)S(1)}, bf16[128,1280]{1,0:T(8,128)(2,1)S(1)}, u32[]{:S(2)}, u32[]{:S(2)}) collective-permute-start(bf16[128,1280]{1,0:T(8,128)(2,1)S(1)} %get-tuple-element.61), channel_id=1, source_target_pairs={{0,2},{1,5},{2,0},{3,7},{4,6},{5,1},{6,4},{7,3},{8,10},{9,13},{10,... | collective-permute-start | bytes 983048 | tf_op jit(solution)/shard_map/ppermute | solution.py:40
  106.1 6.2 %collective-permute-start.26 = (bf16[64,1280]{1,0:T(8,128)(2,1)S(1)}, bf16[64,1280]{1,0:T(8,128)(2,1)S(1)}, u32[]{:S(2)}, u32[]{:S(2)}) collective-permute-start(bf16[64,1280]{1,0:T(8,128)(2,1)S(1)} %slice.73), channel_id=1, source_target_pairs={{0,4},{1,3},{2,6},{3,1},{4,0},{5,7},{6,2},{7,5},{8,12},{9,11},{10,... | collective-permute-start | bytes 491528 | tf_op jit(solution)/shard_map/ppermute | solution.py:40
  111.1 5.4 %collective-permute-start.29 = (bf16[64,1280]{1,0:T(8,128)(2,1)S(1)}, bf16[64,1280]{1,0:T(8,128)(2,1)S(1)}, u32[]{:S(2)}, u32[]{:S(2)}) collective-permute-start(bf16[64,1280]{1,0:T(8,128)(2,1)S(1)} %slice.77), channel_id=1, source_target_pairs={{0,4},{1,3},{2,6},{3,1},{4,0},{5,7},{6,2},{7,5},{8,12},{9,11},{10,... | collective-permute-start | bytes 491528 | tf_op jit(solution)/shard_map/ppermute | solution.py:40
  112.3 9.0 %collective-permute-start.27 = (bf16[32,1280]{1,0:T(8,128)(2,1)S(1)}, bf16[32,1280]{1,0:T(8,128)(2,1)S(1)}, u32[]{:S(2)}, u32[]{:S(2)}) collective-permute-start(bf16[32,1280]{1,0:T(8,128)(2,1)S(1)} %slice.75), channel_id=1, source_target_pairs={{0,8},{4,12},{8,0},{12,4},{16,24},{20,28},{24,16},{28,20},{1,9},{5... | collective-permute-start | bytes 245768 | tf_op jit(solution)/shard_map/ppermute | solution.py:29
  116.5 5.4 %collective-permute-start.30 = (bf16[32,1280]{1,0:T(8,128)(2,1)S(1)}, bf16[32,1280]{1,0:T(8,128)(2,1)S(1)}, u32[]{:S(2)}, u32[]{:S(2)}) collective-permute-start(bf16[32,1280]{1,0:T(8,128)(2,1)S(1)} %get-tuple-element.67), channel_id=1, source_target_pairs={{0,16},{4,20},{8,24},{12,28},{16,0},{20,4},{24,8},{28,12},{1,17},{... | collective-permute-start | bytes 245768 | tf_op jit(solution)/shard_map/ppermute | solution.py:29
  116.6 8.0 %collective-permute-start.31 = (bf16[32,1280]{1,0:T(8,128)(2,1)S(1)}, bf16[32,1280]{1,0:T(8,128)(2,1)S(1)}, u32[]{:S(2)}, u32[]{:S(2)}) collective-permute-start(bf16[32,1280]{1,0:T(8,128)(2,1)S(1)} %get-tuple-element.68), channel_id=1, source_target_pairs={{0,24},{4,28},{8,16},{12,20},{16,8},{20,12},{24,0},{28,4},{1,25},{... | collective-permute-start | bytes 245768 | tf_op jit(solution)/shard_map/ppermute | solution.py:29
  124.7 4.6 %collective-permute-start.34 = (bf16[32,1280]{1,0:T(8,128)(2,1)S(1)}, bf16[32,1280]{1,0:T(8,128)(2,1)S(1)}, u32[]{:S(2)}, u32[]{:S(2)}) collective-permute-start(bf16[32,1280]{1,0:T(8,128)(2,1)S(1)} %add_convert_fusion.4.refs_0_), channel_id=1, source_target_pairs={{0,3},{1,2},{2,1},{3,0},{4,7},{5,6},{6,5},{7,4},{8,11},{9,10},{10,... | collective-permute-start | bytes 245768 | tf_op jit(solution)/shard_map/ppermute | solution.py:29
  124.8 5.3 %collective-permute-start.33 = (bf16[32,1280]{1,0:T(8,128)(2,1)S(1)}, bf16[32,1280]{1,0:T(8,128)(2,1)S(1)}, u32[]{:S(2)}, u32[]{:S(2)}) collective-permute-start(bf16[32,1280]{1,0:T(8,128)(2,1)S(1)} %add_convert_fusion.4.refs_0_), channel_id=1, source_target_pairs={{0,2},{1,3},{2,0},{3,1},{4,6},{5,7},{6,4},{7,5},{8,10},{9,11},{10,... | collective-permute-start | bytes 245768 | tf_op jit(solution)/shard_map/ppermute | solution.py:29
  125.6 4.5 %collective-permute-start.32 = (bf16[32,1280]{1,0:T(8,128)(2,1)S(1)}, bf16[32,1280]{1,0:T(8,128)(2,1)S(1)}, u32[]{:S(2)}, u32[]{:S(2)}) collective-permute-start(bf16[32,1280]{1,0:T(8,128)(2,1)S(1)} %add_convert_fusion.4.refs_0_), channel_id=1, source_target_pairs={{0,1},{1,0},{2,3},{3,2},{4,5},{5,4},{6,7},{7,6},{8,9},{9,8},{10,11... | collective-permute-start | bytes 245768 | tf_op jit(solution)/shard_map/ppermute | solution.py:29

commit v5 on v4

--- a/solution.py
+++ b/solution.py
@@ -229,12 +229,55 @@
         copy.start()
 
 
+def load_kernel(slots, by_rows, part_ref, source_ref, out_ref, sems):
+    size = out_ref.shape[1] if by_rows else out_ref.shape[2]
+    copies = []
+    for i, slot in enumerate(slots):
+        at = pl.ds(pl.multiple_of((part_ref[0] ^ slot) * size, size), size)
+        source = source_ref.at[at] if by_rows else source_ref.at[:, at]
+        copies.append(pltpu.make_async_copy(source, out_ref.at[i], sems.at[i]))
+    start_all(copies)
+    for copy in copies:
+        copy.wait()
+
+
+def load(part, source, slots, size, by_rows, limit):
+    rows, columns = source.shape
+    block = (size, columns) if by_rows else (rows, size)
+    return pl.pallas_call(
+        functools.partial(load_kernel, slots, by_rows),
+        out_shape=jax.ShapeDtypeStruct((len(slots), *block), bf16),
+        in_specs=[smem, hbm],
+        out_specs=vmem,
+        scratch_shapes=[pltpu.SemaphoreType.DMA((len(slots),))],
+        compiler_params=pltpu.CompilerParams(vmem_limit_bytes=limit << 20),
+        cost_estimate=pl.CostEstimate(
+            flops=0, bytes_accessed=2 * len(slots) * block[0] * block[1], transcendentals=0
+        ),
+        name="load",
+    )(part.reshape(1), source)
+
+
 def query_kernel(
-    kv_local, me_ref, slots_ref, lengths_ref, input_ref, gain_ref, weight_hbm,
-    query_ref, normalized_ref, cosine_ref, sine_ref, weight_buf, total_ref, tile_ref, sems,
+    kv_local, me_ref, slots_hbm, lengths_hbm, input_hbm, gain_hbm, weight_hbm,
+    query_ref, normalized_ref, rotary_ref,
+    slots_ref, lengths_ref, input_ref, gain_ref, weight_buf, total_ref, tile_ref, small_sems, sems,
 ):
     steps, row_count, width = input_ref.shape
-    head_dim = cosine_ref.shape[1]
+    head_dim = rotary_ref.shape[2]
+    cosine_ref, sine_ref = rotary_ref.at[0], rotary_ref.at[1]
+    small = [
+        pltpu.make_async_copy(source, target, small_sems.at[i])
+        for i, (source, target) in enumerate(
+            (
+                (input_hbm, input_ref),
+                (gain_hbm, gain_ref),
+                (slots_hbm, slots_ref),
+                (lengths_hbm, lengths_ref),
+            )
+        )
+    ]
+    start_all(small)
     heads = weight_buf.shape[1] // head_dim
     group = heads // kv_local
     chunks = sems.shape[0]
@@ -245,6 +288,8 @@
         copies.append(pltpu.make_async_copy(weight_hbm.at[at], weight_buf.at[at], sems.at[chunk]))
     start_all(copies)
 
+    for copy in small:
+        copy.wait()
     gain = gain_ref[...]
     for step in range(0, steps, 2):
         pair = []
@@ -298,18 +343,22 @@
         out_shape=(
             jax.ShapeDtypeStruct((pairs, tile_rows, head_dim), bf16),
             jax.ShapeDtypeStruct((rows, width), bf16),
-            jax.ShapeDtypeStruct((rows, head_dim), f32),
-            jax.ShapeDtypeStruct((rows, head_dim), f32),
-        ),
-        in_specs=[smem, vmem, vmem, vmem, vmem, hbm],
-        out_specs=(vmem, vmem, vmem, vmem),
+            jax.ShapeDtypeStruct((2, rows, head_dim), f32),
+        ),
+        in_specs=[smem] + [hbm] * 5,
+        out_specs=(vmem, vmem, vmem),
         scratch_shapes=[
+            pltpu.VMEM((1, request_slot.shape[0]), jnp.int32),
+            pltpu.VMEM((1, request_slot.shape[0]), jnp.int32),
+            pltpu.VMEM(token_inputs.shape, bf16),
+            pltpu.VMEM((1, width), f32),
             pltpu.VMEM((width, columns), bf16),
             pltpu.VMEM((rows, columns), f32),
             pltpu.VMEM((pairs * tile_rows, head_dim), f32),
+            pltpu.SemaphoreType.DMA((4,)),
             pltpu.SemaphoreType.DMA((chunks,)),
         ],
-        compiler_params=pltpu.CompilerParams(vmem_limit_bytes=52 << 20),
+        compiler_params=pltpu.CompilerParams(vmem_limit_bytes=54 << 20),
         cost_estimate=pl.CostEstimate(
             flops=2 * rows * width * columns, bytes_accessed=2 * width * columns, transcendentals=0
         ),
@@ -325,13 +374,13 @@
 
 
 def recent_kernel(
-    kv_local, normalized_ref, cosine_ref, sine_ref, query_ref, key_hbm, value_hbm,
+    kv_local, pairs, normalized_ref, rotary_ref, query_ref, key_hbm, value_hbm,
     out_ref, key_buf, value_buf, key_tile, value_tile, sems,
 ):
     rows, width = normalized_ref.shape
-    head_dim = cosine_ref.shape[1]
+    head_dim = rotary_ref.shape[2]
     row_count = rows // STEPS
-    pairs, tile_rows, _ = query_ref.shape
+    tile_rows = query_ref.shape[1]
     pads = key_tile.shape[0] // pairs
     copies = [
         pltpu.make_async_copy(key_hbm, key_buf, sems.at[0]),
@@ -340,7 +389,7 @@
     start_all(copies)
     key_tile[...] = jnp.zeros(key_tile.shape, f32)
     value_tile[...] = jnp.zeros(value_tile.shape, f32)
-    cosine, sine = cosine_ref[...], sine_ref[...]
+    cosine, sine = rotary_ref[0], rotary_ref[1]
     for copy, buf, tile in ((copies[0], key_buf, key_tile), (copies[1], value_buf, value_tile)):
         copy.wait()
         product = jnp.dot(normalized_ref[...], buf[...], preferred_element_type=f32)
@@ -369,15 +418,15 @@
     out_ref[0, pairs] = encode_stats(all_tops, all_totals, pairs)
 
 
-def recent_part(normalized, cosine, sine, query, key_projection, value_projection, kv_local, head_dim):
+def recent_part(normalized, rotary, queries, key_projection, value_projection, pairs, kv_local):
     rows, width = normalized.shape
-    pairs, tile_rows, _ = query.shape
+    _, tile_rows, head_dim = queries.shape
     pads = 16
     columns = key_projection.shape[1]
     return pl.pallas_call(
-        functools.partial(recent_kernel, kv_local),
+        functools.partial(recent_kernel, kv_local, pairs),
         out_shape=jax.ShapeDtypeStruct((1, pairs + 1, tile_rows, head_dim), bf16),
-        in_specs=[vmem, vmem, vmem, vmem, hbm, hbm],
+        in_specs=[vmem, vmem, vmem, hbm, hbm],
         out_specs=vmem,
         scratch_shapes=[
             pltpu.VMEM((width, columns), bf16),
@@ -386,12 +435,12 @@
             pltpu.VMEM((pairs * pads, head_dim), f32),
             pltpu.SemaphoreType.DMA((2,)),
         ],
-        compiler_params=pltpu.CompilerParams(vmem_limit_bytes=50 << 20),
+        compiler_params=pltpu.CompilerParams(vmem_limit_bytes=53 << 20),
         cost_estimate=pl.CostEstimate(
             flops=4 * rows * width * columns, bytes_accessed=4 * width * columns, transcendentals=0
         ),
         name="recent_part",
-    )(normalized, cosine, sine, query, key_projection, value_projection)
+    )(normalized, rotary, queries, key_projection, value_projection)
 
 
 def out_kernel(
@@ -710,6 +759,45 @@
     return outs[:count], outs[count:]
 
 
+def stack_kernel(*refs):
+    at = 0
+    for ref in refs[:-1]:
+        refs[-1][at : at + ref.shape[0]] = ref[...]
+        at += ref.shape[0]
+
+
+def stack_rows(pieces, weight):
+    height = sum(piece.shape[0] for piece in pieces)
+    return pl.pallas_call(
+        stack_kernel,
+        out_shape=jax.ShapeDtypeStruct((height, *pieces[0].shape[1:]), bf16),
+        in_specs=[vmem] * len(pieces),
+        out_specs=vmem,
+        compiler_params=pltpu.CompilerParams(vmem_limit_bytes=8 << 20),
+        cost_estimate=pl.CostEstimate(flops=0, bytes_accessed=weight << 20, transcendentals=0),
+        name="stack_rows",
+    )(*pieces)
+
+
+def total_kernel(*refs):
+    total = refs[0][...].astype(f32)
+    for ref in refs[1:-1]:
+        total = total + ref[...].astype(f32)
+    refs[-1][...] = total
+
+
+def total_of(pieces, weight):
+    return pl.pallas_call(
+        total_kernel,
+        out_shape=jax.ShapeDtypeStruct(pieces[0].shape, f32),
+        in_specs=[vmem] * len(pieces),
+        out_specs=vmem,
+        compiler_params=pltpu.CompilerParams(vmem_limit_bytes=8 << 20),
+        cost_estimate=pl.CostEstimate(flops=0, bytes_accessed=weight << 20, transcendentals=0),
+        name="total_of",
+    )(*pieces)
+
+
 def assemble_kernel(part_ref, *refs):
     out_ref = refs[-1]
     height = out_ref.shape[0]
@@ -775,17 +863,14 @@
     slots = mask % across * deep + mask // across
     slots = slots * row_count + page_row % row_count
 
-    query, normalized, cosine, sine = project_queries(
+    query, normalized, rotary = project_queries(
         me, request_slot, cache_lengths, token_inputs, attn_gain, w_query, kv_local, head_dim
     )
     near = [query] + [swap(query, "seq", across * k) for k in range(1, count)]
     far = [swap(query, "seq", across * k) for k in range(count, deep)]
     shared = jnp.concatenate(near + far, axis=0)
     queries = [shared] + [swap(shared, "seq", k) for k in range(1, across)]
-    normalized, shared = lax.optimization_barrier((normalized, shared))
-    recent = recent_part(
-        normalized, cosine, sine, query, key_projection, value_projection, kv_local, head_dim
-    )
+    recent = recent_part(normalized, rotary, shared, key_projection, value_projection, pairs, kv_local)
     near_parts, far_parts = attend_pages(queries, key_cache, paged_value_cache, slots, valid, count, pairs, recent)
 
     def merge_x(parts):
@@ -851,7 +936,7 @@
     near = collect_group(near)
     far = [swap(far[k], "seq", across * (count + k)) for k in range(deep - count)]
     near = [near[0]] + [swap(near[k], "seq", across * k) for k in range(1, count)]
-    mlp_result = add(near[0], near[1:] + far)
+    mlp_result = add(near[0], near[1:] + [total_of(far, 40)])
     own_out = (own_attended.astype(f32) + mlp_result).astype(bf16)
     pieces = [own_out] + [swap(own_out, "tp", slot) for slot in range(1, tp)]
     layer_out = assemble(part, rows, pieces).reshape(steps, row_count, width)

time: 131 us -> 128 us (0.977)
  local copies, waits for them, and re-layouts: 6.67 us -> 3.7 us
  Pallas kernels: 36.3 us -> 38.9 us
  starting transfers between devices: 42.3 us -> 40.5 us
    unnamed x29 -> x27, local copies, waits for them, and re-layouts: 5.66 us -> 2.69 us
    pallas_call x1, Pallas kernels: 4.91 us -> 6.81 us  [project_queries(): pl.pallas_call(functools.partial(query_kernel, kv_local), out_shape=(jax....]
    ppermute x31, starting transfers between devices: 37.9 us -> 36.4 us  [swap(): return lax.ppermute(value, axis, [(i, i ^ mask) for i in range(size)])]
    pallas_call x1 -> x2, Pallas kernels: 3.05 us -> 3.77 us  [the longest x1 3.75 us: recent_part(): pl.pallas_call(functools.partial(recent_kernel, kv_local, pairs), out_sha...]
  transfers between devices with their start and end apart: 35 -> 35, of which waited for: 22 -> 25; matrix products, arithmetic and copies ran while one was open for 1% -> 2% of each run, Pallas kernels for 10% -> 11%
where the time goes in v5:
time: 128 us
  waiting for transfers between devices  43.2 us (34%)
  starting transfers between devices  40.5 us (32%)
  Pallas kernels  38.9 us (30%)
  local copies, waits for them, and re-layouts  3.7 us (3%)
    ppermute x31, starting transfers between devices, swap(): return lax.ppermute(value, axis, [(i, i ^ mask) for i in range(size)])  36.4 us
    ppermute x31, waiting for transfers between devices, swap(): return lax.ppermute(value, axis, [(i, i ^ mask) for i in range(size)])  34 us
    ppermute x4, waiting for transfers between devices, cross(): return lax.ppermute(value, ('seq', 'tp'), pairs)  9.2 us
    pallas_call x1, Pallas kernels, gate_up_rest(): pl.pallas_call(functools.partial(rest_kernel, width), out_shape=(jax.Shap...  7.21 us
    pallas_call x1, Pallas kernels, project_queries(): pl.pallas_call(functools.partial(query_kernel, kv_local), out_shape=(jax....  6.81 us
    pallas_call x1, Pallas kernels, gate_up_half(): pl.pallas_call(functools.partial(gate_up_kernel, core), out_shape=(jax.Sh...  5.05 us
    pallas_call x1, Pallas kernels, attend_pages(): pl.pallas_call(functools.partial(pages_kernel, block_pages, len(pieces),...  4.81 us
    pallas_call x1, Pallas kernels, project_out(): pl.pallas_call(functools.partial(out_kernel, len(parts), kv_local), out_s...  4.74 us
  transfers between devices with their start and end apart: 35, of which 25 were waited for; matrix products, arithmetic and copies ran while one was open for 2% of the time, Pallas kernels for 11%

profile of v5, /device:TPU:0, one launch (start us, length us, event | category | flops | bytes accessed | tf_op | source)
XLA Modules:
  0.0 128.0 jit_solution(11911708888267829461)
XLA Ops:
  0.7 6.8 %project_queries.1 = (bf16[16,16,128]{2,1,0:T(8,128)(2,1)}, bf16[32,5120]{1,0:T(8,128)(2,1)}, f32[2,32,128]{2,1,0:T(8,128)}) custom-call(s32[1]{0:T(128)} %bitcast.2.me_ref, s32[1,64]{1,0:T(1,128)} %bitcast.34, s32[1,64]{1,0:T(1,128)} %bitcast.33, bf16[4,8,5120]{2,1,0:T(8,128)(2,1)} %input_hbm.1, f32[1,5120]{1,0:T(1,128)} %bitcast.32, ...), custom_call_target="tpu_custom_call" | custom-call | flops 335544320 | bytes 10485760 | tf_op jit(solution)/shard_map/project_queries/pallas_call | solution.py:341
  7.5 5.1 %collective-permute-start.2 = (bf16[16,16,128]{2,1,0:T(8,128)(2,1)}, bf16[16,16,128]{2,1,0:T(8,128)(2,1)S(1)}, u32[]{:S(2)}, u32[]{:S(2)}) collective-permute-start(bf16[16,16,128]{2,1,0:T(8,128)(2,1)} %get-tuple-element.30), channel_id=1, source_target_pairs={{0,24},{4,28},{8,16},{12,20},{16,8},{20,12},{24,0},{28,4},{1,25},{... | collective-permute-start | bytes 196616 | tf_op jit(solution)/shard_map/ppermute | solution.py:29
  12.7 0.6 collective-permute-start
  13.3 0.9 constant_dynamic-update-slice_fusion.3
  14.2 3.0 %collective-permute-done = bf16[16,16,128]{2,1,0:T(8,128)(2,1)S(1)} collective-permute-done((bf16[16,16,128]{2,1,0:T(8,128)(2,1)}, bf16[16,16,128]{2,1,0:T(8,128)(2,1)S(1)}, u32[]{:S(2)}, u32[]{:S(2)}) %collective-permute-start) | collective-permute-done | bytes 65568 | tf_op jit(solution)/shard_map/ppermute | solution.py:29
  17.2 1.3 collective-permute-done.1
  18.5 1.6 %collective-permute-start.3 = (bf16[64,16,128]{2,1,0:T(8,128)(2,1)S(1)}, bf16[64,16,128]{2,1,0:T(8,128)(2,1)S(1)}, u32[]{:S(2)}, u32[]{:S(2)}) collective-permute-start(bf16[64,16,128]{2,1,0:T(8,128)(2,1)S(1)} %constant_dynamic-update-slice_fusion.query_ref.refs_0_), channel_id=1, source_target_pairs={{0,4},{4,0},{8,12},{12,8},{16,20},{20,16},{24,28},{28,24},{1,5},{5... | collective-permute-start | bytes 786440 | tf_op jit(solution)/shard_map/ppermute | solution.py:29
  20.3 1.0 copy-done
  21.3 0.8 copy-done.2
  22.0 3.8 %recent_part.1.refs_4_ = bf16[1,17,16,128]{3,2,1,0:T(8,128)(2,1)S(1)} custom-call(bf16[32,5120]{1,0:T(8,128)(2,1)S(1)} %copy-done, f32[2,32,128]{2,1,0:T(8,128)S(1)} %copy-done.2, bf16[64,16,128]{2,1,0:T(8,128)(2,1)S(1)} %constant_dynamic-update-slice_fusion.query_ref.refs_0_, bf16[5120,256]{1,0:T(8,128)(2,1)} %key_hbm.1, bf16[5120,256]{1,0:T(8,128)(2,1)} %value_hbm.1), custom_call_target="tpu_custom_call" | custom-call | flops 167772160 | bytes 5242880 | tf_op jit(solution)/shard_map/recent_part/pallas_call | solution.py:426
  25.8 0.7 collective-permute-done.3.refs_1_
  26.5 4.8 %attend_pages.1 = (bf16[2,17,16,128]{3,2,1,0:T(8,128)(2,1)S(1)}, bf16[2,17,16,128]{3,2,1,0:T(8,128)(2,1)S(1)}, bf16[2,17,16,128]{3,2,1,0:T(8,128)(2,1)S(1)}, bf16[2,17,16,128]{3,2,1,0:T(8,128)(2,1)S(1)}) custom-call(s32[36]{0:T(128)S(1)} %get-tuple-element.71.slot_ref, s32[36]{0:T(128)S(1)} %get-tuple-element.70.valid_ref, ...), custom_call_target="tpu_custom_call" | custom-call | flops 150994944 | bytes 9437184 | tf_op jit(solution)/shard_map/attend_pages/pallas_call | solution.py:150
  31.3 1.8 %collective-permute-start.4 = (bf16[2,17,16,128]{3,2,1,0:T(8,128)(2,1)S(1)}, bf16[2,17,16,128]{3,2,1,0:T(8,128)(2,1)S(1)}, u32[]{:S(2)}, u32[]{:S(2)}) collective-permute-start(bf16[2,17,16,128]{3,2,1,0:T(8,128)(2,1)S(1)} %get-tuple-element.34), channel_id=1, source_target_pairs={{0,4},{4,0},{8,12},{12,8},{16,20},{20,16},{24,28},{28,24},{1,5},{5... | collective-permute-start | bytes 417800 | tf_op jit(solution)/shard_map/ppermute | solution.py:29
  33.4 3.9 %collective-permute-done.4.refs_1_ = bf16[2,17,16,128]{3,2,1,0:T(8,128)(2,1)S(1)} collective-permute-done((bf16[2,17,16,128]{3,2,1,0:T(8,128)(2,1)S(1)}, bf16[2,17,16,128]{3,2,1,0:T(8,128)(2,1)S(1)}, u32[]{:S(2)}, u32[]{:S(2)}) %collective-permute-start.4) | collective-permute-done | bytes 139296 | tf_op jit(solution)/shard_map/ppermute | solution.py:29
  37.4 0.4 merge_parts.2
  38.1 2.2 %collective-permute-start.6 = (bf16[1,17,16,128]{3,2,1,0:T(8,128)(2,1)S(1)}, bf16[1,17,16,128]{3,2,1,0:T(8,128)(2,1)S(1)}, u32[]{:S(2)}, u32[]{:S(2)}) collective-permute-start(bf16[1,17,16,128]{3,2,1,0:T(8,128)(2,1)S(1)} %get-tuple-element.36), channel_id=1, source_target_pairs={{0,24},{4,28},{8,16},{12,20},{16,8},{20,12},{24,0},{28,4},{1,25},{... | collective-permute-start | bytes 208904 | tf_op jit(solution)/shard_map/ppermute | solution.py:29
  40.2 0.4 merge_parts.3
  40.7 1.2 collective-permute-start.8
  41.9 0.9 constant_dynamic-slice_fusion.input_ref
  42.8 0.5 collective-permute-done.5.refs_0_
  43.3 1.0 collective-permute-done.6.refs_1_
  44.3 0.8 collective-permute-done.8.refs_3_
  45.1 4.7 %project_out.1 = (f32[32,1280]{1,0:T(8,128)S(1)}, bf16[3,32,1280]{2,1,0:T(8,128)(2,1)S(1)}) custom-call(s32[1]{0:T(128)} %bitcast.part_ref, bf16[32,1280]{1,0:T(8,128)(2,1)S(1)} %constant_dynamic-slice_fusion.input_ref, bf16[1024,5120]{1,0:T(8,128)(2,1)} %weight_hbm.3, bf16[1,17,16,128]{3,2,1,0:T(8,128)(2,1)S(1)} %collective-permute-done.5.refs_0_, ...), custom_call_target="tpu_custom_call" | custom-call | flops 335544320 | bytes 10485760 | tf_op jit(solution)/shard_map/project_out/pallas_call | solution.py:493
  49.9 1.7 %collective-permute-start.11 = (bf16[32,1280]{1,0:T(8,128)(2,1)S(1)}, bf16[32,1280]{1,0:T(8,128)(2,1)S(1)}, u32[]{:S(2)}, u32[]{:S(2)}) collective-permute-start(bf16[32,1280]{1,0:T(8,128)(2,1)S(1)} %get-tuple-element.61), channel_id=1, source_target_pairs={{0,3},{1,2},{2,1},{3,0},{4,7},{5,6},{6,5},{7,4},{8,11},{9,10},{10,... | collective-permute-start | bytes 245768 | tf_op jit(solution)/shard_map/ppermute | solution.py:29
  52.1 2.4 %collective-permute-done.11 = bf16[32,1280]{1,0:T(8,128)(2,1)S(1)} collective-permute-done((bf16[32,1280]{1,0:T(8,128)(2,1)S(1)}, bf16[32,1280]{1,0:T(8,128)(2,1)S(1)}, u32[]{:S(2)}, u32[]{:S(2)}) %collective-permute-start.11) | collective-permute-done | bytes 81952 | tf_op jit(solution)/shard_map/ppermute | solution.py:29
  54.4 2.1 %collective-permute-done.10 = bf16[32,1280]{1,0:T(8,128)(2,1)S(1)} collective-permute-done((bf16[32,1280]{1,0:T(8,128)(2,1)S(1)}, bf16[32,1280]{1,0:T(8,128)(2,1)S(1)}, u32[]{:S(2)}, u32[]{:S(2)}) %collective-permute-start.10) | collective-permute-done | bytes 81952 | tf_op jit(solution)/shard_map/ppermute | solution.py:29
  56.5 1.2 collective-permute-start.12
  57.8 1.4 %collective-permute-start.16 = (bf16[32,1280]{1,0:T(8,128)(2,1)S(1)}, bf16[32,1280]{1,0:T(8,128)(2,1)S(1)}, u32[]{:S(2)}, u32[]{:S(2)}) collective-permute-start(bf16[32,1280]{1,0:T(8,128)(2,1)S(1)} %add_convert_fusion.5), channel_id=1, source_target_pairs={{0,24},{4,28},{8,16},{12,20},{16,8},{20,12},{24,0},{28,4},{1,25},{... | collective-permute-start | bytes 245768 | tf_op jit(solution)/shard_map/ppermute | solution.py:29
  59.2 0.9 collective-permute-start.15
  60.1 1.0 collective-permute-done.12
  61.1 1.7 %collective-permute-start.14 = (bf16[64,640]{1,0:T(8,128)(2,1)S(1)}, bf16[64,640]{1,0:T(8,128)(2,1)S(1)}, u32[]{:S(2)}, u32[]{:S(2)}) collective-permute-start(bf16[64,640]{1,0:T(8,128)(2,1)S(1)} %get-tuple-element.45), channel_id=1, source_target_pairs={{0,2},{1,3},{2,0},{3,1},{4,6},{5,7},{6,4},{7,5},{8,10},{9,11},{10,... | collective-permute-start | bytes 245768 | tf_op jit(solution)/shard_map/ppermute | solution.py:29
  62.7 1.5 %collective-permute-start.13 = (bf16[64,640]{1,0:T(8,128)(2,1)S(1)}, bf16[64,640]{1,0:T(8,128)(2,1)S(1)}, u32[]{:S(2)}, u32[]{:S(2)}) collective-permute-start(bf16[64,640]{1,0:T(8,128)(2,1)S(1)} %get-tuple-element.43), channel_id=1, source_target_pairs={{0,4},{4,0},{8,12},{12,8},{16,20},{20,16},{24,28},{28,24},{1,5},{5... | collective-permute-start | bytes 245768 | tf_op jit(solution)/shard_map/ppermute | solution.py:29
  64.3 3.3 %collective-permute-done.15 = bf16[32,1280]{1,0:T(8,128)(2,1)S(1)} collective-permute-done((bf16[32,1280]{1,0:T(8,128)(2,1)S(1)}, bf16[32,1280]{1,0:T(8,128)(2,1)S(1)}, u32[]{:S(2)}, u32[]{:S(2)}) %collective-permute-start.15) | collective-permute-done | bytes 81952 | tf_op jit(solution)/shard_map/ppermute | solution.py:29
  67.7 1.7 %collective-permute-start.21 = (bf16[64,640]{1,0:T(8,128)(2,1)S(1)}, bf16[64,640]{1,0:T(8,128)(2,1)S(1)}, u32[]{:S(2)}, u32[]{:S(2)}) collective-permute-start(bf16[64,640]{1,0:T(8,128)(2,1)S(1)} %get-tuple-element.66), channel_id=1, source_target_pairs={{0,2},{1,3},{2,0},{3,1},{4,6},{5,7},{6,4},{7,5},{8,10},{9,11},{10,... | collective-permute-start | bytes 245768 | tf_op jit(solution)/shard_map/ppermute | solution.py:29
  69.4 1.2 collective-permute-start.19
  70.7 0.9 collective-permute-start.18
  71.6 0.5 collective-permute-start.17
  72.0 2.2 %collective-permute-done.19 = bf16[64,640]{1,0:T(8,128)(2,1)S(1)} collective-permute-done((bf16[64,640]{1,0:T(8,128)(2,1)S(1)}, bf16[64,640]{1,0:T(8,128)(2,1)S(1)}, u32[]{:S(2)}, u32[]{:S(2)}) %collective-permute-start.19) | collective-permute-done | bytes 81952 | tf_op jit(solution)/shard_map/ppermute | solution.py:29
  74.2 0.8 collective-permute-start.20
  75.0 1.0 collective-permute-start.22
  76.0 1.5 %collective-permute-done.18.refs_3_ = bf16[2,64,640]{2,1,0:T(8,128)(2,1)S(1)} collective-permute-done((bf16[2,64,640]{2,1,0:T(8,128)(2,1)S(1)}, bf16[2,64,640]{2,1,0:T(8,128)(2,1)S(1)}, u32[]{:S(2)}, u32[]{:S(2)}) %collective-permute-start.18) | collective-permute-done | bytes 163872 | tf_op jit(solution)/shard_map/ppermute | solution.py:29
  77.9 1.8 %collective-permute-done.20.refs_5_ = bf16[128,640]{1,0:T(8,128)(2,1)S(1)} collective-permute-done((bf16[128,640]{1,0:T(8,128)(2,1)S(1)}, bf16[128,640]{1,0:T(8,128)(2,1)S(1)}, u32[]{:S(2)}, u32[]{:S(2)}) %collective-permute-start.20) | collective-permute-done | bytes 163872 | tf_op jit(solution)/shard_map/ppermute | solution.py:29
  79.6 0.8 collective-permute-done.22.refs_7_
  80.6 5.0 %gate_up_half.1 = (f32[256,1024]{1,0:T(8,128)S(1)}, f32[256,1024]{1,0:T(8,128)S(1)}, f32[256,128]{1,0:T(8,128)S(1)}) custom-call(s32[1]{0:T(128)} %bitcast.part_ref, bf16[2,256,1280]{2,1,0:T(8,128)(2,1)S(1)} %join_groups.1.refs_0_.rows_ref, f32[4,1,1280]{2,1,0:T(1,128)S(1)} %bitcast.24, bf16[5120,1024]{1,0:T(8,128)(2,1)} %gate_hbm.3, bf16[5120,1024]{1,0:T(8,128)(2,1)} %up_hbm.3), custom_call_target="tpu_custom_call" | custom-call | flops 2684354560 | bytes 12582912 | tf_op jit(solution)/shard_map/gate_up_half/pallas_call | solution.py:610
  85.7 7.2 %gate_up_rest.1 = (bf16[256,1024]{1,0:T(8,128)(2,1)S(1)}, bf16[2,256,1280]{2,1,0:T(8,128)(2,1)S(1)}) custom-call(s32[1]{0:T(128)} %bitcast.part_ref, bf16[2,256,1280]{2,1,0:T(8,128)(2,1)S(1)} %collective-permute-done.23.refs_1_.rows_ref, f32[4,1,1280]{2,1,0:T(1,128)S(1)} %bitcast.25, f32[256,1024]{1,0:T(8,128)S(1)} %get-tuple-element.49.old_gate_ref, ...), custom_call_target="tpu_custom_call" | custom-call | flops 4026531840 | bytes 15728640 | tf_op jit(solution)/shard_map/gate_up_rest/pallas_call | solution.py:680
  92.9 0.6 collective-permute-start.24
  93.4 3.7 %down_half.1.own_ref = bf16[2,256,1280]{2,1,0:T(8,128)(2,1)S(1)} custom-call(s32[1]{0:T(128)} %bitcast.part_ref, bf16[256,1024]{1,0:T(8,128)(2,1)S(1)} %get-tuple-element.52.activation_ref, bf16[1024,5120]{1,0:T(8,128)(2,1)} %down_hbm.3), custom_call_target="tpu_custom_call" | custom-call | flops 1342177280 | bytes 5242880 | tf_op jit(solution)/shard_map/down_half/pallas_call | solution.py:719
  97.5 1.4 %collective-permute-start.28 = (bf16[128,1280]{1,0:T(8,128)(2,1)S(1)}, bf16[128,1280]{1,0:T(8,128)(2,1)S(1)}, u32[]{:S(2)}, u32[]{:S(2)}) collective-permute-start(bf16[128,1280]{1,0:T(8,128)(2,1)S(1)} %get-tuple-element.57), channel_id=1, source_target_pairs={{0,2},{1,5},{2,0},{3,7},{4,6},{5,1},{6,4},{7,3},{8,10},{9,13},{10,... | collective-permute-start | bytes 983048 | tf_op jit(solution)/shard_map/ppermute | solution.py:40
  98.9 0.7 collective-permute-start.25
  99.6 5.0 %collective-permute-done.28 = bf16[128,1280]{1,0:T(8,128)(2,1)S(1)} collective-permute-done((bf16[128,1280]{1,0:T(8,128)(2,1)S(1)}, bf16[128,1280]{1,0:T(8,128)(2,1)S(1)}, u32[]{:S(2)}, u32[]{:S(2)}) %collective-permute-start.28) | collective-permute-done | bytes 327712 | tf_op jit(solution)/shard_map/ppermute | solution.py:40
  104.7 1.0 collective-permute-start.29
  105.7 3.9 %collective-permute-done.25 = bf16[128,1280]{1,0:T(8,128)(2,1)S(1)} collective-permute-done((bf16[128,1280]{1,0:T(8,128)(2,1)S(1)}, bf16[128,1280]{1,0:T(8,128)(2,1)S(1)}, u32[]{:S(2)}, u32[]{:S(2)}) %collective-permute-start.25) | collective-permute-done | bytes 327712 | tf_op jit(solution)/shard_map/ppermute | solution.py:40
  109.7 1.0 collective-permute-start.26
  110.8 2.2 %collective-permute-start.31 = (bf16[32,1280]{1,0:T(8,128)(2,1)S(1)}, bf16[32,1280]{1,0:T(8,128)(2,1)S(1)}, u32[]{:S(2)}, u32[]{:S(2)}) collective-permute-start(bf16[32,1280]{1,0:T(8,128)(2,1)S(1)} %get-tuple-element.63), channel_id=1, source_target_pairs={{0,24},{4,28},{8,16},{12,20},{16,8},{20,12},{24,0},{28,4},{1,25},{... | collective-permute-start | bytes 245768 | tf_op jit(solution)/shard_map/ppermute | solution.py:29
  113.0 1.8 %collective-permute-start.30 = (bf16[32,1280]{1,0:T(8,128)(2,1)S(1)}, bf16[32,1280]{1,0:T(8,128)(2,1)S(1)}, u32[]{:S(2)}, u32[]{:S(2)}) collective-permute-start(bf16[32,1280]{1,0:T(8,128)(2,1)S(1)} %get-tuple-element.64), channel_id=1, source_target_pairs={{0,16},{4,20},{8,24},{12,28},{16,0},{20,4},{24,8},{28,12},{1,17},{... | collective-permute-start | bytes 245768 | tf_op jit(solution)/shard_map/ppermute | solution.py:29
  115.2 1.8 %collective-permute-start.27 = (bf16[32,1280]{1,0:T(8,128)(2,1)S(1)}, bf16[32,1280]{1,0:T(8,128)(2,1)S(1)}, u32[]{:S(2)}, u32[]{:S(2)}) collective-permute-start(bf16[32,1280]{1,0:T(8,128)(2,1)S(1)} %slice.75), channel_id=1, source_target_pairs={{0,8},{4,12},{8,0},{12,4},{16,24},{20,28},{24,16},{28,20},{1,9},{5... | collective-permute-start | bytes 245768 | tf_op jit(solution)/shard_map/ppermute | solution.py:29
  117.0 0.7 collective-permute-done.31.refs_1_
  117.7 3.3 %collective-permute-done.30.refs_0_ = bf16[32,1280]{1,0:T(8,128)(2,1)S(1)} collective-permute-done((bf16[32,1280]{1,0:T(8,128)(2,1)S(1)}, bf16[32,1280]{1,0:T(8,128)(2,1)S(1)}, u32[]{:S(2)}, u32[]{:S(2)}) %collective-permute-start.30) | collective-permute-done | bytes 81952 | tf_op jit(solution)/shard_map/ppermute | solution.py:29
  121.3 1.2 collective-permute-start.33
  122.5 0.6 collective-permute-start.32
  123.1 0.7 assemble.2
  123.9 2.1 %collective-permute-done.34.refs_3_ = bf16[32,1280]{1,0:T(8,128)(2,1)S(1)} collective-permute-done((bf16[32,1280]{1,0:T(8,128)(2,1)S(1)}, bf16[32,1280]{1,0:T(8,128)(2,1)S(1)}, u32[]{:S(2)}, u32[]{:S(2)}) %collective-permute-start.34) | collective-permute-done | bytes 81952 | tf_op jit(solution)/shard_map/ppermute | solution.py:29
  126.0 1.2 collective-permute-done.33.refs_2_
  127.2 0.7 assemble.3
  (71 shorter events, 3.3 us)
Async XLA Ops:
  0.6 25.8 %slice-start = ((s8[4718592]{0:T(1024)(128)(4,1)}), s8[4194304]{0:T(1024)(128)(4,1)S(1)}, s32[]{:S(2)}) async-start(s8[4718592]{0:T(1024)(128)(4,1)} %bitcast.20), calls=%async_computation | async-start | bytes 8388608
  0.6 25.8 %slice-start.2 = ((s8[4718592]{0:T(1024)(128)(4,1)}), s8[4194304]{0:T(1024)(128)(4,1)S(1)}, s32[]{:S(2)}) async-start(s8[4718592]{0:T(1024)(128)(4,1)} %bitcast.22), calls=%async_computation.2 | async-start | bytes 8388608
  0.7 19.4 %copy-start.3 = (s32[64]{0:T(128)S(1)}, s32[64]{0:T(128)}, u32[]{:S(2)}) copy-start(s32[64]{0:T(128)} %param.28) | copy-start | bytes 772
  0.7 19.4 %copy-start.4 = (s32[64]{0:T(128)S(1)}, s32[64]{0:T(128)}, u32[]{:S(2)}) copy-start(s32[64]{0:T(128)} %param.31) | copy-start | bytes 772
  0.7 19.4 %copy-start.5 = (s32[36]{0:T(128)S(1)}, s32[36]{0:T(128)}, u32[]{:S(2)}) copy-start(s32[36]{0:T(128)} %param.29) | copy-start | bytes 436
  0.7 19.6 %copy-start.6 = (s32[36]{0:T(128)S(1)}, s32[36]{0:T(128)}, u32[]{:S(2)}) copy-start(s32[36]{0:T(128)} %param.30) | copy-start | bytes 436
  0.7 25.8 %slice-start.1 = ((s8[4718592]{0:T(1024)(128)(4,1)}), s8[524288]{0:T(1024)(128)(4,1)S(1)}, s32[]{:S(2)}) async-start(s8[4718592]{0:T(1024)(128)(4,1)} %bitcast.20), calls=%async_computation.1 | async-start | bytes 1048576
  0.7 25.8 %slice-start.3 = ((s8[4718592]{0:T(1024)(128)(4,1)}), s8[524288]{0:T(1024)(128)(4,1)S(1)}, s32[]{:S(2)}) async-start(s8[4718592]{0:T(1024)(128)(4,1)} %bitcast.22), calls=%async_computation.3 | async-start | bytes 1048576
  7.5 10.9 %collective-permute-start.2 = (bf16[16,16,128]{2,1,0:T(8,128)(2,1)}, bf16[16,16,128]{2,1,0:T(8,128)(2,1)S(1)}, u32[]{:S(2)}, u32[]{:S(2)}) collective-permute-start(bf16[16,16,128]{2,1,0:T(8,128)(2,1)} %get-tuple-element.30), channel_id=1, source_target_pairs={{0,24},{4,28},{8,16},{12,20},{16,8},{20,12},{24,0},{28,4},{1,25},{... | collective-permute-start | bytes 196616 | tf_op jit(solution)/shard_map/ppermute | solution.py:29
  12.7 5.8 %collective-permute-start.1 = (bf16[16,16,128]{2,1,0:T(8,128)(2,1)}, bf16[16,16,128]{2,1,0:T(8,128)(2,1)S(1)}, u32[]{:S(2)}, u32[]{:S(2)}) collective-permute-start(bf16[16,16,128]{2,1,0:T(8,128)(2,1)} %get-tuple-element.30), channel_id=1, source_target_pairs={{0,16},{4,20},{8,24},{12,28},{16,0},{20,4},{24,8},{28,12},{1,17},{... | collective-permute-start | bytes 196616 | tf_op jit(solution)/shard_map/ppermute | solution.py:29
  12.7 4.5 %collective-permute-start = (bf16[16,16,128]{2,1,0:T(8,128)(2,1)}, bf16[16,16,128]{2,1,0:T(8,128)(2,1)S(1)}, u32[]{:S(2)}, u32[]{:S(2)}) collective-permute-start(bf16[16,16,128]{2,1,0:T(8,128)(2,1)} %get-tuple-element.30), channel_id=1, source_target_pairs={{0,8},{4,12},{8,0},{12,4},{16,24},{20,28},{24,16},{28,20},{1,9},{5... | collective-permute-start | bytes 196616 | tf_op jit(solution)/shard_map/ppermute | solution.py:29
  18.5 7.9 %collective-permute-start.3 = (bf16[64,16,128]{2,1,0:T(8,128)(2,1)S(1)}, bf16[64,16,128]{2,1,0:T(8,128)(2,1)S(1)}, u32[]{:S(2)}, u32[]{:S(2)}) collective-permute-start(bf16[64,16,128]{2,1,0:T(8,128)(2,1)S(1)} %constant_dynamic-update-slice_fusion.query_ref.refs_0_), channel_id=1, source_target_pairs={{0,4},{4,0},{8,12},{12,8},{16,20},{20,16},{24,28},{28,24},{1,5},{5... | collective-permute-start | bytes 786440 | tf_op jit(solution)/shard_map/ppermute | solution.py:29
  20.3 1.0 copy-start
  21.3 0.8 copy-start.2
  31.3 6.1 %collective-permute-start.4 = (bf16[2,17,16,128]{3,2,1,0:T(8,128)(2,1)S(1)}, bf16[2,17,16,128]{3,2,1,0:T(8,128)(2,1)S(1)}, u32[]{:S(2)}, u32[]{:S(2)}) collective-permute-start(bf16[2,17,16,128]{3,2,1,0:T(8,128)(2,1)S(1)} %get-tuple-element.34), channel_id=1, source_target_pairs={{0,4},{4,0},{8,12},{12,8},{16,20},{20,16},{24,28},{28,24},{1,5},{5... | collective-permute-start | bytes 417800 | tf_op jit(solution)/shard_map/ppermute | solution.py:29
  33.1 7.2 %collective-permute-start.7 = (bf16[2,17,16,128]{3,2,1,0:T(8,128)(2,1)S(1)}, bf16[2,17,16,128]{3,2,1,0:T(8,128)(2,1)S(1)}, u32[]{:S(2)}, u32[]{:S(2)}) collective-permute-start(bf16[2,17,16,128]{3,2,1,0:T(8,128)(2,1)S(1)} %get-tuple-element.38), channel_id=1, source_target_pairs={{0,4},{4,0},{8,12},{12,8},{16,20},{20,16},{24,28},{28,24},{1,5},{5... | collective-permute-start | bytes 417800 | tf_op jit(solution)/shard_map/ppermute | solution.py:29
  37.8 5.4 %collective-permute-start.5 = (bf16[1,17,16,128]{3,2,1,0:T(8,128)(2,1)S(1)}, bf16[1,17,16,128]{3,2,1,0:T(8,128)(2,1)S(1)}, u32[]{:S(2)}, u32[]{:S(2)}) collective-permute-start(bf16[1,17,16,128]{3,2,1,0:T(8,128)(2,1)S(1)} %get-tuple-element.35), channel_id=1, source_target_pairs={{0,16},{4,20},{8,24},{12,28},{16,0},{20,4},{24,8},{28,12},{1,17},{... | collective-permute-start | bytes 208904 | tf_op jit(solution)/shard_map/ppermute | solution.py:29
  38.1 6.2 %collective-permute-start.6 = (bf16[1,17,16,128]{3,2,1,0:T(8,128)(2,1)S(1)}, bf16[1,17,16,128]{3,2,1,0:T(8,128)(2,1)S(1)}, u32[]{:S(2)}, u32[]{:S(2)}) collective-permute-start(bf16[1,17,16,128]{3,2,1,0:T(8,128)(2,1)S(1)} %get-tuple-element.36), channel_id=1, source_target_pairs={{0,24},{4,28},{8,16},{12,20},{16,8},{20,12},{24,0},{28,4},{1,25},{... | collective-permute-start | bytes 208904 | tf_op jit(solution)/shard_map/ppermute | solution.py:29
  40.7 4.4 %collective-permute-start.8 = (bf16[1,17,16,128]{3,2,1,0:T(8,128)(2,1)S(1)}, bf16[1,17,16,128]{3,2,1,0:T(8,128)(2,1)S(1)}, u32[]{:S(2)}, u32[]{:S(2)}) collective-permute-start(bf16[1,17,16,128]{3,2,1,0:T(8,128)(2,1)S(1)} %get-tuple-element.40), channel_id=1, source_target_pairs={{0,8},{4,12},{8,0},{12,4},{16,24},{20,28},{24,16},{28,20},{1,9},{5... | collective-permute-start | bytes 208904 | tf_op jit(solution)/shard_map/ppermute | solution.py:29
  49.8 30.8 %copy-start.1 = (f32[5120]{0:T(1024)S(1)}, f32[5120]{0:T(1024)}, u32[]{:S(2)}) copy-start(f32[5120]{0:T(1024)} %param.22) | copy-start | bytes 61444
  49.8 2.2 %collective-permute-start.9 = (bf16[32,1280]{1,0:T(8,128)(2,1)S(1)}, bf16[32,1280]{1,0:T(8,128)(2,1)S(1)}, u32[]{:S(2)}, u32[]{:S(2)}) collective-permute-start(bf16[32,1280]{1,0:T(8,128)(2,1)S(1)} %get-tuple-element.60), channel_id=1, source_target_pairs={{0,1},{1,0},{2,3},{3,2},{4,5},{5,4},{6,7},{7,6},{8,9},{9,8},{10,11... | collective-permute-start | bytes 245768 | tf_op jit(solution)/shard_map/ppermute | solution.py:29
  49.9 4.5 %collective-permute-start.11 = (bf16[32,1280]{1,0:T(8,128)(2,1)S(1)}, bf16[32,1280]{1,0:T(8,128)(2,1)S(1)}, u32[]{:S(2)}, u32[]{:S(2)}) collective-permute-start(bf16[32,1280]{1,0:T(8,128)(2,1)S(1)} %get-tuple-element.61), channel_id=1, source_target_pairs={{0,3},{1,2},{2,1},{3,0},{4,7},{5,6},{6,5},{7,4},{8,11},{9,10},{10,... | collective-permute-start | bytes 245768 | tf_op jit(solution)/shard_map/ppermute | solution.py:29
  51.6 4.8 %collective-permute-start.10 = (bf16[32,1280]{1,0:T(8,128)(2,1)S(1)}, bf16[32,1280]{1,0:T(8,128)(2,1)S(1)}, u32[]{:S(2)}, u32[]{:S(2)}) collective-permute-start(bf16[32,1280]{1,0:T(8,128)(2,1)S(1)} %get-tuple-element.62), channel_id=1, source_target_pairs={{0,2},{1,3},{2,0},{3,1},{4,6},{5,7},{6,4},{7,5},{8,10},{9,11},{10,... | collective-permute-start | bytes 245768 | tf_op jit(solution)/shard_map/ppermute | solution.py:29
  56.5 4.5 %collective-permute-start.12 = (bf16[32,1280]{1,0:T(8,128)(2,1)S(1)}, bf16[32,1280]{1,0:T(8,128)(2,1)S(1)}, u32[]{:S(2)}, u32[]{:S(2)}) collective-permute-start(bf16[32,1280]{1,0:T(8,128)(2,1)S(1)} %add_convert_fusion.5), channel_id=1, source_target_pairs={{0,8},{4,12},{8,0},{12,4},{16,24},{20,28},{24,16},{28,20},{1,9},{5... | collective-permute-start | bytes 245768 | tf_op jit(solution)/shard_map/ppermute | solution.py:29
  57.8 6.6 %collective-permute-start.16 = (bf16[32,1280]{1,0:T(8,128)(2,1)S(1)}, bf16[32,1280]{1,0:T(8,128)(2,1)S(1)}, u32[]{:S(2)}, u32[]{:S(2)}) collective-permute-start(bf16[32,1280]{1,0:T(8,128)(2,1)S(1)} %add_convert_fusion.5), channel_id=1, source_target_pairs={{0,24},{4,28},{8,16},{12,20},{16,8},{20,12},{24,0},{28,4},{1,25},{... | collective-permute-start | bytes 245768 | tf_op jit(solution)/shard_map/ppermute | solution.py:29
  59.2 8.5 %collective-permute-start.15 = (bf16[32,1280]{1,0:T(8,128)(2,1)S(1)}, bf16[32,1280]{1,0:T(8,128)(2,1)S(1)}, u32[]{:S(2)}, u32[]{:S(2)}) collective-permute-start(bf16[32,1280]{1,0:T(8,128)(2,1)S(1)} %add_convert_fusion.5), channel_id=1, source_target_pairs={{0,16},{4,20},{8,24},{12,28},{16,0},{20,4},{24,8},{28,12},{1,17},{... | collective-permute-start | bytes 245768 | tf_op jit(solution)/shard_map/ppermute | solution.py:29
  61.1 6.6 %collective-permute-start.14 = (bf16[64,640]{1,0:T(8,128)(2,1)S(1)}, bf16[64,640]{1,0:T(8,128)(2,1)S(1)}, u32[]{:S(2)}, u32[]{:S(2)}) collective-permute-start(bf16[64,640]{1,0:T(8,128)(2,1)S(1)} %get-tuple-element.45), channel_id=1, source_target_pairs={{0,2},{1,3},{2,0},{3,1},{4,6},{5,7},{6,4},{7,5},{8,10},{9,11},{10,... | collective-permute-start | bytes 245768 | tf_op jit(solution)/shard_map/ppermute | solution.py:29
  62.7 4.9 %collective-permute-start.13 = (bf16[64,640]{1,0:T(8,128)(2,1)S(1)}, bf16[64,640]{1,0:T(8,128)(2,1)S(1)}, u32[]{:S(2)}, u32[]{:S(2)}) collective-permute-start(bf16[64,640]{1,0:T(8,128)(2,1)S(1)} %get-tuple-element.43), channel_id=1, source_target_pairs={{0,4},{4,0},{8,12},{12,8},{16,20},{20,16},{24,28},{28,24},{1,5},{5... | collective-permute-start | bytes 245768 | tf_op jit(solution)/shard_map/ppermute | solution.py:29
  67.7 7.3 %collective-permute-start.21 = (bf16[64,640]{1,0:T(8,128)(2,1)S(1)}, bf16[64,640]{1,0:T(8,128)(2,1)S(1)}, u32[]{:S(2)}, u32[]{:S(2)}) collective-permute-start(bf16[64,640]{1,0:T(8,128)(2,1)S(1)} %get-tuple-element.66), channel_id=1, source_target_pairs={{0,2},{1,3},{2,0},{3,1},{4,6},{5,7},{6,4},{7,5},{8,10},{9,11},{10,... | collective-permute-start | bytes 245768 | tf_op jit(solution)/shard_map/ppermute | solution.py:29
  69.4 4.8 %collective-permute-start.19 = (bf16[64,640]{1,0:T(8,128)(2,1)S(1)}, bf16[64,640]{1,0:T(8,128)(2,1)S(1)}, u32[]{:S(2)}, u32[]{:S(2)}) collective-permute-start(bf16[64,640]{1,0:T(8,128)(2,1)S(1)} %get-tuple-element.67), channel_id=1, source_target_pairs={{0,4},{4,0},{8,12},{12,8},{16,20},{20,16},{24,28},{28,24},{1,5},{5... | collective-permute-start | bytes 245768 | tf_op jit(solution)/shard_map/ppermute | solution.py:29
  70.7 6.9 %collective-permute-start.18 = (bf16[2,64,640]{2,1,0:T(8,128)(2,1)S(1)}, bf16[2,64,640]{2,1,0:T(8,128)(2,1)S(1)}, u32[]{:S(2)}, u32[]{:S(2)}) collective-permute-start(bf16[2,64,640]{2,1,0:T(8,128)(2,1)S(1)} %pad_maximum_fusion.refs_2_), channel_id=1, source_target_pairs={{0,4},{4,0},{8,12},{12,8},{16,20},{20,16},{24,28},{28,24},{1,5},{5... | collective-permute-start | bytes 491528 | tf_op jit(solution)/shard_map/ppermute | solution.py:29
  71.6 6.3 %collective-permute-start.17 = (bf16[128,640]{1,0:T(8,128)(2,1)S(1)}, bf16[128,640]{1,0:T(8,128)(2,1)S(1)}, u32[]{:S(2)}, u32[]{:S(2)}) collective-permute-start(bf16[128,640]{1,0:T(8,128)(2,1)S(1)} %constant_dynamic-update-slice_fusion.4.refs_0_), channel_id=1, source_target_pairs={{0,2},{1,3},{2,0},{3,1},{4,6},{5,7},{6,4},{7,5},{8,10},{9,11},{10,... | collective-permute-start | bytes 491528 | tf_op jit(solution)/shard_map/ppermute | solution.py:29
  74.2 5.4 %collective-permute-start.20 = (bf16[128,640]{1,0:T(8,128)(2,1)S(1)}, bf16[128,640]{1,0:T(8,128)(2,1)S(1)}, u32[]{:S(2)}, u32[]{:S(2)}) collective-permute-start(bf16[128,640]{1,0:T(8,128)(2,1)S(1)} %pad_maximum_fusion.1.refs_4_), channel_id=1, source_target_pairs={{0,2},{1,3},{2,0},{3,1},{4,6},{5,7},{6,4},{7,5},{8,10},{9,11},{10,... | collective-permute-start | bytes 491528 | tf_op jit(solution)/shard_map/ppermute | solution.py:29
  75.0 5.4 %collective-permute-start.22 = (bf16[2,64,640]{2,1,0:T(8,128)(2,1)S(1)}, bf16[2,64,640]{2,1,0:T(8,128)(2,1)S(1)}, u32[]{:S(2)}, u32[]{:S(2)}) collective-permute-start(bf16[2,64,640]{2,1,0:T(8,128)(2,1)S(1)} %pad_maximum_fusion.2.refs_6_), channel_id=1, source_target_pairs={{0,4},{4,0},{8,12},{12,8},{16,20},{20,16},{24,28},{28,24},{1,5},{5... | collective-permute-start | bytes 491528 | tf_op jit(solution)/shard_map/ppermute | solution.py:29
  80.5 5.1 %collective-permute-start.23 = (bf16[2,256,1280]{2,1,0:T(8,128)(2,1)S(1)}, bf16[2,256,1280]{2,1,0:T(8,128)(2,1)S(1)}, u32[]{:S(2)}, u32[]{:S(2)}) collective-permute-start(bf16[2,256,1280]{2,1,0:T(8,128)(2,1)S(1)} %join_groups.1.refs_0_.rows_ref), channel_id=1, source_target_pairs={{0,1},{1,0},{2,3},{3,2},{4,5},{5,4},{6,7},{7,6},{8,9},{9,8},{10,11... | collective-permute-start | bytes 3932168 | tf_op jit(solution)/shard_map/ppermute | solution.py:29
  92.9 4.3 %collective-permute-start.24 = (bf16[2,256,1280]{2,1,0:T(8,128)(2,1)S(1)}, bf16[2,256,1280]{2,1,0:T(8,128)(2,1)S(1)}, u32[]{:S(2)}, u32[]{:S(2)}) collective-permute-start(bf16[2,256,1280]{2,1,0:T(8,128)(2,1)S(1)} %get-tuple-element.53), channel_id=1, source_target_pairs={{0,1},{1,0},{2,3},{3,2},{4,5},{5,4},{6,7},{7,6},{8,9},{9,8},{10,11... | collective-permute-start | bytes 3932168 | tf_op jit(solution)/shard_map/ppermute | solution.py:29
  97.5 7.1 %collective-permute-start.28 = (bf16[128,1280]{1,0:T(8,128)(2,1)S(1)}, bf16[128,1280]{1,0:T(8,128)(2,1)S(1)}, u32[]{:S(2)}, u32[]{:S(2)}) collective-permute-start(bf16[128,1280]{1,0:T(8,128)(2,1)S(1)} %get-tuple-element.57), channel_id=1, source_target_pairs={{0,2},{1,5},{2,0},{3,7},{4,6},{5,1},{6,4},{7,3},{8,10},{9,13},{10,... | collective-permute-start | bytes 983048 | tf_op jit(solution)/shard_map/ppermute | solution.py:40
  98.9 10.8 %collective-permute-start.25 = (bf16[128,1280]{1,0:T(8,128)(2,1)S(1)}, bf16[128,1280]{1,0:T(8,128)(2,1)S(1)}, u32[]{:S(2)}, u32[]{:S(2)}) collective-permute-start(bf16[128,1280]{1,0:T(8,128)(2,1)S(1)} %get-tuple-element.55), channel_id=1, source_target_pairs={{0,2},{1,5},{2,0},{3,7},{4,6},{5,1},{6,4},{7,3},{8,10},{9,13},{10,... | collective-permute-start | bytes 983048 | tf_op jit(solution)/shard_map/ppermute | solution.py:40
  104.7 6.0 %collective-permute-start.29 = (bf16[64,1280]{1,0:T(8,128)(2,1)S(1)}, bf16[64,1280]{1,0:T(8,128)(2,1)S(1)}, u32[]{:S(2)}, u32[]{:S(2)}) collective-permute-start(bf16[64,1280]{1,0:T(8,128)(2,1)S(1)} %slice.77), channel_id=1, source_target_pairs={{0,4},{1,3},{2,6},{3,1},{4,0},{5,7},{6,2},{7,5},{8,12},{9,11},{10,... | collective-permute-start | bytes 491528 | tf_op jit(solution)/shard_map/ppermute | solution.py:40
  109.7 5.4 %collective-permute-start.26 = (bf16[64,1280]{1,0:T(8,128)(2,1)S(1)}, bf16[64,1280]{1,0:T(8,128)(2,1)S(1)}, u32[]{:S(2)}, u32[]{:S(2)}) collective-permute-start(bf16[64,1280]{1,0:T(8,128)(2,1)S(1)} %slice.73), channel_id=1, source_target_pairs={{0,4},{1,3},{2,6},{3,1},{4,0},{5,7},{6,2},{7,5},{8,12},{9,11},{10,... | collective-permute-start | bytes 491528 | tf_op jit(solution)/shard_map/ppermute | solution.py:40
  110.8 6.9 %collective-permute-start.31 = (bf16[32,1280]{1,0:T(8,128)(2,1)S(1)}, bf16[32,1280]{1,0:T(8,128)(2,1)S(1)}, u32[]{:S(2)}, u32[]{:S(2)}) collective-permute-start(bf16[32,1280]{1,0:T(8,128)(2,1)S(1)} %get-tuple-element.63), channel_id=1, source_target_pairs={{0,24},{4,28},{8,16},{12,20},{16,8},{20,12},{24,0},{28,4},{1,25},{... | collective-permute-start | bytes 245768 | tf_op jit(solution)/shard_map/ppermute | solution.py:29
  113.0 8.0 %collective-permute-start.30 = (bf16[32,1280]{1,0:T(8,128)(2,1)S(1)}, bf16[32,1280]{1,0:T(8,128)(2,1)S(1)}, u32[]{:S(2)}, u32[]{:S(2)}) collective-permute-start(bf16[32,1280]{1,0:T(8,128)(2,1)S(1)} %get-tuple-element.64), channel_id=1, source_target_pairs={{0,16},{4,20},{8,24},{12,28},{16,0},{20,4},{24,8},{28,12},{1,17},{... | collective-permute-start | bytes 245768 | tf_op jit(solution)/shard_map/ppermute | solution.py:29
  115.2 6.0 %collective-permute-start.27 = (bf16[32,1280]{1,0:T(8,128)(2,1)S(1)}, bf16[32,1280]{1,0:T(8,128)(2,1)S(1)}, u32[]{:S(2)}, u32[]{:S(2)}) collective-permute-start(bf16[32,1280]{1,0:T(8,128)(2,1)S(1)} %slice.75), channel_id=1, source_target_pairs={{0,8},{4,12},{8,0},{12,4},{16,24},{20,28},{24,16},{28,20},{1,9},{5... | collective-permute-start | bytes 245768 | tf_op jit(solution)/shard_map/ppermute | solution.py:29
  121.2 4.8 %collective-permute-start.34 = (bf16[32,1280]{1,0:T(8,128)(2,1)S(1)}, bf16[32,1280]{1,0:T(8,128)(2,1)S(1)}, u32[]{:S(2)}, u32[]{:S(2)}) collective-permute-start(bf16[32,1280]{1,0:T(8,128)(2,1)S(1)} %add_convert_fusion.4.refs_0_), channel_id=1, source_target_pairs={{0,3},{1,2},{2,1},{3,0},{4,7},{5,6},{6,5},{7,4},{8,11},{9,10},{10,... | collective-permute-start | bytes 245768 | tf_op jit(solution)/shard_map/ppermute | solution.py:29
  121.3 6.0 %collective-permute-start.33 = (bf16[32,1280]{1,0:T(8,128)(2,1)S(1)}, bf16[32,1280]{1,0:T(8,128)(2,1)S(1)}, u32[]{:S(2)}, u32[]{:S(2)}) collective-permute-start(bf16[32,1280]{1,0:T(8,128)(2,1)S(1)} %add_convert_fusion.4.refs_0_), channel_id=1, source_target_pairs={{0,2},{1,3},{2,0},{3,1},{4,6},{5,7},{6,4},{7,5},{8,10},{9,11},{10,... | collective-permute-start | bytes 245768 | tf_op jit(solution)/shard_map/ppermute | solution.py:29
  122.5 4.7 %collective-permute-start.32 = (bf16[32,1280]{1,0:T(8,128)(2,1)S(1)}, bf16[32,1280]{1,0:T(8,128)(2,1)S(1)}, u32[]{:S(2)}, u32[]{:S(2)}) collective-permute-start(bf16[32,1280]{1,0:T(8,128)(2,1)S(1)} %add_convert_fusion.4.refs_0_), channel_id=1, source_target_pairs={{0,1},{1,0},{2,3},{3,2},{4,5},{5,4},{6,7},{7,6},{8,9},{9,8},{10,11... | collective-permute-start | bytes 245768 | tf_op jit(solution)/shard_map/ppermute | solution.py:29

commit v6 on v5

--- a/solution.py
+++ b/solution.py
@@ -229,33 +229,33 @@
         copy.start()
 
 
-def load_kernel(slots, by_rows, part_ref, source_ref, out_ref, sems):
-    size = out_ref.shape[1] if by_rows else out_ref.shape[2]
+def load_kernel(slots, part_ref, first_ref, second_ref, first_out, second_out, sems):
+    size = first_out.shape[1]
     copies = []
-    for i, slot in enumerate(slots):
-        at = pl.ds(pl.multiple_of((part_ref[0] ^ slot) * size, size), size)
-        source = source_ref.at[at] if by_rows else source_ref.at[:, at]
-        copies.append(pltpu.make_async_copy(source, out_ref.at[i], sems.at[i]))
+    for number, (source, out) in enumerate(((first_ref, first_out), (second_ref, second_out))):
+        for i, slot in enumerate(slots):
+            at = pl.ds(pl.multiple_of((part_ref[0] ^ slot) * size, size), size)
+            copies.append(pltpu.make_async_copy(source.at[at], out.at[i], sems.at[number, i]))
     start_all(copies)
     for copy in copies:
         copy.wait()
 
 
-def load(part, source, slots, size, by_rows, limit):
-    rows, columns = source.shape
-    block = (size, columns) if by_rows else (rows, size)
-    return pl.pallas_call(
-        functools.partial(load_kernel, slots, by_rows),
-        out_shape=jax.ShapeDtypeStruct((len(slots), *block), bf16),
-        in_specs=[smem, hbm],
-        out_specs=vmem,
-        scratch_shapes=[pltpu.SemaphoreType.DMA((len(slots),))],
-        compiler_params=pltpu.CompilerParams(vmem_limit_bytes=limit << 20),
+def load(part, first, second, slots, size):
+    columns = first.shape[1]
+    shape = jax.ShapeDtypeStruct((len(slots), size, columns), bf16)
+    return pl.pallas_call(
+        functools.partial(load_kernel, slots),
+        out_shape=(shape, shape),
+        in_specs=[smem, hbm, hbm],
+        out_specs=(vmem, vmem),
+        scratch_shapes=[pltpu.SemaphoreType.DMA((2, len(slots)))],
+        compiler_params=pltpu.CompilerParams(vmem_limit_bytes=34 << 20),
         cost_estimate=pl.CostEstimate(
-            flops=0, bytes_accessed=2 * len(slots) * block[0] * block[1], transcendentals=0
+            flops=0, bytes_accessed=4 * len(slots) * size * columns, transcendentals=0
         ),
         name="load",
-    )(part.reshape(1), source)
+    )(part.reshape(1), first, second)
 
 
 def query_kernel(
@@ -531,7 +531,7 @@
 
 
 def join_kernel(ways, near_count, *refs):
-    out_ref = refs[-1]
+    *refs, _, out_ref = refs
     half = refs[0].shape[1]
     row = 0
     for group in range(2):
@@ -546,31 +546,29 @@
         row += height
 
 
-def join_groups(near, far, ways):
+def join_groups(near, far, ways, after):
     pieces = near + far
     columns = pieces[0].shape[1] + pieces[ways].shape[2]
     all_rows = near[0].shape[0] + far[0].shape[0]
     return pl.pallas_call(
         functools.partial(join_kernel, ways, len(near)),
         out_shape=jax.ShapeDtypeStruct((ways, all_rows, columns), bf16),
-        in_specs=[vmem] * len(pieces),
+        in_specs=[vmem] * len(pieces) + [hbm],
         out_specs=vmem,
         compiler_params=pltpu.CompilerParams(vmem_limit_bytes=8 << 20),
         cost_estimate=pl.CostEstimate(
             flops=0, bytes_accessed=4 * ways * all_rows * columns, transcendentals=0
         ),
         name="join_groups",
-    )(*pieces)
-
-
-def gate_up_copies(part, core, ways, quarter, gate_hbm, up_hbm, gate_buf, up_buf, sems):
+    )(*pieces, after)
+
+
+def row_copies(part, core, hbm_ref, buf, sems):
+    ways, size = buf.shape[:2]
     copies = []
     for way in range(ways):
-        at = pl.multiple_of((part ^ (way * CORES + core)) * quarter, quarter)
-        copies.append(
-            pltpu.make_async_copy(gate_hbm.at[pl.ds(at, quarter)], gate_buf.at[way], sems.at[0, way])
-        )
-        copies.append(pltpu.make_async_copy(up_hbm.at[pl.ds(at, quarter)], up_buf.at[way], sems.at[1, way]))
+        at = pl.ds(pl.multiple_of((part ^ (way * CORES + core)) * size, size), size)
+        copies.append(pltpu.make_async_copy(hbm_ref.at[at], buf.at[way], sems.at[way]))
     return copies
 
 
@@ -581,55 +579,54 @@
 
 
 def gate_up_kernel(
-    core, part_ref, rows_ref, gain_ref, gate_hbm, up_hbm, gate_ref, up_ref, square_ref,
-    gate_buf, up_buf, scaled_ref, sems,
+    part_ref, rows_ref, gain_ref, gate_in, up_in, gate_hbm, gate_ref, up_ref, square_ref, next_ref,
+    scaled_ref, next_sems,
 ):
-    ways, _, quarter = rows_ref.shape
+    ways = rows_ref.shape[0]
     part = part_ref[0]
-    copies = gate_up_copies(part, core, ways, quarter, gate_hbm, up_hbm, gate_buf, up_buf, sems)
-    start_all(copies)
+    later = row_copies(part, 1, gate_hbm, next_ref, next_sems)
+    start_all(later)
     square = 0.0
     for way in range(ways):
-        scaled, squares = scaled_rows(part, core, way, rows_ref, gain_ref)
+        scaled, squares = scaled_rows(part, 0, way, rows_ref, gain_ref)
         scaled_ref[way] = scaled
         square = square + squares
     square_ref[...] = jnp.broadcast_to(square, square_ref.shape)
     for way in range(ways):
-        for copy, buf, out in (
-            (copies[2 * way], gate_buf, gate_ref),
-            (copies[2 * way + 1], up_buf, up_ref),
-        ):
-            copy.wait()
-            product = jnp.dot(scaled_ref[way], buf[way], preferred_element_type=f32)
-            out[...] = product if way == 0 else out[...] + product
-
-
-def gate_up_half(part, core, rows, gains, w_gate, w_up):
+        product = jnp.dot(scaled_ref[way], gate_in[way], preferred_element_type=f32)
+        gate_ref[...] = product if way == 0 else gate_ref[...] + product
+    for way in range(ways):
+        product = jnp.dot(scaled_ref[way], up_in[way], preferred_element_type=f32)
+        up_ref[...] = product if way == 0 else up_ref[...] + product
+    for copy in later:
+        copy.wait()
+
+
+def gate_up_half(part, rows, gains, gate_first, up_first, w_gate):
     ways, all_rows, quarter = rows.shape
     hidden = w_gate.shape[1]
     return pl.pallas_call(
-        functools.partial(gate_up_kernel, core),
+        gate_up_kernel,
         out_shape=(
             jax.ShapeDtypeStruct((all_rows, hidden), f32),
             jax.ShapeDtypeStruct((all_rows, hidden), f32),
             jax.ShapeDtypeStruct((all_rows, 128), f32),
-        ),
-        in_specs=[smem, vmem, vmem, hbm, hbm],
-        out_specs=(vmem, vmem, vmem),
+            jax.ShapeDtypeStruct((ways, quarter, hidden), bf16),
+        ),
+        in_specs=[smem, vmem, vmem, vmem, vmem, hbm],
+        out_specs=(vmem, vmem, vmem, vmem),
         scratch_shapes=[
-            pltpu.VMEM((ways, quarter, hidden), bf16),
-            pltpu.VMEM((ways, quarter, hidden), bf16),
             pltpu.VMEM(rows.shape, bf16),
-            pltpu.SemaphoreType.DMA((2, ways)),
+            pltpu.SemaphoreType.DMA((ways,)),
         ],
-        compiler_params=pltpu.CompilerParams(vmem_limit_bytes=46 << 20),
+        compiler_params=pltpu.CompilerParams(vmem_limit_bytes=34 << 20),
         cost_estimate=pl.CostEstimate(
             flops=4 * rows.size * hidden,
             bytes_accessed=4 * ways * quarter * hidden + 8 * all_rows * hidden,
             transcendentals=0,
         ),
         name="gate_up_half",
-    )(part.reshape(1), rows, gains, w_gate, w_up)
+    )(part.reshape(1), rows, gains, gate_first, up_first, w_gate)
 
 
 def down_copies(part, core, ways, quarter, down_hbm, down_buf, sems):
@@ -643,12 +640,12 @@
 
 
 def rest_kernel(
-    width, part_ref, rows_ref, gain_ref, old_gate_ref, old_up_ref, square_ref, gate_hbm, up_hbm, down_hbm,
-    activation_ref, term_ref, gate_buf, up_buf, down_buf, scaled_ref, gate_ref, up_ref, sems, down_sems,
+    width, part_ref, rows_ref, gain_ref, old_gate_ref, old_up_ref, square_ref, gate_buf, up_hbm, down_hbm,
+    activation_ref, term_ref, up_buf, down_buf, scaled_ref, gate_ref, up_ref, sems, down_sems,
 ):
     ways, _, quarter = rows_ref.shape
     part = part_ref[0]
-    copies = gate_up_copies(part, 1, ways, quarter, gate_hbm, up_hbm, gate_buf, up_buf, sems)
+    copies = row_copies(part, 1, up_hbm, up_buf, sems)
     later = down_copies(part, 1, ways, quarter, down_hbm, down_buf, down_sems)
     start_all(copies + later)
     square = square_ref[:, :1]
@@ -658,13 +655,12 @@
         square = square + squares
     factor = lax.rsqrt(square * (1.0 / width) + norm_eps)
     for way in range(ways):
-        for copy, buf, old, out in (
-            (copies[2 * way], gate_buf, old_gate_ref, gate_ref),
-            (copies[2 * way + 1], up_buf, old_up_ref, up_ref),
-        ):
-            copy.wait()
-            product = jnp.dot(scaled_ref[way], buf[way], preferred_element_type=f32)
-            out[...] = (old if way == 0 else out)[...] + product
+        product = jnp.dot(scaled_ref[way], gate_buf[way], preferred_element_type=f32)
+        gate_ref[...] = (old_gate_ref if way == 0 else gate_ref)[...] + product
+    for way in range(ways):
+        copies[way].wait()
+        product = jnp.dot(scaled_ref[way], up_buf[way], preferred_element_type=f32)
+        up_ref[...] = (old_up_ref if way == 0 else up_ref)[...] + product
     gate = gate_ref[...] * factor
     up = up_ref[...] * factor
     activation_ref[...] = (gate / (1.0 + jnp.exp(-gate)) * up).astype(bf16)
@@ -674,33 +670,32 @@
         term_ref[way] = product.astype(bf16)
 
 
-def gate_up_rest(part, rows, gains, w_gate, w_up, w_down, sums, width):
+def gate_up_rest(part, rows, gains, w_up, w_down, sums, width):
     ways, all_rows, quarter = rows.shape
-    hidden = w_gate.shape[1]
+    hidden = w_up.shape[1]
     return pl.pallas_call(
         functools.partial(rest_kernel, width),
         out_shape=(
             jax.ShapeDtypeStruct((all_rows, hidden), bf16),
             jax.ShapeDtypeStruct((ways, all_rows, quarter), bf16),
         ),
-        in_specs=[smem, vmem, vmem, vmem, vmem, vmem, hbm, hbm, hbm],
+        in_specs=[smem] + [vmem] * 6 + [hbm, hbm],
         out_specs=(vmem, vmem),
         scratch_shapes=[
-            pltpu.VMEM((ways, quarter, hidden), bf16),
             pltpu.VMEM((ways, quarter, hidden), bf16),
             pltpu.VMEM((ways, hidden, quarter), bf16),
             pltpu.VMEM(rows.shape, bf16),
             pltpu.VMEM((all_rows, hidden), f32),
             pltpu.VMEM((all_rows, hidden), f32),
-            pltpu.SemaphoreType.DMA((2, ways)),
+            pltpu.SemaphoreType.DMA((ways,)),
             pltpu.SemaphoreType.DMA((ways,)),
         ],
-        compiler_params=pltpu.CompilerParams(vmem_limit_bytes=40 << 20),
+        compiler_params=pltpu.CompilerParams(vmem_limit_bytes=36 << 20),
         cost_estimate=pl.CostEstimate(
             flops=6 * rows.size * hidden, bytes_accessed=6 * ways * quarter * hidden, transcendentals=0
         ),
         name="gate_up_rest",
-    )(part.reshape(1), rows, gains, *sums, w_gate, w_up, w_down)
+    )(part.reshape(1), rows, gains, *sums, w_up, w_down)
 
 
 def down_kernel(part_ref, activation_ref, down_hbm, term_ref, down_buf, sems):
@@ -883,9 +878,13 @@
     layers.append(recent)
     own_input = lax.dynamic_slice_in_dim(token_inputs.reshape(rows, width), part * quarter, quarter, 1)
     own_term, terms = project_out(part, layers, own_input, w_output, tp, kv_local)
-    total = own_term
-    for slot in range(1, tp):
-        total = total + swap(terms[slot - 1], "tp", slot).astype(f32)
+    same = [own_term] + [terms[CORES * k - 1] for k in range(1, ways)]
+    across_cores = jnp.stack([terms[CORES * k] for k in range(ways)])
+    arrived = swap(across_cores, "tp", 1)
+    sums = [same[k].astype(f32) + arrived[k].astype(f32) for k in range(ways)]
+    total = sums[0]
+    for k in range(1, ways):
+        total = total + swap(sums[k].astype(bf16), "tp", CORES * k).astype(f32)
     own_attended = total.astype(bf16)
 
     half = (quarter + 255) // 256 * 128
@@ -908,13 +907,14 @@
     near, far = lax.optimization_barrier((near, far))
     near = spread_second(*near)
     far = spread_second(*spread_first(jnp.concatenate(far, axis=0)))
-    both = join_groups(near, far, ways)
+    gate_first, up_first = load(part, w_gate, w_up, tuple(range(0, tp, CORES)), quarter)
+    both = join_groups(near, far, ways, gate_first)
     other = swap(both, "tp", 1)
     all_rows = both.shape[1]
 
     gains = mlp_gain.reshape(tp, 1, quarter)
-    sums = gate_up_half(part, 0, both, gains, w_gate, w_up)
-    activation, other_terms = gate_up_rest(part, other, gains, w_gate, w_up, w_down, sums, width)
+    sums = gate_up_half(part, both, gains, gate_first, up_first, w_gate)
+    activation, other_terms = gate_up_rest(part, other, gains, w_up, w_down, sums, width)
     received = swap(other_terms, "tp", 1)
     own_terms = down_half(part, activation, w_down, ways)
     far, near = sum_terms(part, own_terms, received)
@@ -938,7 +938,9 @@
     near = [near[0]] + [swap(near[k], "seq", across * k) for k in range(1, count)]
     mlp_result = add(near[0], near[1:] + [total_of(far, 40)])
     own_out = (own_attended.astype(f32) + mlp_result).astype(bf16)
-    pieces = [own_out] + [swap(own_out, "tp", slot) for slot in range(1, tp)]
+    along = jnp.stack([own_out] + [swap(own_out, "tp", CORES * k) for k in range(1, ways)])
+    beside = swap(along, "tp", 1)
+    pieces = [along, beside]
     layer_out = assemble(part, rows, pieces).reshape(steps, row_count, width)
     return attended, layer_out
 

time: 128 us -> 126 us (0.984)
  waiting for transfers between devices: 43.2 us -> 38.3 us
  Pallas kernels: 38.9 us -> 41.6 us
    ppermute x31 -> x29, waiting for transfers between devices: 34 us -> 29.9 us  [swap(): return lax.ppermute(value, axis, [(i, i ^ mask) for i in range(size)])]
    pallas_call x1 -> x2, Pallas kernels: 5.05 us -> 8.18 us  [the longest x1 4.1 us: load(): pl.pallas_call(functools.partial(load_kernel, slots), out_shape=(shape, s...]
    ppermute x31 -> x29, starting transfers between devices: 36.4 us -> 35.6 us  [swap(): return lax.ppermute(value, axis, [(i, i ^ mask) for i in range(size)])]
  transfers between devices with their start and end apart: 35 -> 33, of which waited for: 25 -> 20; matrix products, arithmetic and copies ran while one was open for 2% -> 2% of each run, Pallas kernels for 11% -> 14%
where the time goes in v6:
time: 126 us
  Pallas kernels  41.6 us (33%)
  starting transfers between devices  40.1 us (32%)
  waiting for transfers between devices  38.3 us (30%)
  local copies, waits for them, and re-layouts  4.09 us (3%)
    ppermute x29, starting transfers between devices, swap(): return lax.ppermute(value, axis, [(i, i ^ mask) for i in range(size)])  35.6 us
    ppermute x29, waiting for transfers between devices, swap(): return lax.ppermute(value, axis, [(i, i ^ mask) for i in range(size)])  29.9 us
    ppermute x4, waiting for transfers between devices, cross(): return lax.ppermute(value, ('seq', 'tp'), pairs)  8.41 us
    pallas_call x1, Pallas kernels, project_queries(): pl.pallas_call(functools.partial(query_kernel, kv_local), out_shape=(jax....  6.81 us
    pallas_call x1, Pallas kernels, gate_up_rest(): pl.pallas_call(functools.partial(rest_kernel, width), out_shape=(jax.Shap...  6.8 us
    pallas_call x1, Pallas kernels, attend_pages(): pl.pallas_call(functools.partial(pages_kernel, block_pages, len(pieces),...  4.81 us
    pallas_call x1, Pallas kernels, project_out(): pl.pallas_call(functools.partial(out_kernel, len(parts), kv_local), out_s...  4.74 us
    ppermute x4, starting transfers between devices, cross(): return lax.ppermute(value, ('seq', 'tp'), pairs)  4.47 us
  transfers between devices with their start and end apart: 33, of which 20 were waited for; matrix products, arithmetic and copies ran while one was open for 2% of the time, Pallas kernels for 14%

profile of v6, /device:TPU:0, one launch (start us, length us, event | category | flops | bytes accessed | tf_op | source)
XLA Modules:
  0.0 125.9 jit_solution(15068971475072376320)
XLA Ops:
  0.7 6.8 %project_queries.1 = (bf16[16,16,128]{2,1,0:T(8,128)(2,1)}, bf16[32,5120]{1,0:T(8,128)(2,1)}, f32[2,32,128]{2,1,0:T(8,128)}) custom-call(s32[1]{0:T(128)} %bitcast.2.me_ref, s32[1,64]{1,0:T(1,128)} %bitcast.39, s32[1,64]{1,0:T(1,128)} %bitcast.38, bf16[4,8,5120]{2,1,0:T(8,128)(2,1)} %input_hbm.1, f32[1,5120]{1,0:T(1,128)} %bitcast.37, ...), custom_call_target="tpu_custom_call" | custom-call | flops 335544320 | bytes 10485760 | tf_op jit(solution)/shard_map/project_queries/pallas_call | solution.py:341
  7.5 5.1 %collective-permute-start.2 = (bf16[16,16,128]{2,1,0:T(8,128)(2,1)}, bf16[16,16,128]{2,1,0:T(8,128)(2,1)S(1)}, u32[]{:S(2)}, u32[]{:S(2)}) collective-permute-start(bf16[16,16,128]{2,1,0:T(8,128)(2,1)} %get-tuple-element.33), channel_id=1, source_target_pairs={{0,24},{4,28},{8,16},{12,20},{16,8},{20,12},{24,0},{28,4},{1,25},{... | collective-permute-start | bytes 196616 | tf_op jit(solution)/shard_map/ppermute | solution.py:29
  12.7 0.6 collective-permute-start
  13.3 0.9 constant_dynamic-update-slice_fusion.3
  14.2 3.0 %collective-permute-done = bf16[16,16,128]{2,1,0:T(8,128)(2,1)S(1)} collective-permute-done((bf16[16,16,128]{2,1,0:T(8,128)(2,1)}, bf16[16,16,128]{2,1,0:T(8,128)(2,1)S(1)}, u32[]{:S(2)}, u32[]{:S(2)}) %collective-permute-start) | collective-permute-done | bytes 65568 | tf_op jit(solution)/shard_map/ppermute | solution.py:29
  17.2 1.3 %collective-permute-done.1 = bf16[16,16,128]{2,1,0:T(8,128)(2,1)S(1)} collective-permute-done((bf16[16,16,128]{2,1,0:T(8,128)(2,1)}, bf16[16,16,128]{2,1,0:T(8,128)(2,1)S(1)}, u32[]{:S(2)}, u32[]{:S(2)}) %collective-permute-start.1) | collective-permute-done | bytes 65568 | tf_op jit(solution)/shard_map/ppermute | solution.py:29
  18.5 1.6 %collective-permute-start.3 = (bf16[64,16,128]{2,1,0:T(8,128)(2,1)S(1)}, bf16[64,16,128]{2,1,0:T(8,128)(2,1)S(1)}, u32[]{:S(2)}, u32[]{:S(2)}) collective-permute-start(bf16[64,16,128]{2,1,0:T(8,128)(2,1)S(1)} %constant_dynamic-update-slice_fusion.query_ref.refs_0_), channel_id=1, source_target_pairs={{0,4},{4,0},{8,12},{12,8},{16,20},{20,16},{24,28},{28,24},{1,5},{5... | collective-permute-start | bytes 786440 | tf_op jit(solution)/shard_map/ppermute | solution.py:29
  20.3 1.0 copy-done
  21.3 0.8 copy-done.2
  22.0 3.8 %recent_part.1.refs_4_ = bf16[1,17,16,128]{3,2,1,0:T(8,128)(2,1)S(1)} custom-call(bf16[32,5120]{1,0:T(8,128)(2,1)S(1)} %copy-done, f32[2,32,128]{2,1,0:T(8,128)S(1)} %copy-done.2, bf16[64,16,128]{2,1,0:T(8,128)(2,1)S(1)} %constant_dynamic-update-slice_fusion.query_ref.refs_0_, bf16[5120,256]{1,0:T(8,128)(2,1)} %key_hbm.1, bf16[5120,256]{1,0:T(8,128)(2,1)} %value_hbm.1), custom_call_target="tpu_custom_call" | custom-call | flops 167772160 | bytes 5242880 | tf_op jit(solution)/shard_map/recent_part/pallas_call | solution.py:426
  25.8 0.7 collective-permute-done.3.refs_1_
  26.5 4.8 %attend_pages.1 = (bf16[2,17,16,128]{3,2,1,0:T(8,128)(2,1)S(1)}, bf16[2,17,16,128]{3,2,1,0:T(8,128)(2,1)S(1)}, bf16[2,17,16,128]{3,2,1,0:T(8,128)(2,1)S(1)}, bf16[2,17,16,128]{3,2,1,0:T(8,128)(2,1)S(1)}) custom-call(s32[36]{0:T(128)S(1)} %get-tuple-element.76.slot_ref, s32[36]{0:T(128)S(1)} %get-tuple-element.75.valid_ref, ...), custom_call_target="tpu_custom_call" | custom-call | flops 150994944 | bytes 9437184 | tf_op jit(solution)/shard_map/attend_pages/pallas_call | solution.py:150
  31.3 1.7 %collective-permute-start.4 = (bf16[2,17,16,128]{3,2,1,0:T(8,128)(2,1)S(1)}, bf16[2,17,16,128]{3,2,1,0:T(8,128)(2,1)S(1)}, u32[]{:S(2)}, u32[]{:S(2)}) collective-permute-start(bf16[2,17,16,128]{3,2,1,0:T(8,128)(2,1)S(1)} %get-tuple-element.37), channel_id=1, source_target_pairs={{0,4},{4,0},{8,12},{12,8},{16,20},{20,16},{24,28},{28,24},{1,5},{5... | collective-permute-start | bytes 417800 | tf_op jit(solution)/shard_map/ppermute | solution.py:29
  33.1 0.4 collective-permute-start.7
  33.4 4.0 %collective-permute-done.4.refs_1_ = bf16[2,17,16,128]{3,2,1,0:T(8,128)(2,1)S(1)} collective-permute-done((bf16[2,17,16,128]{3,2,1,0:T(8,128)(2,1)S(1)}, bf16[2,17,16,128]{3,2,1,0:T(8,128)(2,1)S(1)}, u32[]{:S(2)}, u32[]{:S(2)}) %collective-permute-start.4) | collective-permute-done | bytes 139296 | tf_op jit(solution)/shard_map/ppermute | solution.py:29
  37.4 0.4 merge_parts.2
  37.8 0.3 collective-permute-start.5
  38.1 2.1 %collective-permute-start.6 = (bf16[1,17,16,128]{3,2,1,0:T(8,128)(2,1)S(1)}, bf16[1,17,16,128]{3,2,1,0:T(8,128)(2,1)S(1)}, u32[]{:S(2)}, u32[]{:S(2)}) collective-permute-start(bf16[1,17,16,128]{3,2,1,0:T(8,128)(2,1)S(1)} %get-tuple-element.39), channel_id=1, source_target_pairs={{0,24},{4,28},{8,16},{12,20},{16,8},{20,12},{24,0},{28,4},{1,25},{... | collective-permute-start | bytes 208904 | tf_op jit(solution)/shard_map/ppermute | solution.py:29
  40.2 0.4 merge_parts.3
  40.7 1.2 collective-permute-start.8
  41.9 0.9 constant_dynamic-slice_fusion.input_ref
  42.8 0.5 collective-permute-done.5.refs_0_
  43.3 1.0 collective-permute-done.6.refs_1_
  44.3 0.8 collective-permute-done.8.refs_3_
  45.1 4.7 %project_out.1 = (f32[32,1280]{1,0:T(8,128)S(1)}, bf16[3,32,1280]{2,1,0:T(8,128)(2,1)S(1)}) custom-call(s32[1]{0:T(128)} %bitcast.part_ref, bf16[32,1280]{1,0:T(8,128)(2,1)S(1)} %constant_dynamic-slice_fusion.input_ref, bf16[1024,5120]{1,0:T(8,128)(2,1)} %weight_hbm.3, bf16[1,17,16,128]{3,2,1,0:T(8,128)(2,1)S(1)} %collective-permute-done.5.refs_0_, ...), custom_call_target="tpu_custom_call" | custom-call | flops 335544320 | bytes 10485760 | tf_op jit(solution)/shard_map/project_out/pallas_call | solution.py:493
  49.9 1.4 %collective-permute-done.9 = bf16[2,32,1280]{2,1,0:T(8,128)(2,1)S(1)} collective-permute-done((bf16[2,32,1280]{2,1,0:T(8,128)(2,1)S(1)}, bf16[2,32,1280]{2,1,0:T(8,128)(2,1)S(1)}, u32[]{:S(2)}, u32[]{:S(2)}) %collective-permute-start.9) | collective-permute-done | bytes 163872 | tf_op jit(solution)/shard_map/ppermute | solution.py:29
  51.3 1.7 %collective-permute-start.10 = (bf16[32,1280]{1,0:T(8,128)(2,1)S(1)}, bf16[32,1280]{1,0:T(8,128)(2,1)S(1)}, u32[]{:S(2)}, u32[]{:S(2)}) collective-permute-start(bf16[32,1280]{1,0:T(8,128)(2,1)S(1)} %fusion.2), channel_id=1, source_target_pairs={{0,2},{1,3},{2,0},{3,1},{4,6},{5,7},{6,4},{7,5},{8,10},{9,11},{10,... | collective-permute-start | bytes 245768 | tf_op jit(solution)/shard_map/ppermute | solution.py:29
  53.0 2.9 %collective-permute-done.10 = bf16[32,1280]{1,0:T(8,128)(2,1)S(1)} collective-permute-done((bf16[32,1280]{1,0:T(8,128)(2,1)S(1)}, bf16[32,1280]{1,0:T(8,128)(2,1)S(1)}, u32[]{:S(2)}, u32[]{:S(2)}) %collective-permute-start.10) | collective-permute-done | bytes 81952 | tf_op jit(solution)/shard_map/ppermute | solution.py:29
  55.9 1.2 collective-permute-start.11
  57.1 1.4 %collective-permute-start.15 = (bf16[32,1280]{1,0:T(8,128)(2,1)S(1)}, bf16[32,1280]{1,0:T(8,128)(2,1)S(1)}, u32[]{:S(2)}, u32[]{:S(2)}) collective-permute-start(bf16[32,1280]{1,0:T(8,128)(2,1)S(1)} %fusion.1), channel_id=1, source_target_pairs={{0,24},{4,28},{8,16},{12,20},{16,8},{20,12},{24,0},{28,4},{1,25},{... | collective-permute-start | bytes 245768 | tf_op jit(solution)/shard_map/ppermute | solution.py:29
  58.6 0.9 collective-permute-start.14
  59.5 1.0 collective-permute-done.11
  60.5 1.7 %collective-permute-start.13 = (bf16[64,640]{1,0:T(8,128)(2,1)S(1)}, bf16[64,640]{1,0:T(8,128)(2,1)S(1)}, u32[]{:S(2)}, u32[]{:S(2)}) collective-permute-start(bf16[64,640]{1,0:T(8,128)(2,1)S(1)} %get-tuple-element.48), channel_id=1, source_target_pairs={{0,2},{1,3},{2,0},{3,1},{4,6},{5,7},{6,4},{7,5},{8,10},{9,11},{10,... | collective-permute-start | bytes 245768 | tf_op jit(solution)/shard_map/ppermute | solution.py:29
  62.1 1.5 %collective-permute-start.12 = (bf16[64,640]{1,0:T(8,128)(2,1)S(1)}, bf16[64,640]{1,0:T(8,128)(2,1)S(1)}, u32[]{:S(2)}, u32[]{:S(2)}) collective-permute-start(bf16[64,640]{1,0:T(8,128)(2,1)S(1)} %get-tuple-element.46), channel_id=1, source_target_pairs={{0,4},{4,0},{8,12},{12,8},{16,20},{20,16},{24,28},{28,24},{1,5},{5... | collective-permute-start | bytes 245768 | tf_op jit(solution)/shard_map/ppermute | solution.py:29
  63.7 3.1 %collective-permute-done.14 = bf16[32,1280]{1,0:T(8,128)(2,1)S(1)} collective-permute-done((bf16[32,1280]{1,0:T(8,128)(2,1)S(1)}, bf16[32,1280]{1,0:T(8,128)(2,1)S(1)}, u32[]{:S(2)}, u32[]{:S(2)}) %collective-permute-start.14) | collective-permute-done | bytes 81952 | tf_op jit(solution)/shard_map/ppermute | solution.py:29
  66.9 1.7 %collective-permute-start.20 = (bf16[64,640]{1,0:T(8,128)(2,1)S(1)}, bf16[64,640]{1,0:T(8,128)(2,1)S(1)}, u32[]{:S(2)}, u32[]{:S(2)}) collective-permute-start(bf16[64,640]{1,0:T(8,128)(2,1)S(1)} %get-tuple-element.71), channel_id=1, source_target_pairs={{0,2},{1,3},{2,0},{3,1},{4,6},{5,7},{6,4},{7,5},{8,10},{9,11},{10,... | collective-permute-start | bytes 245768 | tf_op jit(solution)/shard_map/ppermute | solution.py:29
  68.6 1.2 collective-permute-start.18
  69.8 0.9 collective-permute-start.17
  70.7 0.4 collective-permute-start.16
  71.2 2.1 %collective-permute-done.18 = bf16[64,640]{1,0:T(8,128)(2,1)S(1)} collective-permute-done((bf16[64,640]{1,0:T(8,128)(2,1)S(1)}, bf16[64,640]{1,0:T(8,128)(2,1)S(1)}, u32[]{:S(2)}, u32[]{:S(2)}) %collective-permute-start.18) | collective-permute-done | bytes 81952 | tf_op jit(solution)/shard_map/ppermute | solution.py:29
  73.2 0.6 collective-permute-start.19
  73.8 1.1 collective-permute-start.21
  75.0 4.1 %load.1 = (bf16[2,1280,1024]{2,1,0:T(8,128)(2,1)S(1)}, bf16[2,1280,1024]{2,1,0:T(8,128)(2,1)S(1)}) custom-call(s32[1]{0:T(128)} %bitcast.part_ref, bf16[5120,1024]{1,0:T(8,128)(2,1)} %gate_hbm.1, bf16[5120,1024]{1,0:T(8,128)(2,1)} %up_hbm.1), custom_call_target="tpu_custom_call" | custom-call | bytes 10485760 | tf_op jit(solution)/shard_map/load/pallas_call | solution.py:247
  79.4 0.4 copy-done.1
  79.8 4.1 %gate_up_half.1 = (f32[256,1024]{1,0:T(8,128)S(1)}, f32[256,1024]{1,0:T(8,128)S(1)}, f32[256,128]{1,0:T(8,128)S(1)}, bf16[2,1280,1024]{2,1,0:T(8,128)(2,1)S(1)}) custom-call(s32[1]{0:T(128)} %bitcast.part_ref, bf16[2,256,1280]{2,1,0:T(8,128)(2,1)S(1)} %join_groups.1.refs_0_.rows_ref, f32[4,1,1280]{2,1,0:T(1,128)S(1)} %bitcast.27, ...), custom_call_target="tpu_custom_call" | custom-call | flops 2684354560 | bytes 12582912 | tf_op jit(solution)/shard_map/gate_up_half/pallas_call | solution.py:608
  83.9 6.8 %gate_up_rest.1 = (bf16[256,1024]{1,0:T(8,128)(2,1)S(1)}, bf16[2,256,1280]{2,1,0:T(8,128)(2,1)S(1)}) custom-call(s32[1]{0:T(128)} %bitcast.part_ref, bf16[2,256,1280]{2,1,0:T(8,128)(2,1)S(1)} %collective-permute-done.22.refs_1_.rows_ref, f32[4,1,1280]{2,1,0:T(1,128)S(1)} %bitcast.28, f32[256,1024]{1,0:T(8,128)S(1)} %get-tuple-element.54.old_gate_ref, ...), custom_call_target="tpu_custom_call" | custom-call | flops 4026531840 | bytes 15728640 | tf_op jit(solution)/shard_map/gate_up_rest/pallas_call | solution.py:676
  90.9 3.7 %down_half.1.own_ref = bf16[2,256,1280]{2,1,0:T(8,128)(2,1)S(1)} custom-call(s32[1]{0:T(128)} %bitcast.part_ref, bf16[256,1024]{1,0:T(8,128)(2,1)S(1)} %get-tuple-element.58.activation_ref, bf16[1024,5120]{1,0:T(8,128)(2,1)} %down_hbm.3), custom_call_target="tpu_custom_call" | custom-call | flops 1342177280 | bytes 5242880 | tf_op jit(solution)/shard_map/down_half/pallas_call | solution.py:714
  94.6 0.3 sum_terms.1
  94.9 1.6 %collective-permute-start.27 = (bf16[128,1280]{1,0:T(8,128)(2,1)S(1)}, bf16[128,1280]{1,0:T(8,128)(2,1)S(1)}, u32[]{:S(2)}, u32[]{:S(2)}) collective-permute-start(bf16[128,1280]{1,0:T(8,128)(2,1)S(1)} %get-tuple-element.63), channel_id=1, source_target_pairs={{0,2},{1,5},{2,0},{3,7},{4,6},{5,1},{6,4},{7,3},{8,10},{9,13},{10,... | collective-permute-start | bytes 983048 | tf_op jit(solution)/shard_map/ppermute | solution.py:40
  96.5 0.5 collective-permute-start.24
  97.0 5.0 %collective-permute-done.27 = bf16[128,1280]{1,0:T(8,128)(2,1)S(1)} collective-permute-done((bf16[128,1280]{1,0:T(8,128)(2,1)S(1)}, bf16[128,1280]{1,0:T(8,128)(2,1)S(1)}, u32[]{:S(2)}, u32[]{:S(2)}) %collective-permute-start.27) | collective-permute-done | bytes 327712 | tf_op jit(solution)/shard_map/ppermute | solution.py:40
  102.2 1.1 collective-permute-start.28
  103.3 3.4 %collective-permute-done.24 = bf16[128,1280]{1,0:T(8,128)(2,1)S(1)} collective-permute-done((bf16[128,1280]{1,0:T(8,128)(2,1)S(1)}, bf16[128,1280]{1,0:T(8,128)(2,1)S(1)}, u32[]{:S(2)}, u32[]{:S(2)}) %collective-permute-start.24) | collective-permute-done | bytes 327712 | tf_op jit(solution)/shard_map/ppermute | solution.py:40
  106.8 1.2 collective-permute-start.25
  108.1 2.6 %collective-permute-start.30 = (bf16[32,1280]{1,0:T(8,128)(2,1)S(1)}, bf16[32,1280]{1,0:T(8,128)(2,1)S(1)}, u32[]{:S(2)}, u32[]{:S(2)}) collective-permute-start(bf16[32,1280]{1,0:T(8,128)(2,1)S(1)} %get-tuple-element.68), channel_id=1, source_target_pairs={{0,24},{4,28},{8,16},{12,20},{16,8},{20,12},{24,0},{28,4},{1,25},{... | collective-permute-start | bytes 245768 | tf_op jit(solution)/shard_map/ppermute | solution.py:29
  110.7 2.1 %collective-permute-start.29 = (bf16[32,1280]{1,0:T(8,128)(2,1)S(1)}, bf16[32,1280]{1,0:T(8,128)(2,1)S(1)}, u32[]{:S(2)}, u32[]{:S(2)}) collective-permute-start(bf16[32,1280]{1,0:T(8,128)(2,1)S(1)} %get-tuple-element.69), channel_id=1, source_target_pairs={{0,16},{4,20},{8,24},{12,28},{16,0},{20,4},{24,8},{28,12},{1,17},{... | collective-permute-start | bytes 245768 | tf_op jit(solution)/shard_map/ppermute | solution.py:29
  112.9 2.2 %collective-permute-start.26 = (bf16[32,1280]{1,0:T(8,128)(2,1)S(1)}, bf16[32,1280]{1,0:T(8,128)(2,1)S(1)}, u32[]{:S(2)}, u32[]{:S(2)}) collective-permute-start(bf16[32,1280]{1,0:T(8,128)(2,1)S(1)} %slice.85), channel_id=1, source_target_pairs={{0,8},{4,12},{8,0},{12,4},{16,24},{20,28},{24,16},{28,20},{1,9},{5... | collective-permute-start | bytes 245768 | tf_op jit(solution)/shard_map/ppermute | solution.py:29
  115.0 0.3 collective-permute-done.30.refs_1_
  115.4 3.7 %collective-permute-done.29.refs_0_ = bf16[32,1280]{1,0:T(8,128)(2,1)S(1)} collective-permute-done((bf16[32,1280]{1,0:T(8,128)(2,1)S(1)}, bf16[32,1280]{1,0:T(8,128)(2,1)S(1)}, u32[]{:S(2)}, u32[]{:S(2)}) %collective-permute-start.29) | collective-permute-done | bytes 81952 | tf_op jit(solution)/shard_map/ppermute | solution.py:29
  119.1 1.0 collective-permute-start.31
  120.2 3.5 %collective-permute-done.31 = bf16[32,1280]{1,0:T(8,128)(2,1)S(1)} collective-permute-done((bf16[32,1280]{1,0:T(8,128)(2,1)S(1)}, bf16[32,1280]{1,0:T(8,128)(2,1)S(1)}, u32[]{:S(2)}, u32[]{:S(2)}) %collective-permute-start.31) | collective-permute-done | bytes 81952 | tf_op jit(solution)/shard_map/ppermute | solution.py:29
  123.8 0.8 assemble.2
  124.5 0.6 collective-permute-done.32.refs_1_
  125.1 0.7 assemble.3
  (71 shorter events, 1.6 us)
Async XLA Ops:
  0.6 25.8 %slice-start = ((s8[4718592]{0:T(1024)(128)(4,1)}), s8[4194304]{0:T(1024)(128)(4,1)S(1)}, s32[]{:S(2)}) async-start(s8[4718592]{0:T(1024)(128)(4,1)} %bitcast.23), calls=%async_computation | async-start | bytes 8388608
  0.6 25.8 %slice-start.2 = ((s8[4718592]{0:T(1024)(128)(4,1)}), s8[4194304]{0:T(1024)(128)(4,1)S(1)}, s32[]{:S(2)}) async-start(s8[4718592]{0:T(1024)(128)(4,1)} %bitcast.25), calls=%async_computation.2 | async-start | bytes 8388608
  0.7 19.4 %copy-start.3 = (s32[64]{0:T(128)S(1)}, s32[64]{0:T(128)}, u32[]{:S(2)}) copy-start(s32[64]{0:T(128)} %param.28) | copy-start | bytes 772
  0.7 19.4 %copy-start.4 = (s32[64]{0:T(128)S(1)}, s32[64]{0:T(128)}, u32[]{:S(2)}) copy-start(s32[64]{0:T(128)} %param.31) | copy-start | bytes 772
  0.7 19.4 %copy-start.5 = (s32[36]{0:T(128)S(1)}, s32[36]{0:T(128)}, u32[]{:S(2)}) copy-start(s32[36]{0:T(128)} %param.29) | copy-start | bytes 436
  0.7 19.6 %copy-start.6 = (s32[36]{0:T(128)S(1)}, s32[36]{0:T(128)}, u32[]{:S(2)}) copy-start(s32[36]{0:T(128)} %param.30) | copy-start | bytes 436
  0.7 25.8 %slice-start.1 = ((s8[4718592]{0:T(1024)(128)(4,1)}), s8[524288]{0:T(1024)(128)(4,1)S(1)}, s32[]{:S(2)}) async-start(s8[4718592]{0:T(1024)(128)(4,1)} %bitcast.23), calls=%async_computation.1 | async-start | bytes 1048576
  0.7 25.8 %slice-start.3 = ((s8[4718592]{0:T(1024)(128)(4,1)}), s8[524288]{0:T(1024)(128)(4,1)S(1)}, s32[]{:S(2)}) async-start(s8[4718592]{0:T(1024)(128)(4,1)} %bitcast.25), calls=%async_computation.3 | async-start | bytes 1048576
  7.5 10.9 %collective-permute-start.2 = (bf16[16,16,128]{2,1,0:T(8,128)(2,1)}, bf16[16,16,128]{2,1,0:T(8,128)(2,1)S(1)}, u32[]{:S(2)}, u32[]{:S(2)}) collective-permute-start(bf16[16,16,128]{2,1,0:T(8,128)(2,1)} %get-tuple-element.33), channel_id=1, source_target_pairs={{0,24},{4,28},{8,16},{12,20},{16,8},{20,12},{24,0},{28,4},{1,25},{... | collective-permute-start | bytes 196616 | tf_op jit(solution)/shard_map/ppermute | solution.py:29
  12.7 5.8 %collective-permute-start.1 = (bf16[16,16,128]{2,1,0:T(8,128)(2,1)}, bf16[16,16,128]{2,1,0:T(8,128)(2,1)S(1)}, u32[]{:S(2)}, u32[]{:S(2)}) collective-permute-start(bf16[16,16,128]{2,1,0:T(8,128)(2,1)} %get-tuple-element.33), channel_id=1, source_target_pairs={{0,16},{4,20},{8,24},{12,28},{16,0},{20,4},{24,8},{28,12},{1,17},{... | collective-permute-start | bytes 196616 | tf_op jit(solution)/shard_map/ppermute | solution.py:29
  12.7 4.5 %collective-permute-start = (bf16[16,16,128]{2,1,0:T(8,128)(2,1)}, bf16[16,16,128]{2,1,0:T(8,128)(2,1)S(1)}, u32[]{:S(2)}, u32[]{:S(2)}) collective-permute-start(bf16[16,16,128]{2,1,0:T(8,128)(2,1)} %get-tuple-element.33), channel_id=1, source_target_pairs={{0,8},{4,12},{8,0},{12,4},{16,24},{20,28},{24,16},{28,20},{1,9},{5... | collective-permute-start | bytes 196616 | tf_op jit(solution)/shard_map/ppermute | solution.py:29
  18.5 7.9 %collective-permute-start.3 = (bf16[64,16,128]{2,1,0:T(8,128)(2,1)S(1)}, bf16[64,16,128]{2,1,0:T(8,128)(2,1)S(1)}, u32[]{:S(2)}, u32[]{:S(2)}) collective-permute-start(bf16[64,16,128]{2,1,0:T(8,128)(2,1)S(1)} %constant_dynamic-update-slice_fusion.query_ref.refs_0_), channel_id=1, source_target_pairs={{0,4},{4,0},{8,12},{12,8},{16,20},{20,16},{24,28},{28,24},{1,5},{5... | collective-permute-start | bytes 786440 | tf_op jit(solution)/shard_map/ppermute | solution.py:29
  20.3 1.0 copy-start
  21.3 0.8 copy-start.2
  31.3 6.1 %collective-permute-start.4 = (bf16[2,17,16,128]{3,2,1,0:T(8,128)(2,1)S(1)}, bf16[2,17,16,128]{3,2,1,0:T(8,128)(2,1)S(1)}, u32[]{:S(2)}, u32[]{:S(2)}) collective-permute-start(bf16[2,17,16,128]{3,2,1,0:T(8,128)(2,1)S(1)} %get-tuple-element.37), channel_id=1, source_target_pairs={{0,4},{4,0},{8,12},{12,8},{16,20},{20,16},{24,28},{28,24},{1,5},{5... | collective-permute-start | bytes 417800 | tf_op jit(solution)/shard_map/ppermute | solution.py:29
  33.1 7.2 %collective-permute-start.7 = (bf16[2,17,16,128]{3,2,1,0:T(8,128)(2,1)S(1)}, bf16[2,17,16,128]{3,2,1,0:T(8,128)(2,1)S(1)}, u32[]{:S(2)}, u32[]{:S(2)}) collective-permute-start(bf16[2,17,16,128]{3,2,1,0:T(8,128)(2,1)S(1)} %get-tuple-element.41), channel_id=1, source_target_pairs={{0,4},{4,0},{8,12},{12,8},{16,20},{20,16},{24,28},{28,24},{1,5},{5... | collective-permute-start | bytes 417800 | tf_op jit(solution)/shard_map/ppermute | solution.py:29
  37.8 5.4 %collective-permute-start.5 = (bf16[1,17,16,128]{3,2,1,0:T(8,128)(2,1)S(1)}, bf16[1,17,16,128]{3,2,1,0:T(8,128)(2,1)S(1)}, u32[]{:S(2)}, u32[]{:S(2)}) collective-permute-start(bf16[1,17,16,128]{3,2,1,0:T(8,128)(2,1)S(1)} %get-tuple-element.38), channel_id=1, source_target_pairs={{0,16},{4,20},{8,24},{12,28},{16,0},{20,4},{24,8},{28,12},{1,17},{... | collective-permute-start | bytes 208904 | tf_op jit(solution)/shard_map/ppermute | solution.py:29
  38.1 6.2 %collective-permute-start.6 = (bf16[1,17,16,128]{3,2,1,0:T(8,128)(2,1)S(1)}, bf16[1,17,16,128]{3,2,1,0:T(8,128)(2,1)S(1)}, u32[]{:S(2)}, u32[]{:S(2)}) collective-permute-start(bf16[1,17,16,128]{3,2,1,0:T(8,128)(2,1)S(1)} %get-tuple-element.39), channel_id=1, source_target_pairs={{0,24},{4,28},{8,16},{12,20},{16,8},{20,12},{24,0},{28,4},{1,25},{... | collective-permute-start | bytes 208904 | tf_op jit(solution)/shard_map/ppermute | solution.py:29
  40.7 4.4 %collective-permute-start.8 = (bf16[1,17,16,128]{3,2,1,0:T(8,128)(2,1)S(1)}, bf16[1,17,16,128]{3,2,1,0:T(8,128)(2,1)S(1)}, u32[]{:S(2)}, u32[]{:S(2)}) collective-permute-start(bf16[1,17,16,128]{3,2,1,0:T(8,128)(2,1)S(1)} %get-tuple-element.43), channel_id=1, source_target_pairs={{0,8},{4,12},{8,0},{12,4},{16,24},{20,28},{24,16},{28,20},{1,9},{5... | collective-permute-start | bytes 208904 | tf_op jit(solution)/shard_map/ppermute | solution.py:29
  49.8 1.5 %collective-permute-start.9 = (bf16[2,32,1280]{2,1,0:T(8,128)(2,1)S(1)}, bf16[2,32,1280]{2,1,0:T(8,128)(2,1)S(1)}, u32[]{:S(2)}, u32[]{:S(2)}) collective-permute-start(bf16[2,32,1280]{2,1,0:T(8,128)(2,1)S(1)} %pad_maximum_fusion), channel_id=1, source_target_pairs={{0,1},{1,0},{2,3},{3,2},{4,5},{5,4},{6,7},{7,6},{8,9},{9,8},{10,11... | collective-permute-start | bytes 491528 | tf_op jit(solution)/shard_map/ppermute | solution.py:29
  51.3 4.6 %collective-permute-start.10 = (bf16[32,1280]{1,0:T(8,128)(2,1)S(1)}, bf16[32,1280]{1,0:T(8,128)(2,1)S(1)}, u32[]{:S(2)}, u32[]{:S(2)}) collective-permute-start(bf16[32,1280]{1,0:T(8,128)(2,1)S(1)} %fusion.2), channel_id=1, source_target_pairs={{0,2},{1,3},{2,0},{3,1},{4,6},{5,7},{6,4},{7,5},{8,10},{9,11},{10,... | collective-permute-start | bytes 245768 | tf_op jit(solution)/shard_map/ppermute | solution.py:29
  55.9 4.5 %collective-permute-start.11 = (bf16[32,1280]{1,0:T(8,128)(2,1)S(1)}, bf16[32,1280]{1,0:T(8,128)(2,1)S(1)}, u32[]{:S(2)}, u32[]{:S(2)}) collective-permute-start(bf16[32,1280]{1,0:T(8,128)(2,1)S(1)} %fusion.1), channel_id=1, source_target_pairs={{0,8},{4,12},{8,0},{12,4},{16,24},{20,28},{24,16},{28,20},{1,9},{5... | collective-permute-start | bytes 245768 | tf_op jit(solution)/shard_map/ppermute | solution.py:29
  57.1 6.6 %collective-permute-start.15 = (bf16[32,1280]{1,0:T(8,128)(2,1)S(1)}, bf16[32,1280]{1,0:T(8,128)(2,1)S(1)}, u32[]{:S(2)}, u32[]{:S(2)}) collective-permute-start(bf16[32,1280]{1,0:T(8,128)(2,1)S(1)} %fusion.1), channel_id=1, source_target_pairs={{0,24},{4,28},{8,16},{12,20},{16,8},{20,12},{24,0},{28,4},{1,25},{... | collective-permute-start | bytes 245768 | tf_op jit(solution)/shard_map/ppermute | solution.py:29
  58.6 8.2 %collective-permute-start.14 = (bf16[32,1280]{1,0:T(8,128)(2,1)S(1)}, bf16[32,1280]{1,0:T(8,128)(2,1)S(1)}, u32[]{:S(2)}, u32[]{:S(2)}) collective-permute-start(bf16[32,1280]{1,0:T(8,128)(2,1)S(1)} %fusion.1), channel_id=1, source_target_pairs={{0,16},{4,20},{8,24},{12,28},{16,0},{20,4},{24,8},{28,12},{1,17},{... | collective-permute-start | bytes 245768 | tf_op jit(solution)/shard_map/ppermute | solution.py:29
  60.5 6.3 %collective-permute-start.13 = (bf16[64,640]{1,0:T(8,128)(2,1)S(1)}, bf16[64,640]{1,0:T(8,128)(2,1)S(1)}, u32[]{:S(2)}, u32[]{:S(2)}) collective-permute-start(bf16[64,640]{1,0:T(8,128)(2,1)S(1)} %get-tuple-element.48), channel_id=1, source_target_pairs={{0,2},{1,3},{2,0},{3,1},{4,6},{5,7},{6,4},{7,5},{8,10},{9,11},{10,... | collective-permute-start | bytes 245768 | tf_op jit(solution)/shard_map/ppermute | solution.py:29
  62.1 4.7 %collective-permute-start.12 = (bf16[64,640]{1,0:T(8,128)(2,1)S(1)}, bf16[64,640]{1,0:T(8,128)(2,1)S(1)}, u32[]{:S(2)}, u32[]{:S(2)}) collective-permute-start(bf16[64,640]{1,0:T(8,128)(2,1)S(1)} %get-tuple-element.46), channel_id=1, source_target_pairs={{0,4},{4,0},{8,12},{12,8},{16,20},{20,16},{24,28},{28,24},{1,5},{5... | collective-permute-start | bytes 245768 | tf_op jit(solution)/shard_map/ppermute | solution.py:29
  66.9 6.9 %collective-permute-start.20 = (bf16[64,640]{1,0:T(8,128)(2,1)S(1)}, bf16[64,640]{1,0:T(8,128)(2,1)S(1)}, u32[]{:S(2)}, u32[]{:S(2)}) collective-permute-start(bf16[64,640]{1,0:T(8,128)(2,1)S(1)} %get-tuple-element.71), channel_id=1, source_target_pairs={{0,2},{1,3},{2,0},{3,1},{4,6},{5,7},{6,4},{7,5},{8,10},{9,11},{10,... | collective-permute-start | bytes 245768 | tf_op jit(solution)/shard_map/ppermute | solution.py:29
  68.6 4.6 %collective-permute-start.18 = (bf16[64,640]{1,0:T(8,128)(2,1)S(1)}, bf16[64,640]{1,0:T(8,128)(2,1)S(1)}, u32[]{:S(2)}, u32[]{:S(2)}) collective-permute-start(bf16[64,640]{1,0:T(8,128)(2,1)S(1)} %get-tuple-element.72), channel_id=1, source_target_pairs={{0,4},{4,0},{8,12},{12,8},{16,20},{20,16},{24,28},{28,24},{1,5},{5... | collective-permute-start | bytes 245768 | tf_op jit(solution)/shard_map/ppermute | solution.py:29
  69.8 9.2 %collective-permute-start.17 = (bf16[2,64,640]{2,1,0:T(8,128)(2,1)S(1)}, bf16[2,64,640]{2,1,0:T(8,128)(2,1)S(1)}, u32[]{:S(2)}, u32[]{:S(2)}) collective-permute-start(bf16[2,64,640]{2,1,0:T(8,128)(2,1)S(1)} %pad_maximum_fusion.1.refs_2_), channel_id=1, source_target_pairs={{0,4},{4,0},{8,12},{12,8},{16,20},{20,16},{24,28},{28,24},{1,5},{5... | collective-permute-start | bytes 491528 | tf_op jit(solution)/shard_map/ppermute | solution.py:29
  70.7 8.4 %collective-permute-start.16 = (bf16[128,640]{1,0:T(8,128)(2,1)S(1)}, bf16[128,640]{1,0:T(8,128)(2,1)S(1)}, u32[]{:S(2)}, u32[]{:S(2)}) collective-permute-start(bf16[128,640]{1,0:T(8,128)(2,1)S(1)} %constant_dynamic-update-slice_fusion.4.refs_0_), channel_id=1, source_target_pairs={{0,2},{1,3},{2,0},{3,1},{4,6},{5,7},{6,4},{7,5},{8,10},{9,11},{10,... | collective-permute-start | bytes 491528 | tf_op jit(solution)/shard_map/ppermute | solution.py:29
  73.2 5.9 %collective-permute-start.19 = (bf16[128,640]{1,0:T(8,128)(2,1)S(1)}, bf16[128,640]{1,0:T(8,128)(2,1)S(1)}, u32[]{:S(2)}, u32[]{:S(2)}) collective-permute-start(bf16[128,640]{1,0:T(8,128)(2,1)S(1)} %pad_maximum_fusion.2.refs_4_), channel_id=1, source_target_pairs={{0,2},{1,3},{2,0},{3,1},{4,6},{5,7},{6,4},{7,5},{8,10},{9,11},{10,... | collective-permute-start | bytes 491528 | tf_op jit(solution)/shard_map/ppermute | solution.py:29
  73.8 5.4 %collective-permute-start.21 = (bf16[2,64,640]{2,1,0:T(8,128)(2,1)S(1)}, bf16[2,64,640]{2,1,0:T(8,128)(2,1)S(1)}, u32[]{:S(2)}, u32[]{:S(2)}) collective-permute-start(bf16[2,64,640]{2,1,0:T(8,128)(2,1)S(1)} %pad_maximum_fusion.3.refs_6_), channel_id=1, source_target_pairs={{0,4},{4,0},{8,12},{12,8},{16,20},{20,16},{24,28},{28,24},{1,5},{5... | collective-permute-start | bytes 491528 | tf_op jit(solution)/shard_map/ppermute | solution.py:29
  79.1 0.7 copy-start.1
  79.3 4.6 %collective-permute-start.22 = (bf16[2,256,1280]{2,1,0:T(8,128)(2,1)S(1)}, bf16[2,256,1280]{2,1,0:T(8,128)(2,1)S(1)}, u32[]{:S(2)}, u32[]{:S(2)}) collective-permute-start(bf16[2,256,1280]{2,1,0:T(8,128)(2,1)S(1)} %join_groups.1.refs_0_.rows_ref), channel_id=1, source_target_pairs={{0,1},{1,0},{2,3},{3,2},{4,5},{5,4},{6,7},{7,6},{8,9},{9,8},{10,11... | collective-permute-start | bytes 3932168 | tf_op jit(solution)/shard_map/ppermute | solution.py:29
  90.7 3.9 %collective-permute-start.23 = (bf16[2,256,1280]{2,1,0:T(8,128)(2,1)S(1)}, bf16[2,256,1280]{2,1,0:T(8,128)(2,1)S(1)}, u32[]{:S(2)}, u32[]{:S(2)}) collective-permute-start(bf16[2,256,1280]{2,1,0:T(8,128)(2,1)S(1)} %get-tuple-element.59), channel_id=1, source_target_pairs={{0,1},{1,0},{2,3},{3,2},{4,5},{5,4},{6,7},{7,6},{8,9},{9,8},{10,11... | collective-permute-start | bytes 3932168 | tf_op jit(solution)/shard_map/ppermute | solution.py:29
  94.9 7.1 %collective-permute-start.27 = (bf16[128,1280]{1,0:T(8,128)(2,1)S(1)}, bf16[128,1280]{1,0:T(8,128)(2,1)S(1)}, u32[]{:S(2)}, u32[]{:S(2)}) collective-permute-start(bf16[128,1280]{1,0:T(8,128)(2,1)S(1)} %get-tuple-element.63), channel_id=1, source_target_pairs={{0,2},{1,5},{2,0},{3,7},{4,6},{5,1},{6,4},{7,3},{8,10},{9,13},{10,... | collective-permute-start | bytes 983048 | tf_op jit(solution)/shard_map/ppermute | solution.py:40
  96.5 10.2 %collective-permute-start.24 = (bf16[128,1280]{1,0:T(8,128)(2,1)S(1)}, bf16[128,1280]{1,0:T(8,128)(2,1)S(1)}, u32[]{:S(2)}, u32[]{:S(2)}) collective-permute-start(bf16[128,1280]{1,0:T(8,128)(2,1)S(1)} %get-tuple-element.61), channel_id=1, source_target_pairs={{0,2},{1,5},{2,0},{3,7},{4,6},{5,1},{6,4},{7,3},{8,10},{9,13},{10,... | collective-permute-start | bytes 983048 | tf_op jit(solution)/shard_map/ppermute | solution.py:40
  102.2 5.9 %collective-permute-start.28 = (bf16[64,1280]{1,0:T(8,128)(2,1)S(1)}, bf16[64,1280]{1,0:T(8,128)(2,1)S(1)}, u32[]{:S(2)}, u32[]{:S(2)}) collective-permute-start(bf16[64,1280]{1,0:T(8,128)(2,1)S(1)} %slice.87), channel_id=1, source_target_pairs={{0,4},{1,3},{2,6},{3,1},{4,0},{5,7},{6,2},{7,5},{8,12},{9,11},{10,... | collective-permute-start | bytes 491528 | tf_op jit(solution)/shard_map/ppermute | solution.py:40
  106.8 6.0 %collective-permute-start.25 = (bf16[64,1280]{1,0:T(8,128)(2,1)S(1)}, bf16[64,1280]{1,0:T(8,128)(2,1)S(1)}, u32[]{:S(2)}, u32[]{:S(2)}) collective-permute-start(bf16[64,1280]{1,0:T(8,128)(2,1)S(1)} %slice.83), channel_id=1, source_target_pairs={{0,4},{1,3},{2,6},{3,1},{4,0},{5,7},{6,2},{7,5},{8,12},{9,11},{10,... | collective-permute-start | bytes 491528 | tf_op jit(solution)/shard_map/ppermute | solution.py:40
  108.1 7.2 %collective-permute-start.30 = (bf16[32,1280]{1,0:T(8,128)(2,1)S(1)}, bf16[32,1280]{1,0:T(8,128)(2,1)S(1)}, u32[]{:S(2)}, u32[]{:S(2)}) collective-permute-start(bf16[32,1280]{1,0:T(8,128)(2,1)S(1)} %get-tuple-element.68), channel_id=1, source_target_pairs={{0,24},{4,28},{8,16},{12,20},{16,8},{20,12},{24,0},{28,4},{1,25},{... | collective-permute-start | bytes 245768 | tf_op jit(solution)/shard_map/ppermute | solution.py:29
  110.7 8.3 %collective-permute-start.29 = (bf16[32,1280]{1,0:T(8,128)(2,1)S(1)}, bf16[32,1280]{1,0:T(8,128)(2,1)S(1)}, u32[]{:S(2)}, u32[]{:S(2)}) collective-permute-start(bf16[32,1280]{1,0:T(8,128)(2,1)S(1)} %get-tuple-element.69), channel_id=1, source_target_pairs={{0,16},{4,20},{8,24},{12,28},{16,0},{20,4},{24,8},{28,12},{1,17},{... | collective-permute-start | bytes 245768 | tf_op jit(solution)/shard_map/ppermute | solution.py:29
  112.9 6.2 %collective-permute-start.26 = (bf16[32,1280]{1,0:T(8,128)(2,1)S(1)}, bf16[32,1280]{1,0:T(8,128)(2,1)S(1)}, u32[]{:S(2)}, u32[]{:S(2)}) collective-permute-start(bf16[32,1280]{1,0:T(8,128)(2,1)S(1)} %slice.85), channel_id=1, source_target_pairs={{0,8},{4,12},{8,0},{12,4},{16,24},{20,28},{24,16},{28,20},{1,9},{5... | collective-permute-start | bytes 245768 | tf_op jit(solution)/shard_map/ppermute | solution.py:29
  119.1 4.5 %collective-permute-start.31 = (bf16[32,1280]{1,0:T(8,128)(2,1)S(1)}, bf16[32,1280]{1,0:T(8,128)(2,1)S(1)}, u32[]{:S(2)}, u32[]{:S(2)}) collective-permute-start(bf16[32,1280]{1,0:T(8,128)(2,1)S(1)} %add_convert_fusion.4), channel_id=1, source_target_pairs={{0,2},{1,3},{2,0},{3,1},{4,6},{5,7},{6,4},{7,5},{8,10},{9,11},{10,... | collective-permute-start | bytes 245768 | tf_op jit(solution)/shard_map/ppermute | solution.py:29
  123.7 1.5 %collective-permute-start.32 = (bf16[2,32,1280]{2,1,0:T(8,128)(2,1)S(1)}, bf16[2,32,1280]{2,1,0:T(8,128)(2,1)S(1)}, u32[]{:S(2)}, u32[]{:S(2)}) collective-permute-start(bf16[2,32,1280]{2,1,0:T(8,128)(2,1)S(1)} %pad_maximum_fusion.4.refs_0_), channel_id=1, source_target_pairs={{0,1},{1,0},{2,3},{3,2},{4,5},{5,4},{6,7},{7,6},{8,9},{9,8},{10,11... | collective-permute-start | bytes 491528 | tf_op jit(solution)/shard_map/ppermute | solution.py:29

commit v7 on v6

--- a/solution.py
+++ b/solution.py
@@ -143,7 +143,7 @@
     height, rows, head_dim = pieces[0].shape
     deep = height // pairs
     page_count, kv_local, page_size, _ = key_cache.shape
-    block_pages = 6
+    block_pages = 9
     while page_count % block_pages:
         block_pages -= 1
     count = height * len(pieces)

time: 126 us -> 126 us (level)
  no operation moved by 1% of the time
where the time goes in v7:
time: 126 us; the launch traced here: 125 us
  Pallas kernels  41 us (33%)
  starting transfers between devices  40.1 us (32%)
  waiting for transfers between devices  38.2 us (30%)
  local copies, waits for them, and re-layouts  4.09 us (3%)
    ppermute x29, starting transfers between devices, swap(): return lax.ppermute(value, axis, [(i, i ^ mask) for i in range(size)])  35.7 us
    ppermute x29, waiting for transfers between devices, swap(): return lax.ppermute(value, axis, [(i, i ^ mask) for i in range(size)])  29.8 us
    ppermute x4, waiting for transfers between devices, cross(): return lax.ppermute(value, ('seq', 'tp'), pairs)  8.4 us
    pallas_call x1, Pallas kernels, project_queries(): pl.pallas_call(functools.partial(query_kernel, kv_local), out_shape=(jax....  6.81 us
    pallas_call x1, Pallas kernels, gate_up_rest(): pl.pallas_call(functools.partial(rest_kernel, width), out_shape=(jax.Shap...  6.8 us
    pallas_call x1, Pallas kernels, project_out(): pl.pallas_call(functools.partial(out_kernel, len(parts), kv_local), out_s...  4.74 us
    ppermute x4, starting transfers between devices, cross(): return lax.ppermute(value, ('seq', 'tp'), pairs)  4.48 us
    pallas_call x1, Pallas kernels, attend_pages(): pl.pallas_call(functools.partial(pages_kernel, block_pages, len(pieces),...  4.16 us
  transfers between devices with their start and end apart: 33, of which 20 were waited for; matrix products, arithmetic and copies ran while one was open for 2% of the time, Pallas kernels for 14%

profile of v7, /device:TPU:0, one launch (start us, length us, event | category | flops | bytes accessed | tf_op | source)
XLA Modules:
  0.0 125.2 jit_solution(7142023295877509726)
XLA Ops:
  0.7 6.8 %project_queries.1 = (bf16[16,16,128]{2,1,0:T(8,128)(2,1)}, bf16[32,5120]{1,0:T(8,128)(2,1)}, f32[2,32,128]{2,1,0:T(8,128)}) custom-call(s32[1]{0:T(128)} %bitcast.2.me_ref, s32[1,64]{1,0:T(1,128)} %bitcast.39, s32[1,64]{1,0:T(1,128)} %bitcast.38, bf16[4,8,5120]{2,1,0:T(8,128)(2,1)} %input_hbm.1, f32[1,5120]{1,0:T(1,128)} %bitcast.37, ...), custom_call_target="tpu_custom_call" | custom-call | flops 335544320 | bytes 10485760 | tf_op jit(solution)/shard_map/project_queries/pallas_call | solution.py:341
  7.5 5.1 %collective-permute-start.2 = (bf16[16,16,128]{2,1,0:T(8,128)(2,1)}, bf16[16,16,128]{2,1,0:T(8,128)(2,1)S(1)}, u32[]{:S(2)}, u32[]{:S(2)}) collective-permute-start(bf16[16,16,128]{2,1,0:T(8,128)(2,1)} %get-tuple-element.33), channel_id=1, source_target_pairs={{0,24},{4,28},{8,16},{12,20},{16,8},{20,12},{24,0},{28,4},{1,25},{... | collective-permute-start | bytes 196616 | tf_op jit(solution)/shard_map/ppermute | solution.py:29
  12.7 0.6 collective-permute-start
  13.3 0.9 constant_dynamic-update-slice_fusion.3
  14.2 3.0 %collective-permute-done = bf16[16,16,128]{2,1,0:T(8,128)(2,1)S(1)} collective-permute-done((bf16[16,16,128]{2,1,0:T(8,128)(2,1)}, bf16[16,16,128]{2,1,0:T(8,128)(2,1)S(1)}, u32[]{:S(2)}, u32[]{:S(2)}) %collective-permute-start) | collective-permute-done | bytes 65568 | tf_op jit(solution)/shard_map/ppermute | solution.py:29
  17.2 1.3 %collective-permute-done.1 = bf16[16,16,128]{2,1,0:T(8,128)(2,1)S(1)} collective-permute-done((bf16[16,16,128]{2,1,0:T(8,128)(2,1)}, bf16[16,16,128]{2,1,0:T(8,128)(2,1)S(1)}, u32[]{:S(2)}, u32[]{:S(2)}) %collective-permute-start.1) | collective-permute-done | bytes 65568 | tf_op jit(solution)/shard_map/ppermute | solution.py:29
  18.5 1.6 %collective-permute-start.3 = (bf16[64,16,128]{2,1,0:T(8,128)(2,1)S(1)}, bf16[64,16,128]{2,1,0:T(8,128)(2,1)S(1)}, u32[]{:S(2)}, u32[]{:S(2)}) collective-permute-start(bf16[64,16,128]{2,1,0:T(8,128)(2,1)S(1)} %constant_dynamic-update-slice_fusion.query_ref.refs_0_), channel_id=1, source_target_pairs={{0,4},{4,0},{8,12},{12,8},{16,20},{20,16},{24,28},{28,24},{1,5},{5... | collective-permute-start | bytes 786440 | tf_op jit(solution)/shard_map/ppermute | solution.py:29
  20.3 1.0 copy-done
  21.3 0.8 copy-done.2
  22.0 3.8 %recent_part.1.refs_4_ = bf16[1,17,16,128]{3,2,1,0:T(8,128)(2,1)S(1)} custom-call(bf16[32,5120]{1,0:T(8,128)(2,1)S(1)} %copy-done, f32[2,32,128]{2,1,0:T(8,128)S(1)} %copy-done.2, bf16[64,16,128]{2,1,0:T(8,128)(2,1)S(1)} %constant_dynamic-update-slice_fusion.query_ref.refs_0_, bf16[5120,256]{1,0:T(8,128)(2,1)} %key_hbm.1, bf16[5120,256]{1,0:T(8,128)(2,1)} %value_hbm.1), custom_call_target="tpu_custom_call" | custom-call | flops 167772160 | bytes 5242880 | tf_op jit(solution)/shard_map/recent_part/pallas_call | solution.py:426
  25.8 0.7 collective-permute-done.3.refs_1_
  26.5 4.2 %attend_pages.1 = (bf16[2,17,16,128]{3,2,1,0:T(8,128)(2,1)S(1)}, bf16[2,17,16,128]{3,2,1,0:T(8,128)(2,1)S(1)}, bf16[2,17,16,128]{3,2,1,0:T(8,128)(2,1)S(1)}, bf16[2,17,16,128]{3,2,1,0:T(8,128)(2,1)S(1)}) custom-call(s32[36]{0:T(128)S(1)} %get-tuple-element.76.slot_ref, s32[36]{0:T(128)S(1)} %get-tuple-element.75.valid_ref, ...), custom_call_target="tpu_custom_call" | custom-call | flops 150994944 | bytes 9437184 | tf_op jit(solution)/shard_map/attend_pages/pallas_call | solution.py:150
  30.7 1.7 %collective-permute-start.4 = (bf16[2,17,16,128]{3,2,1,0:T(8,128)(2,1)S(1)}, bf16[2,17,16,128]{3,2,1,0:T(8,128)(2,1)S(1)}, u32[]{:S(2)}, u32[]{:S(2)}) collective-permute-start(bf16[2,17,16,128]{3,2,1,0:T(8,128)(2,1)S(1)} %get-tuple-element.37), channel_id=1, source_target_pairs={{0,4},{4,0},{8,12},{12,8},{16,20},{20,16},{24,28},{28,24},{1,5},{5... | collective-permute-start | bytes 417800 | tf_op jit(solution)/shard_map/ppermute | solution.py:29
  32.4 0.4 collective-permute-start.7
  32.8 4.0 %collective-permute-done.4.refs_1_ = bf16[2,17,16,128]{3,2,1,0:T(8,128)(2,1)S(1)} collective-permute-done((bf16[2,17,16,128]{3,2,1,0:T(8,128)(2,1)S(1)}, bf16[2,17,16,128]{3,2,1,0:T(8,128)(2,1)S(1)}, u32[]{:S(2)}, u32[]{:S(2)}) %collective-permute-start.4) | collective-permute-done | bytes 139296 | tf_op jit(solution)/shard_map/ppermute | solution.py:29
  36.7 0.4 merge_parts.2
  37.2 0.3 collective-permute-start.5
  37.4 2.2 %collective-permute-start.6 = (bf16[1,17,16,128]{3,2,1,0:T(8,128)(2,1)S(1)}, bf16[1,17,16,128]{3,2,1,0:T(8,128)(2,1)S(1)}, u32[]{:S(2)}, u32[]{:S(2)}) collective-permute-start(bf16[1,17,16,128]{3,2,1,0:T(8,128)(2,1)S(1)} %get-tuple-element.39), channel_id=1, source_target_pairs={{0,24},{4,28},{8,16},{12,20},{16,8},{20,12},{24,0},{28,4},{1,25},{... | collective-permute-start | bytes 208904 | tf_op jit(solution)/shard_map/ppermute | solution.py:29
  39.6 0.4 merge_parts.3
  40.0 1.2 collective-permute-start.8
  41.2 0.9 constant_dynamic-slice_fusion.input_ref
  42.1 0.5 collective-permute-done.5.refs_0_
  42.6 1.0 collective-permute-done.6.refs_1_
  43.6 0.8 collective-permute-done.8.refs_3_
  44.4 4.7 %project_out.1 = (f32[32,1280]{1,0:T(8,128)S(1)}, bf16[3,32,1280]{2,1,0:T(8,128)(2,1)S(1)}) custom-call(s32[1]{0:T(128)} %bitcast.part_ref, bf16[32,1280]{1,0:T(8,128)(2,1)S(1)} %constant_dynamic-slice_fusion.input_ref, bf16[1024,5120]{1,0:T(8,128)(2,1)} %weight_hbm.3, bf16[1,17,16,128]{3,2,1,0:T(8,128)(2,1)S(1)} %collective-permute-done.5.refs_0_, ...), custom_call_target="tpu_custom_call" | custom-call | flops 335544320 | bytes 10485760 | tf_op jit(solution)/shard_map/project_out/pallas_call | solution.py:493
  49.3 1.4 %collective-permute-done.9 = bf16[2,32,1280]{2,1,0:T(8,128)(2,1)S(1)} collective-permute-done((bf16[2,32,1280]{2,1,0:T(8,128)(2,1)S(1)}, bf16[2,32,1280]{2,1,0:T(8,128)(2,1)S(1)}, u32[]{:S(2)}, u32[]{:S(2)}) %collective-permute-start.9) | collective-permute-done | bytes 163872 | tf_op jit(solution)/shard_map/ppermute | solution.py:29
  50.7 1.7 %collective-permute-start.10 = (bf16[32,1280]{1,0:T(8,128)(2,1)S(1)}, bf16[32,1280]{1,0:T(8,128)(2,1)S(1)}, u32[]{:S(2)}, u32[]{:S(2)}) collective-permute-start(bf16[32,1280]{1,0:T(8,128)(2,1)S(1)} %fusion.2), channel_id=1, source_target_pairs={{0,2},{1,3},{2,0},{3,1},{4,6},{5,7},{6,4},{7,5},{8,10},{9,11},{10,... | collective-permute-start | bytes 245768 | tf_op jit(solution)/shard_map/ppermute | solution.py:29
  52.4 2.9 %collective-permute-done.10 = bf16[32,1280]{1,0:T(8,128)(2,1)S(1)} collective-permute-done((bf16[32,1280]{1,0:T(8,128)(2,1)S(1)}, bf16[32,1280]{1,0:T(8,128)(2,1)S(1)}, u32[]{:S(2)}, u32[]{:S(2)}) %collective-permute-start.10) | collective-permute-done | bytes 81952 | tf_op jit(solution)/shard_map/ppermute | solution.py:29
  55.3 1.2 collective-permute-start.11
  56.5 1.4 %collective-permute-start.15 = (bf16[32,1280]{1,0:T(8,128)(2,1)S(1)}, bf16[32,1280]{1,0:T(8,128)(2,1)S(1)}, u32[]{:S(2)}, u32[]{:S(2)}) collective-permute-start(bf16[32,1280]{1,0:T(8,128)(2,1)S(1)} %fusion.1), channel_id=1, source_target_pairs={{0,24},{4,28},{8,16},{12,20},{16,8},{20,12},{24,0},{28,4},{1,25},{... | collective-permute-start | bytes 245768 | tf_op jit(solution)/shard_map/ppermute | solution.py:29
  57.9 0.9 collective-permute-start.14
  58.8 1.0 collective-permute-done.11
  59.8 1.7 %collective-permute-start.13 = (bf16[64,640]{1,0:T(8,128)(2,1)S(1)}, bf16[64,640]{1,0:T(8,128)(2,1)S(1)}, u32[]{:S(2)}, u32[]{:S(2)}) collective-permute-start(bf16[64,640]{1,0:T(8,128)(2,1)S(1)} %get-tuple-element.48), channel_id=1, source_target_pairs={{0,2},{1,3},{2,0},{3,1},{4,6},{5,7},{6,4},{7,5},{8,10},{9,11},{10,... | collective-permute-start | bytes 245768 | tf_op jit(solution)/shard_map/ppermute | solution.py:29
  61.5 1.5 %collective-permute-start.12 = (bf16[64,640]{1,0:T(8,128)(2,1)S(1)}, bf16[64,640]{1,0:T(8,128)(2,1)S(1)}, u32[]{:S(2)}, u32[]{:S(2)}) collective-permute-start(bf16[64,640]{1,0:T(8,128)(2,1)S(1)} %get-tuple-element.46), channel_id=1, source_target_pairs={{0,4},{4,0},{8,12},{12,8},{16,20},{20,16},{24,28},{28,24},{1,5},{5... | collective-permute-start | bytes 245768 | tf_op jit(solution)/shard_map/ppermute | solution.py:29
  63.1 3.1 %collective-permute-done.14 = bf16[32,1280]{1,0:T(8,128)(2,1)S(1)} collective-permute-done((bf16[32,1280]{1,0:T(8,128)(2,1)S(1)}, bf16[32,1280]{1,0:T(8,128)(2,1)S(1)}, u32[]{:S(2)}, u32[]{:S(2)}) %collective-permute-start.14) | collective-permute-done | bytes 81952 | tf_op jit(solution)/shard_map/ppermute | solution.py:29
  66.2 1.7 %collective-permute-start.20 = (bf16[64,640]{1,0:T(8,128)(2,1)S(1)}, bf16[64,640]{1,0:T(8,128)(2,1)S(1)}, u32[]{:S(2)}, u32[]{:S(2)}) collective-permute-start(bf16[64,640]{1,0:T(8,128)(2,1)S(1)} %get-tuple-element.71), channel_id=1, source_target_pairs={{0,2},{1,3},{2,0},{3,1},{4,6},{5,7},{6,4},{7,5},{8,10},{9,11},{10,... | collective-permute-start | bytes 245768 | tf_op jit(solution)/shard_map/ppermute | solution.py:29
  67.9 1.2 collective-permute-start.18
  69.2 0.9 collective-permute-start.17
  70.1 0.4 collective-permute-start.16
  70.5 2.1 %collective-permute-done.18 = bf16[64,640]{1,0:T(8,128)(2,1)S(1)} collective-permute-done((bf16[64,640]{1,0:T(8,128)(2,1)S(1)}, bf16[64,640]{1,0:T(8,128)(2,1)S(1)}, u32[]{:S(2)}, u32[]{:S(2)}) %collective-permute-start.18) | collective-permute-done | bytes 81952 | tf_op jit(solution)/shard_map/ppermute | solution.py:29
  72.6 0.5 collective-permute-start.19
  73.2 1.1 collective-permute-start.21
  74.3 4.1 %load.1 = (bf16[2,1280,1024]{2,1,0:T(8,128)(2,1)S(1)}, bf16[2,1280,1024]{2,1,0:T(8,128)(2,1)S(1)}) custom-call(s32[1]{0:T(128)} %bitcast.part_ref, bf16[5120,1024]{1,0:T(8,128)(2,1)} %gate_hbm.1, bf16[5120,1024]{1,0:T(8,128)(2,1)} %up_hbm.1), custom_call_target="tpu_custom_call" | custom-call | bytes 10485760 | tf_op jit(solution)/shard_map/load/pallas_call | solution.py:247
  78.7 0.4 copy-done.1
  79.1 4.1 %gate_up_half.1 = (f32[256,1024]{1,0:T(8,128)S(1)}, f32[256,1024]{1,0:T(8,128)S(1)}, f32[256,128]{1,0:T(8,128)S(1)}, bf16[2,1280,1024]{2,1,0:T(8,128)(2,1)S(1)}) custom-call(s32[1]{0:T(128)} %bitcast.part_ref, bf16[2,256,1280]{2,1,0:T(8,128)(2,1)S(1)} %join_groups.1.refs_0_.rows_ref, f32[4,1,1280]{2,1,0:T(1,128)S(1)} %bitcast.27, ...), custom_call_target="tpu_custom_call" | custom-call | flops 2684354560 | bytes 12582912 | tf_op jit(solution)/shard_map/gate_up_half/pallas_call | solution.py:608
  83.2 6.8 %gate_up_rest.1 = (bf16[256,1024]{1,0:T(8,128)(2,1)S(1)}, bf16[2,256,1280]{2,1,0:T(8,128)(2,1)S(1)}) custom-call(s32[1]{0:T(128)} %bitcast.part_ref, bf16[2,256,1280]{2,1,0:T(8,128)(2,1)S(1)} %collective-permute-done.22.refs_1_.rows_ref, f32[4,1,1280]{2,1,0:T(1,128)S(1)} %bitcast.28, f32[256,1024]{1,0:T(8,128)S(1)} %get-tuple-element.54.old_gate_ref, ...), custom_call_target="tpu_custom_call" | custom-call | flops 4026531840 | bytes 15728640 | tf_op jit(solution)/shard_map/gate_up_rest/pallas_call | solution.py:676
  90.2 3.7 %down_half.1.own_ref = bf16[2,256,1280]{2,1,0:T(8,128)(2,1)S(1)} custom-call(s32[1]{0:T(128)} %bitcast.part_ref, bf16[256,1024]{1,0:T(8,128)(2,1)S(1)} %get-tuple-element.58.activation_ref, bf16[1024,5120]{1,0:T(8,128)(2,1)} %down_hbm.3), custom_call_target="tpu_custom_call" | custom-call | flops 1342177280 | bytes 5242880 | tf_op jit(solution)/shard_map/down_half/pallas_call | solution.py:714
  94.0 0.3 sum_terms.1
  94.3 1.6 %collective-permute-start.27 = (bf16[128,1280]{1,0:T(8,128)(2,1)S(1)}, bf16[128,1280]{1,0:T(8,128)(2,1)S(1)}, u32[]{:S(2)}, u32[]{:S(2)}) collective-permute-start(bf16[128,1280]{1,0:T(8,128)(2,1)S(1)} %get-tuple-element.63), channel_id=1, source_target_pairs={{0,2},{1,5},{2,0},{3,7},{4,6},{5,1},{6,4},{7,3},{8,10},{9,13},{10,... | collective-permute-start | bytes 983048 | tf_op jit(solution)/shard_map/ppermute | solution.py:40
  95.9 0.5 collective-permute-start.24
  96.4 5.0 %collective-permute-done.27 = bf16[128,1280]{1,0:T(8,128)(2,1)S(1)} collective-permute-done((bf16[128,1280]{1,0:T(8,128)(2,1)S(1)}, bf16[128,1280]{1,0:T(8,128)(2,1)S(1)}, u32[]{:S(2)}, u32[]{:S(2)}) %collective-permute-start.27) | collective-permute-done | bytes 327712 | tf_op jit(solution)/shard_map/ppermute | solution.py:40
  101.5 1.1 collective-permute-start.28
  102.7 3.3 %collective-permute-done.24 = bf16[128,1280]{1,0:T(8,128)(2,1)S(1)} collective-permute-done((bf16[128,1280]{1,0:T(8,128)(2,1)S(1)}, bf16[128,1280]{1,0:T(8,128)(2,1)S(1)}, u32[]{:S(2)}, u32[]{:S(2)}) %collective-permute-start.24) | collective-permute-done | bytes 327712 | tf_op jit(solution)/shard_map/ppermute | solution.py:40
  106.1 1.3 %collective-permute-start.25 = (bf16[64,1280]{1,0:T(8,128)(2,1)S(1)}, bf16[64,1280]{1,0:T(8,128)(2,1)S(1)}, u32[]{:S(2)}, u32[]{:S(2)}) collective-permute-start(bf16[64,1280]{1,0:T(8,128)(2,1)S(1)} %slice.83), channel_id=1, source_target_pairs={{0,4},{1,3},{2,6},{3,1},{4,0},{5,7},{6,2},{7,5},{8,12},{9,11},{10,... | collective-permute-start | bytes 491528 | tf_op jit(solution)/shard_map/ppermute | solution.py:40
  107.5 2.6 %collective-permute-start.30 = (bf16[32,1280]{1,0:T(8,128)(2,1)S(1)}, bf16[32,1280]{1,0:T(8,128)(2,1)S(1)}, u32[]{:S(2)}, u32[]{:S(2)}) collective-permute-start(bf16[32,1280]{1,0:T(8,128)(2,1)S(1)} %get-tuple-element.68), channel_id=1, source_target_pairs={{0,24},{4,28},{8,16},{12,20},{16,8},{20,12},{24,0},{28,4},{1,25},{... | collective-permute-start | bytes 245768 | tf_op jit(solution)/shard_map/ppermute | solution.py:29
  110.1 2.1 %collective-permute-start.29 = (bf16[32,1280]{1,0:T(8,128)(2,1)S(1)}, bf16[32,1280]{1,0:T(8,128)(2,1)S(1)}, u32[]{:S(2)}, u32[]{:S(2)}) collective-permute-start(bf16[32,1280]{1,0:T(8,128)(2,1)S(1)} %get-tuple-element.69), channel_id=1, source_target_pairs={{0,16},{4,20},{8,24},{12,28},{16,0},{20,4},{24,8},{28,12},{1,17},{... | collective-permute-start | bytes 245768 | tf_op jit(solution)/shard_map/ppermute | solution.py:29
  112.2 2.2 %collective-permute-start.26 = (bf16[32,1280]{1,0:T(8,128)(2,1)S(1)}, bf16[32,1280]{1,0:T(8,128)(2,1)S(1)}, u32[]{:S(2)}, u32[]{:S(2)}) collective-permute-start(bf16[32,1280]{1,0:T(8,128)(2,1)S(1)} %slice.85), channel_id=1, source_target_pairs={{0,8},{4,12},{8,0},{12,4},{16,24},{20,28},{24,16},{28,20},{1,9},{5... | collective-permute-start | bytes 245768 | tf_op jit(solution)/shard_map/ppermute | solution.py:29
  114.4 0.3 collective-permute-done.30.refs_1_
  114.7 3.7 %collective-permute-done.29.refs_0_ = bf16[32,1280]{1,0:T(8,128)(2,1)S(1)} collective-permute-done((bf16[32,1280]{1,0:T(8,128)(2,1)S(1)}, bf16[32,1280]{1,0:T(8,128)(2,1)S(1)}, u32[]{:S(2)}, u32[]{:S(2)}) %collective-permute-start.29) | collective-permute-done | bytes 81952 | tf_op jit(solution)/shard_map/ppermute | solution.py:29
  118.5 1.1 collective-permute-start.31
  119.5 3.5 %collective-permute-done.31 = bf16[32,1280]{1,0:T(8,128)(2,1)S(1)} collective-permute-done((bf16[32,1280]{1,0:T(8,128)(2,1)S(1)}, bf16[32,1280]{1,0:T(8,128)(2,1)S(1)}, u32[]{:S(2)}, u32[]{:S(2)}) %collective-permute-start.31) | collective-permute-done | bytes 81952 | tf_op jit(solution)/shard_map/ppermute | solution.py:29
  123.1 0.8 assemble.2
  123.8 0.6 collective-permute-done.32.refs_1_
  124.5 0.7 assemble.3
  (71 shorter events, 1.7 us)
Async XLA Ops:
  0.6 25.8 %slice-start = ((s8[4718592]{0:T(1024)(128)(4,1)}), s8[4194304]{0:T(1024)(128)(4,1)S(1)}, s32[]{:S(2)}) async-start(s8[4718592]{0:T(1024)(128)(4,1)} %bitcast.23), calls=%async_computation | async-start | bytes 8388608
  0.6 25.8 %slice-start.2 = ((s8[4718592]{0:T(1024)(128)(4,1)}), s8[4194304]{0:T(1024)(128)(4,1)S(1)}, s32[]{:S(2)}) async-start(s8[4718592]{0:T(1024)(128)(4,1)} %bitcast.25), calls=%async_computation.2 | async-start | bytes 8388608
  0.7 19.4 %copy-start.3 = (s32[64]{0:T(128)S(1)}, s32[64]{0:T(128)}, u32[]{:S(2)}) copy-start(s32[64]{0:T(128)} %param.28) | copy-start | bytes 772
  0.7 19.4 %copy-start.4 = (s32[64]{0:T(128)S(1)}, s32[64]{0:T(128)}, u32[]{:S(2)}) copy-start(s32[64]{0:T(128)} %param.31) | copy-start | bytes 772
  0.7 19.4 %copy-start.5 = (s32[36]{0:T(128)S(1)}, s32[36]{0:T(128)}, u32[]{:S(2)}) copy-start(s32[36]{0:T(128)} %param.29) | copy-start | bytes 436
  0.7 19.6 %copy-start.6 = (s32[36]{0:T(128)S(1)}, s32[36]{0:T(128)}, u32[]{:S(2)}) copy-start(s32[36]{0:T(128)} %param.30) | copy-start | bytes 436
  0.7 25.8 %slice-start.1 = ((s8[4718592]{0:T(1024)(128)(4,1)}), s8[524288]{0:T(1024)(128)(4,1)S(1)}, s32[]{:S(2)}) async-start(s8[4718592]{0:T(1024)(128)(4,1)} %bitcast.23), calls=%async_computation.1 | async-start | bytes 1048576
  0.7 25.8 %slice-start.3 = ((s8[4718592]{0:T(1024)(128)(4,1)}), s8[524288]{0:T(1024)(128)(4,1)S(1)}, s32[]{:S(2)}) async-start(s8[4718592]{0:T(1024)(128)(4,1)} %bitcast.25), calls=%async_computation.3 | async-start | bytes 1048576
  7.5 10.9 %collective-permute-start.2 = (bf16[16,16,128]{2,1,0:T(8,128)(2,1)}, bf16[16,16,128]{2,1,0:T(8,128)(2,1)S(1)}, u32[]{:S(2)}, u32[]{:S(2)}) collective-permute-start(bf16[16,16,128]{2,1,0:T(8,128)(2,1)} %get-tuple-element.33), channel_id=1, source_target_pairs={{0,24},{4,28},{8,16},{12,20},{16,8},{20,12},{24,0},{28,4},{1,25},{... | collective-permute-start | bytes 196616 | tf_op jit(solution)/shard_map/ppermute | solution.py:29
  12.7 5.8 %collective-permute-start.1 = (bf16[16,16,128]{2,1,0:T(8,128)(2,1)}, bf16[16,16,128]{2,1,0:T(8,128)(2,1)S(1)}, u32[]{:S(2)}, u32[]{:S(2)}) collective-permute-start(bf16[16,16,128]{2,1,0:T(8,128)(2,1)} %get-tuple-element.33), channel_id=1, source_target_pairs={{0,16},{4,20},{8,24},{12,28},{16,0},{20,4},{24,8},{28,12},{1,17},{... | collective-permute-start | bytes 196616 | tf_op jit(solution)/shard_map/ppermute | solution.py:29
  12.7 4.5 %collective-permute-start = (bf16[16,16,128]{2,1,0:T(8,128)(2,1)}, bf16[16,16,128]{2,1,0:T(8,128)(2,1)S(1)}, u32[]{:S(2)}, u32[]{:S(2)}) collective-permute-start(bf16[16,16,128]{2,1,0:T(8,128)(2,1)} %get-tuple-element.33), channel_id=1, source_target_pairs={{0,8},{4,12},{8,0},{12,4},{16,24},{20,28},{24,16},{28,20},{1,9},{5... | collective-permute-start | bytes 196616 | tf_op jit(solution)/shard_map/ppermute | solution.py:29
  18.5 7.9 %collective-permute-start.3 = (bf16[64,16,128]{2,1,0:T(8,128)(2,1)S(1)}, bf16[64,16,128]{2,1,0:T(8,128)(2,1)S(1)}, u32[]{:S(2)}, u32[]{:S(2)}) collective-permute-start(bf16[64,16,128]{2,1,0:T(8,128)(2,1)S(1)} %constant_dynamic-update-slice_fusion.query_ref.refs_0_), channel_id=1, source_target_pairs={{0,4},{4,0},{8,12},{12,8},{16,20},{20,16},{24,28},{28,24},{1,5},{5... | collective-permute-start | bytes 786440 | tf_op jit(solution)/shard_map/ppermute | solution.py:29
  20.3 1.0 copy-start
  21.3 0.8 copy-start.2
  30.7 6.1 %collective-permute-start.4 = (bf16[2,17,16,128]{3,2,1,0:T(8,128)(2,1)S(1)}, bf16[2,17,16,128]{3,2,1,0:T(8,128)(2,1)S(1)}, u32[]{:S(2)}, u32[]{:S(2)}) collective-permute-start(bf16[2,17,16,128]{3,2,1,0:T(8,128)(2,1)S(1)} %get-tuple-element.37), channel_id=1, source_target_pairs={{0,4},{4,0},{8,12},{12,8},{16,20},{20,16},{24,28},{28,24},{1,5},{5... | collective-permute-start | bytes 417800 | tf_op jit(solution)/shard_map/ppermute | solution.py:29
  32.4 7.2 %collective-permute-start.7 = (bf16[2,17,16,128]{3,2,1,0:T(8,128)(2,1)S(1)}, bf16[2,17,16,128]{3,2,1,0:T(8,128)(2,1)S(1)}, u32[]{:S(2)}, u32[]{:S(2)}) collective-permute-start(bf16[2,17,16,128]{3,2,1,0:T(8,128)(2,1)S(1)} %get-tuple-element.41), channel_id=1, source_target_pairs={{0,4},{4,0},{8,12},{12,8},{16,20},{20,16},{24,28},{28,24},{1,5},{5... | collective-permute-start | bytes 417800 | tf_op jit(solution)/shard_map/ppermute | solution.py:29
  37.2 5.4 %collective-permute-start.5 = (bf16[1,17,16,128]{3,2,1,0:T(8,128)(2,1)S(1)}, bf16[1,17,16,128]{3,2,1,0:T(8,128)(2,1)S(1)}, u32[]{:S(2)}, u32[]{:S(2)}) collective-permute-start(bf16[1,17,16,128]{3,2,1,0:T(8,128)(2,1)S(1)} %get-tuple-element.38), channel_id=1, source_target_pairs={{0,16},{4,20},{8,24},{12,28},{16,0},{20,4},{24,8},{28,12},{1,17},{... | collective-permute-start | bytes 208904 | tf_op jit(solution)/shard_map/ppermute | solution.py:29
  37.4 6.2 %collective-permute-start.6 = (bf16[1,17,16,128]{3,2,1,0:T(8,128)(2,1)S(1)}, bf16[1,17,16,128]{3,2,1,0:T(8,128)(2,1)S(1)}, u32[]{:S(2)}, u32[]{:S(2)}) collective-permute-start(bf16[1,17,16,128]{3,2,1,0:T(8,128)(2,1)S(1)} %get-tuple-element.39), channel_id=1, source_target_pairs={{0,24},{4,28},{8,16},{12,20},{16,8},{20,12},{24,0},{28,4},{1,25},{... | collective-permute-start | bytes 208904 | tf_op jit(solution)/shard_map/ppermute | solution.py:29
  40.0 4.4 %collective-permute-start.8 = (bf16[1,17,16,128]{3,2,1,0:T(8,128)(2,1)S(1)}, bf16[1,17,16,128]{3,2,1,0:T(8,128)(2,1)S(1)}, u32[]{:S(2)}, u32[]{:S(2)}) collective-permute-start(bf16[1,17,16,128]{3,2,1,0:T(8,128)(2,1)S(1)} %get-tuple-element.43), channel_id=1, source_target_pairs={{0,8},{4,12},{8,0},{12,4},{16,24},{20,28},{24,16},{28,20},{1,9},{5... | collective-permute-start | bytes 208904 | tf_op jit(solution)/shard_map/ppermute | solution.py:29
  49.2 1.5 %collective-permute-start.9 = (bf16[2,32,1280]{2,1,0:T(8,128)(2,1)S(1)}, bf16[2,32,1280]{2,1,0:T(8,128)(2,1)S(1)}, u32[]{:S(2)}, u32[]{:S(2)}) collective-permute-start(bf16[2,32,1280]{2,1,0:T(8,128)(2,1)S(1)} %pad_maximum_fusion), channel_id=1, source_target_pairs={{0,1},{1,0},{2,3},{3,2},{4,5},{5,4},{6,7},{7,6},{8,9},{9,8},{10,11... | collective-permute-start | bytes 491528 | tf_op jit(solution)/shard_map/ppermute | solution.py:29
  50.7 4.6 %collective-permute-start.10 = (bf16[32,1280]{1,0:T(8,128)(2,1)S(1)}, bf16[32,1280]{1,0:T(8,128)(2,1)S(1)}, u32[]{:S(2)}, u32[]{:S(2)}) collective-permute-start(bf16[32,1280]{1,0:T(8,128)(2,1)S(1)} %fusion.2), channel_id=1, source_target_pairs={{0,2},{1,3},{2,0},{3,1},{4,6},{5,7},{6,4},{7,5},{8,10},{9,11},{10,... | collective-permute-start | bytes 245768 | tf_op jit(solution)/shard_map/ppermute | solution.py:29
  55.3 4.5 %collective-permute-start.11 = (bf16[32,1280]{1,0:T(8,128)(2,1)S(1)}, bf16[32,1280]{1,0:T(8,128)(2,1)S(1)}, u32[]{:S(2)}, u32[]{:S(2)}) collective-permute-start(bf16[32,1280]{1,0:T(8,128)(2,1)S(1)} %fusion.1), channel_id=1, source_target_pairs={{0,8},{4,12},{8,0},{12,4},{16,24},{20,28},{24,16},{28,20},{1,9},{5... | collective-permute-start | bytes 245768 | tf_op jit(solution)/shard_map/ppermute | solution.py:29
  56.5 6.6 %collective-permute-start.15 = (bf16[32,1280]{1,0:T(8,128)(2,1)S(1)}, bf16[32,1280]{1,0:T(8,128)(2,1)S(1)}, u32[]{:S(2)}, u32[]{:S(2)}) collective-permute-start(bf16[32,1280]{1,0:T(8,128)(2,1)S(1)} %fusion.1), channel_id=1, source_target_pairs={{0,24},{4,28},{8,16},{12,20},{16,8},{20,12},{24,0},{28,4},{1,25},{... | collective-permute-start | bytes 245768 | tf_op jit(solution)/shard_map/ppermute | solution.py:29
  57.9 8.2 %collective-permute-start.14 = (bf16[32,1280]{1,0:T(8,128)(2,1)S(1)}, bf16[32,1280]{1,0:T(8,128)(2,1)S(1)}, u32[]{:S(2)}, u32[]{:S(2)}) collective-permute-start(bf16[32,1280]{1,0:T(8,128)(2,1)S(1)} %fusion.1), channel_id=1, source_target_pairs={{0,16},{4,20},{8,24},{12,28},{16,0},{20,4},{24,8},{28,12},{1,17},{... | collective-permute-start | bytes 245768 | tf_op jit(solution)/shard_map/ppermute | solution.py:29
  59.8 6.3 %collective-permute-start.13 = (bf16[64,640]{1,0:T(8,128)(2,1)S(1)}, bf16[64,640]{1,0:T(8,128)(2,1)S(1)}, u32[]{:S(2)}, u32[]{:S(2)}) collective-permute-start(bf16[64,640]{1,0:T(8,128)(2,1)S(1)} %get-tuple-element.48), channel_id=1, source_target_pairs={{0,2},{1,3},{2,0},{3,1},{4,6},{5,7},{6,4},{7,5},{8,10},{9,11},{10,... | collective-permute-start | bytes 245768 | tf_op jit(solution)/shard_map/ppermute | solution.py:29
  61.5 4.7 %collective-permute-start.12 = (bf16[64,640]{1,0:T(8,128)(2,1)S(1)}, bf16[64,640]{1,0:T(8,128)(2,1)S(1)}, u32[]{:S(2)}, u32[]{:S(2)}) collective-permute-start(bf16[64,640]{1,0:T(8,128)(2,1)S(1)} %get-tuple-element.46), channel_id=1, source_target_pairs={{0,4},{4,0},{8,12},{12,8},{16,20},{20,16},{24,28},{28,24},{1,5},{5... | collective-permute-start | bytes 245768 | tf_op jit(solution)/shard_map/ppermute | solution.py:29
  66.2 6.9 %collective-permute-start.20 = (bf16[64,640]{1,0:T(8,128)(2,1)S(1)}, bf16[64,640]{1,0:T(8,128)(2,1)S(1)}, u32[]{:S(2)}, u32[]{:S(2)}) collective-permute-start(bf16[64,640]{1,0:T(8,128)(2,1)S(1)} %get-tuple-element.71), channel_id=1, source_target_pairs={{0,2},{1,3},{2,0},{3,1},{4,6},{5,7},{6,4},{7,5},{8,10},{9,11},{10,... | collective-permute-start | bytes 245768 | tf_op jit(solution)/shard_map/ppermute | solution.py:29
  67.9 4.6 %collective-permute-start.18 = (bf16[64,640]{1,0:T(8,128)(2,1)S(1)}, bf16[64,640]{1,0:T(8,128)(2,1)S(1)}, u32[]{:S(2)}, u32[]{:S(2)}) collective-permute-start(bf16[64,640]{1,0:T(8,128)(2,1)S(1)} %get-tuple-element.72), channel_id=1, source_target_pairs={{0,4},{4,0},{8,12},{12,8},{16,20},{20,16},{24,28},{28,24},{1,5},{5... | collective-permute-start | bytes 245768 | tf_op jit(solution)/shard_map/ppermute | solution.py:29
  69.2 9.2 %collective-permute-start.17 = (bf16[2,64,640]{2,1,0:T(8,128)(2,1)S(1)}, bf16[2,64,640]{2,1,0:T(8,128)(2,1)S(1)}, u32[]{:S(2)}, u32[]{:S(2)}) collective-permute-start(bf16[2,64,640]{2,1,0:T(8,128)(2,1)S(1)} %pad_maximum_fusion.1.refs_2_), channel_id=1, source_target_pairs={{0,4},{4,0},{8,12},{12,8},{16,20},{20,16},{24,28},{28,24},{1,5},{5... | collective-permute-start | bytes 491528 | tf_op jit(solution)/shard_map/ppermute | solution.py:29
  70.1 8.4 %collective-permute-start.16 = (bf16[128,640]{1,0:T(8,128)(2,1)S(1)}, bf16[128,640]{1,0:T(8,128)(2,1)S(1)}, u32[]{:S(2)}, u32[]{:S(2)}) collective-permute-start(bf16[128,640]{1,0:T(8,128)(2,1)S(1)} %constant_dynamic-update-slice_fusion.4.refs_0_), channel_id=1, source_target_pairs={{0,2},{1,3},{2,0},{3,1},{4,6},{5,7},{6,4},{7,5},{8,10},{9,11},{10,... | collective-permute-start | bytes 491528 | tf_op jit(solution)/shard_map/ppermute | solution.py:29
  72.6 5.9 %collective-permute-start.19 = (bf16[128,640]{1,0:T(8,128)(2,1)S(1)}, bf16[128,640]{1,0:T(8,128)(2,1)S(1)}, u32[]{:S(2)}, u32[]{:S(2)}) collective-permute-start(bf16[128,640]{1,0:T(8,128)(2,1)S(1)} %pad_maximum_fusion.2.refs_4_), channel_id=1, source_target_pairs={{0,2},{1,3},{2,0},{3,1},{4,6},{5,7},{6,4},{7,5},{8,10},{9,11},{10,... | collective-permute-start | bytes 491528 | tf_op jit(solution)/shard_map/ppermute | solution.py:29
  73.2 5.4 %collective-permute-start.21 = (bf16[2,64,640]{2,1,0:T(8,128)(2,1)S(1)}, bf16[2,64,640]{2,1,0:T(8,128)(2,1)S(1)}, u32[]{:S(2)}, u32[]{:S(2)}) collective-permute-start(bf16[2,64,640]{2,1,0:T(8,128)(2,1)S(1)} %pad_maximum_fusion.3.refs_6_), channel_id=1, source_target_pairs={{0,4},{4,0},{8,12},{12,8},{16,20},{20,16},{24,28},{28,24},{1,5},{5... | collective-permute-start | bytes 491528 | tf_op jit(solution)/shard_map/ppermute | solution.py:29
  78.4 0.7 copy-start.1
  78.7 4.6 %collective-permute-start.22 = (bf16[2,256,1280]{2,1,0:T(8,128)(2,1)S(1)}, bf16[2,256,1280]{2,1,0:T(8,128)(2,1)S(1)}, u32[]{:S(2)}, u32[]{:S(2)}) collective-permute-start(bf16[2,256,1280]{2,1,0:T(8,128)(2,1)S(1)} %join_groups.1.refs_0_.rows_ref), channel_id=1, source_target_pairs={{0,1},{1,0},{2,3},{3,2},{4,5},{5,4},{6,7},{7,6},{8,9},{9,8},{10,11... | collective-permute-start | bytes 3932168 | tf_op jit(solution)/shard_map/ppermute | solution.py:29
  90.0 3.9 %collective-permute-start.23 = (bf16[2,256,1280]{2,1,0:T(8,128)(2,1)S(1)}, bf16[2,256,1280]{2,1,0:T(8,128)(2,1)S(1)}, u32[]{:S(2)}, u32[]{:S(2)}) collective-permute-start(bf16[2,256,1280]{2,1,0:T(8,128)(2,1)S(1)} %get-tuple-element.59), channel_id=1, source_target_pairs={{0,1},{1,0},{2,3},{3,2},{4,5},{5,4},{6,7},{7,6},{8,9},{9,8},{10,11... | collective-permute-start | bytes 3932168 | tf_op jit(solution)/shard_map/ppermute | solution.py:29
  94.3 7.1 %collective-permute-start.27 = (bf16[128,1280]{1,0:T(8,128)(2,1)S(1)}, bf16[128,1280]{1,0:T(8,128)(2,1)S(1)}, u32[]{:S(2)}, u32[]{:S(2)}) collective-permute-start(bf16[128,1280]{1,0:T(8,128)(2,1)S(1)} %get-tuple-element.63), channel_id=1, source_target_pairs={{0,2},{1,5},{2,0},{3,7},{4,6},{5,1},{6,4},{7,3},{8,10},{9,13},{10,... | collective-permute-start | bytes 983048 | tf_op jit(solution)/shard_map/ppermute | solution.py:40
  95.9 10.1 %collective-permute-start.24 = (bf16[128,1280]{1,0:T(8,128)(2,1)S(1)}, bf16[128,1280]{1,0:T(8,128)(2,1)S(1)}, u32[]{:S(2)}, u32[]{:S(2)}) collective-permute-start(bf16[128,1280]{1,0:T(8,128)(2,1)S(1)} %get-tuple-element.61), channel_id=1, source_target_pairs={{0,2},{1,5},{2,0},{3,7},{4,6},{5,1},{6,4},{7,3},{8,10},{9,13},{10,... | collective-permute-start | bytes 983048 | tf_op jit(solution)/shard_map/ppermute | solution.py:40
  101.5 5.9 %collective-permute-start.28 = (bf16[64,1280]{1,0:T(8,128)(2,1)S(1)}, bf16[64,1280]{1,0:T(8,128)(2,1)S(1)}, u32[]{:S(2)}, u32[]{:S(2)}) collective-permute-start(bf16[64,1280]{1,0:T(8,128)(2,1)S(1)} %slice.87), channel_id=1, source_target_pairs={{0,4},{1,3},{2,6},{3,1},{4,0},{5,7},{6,2},{7,5},{8,12},{9,11},{10,... | collective-permute-start | bytes 491528 | tf_op jit(solution)/shard_map/ppermute | solution.py:40
  106.1 6.0 %collective-permute-start.25 = (bf16[64,1280]{1,0:T(8,128)(2,1)S(1)}, bf16[64,1280]{1,0:T(8,128)(2,1)S(1)}, u32[]{:S(2)}, u32[]{:S(2)}) collective-permute-start(bf16[64,1280]{1,0:T(8,128)(2,1)S(1)} %slice.83), channel_id=1, source_target_pairs={{0,4},{1,3},{2,6},{3,1},{4,0},{5,7},{6,2},{7,5},{8,12},{9,11},{10,... | collective-permute-start | bytes 491528 | tf_op jit(solution)/shard_map/ppermute | solution.py:40
  107.5 7.3 %collective-permute-start.30 = (bf16[32,1280]{1,0:T(8,128)(2,1)S(1)}, bf16[32,1280]{1,0:T(8,128)(2,1)S(1)}, u32[]{:S(2)}, u32[]{:S(2)}) collective-permute-start(bf16[32,1280]{1,0:T(8,128)(2,1)S(1)} %get-tuple-element.68), channel_id=1, source_target_pairs={{0,24},{4,28},{8,16},{12,20},{16,8},{20,12},{24,0},{28,4},{1,25},{... | collective-permute-start | bytes 245768 | tf_op jit(solution)/shard_map/ppermute | solution.py:29
  110.1 8.3 %collective-permute-start.29 = (bf16[32,1280]{1,0:T(8,128)(2,1)S(1)}, bf16[32,1280]{1,0:T(8,128)(2,1)S(1)}, u32[]{:S(2)}, u32[]{:S(2)}) collective-permute-start(bf16[32,1280]{1,0:T(8,128)(2,1)S(1)} %get-tuple-element.69), channel_id=1, source_target_pairs={{0,16},{4,20},{8,24},{12,28},{16,0},{20,4},{24,8},{28,12},{1,17},{... | collective-permute-start | bytes 245768 | tf_op jit(solution)/shard_map/ppermute | solution.py:29
  112.2 6.2 %collective-permute-start.26 = (bf16[32,1280]{1,0:T(8,128)(2,1)S(1)}, bf16[32,1280]{1,0:T(8,128)(2,1)S(1)}, u32[]{:S(2)}, u32[]{:S(2)}) collective-permute-start(bf16[32,1280]{1,0:T(8,128)(2,1)S(1)} %slice.85), channel_id=1, source_target_pairs={{0,8},{4,12},{8,0},{12,4},{16,24},{20,28},{24,16},{28,20},{1,9},{5... | collective-permute-start | bytes 245768 | tf_op jit(solution)/shard_map/ppermute | solution.py:29
  118.5 4.5 %collective-permute-start.31 = (bf16[32,1280]{1,0:T(8,128)(2,1)S(1)}, bf16[32,1280]{1,0:T(8,128)(2,1)S(1)}, u32[]{:S(2)}, u32[]{:S(2)}) collective-permute-start(bf16[32,1280]{1,0:T(8,128)(2,1)S(1)} %add_convert_fusion.4), channel_id=1, source_target_pairs={{0,2},{1,3},{2,0},{3,1},{4,6},{5,7},{6,4},{7,5},{8,10},{9,11},{10,... | collective-permute-start | bytes 245768 | tf_op jit(solution)/shard_map/ppermute | solution.py:29
  123.0 1.5 %collective-permute-start.32 = (bf16[2,32,1280]{2,1,0:T(8,128)(2,1)S(1)}, bf16[2,32,1280]{2,1,0:T(8,128)(2,1)S(1)}, u32[]{:S(2)}, u32[]{:S(2)}) collective-permute-start(bf16[2,32,1280]{2,1,0:T(8,128)(2,1)S(1)} %pad_maximum_fusion.4.refs_0_), channel_id=1, source_target_pairs={{0,1},{1,0},{2,3},{3,2},{4,5},{5,4},{6,7},{7,6},{8,9},{9,8},{10,11... | collective-permute-start | bytes 491528 | tf_op jit(solution)/shard_map/ppermute | solution.py:29
